TPU v7x, 32 devices: a whole 2x2x4 slice. The times are simulated.
32 devices in a mesh: lat: 4 (over y, core), wave: 8 (over z, x).
Axes of the slice: x: 2, y: 2, z: 4, core: 2. Of those that a mesh axis runs over, the one named last changes fastest.
Arguments:
- fourier: bfloat16 [256, 12, 1280], P(('lat', 'wave')), may hold values from -6 to 6
- wave_table: int32 [1280], replicated, may hold values from 0 to 1279, each once
- legendre: bfloat16 [1280, 128, 1280], P('wave', 'lat'), may hold values from -0.5 to 0.5
Outputs:
- spectral: float32 [1280, 12, 1280], P('wave', None, 'lat')
Inputs may be any that keep to these rules, and one draw needn't show every extreme that they name: `wave_table`: every wavenumber 0 to 1279 stands in exactly one slot.
All inputs are finite; a program needn't handle non-finite values.
Results may differ from a plain program's by a relative error of at most 0.0031.
Values may be sent and summed in bfloat16 or wider, within the bound.
No kernel may reach another device: no remote copies, remote signals or barrier semaphores. Data moves between devices by JAX's collectives and lax.ppermute only.
A program may use at most 192 MiB of HBM per device.

v0:
```python
import jax
import jax.numpy as jnp
from jax import lax
from jax.sharding import PartitionSpec as P


def partner(block, axis, stride):
    count = lax.axis_size(axis)
    route = []
    for low in range(count):
        high = low | 1 << stride
        if high != low and high < count:
            route += [(low, high), (high, low)]
    return lax.ppermute(block, axis, route)


def local(fourier, wave_table, legendre):
    slot_count, pair_count, degree_count = legendre.shape
    lat_count = lax.axis_size("lat")
    half_degrees = degree_count // 2
    slice_width = degree_count // lat_count
    lat_index = lax.axis_index("lat")
    ordered = jnp.take(fourier, wave_table, axis=2)
    arrived = lax.all_to_all(ordered, "wave", split_axis=2, concat_axis=0, tiled=True)
    local_rows = jnp.transpose(arrived, (2, 1, 0))
    kept_rows = local_rows[:, :, :pair_count]
    received = local_rows[:, :, pair_count:]
    for bit_number in range(lat_count.bit_length() - 1):
        received = partner(received, "lat", bit_number)
    northern = lat_index < lat_count // 2
    north_rows = jnp.where(northern, kept_rows, received).astype(jnp.float32)
    south_rows = jnp.where(northern, jnp.flip(received, 2), jnp.flip(kept_rows, 2)).astype(
        jnp.float32
    )
    even_part = (north_rows + south_rows).astype(jnp.bfloat16)
    odd_part = (north_rows - south_rows).astype(jnp.bfloat16)
    my_waves = lax.dynamic_slice_in_dim(wave_table, lax.axis_index("wave") * slot_count, slot_count)
    even_out = jnp.einsum(
        "mcp,mpk->mck", even_part, legendre[:, :, :half_degrees], preferred_element_type=jnp.float32
    )
    odd_out = jnp.einsum(
        "mcp,mpk->mck", odd_part, legendre[:, :, half_degrees:], preferred_element_type=jnp.float32
    )
    partial_terms = jnp.concatenate([even_out, odd_out], axis=2)
    spectral = lax.psum_scatter(partial_terms, "lat", scatter_dimension=2, tiled=True)
    degree_slot = lat_index * slice_width + jnp.arange(slice_width, dtype=jnp.int32)
    offsets = jnp.where(
        degree_slot < half_degrees, 2 * degree_slot, 2 * (degree_slot - half_degrees) + 1
    )
    inside = offsets[None, None, :] < (degree_count - my_waves)[:, None, None]
    return jnp.where(inside, spectral, jnp.zeros_like(spectral))


def solution(mesh):
    in_specs = (P(("lat", "wave"), None, None), P(), P("wave", "lat", None))
    out_specs = P("wave", None, "lat")
    return jax.shard_map(local, mesh=mesh, in_specs=in_specs, out_specs=out_specs, check_vma=False)
```

profile of v0, /device:TPU:0, one launch (start us, length us, event | category | flops | bytes accessed | tf_op | source)
XLA Modules:
  0.0 351.0 jit_solution(13069990917412926203)
XLA Ops:
  6.5 0.0 reduce-scatter.4.cloned.1.call-start
  6.5 0.7 compare_select_fusion
  7.2 0.7 compare_and_fusion
  7.9 2.8 copy.11
  10.8 4.4 %gather_fusion = bf16[1280,8,12]{2,1,0:T(8,128)(2,1)} fusion(bf16[8,12,1280]{1,0,2:T(8,128)(2,1)S(1)} %copy.11, s32[2048]{0:T(1024)S(1)} %pad_clamp_fusion), kind=kCustom, calls=%fused_computation | custom fusion | bytes 496640 | tf_op jit(solution)/shard_map/jit(_take)/gather | solution.py:23
  15.2 6.6 %fusion.8 = bf16[1280,8,12]{2,1,0:T(8,128)(2,1)S(1)} fusion(bf16[1280,8,12]{2,1,0:T(8,128)(2,1)} %gather_fusion, pred[1280]{0:T(1024)(128)(4,1)S(1)} %compare_and_fusion), kind=kLoop, calls=%fused_computation.23 | loop fusion | flops 122880 | bytes 492800
  21.8 5.3 %reshape.55 = bf16[8,2,7680]{2,1,0:T(2,128)(2,1)S(1)} reshape(bf16[1280,8,12]{2,1,0:T(8,128)(2,1)S(1)} %fusion.8) | data formatting | bytes 491520
  27.2 15.7 %all_to_all.18 = bf16[8,2,7680]{2,1,0:T(2,128)(2,1)S(1)} all-to-all(bf16[8,2,7680]{2,1,0:T(2,128)(2,1)S(1)} %reshape.55), channel_id=1, replica_groups=mesh['lat'=4,'wave'=8] {'wave'}, dimensions={0} | all-to-all | bytes 491520 | tf_op jit(solution)/shard_map/all_to_all | solution.py:24
  42.9 6.2 %reshape.56 = bf16[1280,8,12]{2,1,0:T(8,128)(2,1)S(1)} reshape(bf16[8,2,7680]{2,1,0:T(2,128)(2,1)S(1)} %all_to_all.18) | data formatting | bytes 491520
  49.1 1.9 copy.12
  51.1 0.1 collective-permute-start
  51.2 1.4 collective-permute-done
  52.6 1.5 collective-permute-start.1
  54.1 0.2 rev.8
  54.3 5.2 %collective-permute-done.1 = bf16[160,12,32]{0,2,1:T(8,128)(2,1)S(1)} collective-permute-done((bf16[160,12,32]{0,2,1:T(8,128)(2,1)S(1)}, bf16[160,12,32]{0,2,1:T(8,128)(2,1)S(1)}, u32[]{:S(2)}, u32[]{:S(2)}) %collective-permute-start.1) | collective-permute-done | bytes 122912 | tf_op jit(solution)/shard_map/ppermute | solution.py:14
  59.5 0.2 rev.7
  59.7 0.1 fusion.4
  59.9 0.5 copy.14
  60.4 0.5 copy.13
  60.9 4.0 %fusion = f32[160,12,640]{2,1,0:T(8,128)S(1)} fusion(bf16[160,12,32]{2,1,0:T(8,128)(2,1)S(1)} %copy.14, bf16[160,32,1280]{2,1,0:T(8,128)(2,1)} %param.5), kind=kOutput, calls=%fused_computation.2 | convolution fusion | flops 78643200 | bytes 11591680 | tf_op jit(solution)/shard_map/mcp,mpk->mck/dot_general | solution.py:41
  65.0 4.0 %fusion.2 = f32[160,12,640]{2,1,0:T(8,128)S(1)} fusion(bf16[160,12,32]{2,1,0:T(8,128)(2,1)S(1)} %copy.13, bf16[160,32,1280]{2,1,0:T(8,128)(2,1)} %param.5), kind=kOutput, calls=%fused_computation.4 | convolution fusion | flops 78643200 | bytes 11591680 | tf_op jit(solution)/shard_map/mcp,mpk->mck/dot_general | solution.py:38
  69.0 5.3 %pad_maximum_fusion = f32[160,12,1280]{2,1,0:T(8,128)} fusion(f32[160,12,640]{2,1,0:T(8,128)S(1)} %fusion, f32[160,12,640]{2,1,0:T(8,128)S(1)} %fusion.2), kind=kLoop, calls=%fused_computation.1 | loop fusion | flops 2457600 | bytes 19660800 | tf_op jit(solution)/shard_map/concatenate | solution.py:44
  74.3 49.8 %copy.16 = f32[160,12,1280]{1,0,2:T(8,128)} copy(f32[160,12,1280]{2,1,0:T(8,128)} %pad_maximum_fusion) | data formatting | bytes 19660800
  124.1 85.8 %reshape.53 = f32[1280,1920]{1,0:T(8,128)} reshape(f32[1280,160,12]{2,1,0:T(8,128)} %bitcast.7) | data formatting | bytes 19660800
  210.0 0.0 reduce-scatter.4.cloned.1.call-update
  210.0 0.8 dynamic-slice_subtract_fusion
  210.8 0.1 broadcast_compare_fusion
  210.9 79.2 %reduce-scatter.4.cloned.1.call-done = f32[320,1920]{1,0:T(8,128)} async-done(((f32[1280,1920]{1,0:T(8,128)}), f32[320,1920]{1,0:T(8,128)}) %reduce-scatter.4.cloned.1.call-update) | async-done | bytes 2457616
  290.1 30.8 %reshape.54 = f32[320,160,12]{2,1,0:T(8,128)} reshape(f32[320,1920]{1,0:T(8,128)} %reduce-scatter.4.cloned.1.call-done) | data formatting | bytes 4915200
  320.9 18.2 %copy.17 = f32[160,12,320]{2,1,0:T(8,128)} copy(f32[160,12,320]{1,0,2:T(8,128)} %bitcast.17) | data formatting | bytes 4915200
  339.1 2.6 broadcast_select_fusion
  341.7 2.5 copy.15
  (3 shorter events, 0.0 us)
Async XLA Ops:
  6.5 283.5 %reduce-scatter.4.cloned.1.call-start = ((), (), s32[]{:S(2)}) async-start(), calls=%async_computation.2 | async-start | bytes 12288000
  51.1 1.5 collective-permute-start
  52.6 6.9 %collective-permute-start.1 = (bf16[160,12,32]{0,2,1:T(8,128)(2,1)S(1)}, bf16[160,12,32]{0,2,1:T(8,128)(2,1)S(1)}, u32[]{:S(2)}, u32[]{:S(2)}) collective-permute-start(bf16[160,12,32]{0,2,1:T(8,128)(2,1)S(1)} %collective-permute-done), channel_id=1, source_target_pairs={{0,16},{16,0},{8,24},{24,8},{1,17},{17,1},{9,25},{25,9},{2,18},{18... | collective-permute-start | bytes 368648 | tf_op jit(solution)/shard_map/ppermute | solution.py:14
Sparse Core Ops, SparseCore 0:
  210.1 79.9 reduce-scatter.3
where the time goes:
time: 355 us; the launch traced here: 351 us
  local copies, waits for them, and re-layouts  209 us (59%)
  waiting for transfers between devices  85.9 us (24%)
  other arithmetic  17 us (5%)
  blocking collectives  15.7 us (4%)
  between operations  13.5 us (4%)
  matrix products  8.06 us (2%)
    unnamed x7, local copies, waits for them, and re-layouts  199 us
    unnamed x2, waiting for transfers between devices  79.2 us
    all_to_all x1, blocking collectives, local(): lax.all_to_all(ordered, 'wave', split_axis=2, concat_axis=0, tiled=True)  15.7 us
  transfers between devices with their start and end apart: 3, of which 3 were waited for; matrix products, arithmetic and copies ran while one was open for 0% of the time, Pallas kernels for 0%

commit v1 on v0

--- a/solution.py
+++ b/solution.py
@@ -1,7 +1,16 @@
+import functools
+
 import jax
 import jax.numpy as jnp
+import numpy as np
 from jax import lax
+from jax.experimental import pallas as pl
+from jax.experimental.pallas import tpu as pltpu
 from jax.sharding import PartitionSpec as P
+
+LANES = 128
+STEP = 16
+VMEM = 48 * 1024 * 1024
 
 
 def partner(block, axis, stride):
@@ -14,7 +23,7 @@
     return lax.ppermute(block, axis, route)
 
 
-def local(fourier, wave_table, legendre):
+def plain(fourier, wave_table, legendre):
     slot_count, pair_count, degree_count = legendre.shape
     lat_count = lax.axis_size("lat")
     half_degrees = degree_count // 2
@@ -51,6 +60,268 @@
     return jnp.where(inside, spectral, jnp.zeros_like(spectral))
 
 
+def gather_kernel(slots, cols, pad, table_ref, fourier_ref, *refs):
+    outs, (rows, turned) = refs[:-2], refs[-2:]
+    row_count, _, waves = fourier_ref.shape
+    me = lax.axis_index("wave")
+    rows[...] = jnp.zeros_like(rows)
+    for row in range(row_count):
+        rows[row * pad : row * pad + cols, :] = fourier_ref[row]
+    width = 2 * LANES
+    total = table_ref.shape[1]
+    number = lax.broadcasted_iota(jnp.int32, (waves, width), 0)
+    for start in range(0, total, width):
+        chosen = (number == table_ref[:, start : start + width]).astype(jnp.bfloat16)
+        got = jnp.dot(rows[...], chosen, preferred_element_type=jnp.float32)
+        turned[start : start + width, :] = got.T.astype(jnp.bfloat16)
+    for turn, out in enumerate(outs):
+        first = pl.multiple_of((me ^ turn) * slots, STEP)
+        out[...] = turned[pl.ds(first, slots), :]
+
+
+def pack(terms, core, lane_low):
+    rows = terms.shape[0]
+    main = jnp.where(core == 0, terms[:, : 2 * LANES], terms[:, 3 * LANES :])
+    mid = terms[:, 2 * LANES : 3 * LANES]
+    turned = pltpu.roll(mid, LANES // 2, 1)
+    part = rows // 4
+    tails = []
+    for j in range(2):
+        low, high = slice(2 * j * part, (2 * j + 1) * part), slice((2 * j + 1) * part, (2 * j + 2) * part)
+        zero = jnp.where(lane_low, mid[low], turned[high])
+        one = jnp.where(lane_low, turned[low], mid[high])
+        tails.append(jnp.where(core == 0, zero, one))
+    return main, tails
+
+
+def product_kernel(wave_count, lat_count, row_count, pad, cols, spread_ref, column_ref, diagonal_ref, leg_ref, *refs):
+    sources = refs[:wave_count]
+    far_out, far_own, near_out, near_own, place = refs[wave_count:]
+    pairs = leg_ref.shape[1]
+    half = leg_ref.shape[2] // 2
+    lat, me = lax.axis_index("lat"), lax.axis_index("wave")
+    northern = lat < lat_count // 2
+    y, core = lat // 2, lat % 2
+    lanes = row_count * pad
+
+    @pl.when(pl.program_id(0) == 0)
+    def _():
+        row = lax.broadcasted_iota(jnp.int32, (lanes, 2 * LANES), 0) // pad
+        col = lax.broadcasted_iota(jnp.int32, (lanes, 2 * LANES), 1)
+        for turn in range(wave_count):
+            source = me ^ turn
+            ascending = (source < wave_count // 2) == northern
+            position = (source % (wave_count // 2)) * row_count + row
+            position = jnp.where(ascending, position, pairs - 1 - position)
+            target = position + jnp.where(ascending, 0, LANES)
+            place[turn * lanes : (turn + 1) * lanes, :] = (
+                (col & (pairs - 1 | LANES)) == target
+            ).astype(jnp.bfloat16)
+
+    spread = spread_ref[...]
+    column = column_ref[...]
+    parts = [
+        jnp.dot(spread, source[...], preferred_element_type=jnp.float32).astype(jnp.bfloat16) * column
+        for source in sources
+    ]
+    both = jnp.dot(
+        jnp.concatenate(parts, axis=1), place[...], preferred_element_type=jnp.float32
+    )
+    north, south = both[:, :LANES], both[:, LANES:]
+    even, odd = north + south, north - south
+    rows = STEP * cols
+    group = 2 * LANES // pairs
+    group_rows = group * cols
+    lane_low = lax.broadcasted_iota(jnp.int32, (rows // 4, LANES), 1) < LANES // 2
+    diagonal = diagonal_ref[...]
+    for which, sent, kept in ((1 - y, far_out, far_own), (y, near_out, near_own)):
+        coefs = jnp.where(which == 0, even, odd).astype(jnp.bfloat16)
+        first = pl.multiple_of(which * half, LANES)
+        done = []
+        for g in range(STEP // group):
+            block = coefs[g * group_rows : (g + 1) * group_rows]
+            block = jnp.concatenate([block, block], axis=1) * diagonal
+            table = leg_ref[g * group : (g + 1) * group, :, pl.ds(first, half)]
+            done.append(
+                jnp.dot(block, table.reshape(group * pairs, half), preferred_element_type=jnp.float32)
+            )
+        terms = jnp.concatenate(done, axis=0)
+        for out, target in ((sent, 1 - core), (kept, core)):
+            main, tails = pack(terms, target, lane_low)
+            out[:rows, :] = main.astype(out.dtype)
+            out[rows:, :LANES] = tails[0].astype(out.dtype)
+            out[rows:, LANES:] = tails[1].astype(out.dtype)
+
+
+def final_kernel(slots, base, degrees, cols, table_ref, own_ref, near_ref, far_ref, *refs):
+    out = refs[-1]
+    lat, me = lax.axis_index("lat"), lax.axis_index("wave")
+    core = lat % 2
+    half = degrees // 2
+    width = out.shape[2]
+    rows = STEP * cols
+    part = rows // 4
+    value = own_ref[...] + near_ref[...].astype(jnp.float32) + far_ref[...].astype(jnp.float32)
+    main0, main1 = value[:rows, :LANES], value[:rows, LANES:]
+    tails = []
+    for j in range(4):
+        tail = value[rows:, (j // 2) * LANES : (j // 2 + 1) * LANES]
+        tails.append(pltpu.roll(tail, LANES // 2, 1) if j % 2 else tail)
+    tail = jnp.concatenate(tails, axis=0)
+    lane_low = lax.broadcasted_iota(jnp.int32, (rows, LANES), 1) < LANES // 2
+    turn0, turn1 = pltpu.roll(main0, LANES // 2, 1), pltpu.roll(main1, LANES // 2, 1)
+    first = core == 0
+    ordered = jnp.concatenate(
+        [
+            jnp.where(first, main0, jnp.where(lane_low, tail, turn0)),
+            jnp.where(first, main1, jnp.where(lane_low, turn0, turn1)),
+            jnp.where(first, tail, turn1),
+        ],
+        axis=1,
+    )
+    slot = lat * width + lax.broadcasted_iota(jnp.int32, (cols, 3 * LANES), 1)
+    offsets = jnp.where(slot < half, 2 * slot, 2 * (slot - half) + 1)
+    start = me * slots + base + pl.program_id(0) * STEP
+    for s in range(STEP):
+        inside = offsets < degrees - table_ref[start + s]
+        out[s] = jnp.where(inside, ordered[s * cols : (s + 1) * cols], 0.0)[:, :width]
+
+
+def packed(fourier, wave_table, legendre, chunks):
+    slots, pairs, degrees = legendre.shape
+    row_count, cols, waves = fourier.shape
+    wave_count, lat_count = lax.axis_size("wave"), lax.axis_size("lat")
+    width = degrees // lat_count
+    pad = LANES // row_count
+    params = pltpu.CompilerParams(vmem_limit_bytes=VMEM)
+    whole = pl.BlockSpec(memory_space=pltpu.VMEM)
+
+    ordered = pl.pallas_call(
+        functools.partial(gather_kernel, slots, cols, pad),
+        out_shape=[jax.ShapeDtypeStruct((slots, LANES), jnp.bfloat16)] * wave_count,
+        in_specs=[whole, whole],
+        out_specs=[whole] * wave_count,
+        scratch_shapes=[
+            pltpu.VMEM((LANES, waves), jnp.bfloat16),
+            pltpu.VMEM((slots * wave_count, LANES), jnp.bfloat16),
+        ],
+        compiler_params=params,
+        name="gather",
+    )(wave_table.reshape(1, -1), fourier)
+
+    arrived = []
+    for turn in range(wave_count):
+        route = []
+        for lat in range(lat_count):
+            for wave in range(wave_count):
+                to = lat if wave < wave_count // 2 else lat_count - 1 - lat
+                route.append((lat * wave_count + wave, to * wave_count + (wave ^ turn)))
+        arrived.append(lax.ppermute(ordered[turn], ("lat", "wave"), route))
+
+    rows = STEP * cols
+    step_rows = rows + rows // 4
+    group = 2 * LANES // pairs
+    at = np.arange(rows)
+    spread = jnp.asarray(at[:, None] // cols == np.arange(STEP)[None, :], jnp.bfloat16)
+    column = jnp.asarray(at[:, None] % cols == np.arange(LANES)[None, :] % pad, jnp.bfloat16)
+    diagonal = jnp.asarray(
+        at[: group * cols, None] // cols == np.arange(2 * LANES)[None, :] // pairs, jnp.bfloat16
+    )
+
+    core_route = [(lat, lat ^ 1) for lat in range(lat_count)]
+    y_route = [(lat, lat ^ 2) for lat in range(lat_count)]
+    out = None
+    base = 0
+    waiting = []
+    for steps in chunks:
+        message = (steps * step_rows, 2 * LANES)
+        first = base // STEP
+        block = pl.BlockSpec((step_rows, 2 * LANES), lambda g: (g, 0))
+        far_out, far_own, near_out, near_own = pl.pallas_call(
+            functools.partial(product_kernel, wave_count, lat_count, row_count, pad, cols),
+            grid=(steps,),
+            out_shape=[
+                jax.ShapeDtypeStruct(message, jnp.bfloat16),
+                jax.ShapeDtypeStruct(message, jnp.float32),
+                jax.ShapeDtypeStruct(message, jnp.bfloat16),
+                jax.ShapeDtypeStruct(message, jnp.float32),
+            ],
+            in_specs=[
+                pl.BlockSpec(spread.shape, lambda g: (0, 0)),
+                pl.BlockSpec(column.shape, lambda g: (0, 0)),
+                pl.BlockSpec(diagonal.shape, lambda g: (0, 0)),
+                pl.BlockSpec((STEP, pairs, degrees), lambda g, first=first: (first + g, 0, 0)),
+            ]
+            + [pl.BlockSpec((STEP, LANES), lambda g, first=first: (first + g, 0))] * wave_count,
+            out_specs=[block] * 4,
+            scratch_shapes=[pltpu.VMEM((wave_count * LANES, 2 * LANES), jnp.bfloat16)],
+            compiler_params=params,
+            cost_estimate=pl.CostEstimate(
+                flops=2 * steps * STEP * pairs * group * cols * degrees,
+                bytes_accessed=2 * steps * STEP * pairs * degrees,
+                transcendentals=0,
+            ),
+            name="product",
+        )(spread, column, diagonal, legendre, *arrived)
+        far_in = lax.ppermute(far_out, "lat", core_route)
+        near_in = lax.ppermute(near_out, "lat", core_route)
+        across = (far_own + far_in.astype(jnp.float32)).astype(jnp.bfloat16)
+        far_sum = lax.ppermute(across, "lat", y_route)
+        waiting.append((steps, base, near_own, near_in, far_sum))
+        base += steps * STEP
+
+    for steps, base, near_own, near_in, far_sum in waiting:
+        first = base // STEP
+        block = pl.BlockSpec((step_rows, 2 * LANES), lambda g, table: (g, 0))
+        carried = [] if out is None else [out]
+        out = pl.pallas_call(
+            functools.partial(final_kernel, slots, base, degrees, cols),
+            grid_spec=pltpu.PrefetchScalarGridSpec(
+                num_scalar_prefetch=1,
+                grid=(steps,),
+                in_specs=[block] * 3 + [pl.BlockSpec(memory_space=pl.ANY)] * len(carried),
+                out_specs=pl.BlockSpec(
+                    (STEP, cols, width), lambda g, table, first=first: (first + g, 0, 0)
+                ),
+            ),
+            out_shape=jax.ShapeDtypeStruct((slots, cols, width), jnp.float32),
+            input_output_aliases={4: 0} if carried else {},
+            compiler_params=params,
+            cost_estimate=pl.CostEstimate(
+                flops=0, bytes_accessed=16 * steps * STEP * cols * width, transcendentals=0
+            ),
+            name="final",
+        )(wave_table, near_own, near_in, far_sum, *carried)
+    return out
+
+
+def local(fourier, wave_table, legendre):
+    slots, pairs, degrees = legendre.shape
+    row_count, cols, waves = fourier.shape
+    wave_count, lat_count = lax.axis_size("wave"), lax.axis_size("lat")
+    half_tile = LANES // 2
+    fits = (
+        lat_count == 4
+        and wave_count & (wave_count - 1) == 0
+        and slots % STEP == 0
+        and degrees // 2 == 5 * LANES
+        and row_count * 2 * 8 == LANES
+        and cols <= LANES // row_count
+        and pairs == row_count * wave_count // 2
+        and LANES % pairs == 0
+        and STEP % (2 * LANES // pairs) == 0
+        and STEP * cols % half_tile == 0
+        and waves % (2 * LANES) == 0
+    )
+    if not fits:
+        return plain(fourier, wave_table, legendre)
+    steps = slots // STEP
+    sizes = [steps // 4] * 4
+    for extra in range(steps % 4):
+        sizes[1 + extra] += 1
+    return packed(fourier, wave_table, legendre, [size for size in sizes if size])
+
+
 def solution(mesh):
     in_specs = (P(("lat", "wave"), None, None), P(), P("wave", "lat", None))
     out_specs = P("wave", None, "lat")

time: 355 us -> 79.9 us (0.23)
  local copies, waits for them, and re-layouts: 209 us -> 6.59 us
  waiting for transfers between devices: 85.9 us -> 29.5 us
  Pallas kernels: 0 us -> 20.7 us
  starting transfers between devices: 1.59 us -> 22.1 us
  other arithmetic: 17 us -> 0.32 us
  blocking collectives: 15.7 us -> 0 us
  between operations: 13.5 us -> 0.18 us
  matrix products: 8.06 us -> 0 us
    unnamed x7 -> x9, local copies, waits for them, and re-layouts: 199 us -> 3.39 us
    unnamed x2 -> x0, waiting for transfers between devices: 79.2 us -> none
    ppermute x2 -> x20, waiting for transfers between devices: 6.68 us -> 29.5 us  [the longest x4 22.4 us: packed(): far_sum = lax.ppermute(across, 'lat', y_route)]
    pallas_call x0 -> x9, Pallas kernels: none -> 20.7 us  [the longest x4 16 us: packed(): pl.pallas_call(functools.partial(product_kernel, wave_count, lat_count, r...]
    ppermute x2 -> x20, starting transfers between devices: 1.59 us -> 22.1 us  [the longest x8 16.3 us: packed(): arrived.append(lax.ppermute(ordered[turn], ('lat', 'wave'), route))]
    all_to_all x1 -> x0, blocking collectives: 15.7 us -> none  [local(): lax.all_to_all(ordered, 'wave', split_axis=2, concat_axis=0, tiled=True)]
    dot_general x2 -> x0, matrix products: 8.06 us -> none  [the longest x1 4.03 us: local(): jnp.einsum('mcp,mpk->mck', even_part, legendre[:, :, :half_degrees], pref...]
    unnamed x1 -> x0, other arithmetic: 6.61 us -> none
  transfers between devices with their start and end apart: 3 -> 20, of which waited for: 3 -> 7; matrix products, arithmetic and copies ran while one was open for 0% -> 0% of each run, Pallas kernels for 0% -> 20%
where the time goes in v1:
time: 79.9 us; the launch traced here: 79.4 us
  waiting for transfers between devices  29.5 us (37%)
  starting transfers between devices  22.1 us (28%)
  Pallas kernels  20.7 us (26%)
  local copies, waits for them, and re-layouts  6.59 us (8%)
    ppermute x4, waiting for transfers between devices, packed(): far_sum = lax.ppermute(across, 'lat', y_route)  22.4 us
    ppermute x8, starting transfers between devices, packed(): arrived.append(lax.ppermute(ordered[turn], ('lat', 'wave'), route))  16.3 us
    pallas_call x4, Pallas kernels, packed(): pl.pallas_call(functools.partial(product_kernel, wave_count, lat_count, r...  16 us
    ppermute x8, waiting for transfers between devices, packed(): arrived.append(lax.ppermute(ordered[turn], ('lat', 'wave'), route))  6.99 us
    pallas_call x4, Pallas kernels, packed(): pl.pallas_call(functools.partial(final_kernel, slots, base, degrees, cols...  4.06 us
    unnamed x9, local copies, waits for them, and re-layouts  3.39 us
    ppermute x4, starting transfers between devices, packed(): far_sum = lax.ppermute(across, 'lat', y_route)  3.19 us
    pallas_call x1, local copies, waits for them, and re-layouts, packed(): pl.pallas_call(functools.partial(final_kernel, slots, base, degrees, cols...  2.5 us
  transfers between devices with their start and end apart: 20, of which 7 were waited for; matrix products, arithmetic and copies ran while one was open for 0% of the time, Pallas kernels for 20%

profile of v1, /device:TPU:0, one launch (start us, length us, event | category | flops | bytes accessed | tf_op | source)
XLA Modules:
  0.0 79.4 jit_solution(372404313306099780)
XLA Ops:
  0.0 1.0 %copy.10.fourier_ref = bf16[8,12,1280]{2,1,0:T(8,128)(2,1)S(1)} copy(bf16[8,12,1280]{2,0,1:T(8,128)(2,1)} %param.6) | data formatting | bytes 491520 | tf_op args[0]
  1.0 0.7 reshape.3.table_ref
  1.7 0.7 gather.1
  2.4 0.7 collective-permute-start
  3.1 3.0 %collective-permute-start.1 = (bf16[160,128]{1,0:T(8,128)(2,1)S(1)}, bf16[160,128]{1,0:T(8,128)(2,1)S(1)}, u32[]{:S(2)}, u32[]{:S(2)}) collective-permute-start(bf16[160,128]{1,0:T(8,128)(2,1)S(1)} %get-tuple-element.30), channel_id=1, source_target_pairs={{0,1},{1,0},{2,3},{3,2},{4,29},{5,28},{6,31},{7,30},{8,9},{9,8},{1... | collective-permute-start | bytes 122888 | tf_op jit(solution)/shard_map/ppermute | solution.py:219
  6.1 1.6 %collective-permute-start.2 = (bf16[160,128]{1,0:T(8,128)(2,1)S(1)}, bf16[160,128]{1,0:T(8,128)(2,1)S(1)}, u32[]{:S(2)}, u32[]{:S(2)}) collective-permute-start(bf16[160,128]{1,0:T(8,128)(2,1)S(1)} %get-tuple-element.31), channel_id=1, source_target_pairs={{0,2},{1,3},{2,0},{3,1},{4,30},{5,31},{6,28},{7,29},{8,10},{9,11},... | collective-permute-start | bytes 122888 | tf_op jit(solution)/shard_map/ppermute | solution.py:219
  7.7 0.0 collective-permute-start.3
  7.7 6.1 %collective-permute-start.4 = (bf16[160,128]{1,0:T(8,128)(2,1)S(1)}, bf16[160,128]{1,0:T(8,128)(2,1)S(1)}, u32[]{:S(2)}, u32[]{:S(2)}) collective-permute-start(bf16[160,128]{1,0:T(8,128)(2,1)S(1)} %get-tuple-element.33), channel_id=1, source_target_pairs={{0,4},{1,5},{2,6},{3,7},{4,24},{5,25},{6,26},{7,27},{8,12},{9,13},... | collective-permute-start | bytes 122888 | tf_op jit(solution)/shard_map/ppermute | solution.py:219
  13.7 0.0 collective-permute-done.refs_0_
  13.7 0.9 %collective-permute-start.5 = (bf16[160,128]{1,0:T(8,128)(2,1)S(1)}, bf16[160,128]{1,0:T(8,128)(2,1)S(1)}, u32[]{:S(2)}, u32[]{:S(2)}) collective-permute-start(bf16[160,128]{1,0:T(8,128)(2,1)S(1)} %get-tuple-element.34), channel_id=1, source_target_pairs={{0,5},{1,4},{2,7},{3,6},{4,25},{5,24},{6,27},{7,26},{8,13},{9,12},... | collective-permute-start | bytes 122888 | tf_op jit(solution)/shard_map/ppermute | solution.py:219
  14.7 0.0 collective-permute-done.1.refs_1_
  14.7 4.1 %collective-permute-start.6 = (bf16[160,128]{1,0:T(8,128)(2,1)S(1)}, bf16[160,128]{1,0:T(8,128)(2,1)S(1)}, u32[]{:S(2)}, u32[]{:S(2)}) collective-permute-start(bf16[160,128]{1,0:T(8,128)(2,1)S(1)} %get-tuple-element.35), channel_id=1, source_target_pairs={{0,6},{1,7},{2,4},{3,5},{4,26},{5,27},{6,24},{7,25},{8,14},{9,15},... | collective-permute-start | bytes 122888 | tf_op jit(solution)/shard_map/ppermute | solution.py:219
  18.7 0.0 collective-permute-done.2.refs_2_
  18.7 0.0 collective-permute-start.7
  18.8 0.0 collective-permute-done.3.refs_3_
  18.8 0.0 collective-permute-done.4.refs_4_
  18.8 1.5 %collective-permute-done.5.refs_5_ = bf16[160,128]{1,0:T(8,128)(2,1)S(1)} collective-permute-done((bf16[160,128]{1,0:T(8,128)(2,1)S(1)}, bf16[160,128]{1,0:T(8,128)(2,1)S(1)}, u32[]{:S(2)}, u32[]{:S(2)}) %collective-permute-start.5) | collective-permute-done | bytes 40992 | tf_op jit(solution)/shard_map/ppermute | solution.py:219
  20.3 1.8 %collective-permute-done.6.refs_6_ = bf16[160,128]{1,0:T(8,128)(2,1)S(1)} collective-permute-done((bf16[160,128]{1,0:T(8,128)(2,1)S(1)}, bf16[160,128]{1,0:T(8,128)(2,1)S(1)}, u32[]{:S(2)}, u32[]{:S(2)}) %collective-permute-start.6) | collective-permute-done | bytes 40992 | tf_op jit(solution)/shard_map/ppermute | solution.py:219
  22.1 3.6 %collective-permute-done.7.refs_7_ = bf16[160,128]{1,0:T(8,128)(2,1)S(1)} collective-permute-done((bf16[160,128]{1,0:T(8,128)(2,1)S(1)}, bf16[160,128]{1,0:T(8,128)(2,1)S(1)}, u32[]{:S(2)}, u32[]{:S(2)}) %collective-permute-start.7) | collective-permute-done | bytes 40992 | tf_op jit(solution)/shard_map/ppermute | solution.py:219
  25.8 0.0 copy-start
  25.8 0.8 %copy-done = bf16[192,16]{1,0:T(8,128)(2,1)S(1)} copy-done((bf16[192,16]{1,0:T(8,128)(2,1)S(1)}, bf16[192,16]{1,0:T(8,128)(2,1)}, u32[]{:S(2)}) %copy-start) | copy-done | bytes 6168
  26.6 0.0 copy-start.1
  26.6 0.8 %copy-done.1 = bf16[192,128]{1,0:T(8,128)(2,1)S(1)} copy-done((bf16[192,128]{1,0:T(8,128)(2,1)S(1)}, bf16[192,128]{1,0:T(8,128)(2,1)}, u32[]{:S(2)}) %copy-start.1) | copy-done | bytes 49176
  27.4 0.0 copy-start.2
  27.4 0.8 %copy-done.2 = bf16[96,256]{1,0:T(8,128)(2,1)S(1)} copy-done((bf16[96,256]{1,0:T(8,128)(2,1)S(1)}, bf16[96,256]{1,0:T(8,128)(2,1)}, u32[]{:S(2)}) %copy-start.2) | copy-done | bytes 49176
  28.2 3.3 %product.7 = (bf16[480,256]{1,0:T(8,128)(2,1)S(1)}, f32[480,256]{1,0:T(8,128)S(1)}, bf16[480,256]{1,0:T(8,128)(2,1)S(1)}, f32[480,256]{1,0:T(8,128)S(1)}) custom-call(bf16[192,16]{1,0:T(8,128)(2,1)S(1)} %copy-done, bf16[192,128]{1,0:T(8,128)(2,1)S(1)} %copy-done.1, bf16[96,256]{1,0:T(8,128)(2,1)S(1)} %copy-done.2, bf16[160,32,1280]{2,1,0:T(8,128)(2,1)} %leg_ref.7, ...), custom_call_target="tpu_custom_call" | custom-call | flops 251658240 | bytes 2621440 | tf_op jit(solution)/shard_map/product/pallas_call | solution.py:240
  31.5 0.7 collective-permute-start.18
  32.3 4.6 %product.6 = (bf16[720,256]{1,0:T(8,128)(2,1)S(1)}, f32[720,256]{1,0:T(8,128)S(1)}, bf16[720,256]{1,0:T(8,128)(2,1)S(1)}, f32[720,256]{1,0:T(8,128)S(1)}) custom-call(bf16[192,16]{1,0:T(8,128)(2,1)S(1)} %copy-done, bf16[192,128]{1,0:T(8,128)(2,1)S(1)} %copy-done.1, bf16[96,256]{1,0:T(8,128)(2,1)S(1)} %copy-done.2, bf16[160,32,1280]{2,1,0:T(8,128)(2,1)} %leg_ref.7, ...), custom_call_target="tpu_custom_call" | custom-call | flops 377487360 | bytes 3932160 | tf_op jit(solution)/shard_map/product/pallas_call | solution.py:240
  36.9 0.1 collective-permute-start.15
  37.0 0.5 collective-permute-start.17
  37.5 0.1 collective-permute-start.14
  37.5 4.6 %product.5 = (bf16[720,256]{1,0:T(8,128)(2,1)S(1)}, f32[720,256]{1,0:T(8,128)S(1)}, bf16[720,256]{1,0:T(8,128)(2,1)S(1)}, f32[720,256]{1,0:T(8,128)S(1)}) custom-call(bf16[192,16]{1,0:T(8,128)(2,1)S(1)} %copy-done, bf16[192,128]{1,0:T(8,128)(2,1)S(1)} %copy-done.1, bf16[96,256]{1,0:T(8,128)(2,1)S(1)} %copy-done.2, bf16[160,32,1280]{2,1,0:T(8,128)(2,1)} %leg_ref.7, ...), custom_call_target="tpu_custom_call" | custom-call | flops 377487360 | bytes 3932160 | tf_op jit(solution)/shard_map/product/pallas_call | solution.py:240
  42.2 0.5 collective-permute-start.12
  42.7 3.3 %product.4 = (bf16[480,256]{1,0:T(8,128)(2,1)S(1)}, f32[480,256]{1,0:T(8,128)S(1)}, bf16[480,256]{1,0:T(8,128)(2,1)S(1)}, f32[480,256]{1,0:T(8,128)S(1)}) custom-call(bf16[192,16]{1,0:T(8,128)(2,1)S(1)} %copy-done, bf16[192,128]{1,0:T(8,128)(2,1)S(1)} %copy-done.1, bf16[96,256]{1,0:T(8,128)(2,1)S(1)} %copy-done.2, bf16[160,32,1280]{2,1,0:T(8,128)(2,1)} %leg_ref.7, ...), custom_call_target="tpu_custom_call" | custom-call | flops 251658240 | bytes 2621440 | tf_op jit(solution)/shard_map/product/pallas_call | solution.py:240
  46.0 0.0 copy-start.3
  46.0 0.0 collective-permute-done.18
  46.1 0.2 collective-permute-start.11
  46.2 0.1 add_convert_fusion.2
  46.3 0.0 collective-permute-done.15
  46.3 0.5 collective-permute-start.9
  46.8 0.1 add_convert_fusion
  46.9 0.0 collective-permute-done.12
  46.9 0.6 collective-permute-start.19
  47.5 0.1 add_convert_fusion.1
  47.6 0.0 collective-permute-done.17.near_ref
  47.6 1.6 %collective-permute-start.16 = (bf16[720,256]{1,0:T(8,128)(2,1)S(1)}, bf16[720,256]{1,0:T(8,128)(2,1)S(1)}, u32[]{:S(2)}, u32[]{:S(2)}) collective-permute-start(bf16[720,256]{1,0:T(8,128)(2,1)S(1)} %add_convert_fusion), channel_id=1, source_target_pairs={{0,16},{8,24},{16,0},{24,8},{1,17},{9,25},{17,1},{25,9},{2,18},{10... | collective-permute-start | bytes 1105928 | tf_op jit(solution)/shard_map/ppermute | solution.py:269
  49.2 0.0 collective-permute-done.9
  49.2 0.5 collective-permute-start.13
  49.7 0.1 add_convert_fusion.3
  49.7 0.0 collective-permute-done.14.near_ref
  49.7 0.1 collective-permute-start.8
  49.8 5.9 %collective-permute-done.19.far_ref = bf16[480,256]{1,0:T(8,128)(2,1)S(1)} collective-permute-done((bf16[480,256]{1,0:T(8,128)(2,1)S(1)}, bf16[480,256]{1,0:T(8,128)(2,1)S(1)}, u32[]{:S(2)}, u32[]{:S(2)}) %collective-permute-start.19) | collective-permute-done | bytes 245792 | tf_op jit(solution)/shard_map/ppermute | solution.py:269
  55.8 0.5 collective-permute-start.10
  56.3 0.0 copy-done.3
  56.3 0.9 %final.4.refs_0_ = f32[160,12,320]{2,1,0:T(8,128)S(1)} custom-call(s32[1280]{0:T(1024)S(1)} %copy-done.3, f32[480,256]{1,0:T(8,128)S(1)} %get-tuple-element.49.own_ref, bf16[480,256]{1,0:T(8,128)(2,1)S(1)} %collective-permute-done.17.near_ref, bf16[480,256]{1,0:T(8,128)(2,1)S(1)} %collective-permute-done.19.far_ref), custom_call_target="tpu_custom_call" | custom-call | bytes 1966080 | tf_op jit(solution)/shard_map/final/pallas_call | solution.py:277
  57.2 6.4 %collective-permute-done.16.far_ref = bf16[720,256]{1,0:T(8,128)(2,1)S(1)} collective-permute-done((bf16[720,256]{1,0:T(8,128)(2,1)S(1)}, bf16[720,256]{1,0:T(8,128)(2,1)S(1)}, u32[]{:S(2)}, u32[]{:S(2)}) %collective-permute-start.16) | collective-permute-done | bytes 368672 | tf_op jit(solution)/shard_map/ppermute | solution.py:269
  63.7 1.1 %final.5.refs_0_ = f32[160,12,320]{2,1,0:T(8,128)S(1)} custom-call(s32[1280]{0:T(1024)S(1)} %copy-done.3, f32[720,256]{1,0:T(8,128)S(1)} %get-tuple-element.45.own_ref, bf16[720,256]{1,0:T(8,128)(2,1)S(1)} %collective-permute-done.14.near_ref, bf16[720,256]{1,0:T(8,128)(2,1)S(1)} %collective-permute-done.16.far_ref, ...), custom_call_target="tpu_custom_call", output_to_operand_aliasing={{}: (4, {})} | custom-call | bytes 2949120 | tf_op jit(solution)/shard_map/final/pallas_call | solution.py:277
  64.8 0.0 collective-permute-done.11.near_ref
  64.8 6.8 %collective-permute-done.13.far_ref = bf16[720,256]{1,0:T(8,128)(2,1)S(1)} collective-permute-done((bf16[720,256]{1,0:T(8,128)(2,1)S(1)}, bf16[720,256]{1,0:T(8,128)(2,1)S(1)}, u32[]{:S(2)}, u32[]{:S(2)}) %collective-permute-start.13) | collective-permute-done | bytes 368672 | tf_op jit(solution)/shard_map/ppermute | solution.py:269
  71.6 1.1 %final.6.refs_0_ = f32[160,12,320]{2,1,0:T(8,128)S(1)} custom-call(s32[1280]{0:T(1024)S(1)} %copy-done.3, f32[720,256]{1,0:T(8,128)S(1)} %get-tuple-element.41.own_ref, bf16[720,256]{1,0:T(8,128)(2,1)S(1)} %collective-permute-done.11.near_ref, bf16[720,256]{1,0:T(8,128)(2,1)S(1)} %collective-permute-done.13.far_ref, ...), custom_call_target="tpu_custom_call", output_to_operand_aliasing={{}: (4, {})} | custom-call | bytes 2949120 | tf_op jit(solution)/shard_map/final/pallas_call | solution.py:277
  72.6 0.0 collective-permute-done.8.near_ref
  72.7 3.3 %collective-permute-done.10.far_ref = bf16[480,256]{1,0:T(8,128)(2,1)S(1)} collective-permute-done((bf16[480,256]{1,0:T(8,128)(2,1)S(1)}, bf16[480,256]{1,0:T(8,128)(2,1)S(1)}, u32[]{:S(2)}, u32[]{:S(2)}) %collective-permute-start.10) | collective-permute-done | bytes 245792 | tf_op jit(solution)/shard_map/ppermute | solution.py:269
  76.0 0.9 %final.7 = f32[160,12,320]{2,1,0:T(8,128)S(1)} custom-call(s32[1280]{0:T(1024)S(1)} %copy-done.3, f32[480,256]{1,0:T(8,128)S(1)} %get-tuple-element.37.own_ref, bf16[480,256]{1,0:T(8,128)(2,1)S(1)} %collective-permute-done.8.near_ref, bf16[480,256]{1,0:T(8,128)(2,1)S(1)} %collective-permute-done.10.far_ref, ...), custom_call_target="tpu_custom_call", output_to_operand_aliasing={{}: (4, {})} | custom-call | bytes 1966080 | tf_op jit(solution)/shard_map/final/pallas_call | solution.py:277
  76.9 2.5 %copy.11 = f32[160,12,320]{2,0,1:T(8,128)} copy(f32[160,12,320]{2,1,0:T(8,128)S(1)} %final.7) | data formatting | bytes 4915200 | tf_op jit(solution)/shard_map/final/pallas_call | solution.py:277
Async XLA Ops:
  2.4 11.3 %collective-permute-start = (bf16[160,128]{1,0:T(8,128)(2,1)S(1)}, bf16[160,128]{1,0:T(8,128)(2,1)S(1)}, u32[]{:S(2)}, u32[]{:S(2)}) collective-permute-start(bf16[160,128]{1,0:T(8,128)(2,1)S(1)} %get-tuple-element.29), channel_id=1, source_target_pairs={{0,0},{1,1},{2,2},{3,3},{4,28},{5,29},{6,30},{7,31},{8,8},{9,9},{1... | collective-permute-start | bytes 122888 | tf_op jit(solution)/shard_map/ppermute | solution.py:219
  3.1 11.6 %collective-permute-start.1 = (bf16[160,128]{1,0:T(8,128)(2,1)S(1)}, bf16[160,128]{1,0:T(8,128)(2,1)S(1)}, u32[]{:S(2)}, u32[]{:S(2)}) collective-permute-start(bf16[160,128]{1,0:T(8,128)(2,1)S(1)} %get-tuple-element.30), channel_id=1, source_target_pairs={{0,1},{1,0},{2,3},{3,2},{4,29},{5,28},{6,31},{7,30},{8,9},{9,8},{1... | collective-permute-start | bytes 122888 | tf_op jit(solution)/shard_map/ppermute | solution.py:219
  6.1 12.6 %collective-permute-start.2 = (bf16[160,128]{1,0:T(8,128)(2,1)S(1)}, bf16[160,128]{1,0:T(8,128)(2,1)S(1)}, u32[]{:S(2)}, u32[]{:S(2)}) collective-permute-start(bf16[160,128]{1,0:T(8,128)(2,1)S(1)} %get-tuple-element.31), channel_id=1, source_target_pairs={{0,2},{1,3},{2,0},{3,1},{4,30},{5,31},{6,28},{7,29},{8,10},{9,11},... | collective-permute-start | bytes 122888 | tf_op jit(solution)/shard_map/ppermute | solution.py:219
  7.7 11.1 %collective-permute-start.3 = (bf16[160,128]{1,0:T(8,128)(2,1)S(1)}, bf16[160,128]{1,0:T(8,128)(2,1)S(1)}, u32[]{:S(2)}, u32[]{:S(2)}) collective-permute-start(bf16[160,128]{1,0:T(8,128)(2,1)S(1)} %get-tuple-element.32), channel_id=1, source_target_pairs={{0,3},{1,2},{2,1},{3,0},{4,31},{5,30},{6,29},{7,28},{8,11},{9,10},... | collective-permute-start | bytes 122888 | tf_op jit(solution)/shard_map/ppermute | solution.py:219
  7.7 11.1 %collective-permute-start.4 = (bf16[160,128]{1,0:T(8,128)(2,1)S(1)}, bf16[160,128]{1,0:T(8,128)(2,1)S(1)}, u32[]{:S(2)}, u32[]{:S(2)}) collective-permute-start(bf16[160,128]{1,0:T(8,128)(2,1)S(1)} %get-tuple-element.33), channel_id=1, source_target_pairs={{0,4},{1,5},{2,6},{3,7},{4,24},{5,25},{6,26},{7,27},{8,12},{9,13},... | collective-permute-start | bytes 122888 | tf_op jit(solution)/shard_map/ppermute | solution.py:219
  13.7 6.6 %collective-permute-start.5 = (bf16[160,128]{1,0:T(8,128)(2,1)S(1)}, bf16[160,128]{1,0:T(8,128)(2,1)S(1)}, u32[]{:S(2)}, u32[]{:S(2)}) collective-permute-start(bf16[160,128]{1,0:T(8,128)(2,1)S(1)} %get-tuple-element.34), channel_id=1, source_target_pairs={{0,5},{1,4},{2,7},{3,6},{4,25},{5,24},{6,27},{7,26},{8,13},{9,12},... | collective-permute-start | bytes 122888 | tf_op jit(solution)/shard_map/ppermute | solution.py:219
  14.7 7.5 %collective-permute-start.6 = (bf16[160,128]{1,0:T(8,128)(2,1)S(1)}, bf16[160,128]{1,0:T(8,128)(2,1)S(1)}, u32[]{:S(2)}, u32[]{:S(2)}) collective-permute-start(bf16[160,128]{1,0:T(8,128)(2,1)S(1)} %get-tuple-element.35), channel_id=1, source_target_pairs={{0,6},{1,7},{2,4},{3,5},{4,26},{5,27},{6,24},{7,25},{8,14},{9,15},... | collective-permute-start | bytes 122888 | tf_op jit(solution)/shard_map/ppermute | solution.py:219
  18.7 7.0 %collective-permute-start.7 = (bf16[160,128]{1,0:T(8,128)(2,1)S(1)}, bf16[160,128]{1,0:T(8,128)(2,1)S(1)}, u32[]{:S(2)}, u32[]{:S(2)}) collective-permute-start(bf16[160,128]{1,0:T(8,128)(2,1)S(1)} %get-tuple-element.36), channel_id=1, source_target_pairs={{0,7},{1,6},{2,5},{3,4},{4,27},{5,26},{6,25},{7,24},{8,15},{9,14},... | collective-permute-start | bytes 122888 | tf_op jit(solution)/shard_map/ppermute | solution.py:219
  25.8 0.8 %copy-start = (bf16[192,16]{1,0:T(8,128)(2,1)S(1)}, bf16[192,16]{1,0:T(8,128)(2,1)}, u32[]{:S(2)}) copy-start(bf16[192,16]{1,0:T(8,128)(2,1)} %constant.6.clone.spread_ref) | copy-start | bytes 18436
  26.6 0.8 %copy-start.1 = (bf16[192,128]{1,0:T(8,128)(2,1)S(1)}, bf16[192,128]{1,0:T(8,128)(2,1)}, u32[]{:S(2)}) copy-start(bf16[192,128]{1,0:T(8,128)(2,1)} %constant.7.clone.column_ref) | copy-start | bytes 147460
  27.4 0.8 %copy-start.2 = (bf16[96,256]{1,0:T(8,128)(2,1)S(1)}, bf16[96,256]{1,0:T(8,128)(2,1)}, u32[]{:S(2)}) copy-start(bf16[96,256]{1,0:T(8,128)(2,1)} %constant.8.clone.diagonal_ref) | copy-start | bytes 147460
  31.5 14.5 %collective-permute-start.18 = (bf16[480,256]{1,0:T(8,128)(2,1)S(1)}, bf16[480,256]{1,0:T(8,128)(2,1)S(1)}, u32[]{:S(2)}, u32[]{:S(2)}) collective-permute-start(bf16[480,256]{1,0:T(8,128)(2,1)S(1)} %get-tuple-element.52), channel_id=1, source_target_pairs={{0,8},{8,0},{16,24},{24,16},{1,9},{9,1},{17,25},{25,17},{2,10},{10... | collective-permute-start | bytes 737288 | tf_op jit(solution)/shard_map/ppermute | solution.py:266
  36.9 9.4 %collective-permute-start.15 = (bf16[720,256]{1,0:T(8,128)(2,1)S(1)}, bf16[720,256]{1,0:T(8,128)(2,1)S(1)}, u32[]{:S(2)}, u32[]{:S(2)}) collective-permute-start(bf16[720,256]{1,0:T(8,128)(2,1)S(1)} %get-tuple-element.48), channel_id=1, source_target_pairs={{0,8},{8,0},{16,24},{24,16},{1,9},{9,1},{17,25},{25,17},{2,10},{10... | collective-permute-start | bytes 1105928 | tf_op jit(solution)/shard_map/ppermute | solution.py:266
  37.0 10.6 %collective-permute-start.17 = (bf16[480,256]{1,0:T(8,128)(2,1)S(1)}, bf16[480,256]{1,0:T(8,128)(2,1)S(1)}, u32[]{:S(2)}, u32[]{:S(2)}) collective-permute-start(bf16[480,256]{1,0:T(8,128)(2,1)S(1)} %get-tuple-element.50), channel_id=1, source_target_pairs={{0,8},{8,0},{16,24},{24,16},{1,9},{9,1},{17,25},{25,17},{2,10},{10... | collective-permute-start | bytes 737288 | tf_op jit(solution)/shard_map/ppermute | solution.py:267
  37.5 12.3 %collective-permute-start.14 = (bf16[720,256]{1,0:T(8,128)(2,1)S(1)}, bf16[720,256]{1,0:T(8,128)(2,1)S(1)}, u32[]{:S(2)}, u32[]{:S(2)}) collective-permute-start(bf16[720,256]{1,0:T(8,128)(2,1)S(1)} %get-tuple-element.46), channel_id=1, source_target_pairs={{0,8},{8,0},{16,24},{24,16},{1,9},{9,1},{17,25},{25,17},{2,10},{10... | collective-permute-start | bytes 1105928 | tf_op jit(solution)/shard_map/ppermute | solution.py:267
  42.2 4.7 %collective-permute-start.12 = (bf16[720,256]{1,0:T(8,128)(2,1)S(1)}, bf16[720,256]{1,0:T(8,128)(2,1)S(1)}, u32[]{:S(2)}, u32[]{:S(2)}) collective-permute-start(bf16[720,256]{1,0:T(8,128)(2,1)S(1)} %get-tuple-element.44), channel_id=1, source_target_pairs={{0,8},{8,0},{16,24},{24,16},{1,9},{9,1},{17,25},{25,17},{2,10},{10... | collective-permute-start | bytes 1105928 | tf_op jit(solution)/shard_map/ppermute | solution.py:266
  46.0 10.2 %copy-start.3 = (s32[1280]{0:T(1024)S(1)}, s32[1280]{0:T(1024)}, u32[]{:S(2)}) copy-start(s32[1280]{0:T(1024)} %table_ref.7) | copy-start | bytes 15364
  46.1 18.7 %collective-permute-start.11 = (bf16[720,256]{1,0:T(8,128)(2,1)S(1)}, bf16[720,256]{1,0:T(8,128)(2,1)S(1)}, u32[]{:S(2)}, u32[]{:S(2)}) collective-permute-start(bf16[720,256]{1,0:T(8,128)(2,1)S(1)} %get-tuple-element.42), channel_id=1, source_target_pairs={{0,8},{8,0},{16,24},{24,16},{1,9},{9,1},{17,25},{25,17},{2,10},{10... | collective-permute-start | bytes 1105928 | tf_op jit(solution)/shard_map/ppermute | solution.py:267
  46.3 2.9 %collective-permute-start.9 = (bf16[480,256]{1,0:T(8,128)(2,1)S(1)}, bf16[480,256]{1,0:T(8,128)(2,1)S(1)}, u32[]{:S(2)}, u32[]{:S(2)}) collective-permute-start(bf16[480,256]{1,0:T(8,128)(2,1)S(1)} %get-tuple-element.40), channel_id=1, source_target_pairs={{0,8},{8,0},{16,24},{24,16},{1,9},{9,1},{17,25},{25,17},{2,10},{10... | collective-permute-start | bytes 737288 | tf_op jit(solution)/shard_map/ppermute | solution.py:266
  46.9 8.9 %collective-permute-start.19 = (bf16[480,256]{1,0:T(8,128)(2,1)S(1)}, bf16[480,256]{1,0:T(8,128)(2,1)S(1)}, u32[]{:S(2)}, u32[]{:S(2)}) collective-permute-start(bf16[480,256]{1,0:T(8,128)(2,1)S(1)} %add_convert_fusion.2), channel_id=1, source_target_pairs={{0,16},{8,24},{16,0},{24,8},{1,17},{9,25},{17,1},{25,9},{2,18},{10... | collective-permute-start | bytes 737288 | tf_op jit(solution)/shard_map/ppermute | solution.py:269
  47.6 16.1 %collective-permute-start.16 = (bf16[720,256]{1,0:T(8,128)(2,1)S(1)}, bf16[720,256]{1,0:T(8,128)(2,1)S(1)}, u32[]{:S(2)}, u32[]{:S(2)}) collective-permute-start(bf16[720,256]{1,0:T(8,128)(2,1)S(1)} %add_convert_fusion), channel_id=1, source_target_pairs={{0,16},{8,24},{16,0},{24,8},{1,17},{9,25},{17,1},{25,9},{2,18},{10... | collective-permute-start | bytes 1105928 | tf_op jit(solution)/shard_map/ppermute | solution.py:269
  49.2 22.4 %collective-permute-start.13 = (bf16[720,256]{1,0:T(8,128)(2,1)S(1)}, bf16[720,256]{1,0:T(8,128)(2,1)S(1)}, u32[]{:S(2)}, u32[]{:S(2)}) collective-permute-start(bf16[720,256]{1,0:T(8,128)(2,1)S(1)} %add_convert_fusion.1), channel_id=1, source_target_pairs={{0,16},{8,24},{16,0},{24,8},{1,17},{9,25},{17,1},{25,9},{2,18},{10... | collective-permute-start | bytes 1105928 | tf_op jit(solution)/shard_map/ppermute | solution.py:269
  49.7 22.9 %collective-permute-start.8 = (bf16[480,256]{1,0:T(8,128)(2,1)S(1)}, bf16[480,256]{1,0:T(8,128)(2,1)S(1)}, u32[]{:S(2)}, u32[]{:S(2)}) collective-permute-start(bf16[480,256]{1,0:T(8,128)(2,1)S(1)} %get-tuple-element.38), channel_id=1, source_target_pairs={{0,8},{8,0},{16,24},{24,16},{1,9},{9,1},{17,25},{25,17},{2,10},{10... | collective-permute-start | bytes 737288 | tf_op jit(solution)/shard_map/ppermute | solution.py:267
  55.8 20.2 %collective-permute-start.10 = (bf16[480,256]{1,0:T(8,128)(2,1)S(1)}, bf16[480,256]{1,0:T(8,128)(2,1)S(1)}, u32[]{:S(2)}, u32[]{:S(2)}) collective-permute-start(bf16[480,256]{1,0:T(8,128)(2,1)S(1)} %add_convert_fusion.3), channel_id=1, source_target_pairs={{0,16},{8,24},{16,0},{24,8},{1,17},{9,25},{17,1},{25,9},{2,18},{10... | collective-permute-start | bytes 737288 | tf_op jit(solution)/shard_map/ppermute | solution.py:269

commit v2 on v0

--- a/solution.py
+++ b/solution.py
@@ -1,7 +1,16 @@
+import functools
+
 import jax
 import jax.numpy as jnp
 from jax import lax
+from jax.experimental import pallas as pl
+from jax.experimental.pallas import tpu as pltpu
 from jax.sharding import PartitionSpec as P
+
+LANES = 128
+STEP = 32
+TILE = 8
+VMEM = 48 * 1024 * 1024
 
 
 def partner(block, axis, stride):
@@ -14,7 +23,7 @@
     return lax.ppermute(block, axis, route)
 
 
-def local(fourier, wave_table, legendre):
+def plain(fourier, wave_table, legendre):
     slot_count, pair_count, degree_count = legendre.shape
     lat_count = lax.axis_size("lat")
     half_degrees = degree_count // 2
@@ -51,6 +60,263 @@
     return jnp.where(inside, spectral, jnp.zeros_like(spectral))
 
 
+def gather_kernel(slots, table_ref, rows_ref, *refs):
+    outs, turned = refs[:-1], refs[-1]
+    count, waves = rows_ref.shape
+    me = lax.axis_index("wave")
+    rows = jnp.concatenate([rows_ref[...], jnp.zeros((LANES - count, waves), jnp.bfloat16)], axis=0)
+    number = lax.broadcasted_iota(jnp.int32, (waves, LANES), 0)
+    for j in range(0, table_ref.shape[0], 2):
+        chosen = jnp.concatenate(
+            [(number == table_ref[k : k + 1, :]).astype(jnp.bfloat16) for k in (j, j + 1)], axis=1
+        )
+        got = jnp.dot(rows, chosen, preferred_element_type=jnp.float32)
+        turned[j * LANES : (j + 2) * LANES, :] = got.T.astype(jnp.bfloat16)
+    for turn, out in enumerate(outs):
+        first = pl.multiple_of((me ^ turn) * slots, STEP)
+        out[...] = turned[pl.ds(first, slots), :]
+
+
+def place_kernel(wave_count, lat_count, row_count, pairs, out):
+    northern = lax.axis_index("lat") < lat_count // 2
+    me = lax.axis_index("wave")
+    row = lax.broadcasted_iota(jnp.int32, (LANES, 2 * LANES), 0) & (row_count - 1)
+    col = lax.broadcasted_iota(jnp.int32, (LANES, 2 * LANES), 1) & (pairs - 1 | LANES)
+    for turn in range(wave_count):
+        source = me ^ turn
+        ascending = (source < wave_count // 2) == northern
+        position = (source % (wave_count // 2)) * row_count + row
+        position = jnp.where(ascending, position, pairs - 1 - position)
+        target = position + jnp.where(ascending, 0, LANES)
+        out[turn * LANES : (turn + 1) * LANES, :] = (col == target).astype(jnp.bfloat16)
+
+
+def product_kernel(base, row_count, cols, wave_count, place_ref, leg_ref, *refs):
+    sources = refs[:wave_count]
+    far_out, far_own, near_out, near_own, table, terms, sems = refs[wave_count:]
+    pairs, degrees = leg_ref.shape[1:]
+    half = degrees // 2
+    group = 2 * LANES // pairs
+    lat = lax.axis_index("lat")
+    y, core = lat // 2, lat % 2
+    copies = []
+    for g in range(STEP // group):
+        at = g * group
+        copies.append(
+            pltpu.make_async_copy(
+                leg_ref.at[pl.ds(base + at, group)], table.at[pl.ds(at, group)], sems.at[g]
+            )
+        )
+        copies[-1].start()
+    held = lax.broadcasted_iota(jnp.int32, (STEP, LANES), 1) // row_count
+    zero = jnp.zeros((STEP, LANES), jnp.bfloat16)
+    parts = []
+    for source in sources:
+        value = source[base : base + STEP, :]
+        parts.append(jnp.concatenate([jnp.where(held == c, value, zero) for c in range(cols)], axis=0))
+    both = jnp.dot(
+        jnp.concatenate(parts, axis=1), place_ref[...], preferred_element_type=jnp.float32
+    )
+    north, south = both[:, :LANES], both[:, LANES:]
+    even, odd = north + south, north - south
+    far, near = jnp.where(y == 0, odd, even), jnp.where(y == 0, even, odd)
+    mask_shape = (cols * group, 2 * LANES)
+    diagonal = (lax.broadcasted_iota(jnp.int32, mask_shape, 0) & (group - 1)) == (
+        lax.broadcasted_iota(jnp.int32, mask_shape, 1) // pairs
+    )
+    blank = jnp.zeros(mask_shape, jnp.bfloat16)
+    for side, coefs, which in ((0, far, 1 - y), (1, near, y)):
+        first = pl.multiple_of(which * half, LANES)
+        for g in range(STEP // group):
+            if side == 0:
+                copies[g].wait()
+            block = jnp.concatenate(
+                [coefs[c * STEP + g * group : c * STEP + (g + 1) * group] for c in range(cols)], axis=0
+            ).astype(jnp.bfloat16)
+            block = jnp.where(diagonal, jnp.concatenate([block, block], axis=1), blank)
+            weights = table[g * group : (g + 1) * group, :, pl.ds(first, half)]
+            got = jnp.dot(
+                block, weights.reshape(group * pairs, half), preferred_element_type=jnp.float32
+            )
+            for c in range(cols):
+                terms[side, pl.ds(c * STEP + g * group, group), :] = got[c * group : (c + 1) * group]
+    rows = STEP * cols
+    part = rows // 4
+    lane_low = lax.broadcasted_iota(jnp.int32, (part, LANES), 1) < LANES // 2
+    for side, sent, kept in ((0, far_out, far_own), (1, near_out, near_own)):
+        for out, target in ((sent, 1 - core), (kept, core)):
+            first = pl.multiple_of(target * 3 * LANES, LANES)
+            out[:rows, :] = terms[side, :, pl.ds(first, 2 * LANES)].astype(out.dtype)
+        for j in range(2):
+            low = terms[side, pl.ds(2 * j * part, part), pl.ds(2 * LANES, LANES)]
+            high = terms[side, pl.ds((2 * j + 1) * part, part), pl.ds(2 * LANES, LANES)]
+            zeroth = jnp.where(lane_low, low, pltpu.roll(high, LANES // 2, 1))
+            other = jnp.where(lane_low, pltpu.roll(low, LANES // 2, 1), high)
+            for out, target in ((sent, 1 - core), (kept, core)):
+                out[rows:, j * LANES : (j + 1) * LANES] = jnp.where(target == 0, zeroth, other).astype(
+                    out.dtype
+                )
+
+
+def final_kernel(slots, base, degrees, cols, table_ref, own_ref, near_ref, far_ref, *refs):
+    out = refs[-1]
+    lat, me = lax.axis_index("lat"), lax.axis_index("wave")
+    first = lat % 2 == 0
+    half = degrees // 2
+    width = out.shape[2]
+    rows = STEP * cols
+    value = own_ref[...] + near_ref[...].astype(jnp.float32) + far_ref[...].astype(jnp.float32)
+    main0, main1 = value[:rows, :LANES], value[:rows, LANES:]
+    tails = []
+    for j in range(4):
+        tail = value[rows:, (j // 2) * LANES : (j // 2 + 1) * LANES]
+        tails.append(pltpu.roll(tail, LANES // 2, 1) if j % 2 else tail)
+    tail = jnp.concatenate(tails, axis=0)
+    lane_low = lax.broadcasted_iota(jnp.int32, (rows, LANES), 1) < LANES // 2
+    turn0, turn1 = pltpu.roll(main0, LANES // 2, 1), pltpu.roll(main1, LANES // 2, 1)
+    ordered = jnp.concatenate(
+        [
+            jnp.where(first, main0, jnp.where(lane_low, tail, turn0)),
+            jnp.where(first, main1, jnp.where(lane_low, turn0, turn1)),
+            jnp.where(first, tail, turn1),
+        ],
+        axis=1,
+    )
+    shape = (STEP, 3 * LANES)
+    degree = lat * width + lax.broadcasted_iota(jnp.int32, shape, 1)
+    offsets = jnp.where(degree < half, 2 * degree, 2 * (degree - half) + 1)
+    line = lax.broadcasted_iota(jnp.int32, shape, 0)
+    start = me * slots + base
+    limits = jnp.zeros(shape, jnp.int32)
+    for s in range(STEP):
+        limits = jnp.where(line == s, degrees - table_ref[start + s], limits)
+    inside = offsets < limits
+    for c in range(cols):
+        out[c] = jnp.where(inside, ordered[c * STEP : (c + 1) * STEP], 0.0)[:, :width]
+
+
+def packed(fourier, wave_table, legendre):
+    slots, pairs, degrees = legendre.shape
+    row_count, cols, waves = fourier.shape
+    wave_count, lat_count = lax.axis_size("wave"), lax.axis_size("lat")
+    width = degrees // lat_count
+    params = pltpu.CompilerParams(vmem_limit_bytes=VMEM)
+    whole = pl.BlockSpec(memory_space=pltpu.VMEM)
+    anywhere = pl.BlockSpec(memory_space=pl.ANY)
+
+    ordered = pl.pallas_call(
+        functools.partial(gather_kernel, slots),
+        out_shape=[jax.ShapeDtypeStruct((slots, LANES), jnp.bfloat16)] * wave_count,
+        in_specs=[whole, whole],
+        out_specs=[whole] * wave_count,
+        scratch_shapes=[pltpu.VMEM((slots * wave_count, LANES), jnp.bfloat16)],
+        compiler_params=params,
+        name="gather",
+    )(
+        wave_table.reshape(-1, LANES),
+        jnp.transpose(fourier, (1, 0, 2)).reshape(cols * row_count, waves),
+    )
+    place = pl.pallas_call(
+        functools.partial(place_kernel, wave_count, lat_count, row_count, pairs),
+        out_shape=jax.ShapeDtypeStruct((wave_count * LANES, 2 * LANES), jnp.bfloat16),
+        out_specs=whole,
+        compiler_params=params,
+        name="place",
+    )()
+
+    arrived = []
+    for turn in range(wave_count):
+        route = []
+        for lat in range(lat_count):
+            for wave in range(wave_count):
+                to = lat if wave < wave_count // 2 else lat_count - 1 - lat
+                route.append((lat * wave_count + wave, to * wave_count + (wave ^ turn)))
+        arrived.append(lax.ppermute(ordered[turn], ("lat", "wave"), route))
+
+    rows = STEP * cols
+    message = (rows + rows // 4, 2 * LANES)
+    group = 2 * LANES // pairs
+    core_route = [(lat, lat ^ 1) for lat in range(lat_count)]
+    y_route = [(lat, lat ^ 2) for lat in range(lat_count)]
+    waiting, sent = [], []
+    for base in range(0, slots, STEP):
+        held = list(arrived)
+        if len(sent) > 1:
+            held, sent[-2] = lax.optimization_barrier((held, sent[-2]))
+        far_out, far_own, near_out, near_own = pl.pallas_call(
+            functools.partial(product_kernel, base, row_count, cols, wave_count),
+            out_shape=[
+                jax.ShapeDtypeStruct(message, jnp.bfloat16),
+                jax.ShapeDtypeStruct(message, jnp.float32),
+                jax.ShapeDtypeStruct(message, jnp.bfloat16),
+                jax.ShapeDtypeStruct(message, jnp.float32),
+            ],
+            in_specs=[whole, anywhere] + [whole] * wave_count,
+            out_specs=[whole] * 4,
+            scratch_shapes=[
+                pltpu.VMEM((STEP, pairs, degrees), jnp.bfloat16),
+                pltpu.VMEM((2, rows, degrees // 2), jnp.float32),
+                pltpu.SemaphoreType.DMA((STEP // group,)),
+            ],
+            compiler_params=params,
+            cost_estimate=pl.CostEstimate(
+                flops=2 * STEP * pairs * group * cols * degrees,
+                bytes_accessed=2 * STEP * pairs * degrees,
+                transcendentals=0,
+            ),
+            name="product",
+        )(place, legendre, *held)
+        far_in = lax.ppermute(far_out, "lat", core_route)
+        sent.append((far_own + far_in.astype(jnp.float32)).astype(jnp.bfloat16))
+        waiting.append((base, near_own, near_out))
+
+    out = None
+    for (base, near_own, near_out), across in zip(waiting, sent):
+        near_in = lax.ppermute(near_out, "lat", core_route)
+        far_sum = lax.ppermute(across, "lat", y_route)
+        carried = [] if out is None else [out]
+        out = pl.pallas_call(
+            functools.partial(final_kernel, slots, base, degrees, cols),
+            grid_spec=pltpu.PrefetchScalarGridSpec(
+                num_scalar_prefetch=1,
+                grid=(1,),
+                in_specs=[pl.BlockSpec(message, lambda g, table: (0, 0))] * 3
+                + [anywhere] * len(carried),
+                out_specs=pl.BlockSpec(
+                    (cols, STEP, width), lambda g, table, at=base // STEP: (0, at, 0)
+                ),
+            ),
+            out_shape=jax.ShapeDtypeStruct((cols, slots, width), jnp.float32),
+            input_output_aliases={4: 0} if carried else {},
+            compiler_params=params,
+            cost_estimate=pl.CostEstimate(
+                flops=0, bytes_accessed=16 * STEP * cols * width, transcendentals=0
+            ),
+            name="final",
+        )(wave_table, near_own, near_in, far_sum, *carried)
+    return jnp.transpose(out, (1, 0, 2))
+
+
+def local(fourier, wave_table, legendre):
+    slots, pairs, degrees = legendre.shape
+    row_count, cols, waves = fourier.shape
+    wave_count, lat_count = lax.axis_size("wave"), lax.axis_size("lat")
+    fits = (
+        lat_count == 4
+        and wave_count & (wave_count - 1) == 0
+        and slots % STEP == 0
+        and degrees // 2 == 5 * LANES
+        and row_count & (row_count - 1) == 0
+        and row_count * cols <= LANES
+        and pairs == row_count * wave_count // 2
+        and pairs * TILE == 2 * LANES
+        and waves % (2 * LANES) == 0
+    )
+    if not fits:
+        return plain(fourier, wave_table, legendre)
+    return packed(fourier, wave_table, legendre)
+
+
 def solution(mesh):
     in_specs = (P(("lat", "wave"), None, None), P(), P("wave", "lat", None))
     out_specs = P("wave", None, "lat")

time: 355 us -> 66 us (0.19); the launches traced: 351 us -> 65.7 us
  local copies, waits for them, and re-layouts: 209 us -> 1.65 us
  waiting for transfers between devices: 85.9 us -> 17 us
  Pallas kernels: 0 us -> 22.5 us
  starting transfers between devices: 1.59 us -> 24 us
  other arithmetic: 17 us -> 0.34 us
  blocking collectives: 15.7 us -> 0 us
  between operations: 13.5 us -> 0.14 us
  matrix products: 8.06 us -> 0 us
    unnamed x7 -> x6, local copies, waits for them, and re-layouts: 199 us -> 1.65 us
    unnamed x2 -> x0, waiting for transfers between devices: 79.2 us -> none
    pallas_call x0 -> x12, Pallas kernels: none -> 22.5 us  [the longest x5 13.5 us: packed(): pl.pallas_call(functools.partial(product_kernel, base, row_count, cols, w...]
    ppermute x2 -> x23, starting transfers between devices: 1.59 us -> 24 us  [the longest x8 16.3 us: packed(): arrived.append(lax.ppermute(ordered[turn], ('lat', 'wave'), route))]
    all_to_all x1 -> x0, blocking collectives: 15.7 us -> none  [local(): lax.all_to_all(ordered, 'wave', split_axis=2, concat_axis=0, tiled=True)]
    ppermute x2 -> x23, waiting for transfers between devices: 6.68 us -> 17 us  [the longest x5 9.09 us: packed(): far_sum = lax.ppermute(across, 'lat', y_route)]
    dot_general x2 -> x0, matrix products: 8.06 us -> none  [the longest x1 4.03 us: local(): jnp.einsum('mcp,mpk->mck', even_part, legendre[:, :, :half_degrees], pref...]
    unnamed x1 -> x0, other arithmetic: 6.61 us -> none
  transfers between devices with their start and end apart: 3 -> 23, of which waited for: 3 -> 7; matrix products, arithmetic and copies ran while one was open for 0% -> 1% of each run, Pallas kernels for 0% -> 27%
where the time goes in v2:
time: 66 us; the launch traced here: 65.7 us
  starting transfers between devices  24 us (36%)
  Pallas kernels  22.5 us (34%)
  waiting for transfers between devices  17 us (26%)
  local copies, waits for them, and re-layouts  1.65 us (2%)
    ppermute x8, starting transfers between devices, packed(): arrived.append(lax.ppermute(ordered[turn], ('lat', 'wave'), route))  16.3 us
    pallas_call x5, Pallas kernels, packed(): pl.pallas_call(functools.partial(product_kernel, base, row_count, cols, w...  13.5 us
    ppermute x5, waiting for transfers between devices, packed(): far_sum = lax.ppermute(across, 'lat', y_route)  9.09 us
    pallas_call x5, Pallas kernels, packed(): pl.pallas_call(functools.partial(final_kernel, slots, base, degrees, cols...  8.2 us
    ppermute x8, waiting for transfers between devices, packed(): arrived.append(lax.ppermute(ordered[turn], ('lat', 'wave'), route))  6.81 us
    ppermute x5, starting transfers between devices, packed(): far_sum = lax.ppermute(across, 'lat', y_route)  4.92 us
    ppermute x5, starting transfers between devices, packed(): far_in = lax.ppermute(far_out, 'lat', core_route)  2.09 us
    unnamed x6, local copies, waits for them, and re-layouts  1.65 us
  transfers between devices with their start and end apart: 23, of which 7 were waited for; matrix products, arithmetic and copies ran while one was open for 1% of the time, Pallas kernels for 27%

profile of v2, /device:TPU:0, one launch (start us, length us, event | category | flops | bytes accessed | tf_op | source)
XLA Modules:
  0.0 65.7 jit_solution(10125975939432789337)
XLA Ops:
  0.0 0.7 %copy-done = s32[1280]{0:T(1024)S(1)} copy-done((s32[1280]{0:T(1024)S(1)}, s32[1280]{0:T(1024)}, u32[]{:S(2)}) %copy-start) | copy-done | bytes 5144
  0.7 0.9 %copy-done.2 = bf16[8,12,1280]{2,0,1:T(8,128)(2,1)S(1)} copy-done((bf16[8,12,1280]{2,0,1:T(8,128)(2,1)S(1)}, bf16[8,12,1280]{2,0,1:T(8,128)(2,1)}, u32[]{:S(2)}) %copy-start.2) | copy-done | bytes 245784
  1.6 0.7 %gather.1 = (bf16[160,128]{1,0:T(8,128)(2,1)S(1)}, bf16[160,128]{1,0:T(8,128)(2,1)S(1)}, bf16[160,128]{1,0:T(8,128)(2,1)S(1)}, bf16[160,128]{1,0:T(8,128)(2,1)S(...) custom-call(s32[10,128]{1,0:T(8,128)S(1)} %bitcast.5, ...), custom_call_target="tpu_custom_call" | custom-call | tf_op jit(solution)/shard_map/gather/pallas_call | solution.py:207
  2.4 0.7 %collective-permute-start = (bf16[160,128]{1,0:T(8,128)(2,1)S(1)}, bf16[160,128]{1,0:T(8,128)(2,1)S(1)}, u32[]{:S(2)}, u32[]{:S(2)}) collective-permute-start(bf16[160,128]{1,0:T(8,128)(2,1)S(1)} %get-tuple-element.60), channel_id=1, source_target_pairs={{0,0},{1,1},{2,2},{3,3},{4,28},{5,29},{6,30},{7,31},{8,8},{9,9},{1... | collective-permute-start | bytes 122888 | tf_op jit(solution)/shard_map/ppermute | solution.py:234
  3.0 3.0 %collective-permute-start.1 = (bf16[160,128]{1,0:T(8,128)(2,1)S(1)}, bf16[160,128]{1,0:T(8,128)(2,1)S(1)}, u32[]{:S(2)}, u32[]{:S(2)}) collective-permute-start(bf16[160,128]{1,0:T(8,128)(2,1)S(1)} %get-tuple-element.61), channel_id=1, source_target_pairs={{0,1},{1,0},{2,3},{3,2},{4,29},{5,28},{6,31},{7,30},{8,9},{9,8},{1... | collective-permute-start | bytes 122888 | tf_op jit(solution)/shard_map/ppermute | solution.py:234
  6.0 1.6 %collective-permute-start.2 = (bf16[160,128]{1,0:T(8,128)(2,1)S(1)}, bf16[160,128]{1,0:T(8,128)(2,1)S(1)}, u32[]{:S(2)}, u32[]{:S(2)}) collective-permute-start(bf16[160,128]{1,0:T(8,128)(2,1)S(1)} %get-tuple-element.62), channel_id=1, source_target_pairs={{0,2},{1,3},{2,0},{3,1},{4,30},{5,31},{6,28},{7,29},{8,10},{9,11},... | collective-permute-start | bytes 122888 | tf_op jit(solution)/shard_map/ppermute | solution.py:234
  7.6 0.0 collective-permute-start.3
  7.6 6.1 %collective-permute-start.4 = (bf16[160,128]{1,0:T(8,128)(2,1)S(1)}, bf16[160,128]{1,0:T(8,128)(2,1)S(1)}, u32[]{:S(2)}, u32[]{:S(2)}) collective-permute-start(bf16[160,128]{1,0:T(8,128)(2,1)S(1)} %get-tuple-element.64), channel_id=1, source_target_pairs={{0,4},{1,5},{2,6},{3,7},{4,24},{5,25},{6,26},{7,27},{8,12},{9,13},... | collective-permute-start | bytes 122888 | tf_op jit(solution)/shard_map/ppermute | solution.py:234
  13.7 0.0 collective-permute-done.refs_0_
  13.7 0.9 %collective-permute-start.5 = (bf16[160,128]{1,0:T(8,128)(2,1)S(1)}, bf16[160,128]{1,0:T(8,128)(2,1)S(1)}, u32[]{:S(2)}, u32[]{:S(2)}) collective-permute-start(bf16[160,128]{1,0:T(8,128)(2,1)S(1)} %get-tuple-element.65), channel_id=1, source_target_pairs={{0,5},{1,4},{2,7},{3,6},{4,25},{5,24},{6,27},{7,26},{8,13},{9,12},... | collective-permute-start | bytes 122888 | tf_op jit(solution)/shard_map/ppermute | solution.py:234
  14.6 0.0 collective-permute-done.1.refs_1_
  14.6 4.1 %collective-permute-start.6 = (bf16[160,128]{1,0:T(8,128)(2,1)S(1)}, bf16[160,128]{1,0:T(8,128)(2,1)S(1)}, u32[]{:S(2)}, u32[]{:S(2)}) collective-permute-start(bf16[160,128]{1,0:T(8,128)(2,1)S(1)} %get-tuple-element.66), channel_id=1, source_target_pairs={{0,6},{1,7},{2,4},{3,5},{4,26},{5,27},{6,24},{7,25},{8,14},{9,15},... | collective-permute-start | bytes 122888 | tf_op jit(solution)/shard_map/ppermute | solution.py:234
  18.7 0.0 collective-permute-done.2.refs_2_
  18.7 0.0 collective-permute-start.7
  18.7 0.2 place.1.place_ref
  18.9 0.0 collective-permute-done.3.refs_3_
  18.9 0.0 collective-permute-done.4.refs_4_
  18.9 1.3 %collective-permute-done.5.refs_5_ = bf16[160,128]{1,0:T(8,128)(2,1)S(1)} collective-permute-done((bf16[160,128]{1,0:T(8,128)(2,1)S(1)}, bf16[160,128]{1,0:T(8,128)(2,1)S(1)}, u32[]{:S(2)}, u32[]{:S(2)}) %collective-permute-start.5) | collective-permute-done | bytes 40992 | tf_op jit(solution)/shard_map/ppermute | solution.py:234
  20.2 1.8 %collective-permute-done.6.refs_6_ = bf16[160,128]{1,0:T(8,128)(2,1)S(1)} collective-permute-done((bf16[160,128]{1,0:T(8,128)(2,1)S(1)}, bf16[160,128]{1,0:T(8,128)(2,1)S(1)}, u32[]{:S(2)}, u32[]{:S(2)}) %collective-permute-start.6) | collective-permute-done | bytes 40992 | tf_op jit(solution)/shard_map/ppermute | solution.py:234
  22.1 3.6 %collective-permute-done.7.refs_7_ = bf16[160,128]{1,0:T(8,128)(2,1)S(1)} collective-permute-done((bf16[160,128]{1,0:T(8,128)(2,1)S(1)}, bf16[160,128]{1,0:T(8,128)(2,1)S(1)}, u32[]{:S(2)}, u32[]{:S(2)}) %collective-permute-start.7) | collective-permute-done | bytes 40992 | tf_op jit(solution)/shard_map/ppermute | solution.py:234
  25.7 2.7 %product.5 = (bf16[480,256]{1,0:T(8,128)(2,1)S(1)}, f32[480,256]{1,0:T(8,128)S(1)}, bf16[480,256]{1,0:T(8,128)(2,1)S(1)}, f32[480,256]{1,0:T(8,128)S(1)}) custom-call(bf16[1024,256]{1,0:T(8,128)(2,1)S(1)} %place.1.place_ref, bf16[160,32,1280]{2,1,0:T(8,128)(2,1)} %leg_ref.9, bf16[160,128]{1,0:T(8,128)(2,1)S(1)} %collective-permute-done.refs_0_, ...), custom_call_target="tpu_custom_call" | custom-call | flops 251658240 | bytes 2621440 | tf_op jit(solution)/shard_map/product/pallas_call | solution.py:246
  28.4 0.7 %collective-permute-start.8 = (bf16[480,256]{1,0:T(8,128)(2,1)S(1)}, bf16[480,256]{1,0:T(8,128)(2,1)S(1)}, u32[]{:S(2)}, u32[]{:S(2)}) collective-permute-start(bf16[480,256]{1,0:T(8,128)(2,1)S(1)} %get-tuple-element.69), channel_id=1, source_target_pairs={{0,8},{8,0},{16,24},{24,16},{1,9},{9,1},{17,25},{25,17},{2,10},{10... | collective-permute-start | bytes 737288 | tf_op jit(solution)/shard_map/ppermute | solution.py:269
  29.1 0.1 collective-permute-start.21
  29.2 2.7 %product.8 = (bf16[480,256]{1,0:T(8,128)(2,1)S(1)}, f32[480,256]{1,0:T(8,128)S(1)}, bf16[480,256]{1,0:T(8,128)(2,1)S(1)}, f32[480,256]{1,0:T(8,128)S(1)}) custom-call(bf16[1024,256]{1,0:T(8,128)(2,1)S(1)} %place.1.place_ref, bf16[160,32,1280]{2,1,0:T(8,128)(2,1)} %leg_ref.9, bf16[160,128]{1,0:T(8,128)(2,1)S(1)} %collective-permute-done.refs_0_, ...), custom_call_target="tpu_custom_call" | custom-call | flops 251658240 | bytes 2621440 | tf_op jit(solution)/shard_map/product/pallas_call | solution.py:246
  31.9 0.5 collective-permute-start.13
  32.4 0.1 collective-permute-start.19
  32.5 0.0 collective-permute-done.8
  32.5 0.1 add_convert_fusion.4
  32.6 0.6 collective-permute-start.22
  33.2 2.7 %product.6 = (bf16[480,256]{1,0:T(8,128)(2,1)S(1)}, f32[480,256]{1,0:T(8,128)S(1)}, bf16[480,256]{1,0:T(8,128)(2,1)S(1)}, f32[480,256]{1,0:T(8,128)S(1)}) custom-call(bf16[1024,256]{1,0:T(8,128)(2,1)S(1)} %place.1.place_ref, bf16[160,32,1280]{2,1,0:T(8,128)(2,1)} %leg_ref.9, bf16[160,128]{1,0:T(8,128)(2,1)S(1)} %collective-permute-done.refs_0_, ...), custom_call_target="tpu_custom_call" | custom-call | flops 251658240 | bytes 2621440 | tf_op jit(solution)/shard_map/product/pallas_call | solution.py:246
  35.9 0.2 collective-permute-start.9
  36.1 0.0 collective-permute-done.13
  36.1 0.1 add_convert_fusion.1
  36.2 1.6 %collective-permute-start.20 = (bf16[480,256]{1,0:T(8,128)(2,1)S(1)}, bf16[480,256]{1,0:T(8,128)(2,1)S(1)}, u32[]{:S(2)}, u32[]{:S(2)}) collective-permute-start(bf16[480,256]{1,0:T(8,128)(2,1)S(1)} %add_convert_fusion.1), channel_id=1, source_target_pairs={{0,16},{8,24},{16,0},{24,8},{1,17},{9,25},{17,1},{25,9},{2,18},{10... | collective-permute-start | bytes 737288 | tf_op jit(solution)/shard_map/ppermute | solution.py:276
  37.7 2.7 %product.9 = (bf16[480,256]{1,0:T(8,128)(2,1)S(1)}, f32[480,256]{1,0:T(8,128)S(1)}, bf16[480,256]{1,0:T(8,128)(2,1)S(1)}, f32[480,256]{1,0:T(8,128)S(1)}) custom-call(bf16[1024,256]{1,0:T(8,128)(2,1)S(1)} %place.1.place_ref, bf16[160,32,1280]{2,1,0:T(8,128)(2,1)} %leg_ref.9, bf16[160,128]{1,0:T(8,128)(2,1)S(1)} %collective-permute-done.refs_0_, ...), custom_call_target="tpu_custom_call" | custom-call | flops 251658240 | bytes 2621440 | tf_op jit(solution)/shard_map/product/pallas_call | solution.py:246
  40.4 0.0 collective-permute-done.9
  40.5 0.1 collective-permute-start.15
  40.6 0.1 add_convert_fusion.3
  40.6 0.0 copy-start.1
  40.7 2.7 %product.7 = (bf16[480,256]{1,0:T(8,128)(2,1)S(1)}, f32[480,256]{1,0:T(8,128)S(1)}, bf16[480,256]{1,0:T(8,128)(2,1)S(1)}, f32[480,256]{1,0:T(8,128)S(1)}) custom-call(bf16[1024,256]{1,0:T(8,128)(2,1)S(1)} %place.1.place_ref, bf16[160,32,1280]{2,1,0:T(8,128)(2,1)} %leg_ref.9, bf16[160,128]{1,0:T(8,128)(2,1)S(1)} %collective-permute-done.refs_0_, ...), custom_call_target="tpu_custom_call" | custom-call | flops 251658240 | bytes 2621440 | tf_op jit(solution)/shard_map/product/pallas_call | solution.py:246
  43.4 0.0 collective-permute-done.15
  43.4 0.5 collective-permute-start.11
  43.9 0.1 add_convert_fusion
  43.9 1.1 %collective-permute-done.11 = bf16[480,256]{1,0:T(8,128)(2,1)S(1)} collective-permute-done((bf16[480,256]{1,0:T(8,128)(2,1)S(1)}, bf16[480,256]{1,0:T(8,128)(2,1)S(1)}, u32[]{:S(2)}, u32[]{:S(2)}) %collective-permute-start.11) | collective-permute-done | bytes 245792 | tf_op jit(solution)/shard_map/ppermute | solution.py:269
  45.0 0.4 collective-permute-start.17
  45.4 0.1 add_convert_fusion.2
  45.4 0.0 collective-permute-done.21.near_ref
  45.5 0.7 collective-permute-start.18
  46.1 0.0 collective-permute-done.19.near_ref
  46.1 0.0 collective-permute-start.14
  46.1 0.0 collective-permute-done.22.far_ref
  46.1 1.5 %collective-permute-start.16 = (bf16[480,256]{1,0:T(8,128)(2,1)S(1)}, bf16[480,256]{1,0:T(8,128)(2,1)S(1)}, u32[]{:S(2)}, u32[]{:S(2)}) collective-permute-start(bf16[480,256]{1,0:T(8,128)(2,1)S(1)} %add_convert_fusion), channel_id=1, source_target_pairs={{0,16},{8,24},{16,0},{24,8},{1,17},{9,25},{17,1},{25,9},{2,18},{10... | collective-permute-start | bytes 737288 | tf_op jit(solution)/shard_map/ppermute | solution.py:276
  47.6 0.0 collective-permute-done.20.far_ref
  47.6 0.2 collective-permute-start.10
  47.8 0.0 collective-permute-done.17.near_ref
  47.8 0.6 collective-permute-start.12
  48.4 1.6 %final.5.refs_0_ = f32[12,160,320]{2,1,0:T(8,128)} custom-call(s32[1280]{0:T(1024)S(1)} %copy-done.1, f32[480,256]{1,0:T(8,128)S(1)} %get-tuple-element.112.own_ref, bf16[480,256]{1,0:T(8,128)(2,1)S(1)} %collective-permute-done.21.near_ref, bf16[480,256]{1,0:T(8,128)(2,1)S(1)} %collective-permute-done.22.far_ref), custom_call_target="tpu_custom_call" | custom-call | bytes 1966080 | tf_op jit(solution)/shard_map/final/pallas_call | solution.py:278
  50.0 1.7 %final.6.refs_0_ = f32[12,160,320]{2,1,0:T(8,128)} custom-call(s32[1280]{0:T(1024)S(1)} %copy-done.1, f32[480,256]{1,0:T(8,128)S(1)} %get-tuple-element.109.own_ref, bf16[480,256]{1,0:T(8,128)(2,1)S(1)} %collective-permute-done.19.near_ref, bf16[480,256]{1,0:T(8,128)(2,1)S(1)} %collective-permute-done.20.far_ref, ...), custom_call_target="tpu_custom_call", output_to_operand_aliasing={{}: (4, {})} | custom-call | bytes 1966080 | tf_op jit(solution)/shard_map/final/pallas_call | solution.py:278
  51.7 2.6 %collective-permute-done.18.far_ref = bf16[480,256]{1,0:T(8,128)(2,1)S(1)} collective-permute-done((bf16[480,256]{1,0:T(8,128)(2,1)S(1)}, bf16[480,256]{1,0:T(8,128)(2,1)S(1)}, u32[]{:S(2)}, u32[]{:S(2)}) %collective-permute-start.18) | collective-permute-done | bytes 245792 | tf_op jit(solution)/shard_map/ppermute | solution.py:276
  54.3 1.6 %final.7.refs_0_ = f32[12,160,320]{2,1,0:T(8,128)} custom-call(s32[1280]{0:T(1024)S(1)} %copy-done.1, f32[480,256]{1,0:T(8,128)S(1)} %get-tuple-element.106.own_ref, bf16[480,256]{1,0:T(8,128)(2,1)S(1)} %collective-permute-done.17.near_ref, bf16[480,256]{1,0:T(8,128)(2,1)S(1)} %collective-permute-done.18.far_ref, ...), custom_call_target="tpu_custom_call", output_to_operand_aliasing={{}: (4, {})} | custom-call | bytes 1966080 | tf_op jit(solution)/shard_map/final/pallas_call | solution.py:278
  56.0 3.6 %collective-permute-done.16.far_ref = bf16[480,256]{1,0:T(8,128)(2,1)S(1)} collective-permute-done((bf16[480,256]{1,0:T(8,128)(2,1)S(1)}, bf16[480,256]{1,0:T(8,128)(2,1)S(1)}, u32[]{:S(2)}, u32[]{:S(2)}) %collective-permute-start.16) | collective-permute-done | bytes 245792 | tf_op jit(solution)/shard_map/ppermute | solution.py:276
  59.6 1.6 %final.8.refs_0_ = f32[12,160,320]{2,1,0:T(8,128)} custom-call(s32[1280]{0:T(1024)S(1)} %copy-done.1, f32[480,256]{1,0:T(8,128)S(1)} %get-tuple-element.102.own_ref, bf16[480,256]{1,0:T(8,128)(2,1)S(1)} %collective-permute-done.14.near_ref, bf16[480,256]{1,0:T(8,128)(2,1)S(1)} %collective-permute-done.16.far_ref, ...), custom_call_target="tpu_custom_call", output_to_operand_aliasing={{}: (4, {})} | custom-call | bytes 1966080 | tf_op jit(solution)/shard_map/final/pallas_call | solution.py:278
  61.2 2.8 %collective-permute-done.12.far_ref = bf16[480,256]{1,0:T(8,128)(2,1)S(1)} collective-permute-done((bf16[480,256]{1,0:T(8,128)(2,1)S(1)}, bf16[480,256]{1,0:T(8,128)(2,1)S(1)}, u32[]{:S(2)}, u32[]{:S(2)}) %collective-permute-start.12) | collective-permute-done | bytes 245792 | tf_op jit(solution)/shard_map/ppermute | solution.py:276
  64.1 1.6 %final.9 = f32[12,160,320]{2,1,0:T(8,128)} custom-call(s32[1280]{0:T(1024)S(1)} %copy-done.1, f32[480,256]{1,0:T(8,128)S(1)} %get-tuple-element.88.own_ref, bf16[480,256]{1,0:T(8,128)(2,1)S(1)} %collective-permute-done.10.near_ref, bf16[480,256]{1,0:T(8,128)(2,1)S(1)} %collective-permute-done.12.far_ref, ...), custom_call_target="tpu_custom_call", output_to_operand_aliasing={{}: (4, {})} | custom-call | bytes 1966080 | tf_op jit(solution)/shard_map/final/pallas_call | solution.py:278
  (5 shorter events, 0.0 us)
Async XLA Ops:
  0.0 0.7 %copy-start = (s32[1280]{0:T(1024)S(1)}, s32[1280]{0:T(1024)}, u32[]{:S(2)}) copy-start(s32[1280]{0:T(1024)} %table_ref.9) | copy-start | bytes 15364
  0.7 0.9 %copy-start.2 = (bf16[8,12,1280]{2,0,1:T(8,128)(2,1)S(1)}, bf16[8,12,1280]{2,0,1:T(8,128)(2,1)}, u32[]{:S(2)}) copy-start(bf16[8,12,1280]{2,0,1:T(8,128)(2,1)} %param.3) | copy-start | bytes 737284
  2.4 11.3 %collective-permute-start = (bf16[160,128]{1,0:T(8,128)(2,1)S(1)}, bf16[160,128]{1,0:T(8,128)(2,1)S(1)}, u32[]{:S(2)}, u32[]{:S(2)}) collective-permute-start(bf16[160,128]{1,0:T(8,128)(2,1)S(1)} %get-tuple-element.60), channel_id=1, source_target_pairs={{0,0},{1,1},{2,2},{3,3},{4,28},{5,29},{6,30},{7,31},{8,8},{9,9},{1... | collective-permute-start | bytes 122888 | tf_op jit(solution)/shard_map/ppermute | solution.py:234
  3.0 11.6 %collective-permute-start.1 = (bf16[160,128]{1,0:T(8,128)(2,1)S(1)}, bf16[160,128]{1,0:T(8,128)(2,1)S(1)}, u32[]{:S(2)}, u32[]{:S(2)}) collective-permute-start(bf16[160,128]{1,0:T(8,128)(2,1)S(1)} %get-tuple-element.61), channel_id=1, source_target_pairs={{0,1},{1,0},{2,3},{3,2},{4,29},{5,28},{6,31},{7,30},{8,9},{9,8},{1... | collective-permute-start | bytes 122888 | tf_op jit(solution)/shard_map/ppermute | solution.py:234
  6.0 12.6 %collective-permute-start.2 = (bf16[160,128]{1,0:T(8,128)(2,1)S(1)}, bf16[160,128]{1,0:T(8,128)(2,1)S(1)}, u32[]{:S(2)}, u32[]{:S(2)}) collective-permute-start(bf16[160,128]{1,0:T(8,128)(2,1)S(1)} %get-tuple-element.62), channel_id=1, source_target_pairs={{0,2},{1,3},{2,0},{3,1},{4,30},{5,31},{6,28},{7,29},{8,10},{9,11},... | collective-permute-start | bytes 122888 | tf_op jit(solution)/shard_map/ppermute | solution.py:234
  7.6 11.3 %collective-permute-start.3 = (bf16[160,128]{1,0:T(8,128)(2,1)S(1)}, bf16[160,128]{1,0:T(8,128)(2,1)S(1)}, u32[]{:S(2)}, u32[]{:S(2)}) collective-permute-start(bf16[160,128]{1,0:T(8,128)(2,1)S(1)} %get-tuple-element.63), channel_id=1, source_target_pairs={{0,3},{1,2},{2,1},{3,0},{4,31},{5,30},{6,29},{7,28},{8,11},{9,10},... | collective-permute-start | bytes 122888 | tf_op jit(solution)/shard_map/ppermute | solution.py:234
  7.6 11.3 %collective-permute-start.4 = (bf16[160,128]{1,0:T(8,128)(2,1)S(1)}, bf16[160,128]{1,0:T(8,128)(2,1)S(1)}, u32[]{:S(2)}, u32[]{:S(2)}) collective-permute-start(bf16[160,128]{1,0:T(8,128)(2,1)S(1)} %get-tuple-element.64), channel_id=1, source_target_pairs={{0,4},{1,5},{2,6},{3,7},{4,24},{5,25},{6,26},{7,27},{8,12},{9,13},... | collective-permute-start | bytes 122888 | tf_op jit(solution)/shard_map/ppermute | solution.py:234
  13.7 6.6 %collective-permute-start.5 = (bf16[160,128]{1,0:T(8,128)(2,1)S(1)}, bf16[160,128]{1,0:T(8,128)(2,1)S(1)}, u32[]{:S(2)}, u32[]{:S(2)}) collective-permute-start(bf16[160,128]{1,0:T(8,128)(2,1)S(1)} %get-tuple-element.65), channel_id=1, source_target_pairs={{0,5},{1,4},{2,7},{3,6},{4,25},{5,24},{6,27},{7,26},{8,13},{9,12},... | collective-permute-start | bytes 122888 | tf_op jit(solution)/shard_map/ppermute | solution.py:234
  14.6 7.5 %collective-permute-start.6 = (bf16[160,128]{1,0:T(8,128)(2,1)S(1)}, bf16[160,128]{1,0:T(8,128)(2,1)S(1)}, u32[]{:S(2)}, u32[]{:S(2)}) collective-permute-start(bf16[160,128]{1,0:T(8,128)(2,1)S(1)} %get-tuple-element.66), channel_id=1, source_target_pairs={{0,6},{1,7},{2,4},{3,5},{4,26},{5,27},{6,24},{7,25},{8,14},{9,15},... | collective-permute-start | bytes 122888 | tf_op jit(solution)/shard_map/ppermute | solution.py:234
  18.7 7.0 %collective-permute-start.7 = (bf16[160,128]{1,0:T(8,128)(2,1)S(1)}, bf16[160,128]{1,0:T(8,128)(2,1)S(1)}, u32[]{:S(2)}, u32[]{:S(2)}) collective-permute-start(bf16[160,128]{1,0:T(8,128)(2,1)S(1)} %get-tuple-element.67), channel_id=1, source_target_pairs={{0,7},{1,6},{2,5},{3,4},{4,27},{5,26},{6,25},{7,24},{8,15},{9,14},... | collective-permute-start | bytes 122888 | tf_op jit(solution)/shard_map/ppermute | solution.py:234
  28.4 4.1 %collective-permute-start.8 = (bf16[480,256]{1,0:T(8,128)(2,1)S(1)}, bf16[480,256]{1,0:T(8,128)(2,1)S(1)}, u32[]{:S(2)}, u32[]{:S(2)}) collective-permute-start(bf16[480,256]{1,0:T(8,128)(2,1)S(1)} %get-tuple-element.69), channel_id=1, source_target_pairs={{0,8},{8,0},{16,24},{24,16},{1,9},{9,1},{17,25},{25,17},{2,10},{10... | collective-permute-start | bytes 737288 | tf_op jit(solution)/shard_map/ppermute | solution.py:269
  29.1 16.3 %collective-permute-start.21 = (bf16[480,256]{1,0:T(8,128)(2,1)S(1)}, bf16[480,256]{1,0:T(8,128)(2,1)S(1)}, u32[]{:S(2)}, u32[]{:S(2)}) collective-permute-start(bf16[480,256]{1,0:T(8,128)(2,1)S(1)} %get-tuple-element.113), channel_id=1, source_target_pairs={{0,8},{8,0},{16,24},{24,16},{1,9},{9,1},{17,25},{25,17},{2,10},{10... | collective-permute-start | bytes 737288 | tf_op jit(solution)/shard_map/ppermute | solution.py:275
  31.9 4.2 %collective-permute-start.13 = (bf16[480,256]{1,0:T(8,128)(2,1)S(1)}, bf16[480,256]{1,0:T(8,128)(2,1)S(1)}, u32[]{:S(2)}, u32[]{:S(2)}) collective-permute-start(bf16[480,256]{1,0:T(8,128)(2,1)S(1)} %get-tuple-element.93), channel_id=1, source_target_pairs={{0,8},{8,0},{16,24},{24,16},{1,9},{9,1},{17,25},{25,17},{2,10},{10... | collective-permute-start | bytes 737288 | tf_op jit(solution)/shard_map/ppermute | solution.py:269
  32.4 13.7 %collective-permute-start.19 = (bf16[480,256]{1,0:T(8,128)(2,1)S(1)}, bf16[480,256]{1,0:T(8,128)(2,1)S(1)}, u32[]{:S(2)}, u32[]{:S(2)}) collective-permute-start(bf16[480,256]{1,0:T(8,128)(2,1)S(1)} %get-tuple-element.110), channel_id=1, source_target_pairs={{0,8},{8,0},{16,24},{24,16},{1,9},{9,1},{17,25},{25,17},{2,10},{10... | collective-permute-start | bytes 737288 | tf_op jit(solution)/shard_map/ppermute | solution.py:275
  32.6 13.6 %collective-permute-start.22 = (bf16[480,256]{1,0:T(8,128)(2,1)S(1)}, bf16[480,256]{1,0:T(8,128)(2,1)S(1)}, u32[]{:S(2)}, u32[]{:S(2)}) collective-permute-start(bf16[480,256]{1,0:T(8,128)(2,1)S(1)} %add_convert_fusion.4), channel_id=1, source_target_pairs={{0,16},{8,24},{16,0},{24,8},{1,17},{9,25},{17,1},{25,9},{2,18},{10... | collective-permute-start | bytes 737288 | tf_op jit(solution)/shard_map/ppermute | solution.py:276
  35.9 4.6 %collective-permute-start.9 = (bf16[480,256]{1,0:T(8,128)(2,1)S(1)}, bf16[480,256]{1,0:T(8,128)(2,1)S(1)}, u32[]{:S(2)}, u32[]{:S(2)}) collective-permute-start(bf16[480,256]{1,0:T(8,128)(2,1)S(1)} %get-tuple-element.79), channel_id=1, source_target_pairs={{0,8},{8,0},{16,24},{24,16},{1,9},{9,1},{17,25},{25,17},{2,10},{10... | collective-permute-start | bytes 737288 | tf_op jit(solution)/shard_map/ppermute | solution.py:269
  36.2 11.5 %collective-permute-start.20 = (bf16[480,256]{1,0:T(8,128)(2,1)S(1)}, bf16[480,256]{1,0:T(8,128)(2,1)S(1)}, u32[]{:S(2)}, u32[]{:S(2)}) collective-permute-start(bf16[480,256]{1,0:T(8,128)(2,1)S(1)} %add_convert_fusion.1), channel_id=1, source_target_pairs={{0,16},{8,24},{16,0},{24,8},{1,17},{9,25},{17,1},{25,9},{2,18},{10... | collective-permute-start | bytes 737288 | tf_op jit(solution)/shard_map/ppermute | solution.py:276
  40.5 2.9 %collective-permute-start.15 = (bf16[480,256]{1,0:T(8,128)(2,1)S(1)}, bf16[480,256]{1,0:T(8,128)(2,1)S(1)}, u32[]{:S(2)}, u32[]{:S(2)}) collective-permute-start(bf16[480,256]{1,0:T(8,128)(2,1)S(1)} %get-tuple-element.105), channel_id=1, source_target_pairs={{0,8},{8,0},{16,24},{24,16},{1,9},{9,1},{17,25},{25,17},{2,10},{10... | collective-permute-start | bytes 737288 | tf_op jit(solution)/shard_map/ppermute | solution.py:269
  40.6 7.7 %copy-start.1 = (s32[1280]{0:T(1024)S(1)}, s32[1280]{0:T(1024)}, u32[]{:S(2)}) copy-start(s32[1280]{0:T(1024)} %table_ref.9) | copy-start | bytes 15364
  43.4 1.7 %collective-permute-start.11 = (bf16[480,256]{1,0:T(8,128)(2,1)S(1)}, bf16[480,256]{1,0:T(8,128)(2,1)S(1)}, u32[]{:S(2)}, u32[]{:S(2)}) collective-permute-start(bf16[480,256]{1,0:T(8,128)(2,1)S(1)} %get-tuple-element.91), channel_id=1, source_target_pairs={{0,8},{8,0},{16,24},{24,16},{1,9},{9,1},{17,25},{25,17},{2,10},{10... | collective-permute-start | bytes 737288 | tf_op jit(solution)/shard_map/ppermute | solution.py:269
  45.0 2.8 %collective-permute-start.17 = (bf16[480,256]{1,0:T(8,128)(2,1)S(1)}, bf16[480,256]{1,0:T(8,128)(2,1)S(1)}, u32[]{:S(2)}, u32[]{:S(2)}) collective-permute-start(bf16[480,256]{1,0:T(8,128)(2,1)S(1)} %get-tuple-element.107), channel_id=1, source_target_pairs={{0,8},{8,0},{16,24},{24,16},{1,9},{9,1},{17,25},{25,17},{2,10},{10... | collective-permute-start | bytes 737288 | tf_op jit(solution)/shard_map/ppermute | solution.py:275
  45.5 8.9 %collective-permute-start.18 = (bf16[480,256]{1,0:T(8,128)(2,1)S(1)}, bf16[480,256]{1,0:T(8,128)(2,1)S(1)}, u32[]{:S(2)}, u32[]{:S(2)}) collective-permute-start(bf16[480,256]{1,0:T(8,128)(2,1)S(1)} %add_convert_fusion.3), channel_id=1, source_target_pairs={{0,16},{8,24},{16,0},{24,8},{1,17},{9,25},{17,1},{25,9},{2,18},{10... | collective-permute-start | bytes 737288 | tf_op jit(solution)/shard_map/ppermute | solution.py:276
  46.1 9.8 %collective-permute-start.14 = (bf16[480,256]{1,0:T(8,128)(2,1)S(1)}, bf16[480,256]{1,0:T(8,128)(2,1)S(1)}, u32[]{:S(2)}, u32[]{:S(2)}) collective-permute-start(bf16[480,256]{1,0:T(8,128)(2,1)S(1)} %get-tuple-element.103), channel_id=1, source_target_pairs={{0,8},{8,0},{16,24},{24,16},{1,9},{9,1},{17,25},{25,17},{2,10},{10... | collective-permute-start | bytes 737288 | tf_op jit(solution)/shard_map/ppermute | solution.py:275
  46.1 13.5 %collective-permute-start.16 = (bf16[480,256]{1,0:T(8,128)(2,1)S(1)}, bf16[480,256]{1,0:T(8,128)(2,1)S(1)}, u32[]{:S(2)}, u32[]{:S(2)}) collective-permute-start(bf16[480,256]{1,0:T(8,128)(2,1)S(1)} %add_convert_fusion), channel_id=1, source_target_pairs={{0,16},{8,24},{16,0},{24,8},{1,17},{9,25},{17,1},{25,9},{2,18},{10... | collective-permute-start | bytes 737288 | tf_op jit(solution)/shard_map/ppermute | solution.py:276
  47.6 13.6 %collective-permute-start.10 = (bf16[480,256]{1,0:T(8,128)(2,1)S(1)}, bf16[480,256]{1,0:T(8,128)(2,1)S(1)}, u32[]{:S(2)}, u32[]{:S(2)}) collective-permute-start(bf16[480,256]{1,0:T(8,128)(2,1)S(1)} %get-tuple-element.89), channel_id=1, source_target_pairs={{0,8},{8,0},{16,24},{24,16},{1,9},{9,1},{17,25},{25,17},{2,10},{10... | collective-permute-start | bytes 737288 | tf_op jit(solution)/shard_map/ppermute | solution.py:275
  47.8 16.3 %collective-permute-start.12 = (bf16[480,256]{1,0:T(8,128)(2,1)S(1)}, bf16[480,256]{1,0:T(8,128)(2,1)S(1)}, u32[]{:S(2)}, u32[]{:S(2)}) collective-permute-start(bf16[480,256]{1,0:T(8,128)(2,1)S(1)} %add_convert_fusion.2), channel_id=1, source_target_pairs={{0,16},{8,24},{16,0},{24,8},{1,17},{9,25},{17,1},{25,9},{2,18},{10... | collective-permute-start | bytes 737288 | tf_op jit(solution)/shard_map/ppermute | solution.py:276

commit v3 on v0

--- a/solution.py
+++ b/solution.py
@@ -1,7 +1,16 @@
+import functools
+
 import jax
 import jax.numpy as jnp
 from jax import lax
+from jax.experimental import pallas as pl
+from jax.experimental.pallas import tpu as pltpu
 from jax.sharding import PartitionSpec as P
+
+LANES = 128
+STEP = 32
+TILE = 8
+VMEM = 48 * 1024 * 1024
 
 
 def partner(block, axis, stride):
@@ -14,7 +23,7 @@
     return lax.ppermute(block, axis, route)
 
 
-def local(fourier, wave_table, legendre):
+def plain(fourier, wave_table, legendre):
     slot_count, pair_count, degree_count = legendre.shape
     lat_count = lax.axis_size("lat")
     half_degrees = degree_count // 2
@@ -51,6 +60,319 @@
     return jnp.where(inside, spectral, jnp.zeros_like(spectral))
 
 
+def shift_of(block, used):
+    return block * used // LANES, block * used % LANES
+
+
+def gather_kernel(slots, table_ref, rows_ref, out, turned):
+    used, waves = rows_ref.shape
+    rows = jnp.concatenate([rows_ref[...], jnp.zeros((LANES - used, waves), jnp.bfloat16)], axis=0)
+    number = lax.broadcasted_iota(jnp.int32, (waves, LANES), 0)
+    for j in range(0, table_ref.shape[0], 2):
+        chosen = jnp.concatenate(
+            [(number == table_ref[k : k + 1, :]).astype(jnp.bfloat16) for k in (j, j + 1)], axis=1
+        )
+        got = jnp.dot(rows, chosen, preferred_element_type=jnp.float32)
+        turned[j * LANES : (j + 2) * LANES, :] = got.T
+    lane = lax.broadcasted_iota(jnp.int32, (STEP, LANES), 1)
+    for wave in range(out.shape[0]):
+        tiles = [jnp.zeros((STEP, LANES), jnp.float32)] * (out.shape[2] // LANES)
+        for block in range(slots // STEP):
+            tile, off = shift_of(block, used)
+            first = wave * slots + block * STEP
+            value = turned[first : first + STEP, :]
+            value = pltpu.roll(value, off, 1) if off else value
+            tiles[tile] = jnp.where(lane >= off, value, tiles[tile])
+            if off + used > LANES:
+                tiles[tile + 1] = jnp.where(lane < off + used - LANES, value, tiles[tile + 1])
+        for k, tile in enumerate(tiles):
+            out[wave, :, k * LANES : (k + 1) * LANES] = tile.astype(jnp.bfloat16)
+
+
+def place_kernel(source_count, lat_count, row_count, pairs, out):
+    northern = lax.axis_index("lat") < lat_count // 2
+    row = lax.broadcasted_iota(jnp.int32, (LANES, 2 * LANES), 0) & (row_count - 1)
+    col = lax.broadcasted_iota(jnp.int32, (LANES, 2 * LANES), 1) & (pairs - 1 | LANES)
+    for source in range(source_count):
+        ascending = (source < source_count // 2) == northern
+        position = (source % (source_count // 2)) * row_count + row
+        position = jnp.where(ascending, position, pairs - 1 - position)
+        target = position + jnp.where(ascending, 0, LANES)
+        out[source * LANES : (source + 1) * LANES, :] = (col == target).astype(jnp.bfloat16)
+
+
+def fetch(base, which, leg_ref, table, sems):
+    half = table.shape[2]
+    group = 2 * LANES // table.shape[1]
+    first = pl.multiple_of(which * half, LANES)
+    copies = []
+    for g in range(STEP // group):
+        copies.append(
+            pltpu.make_async_copy(
+                leg_ref.at[pl.ds(base + g * group, group), :, pl.ds(first, half)],
+                table.at[pl.ds(g * group, group)],
+                sems.at[g],
+            )
+        )
+        copies[-1].start()
+    return copies
+
+
+def multiply(copies, coefs, table, terms):
+    pairs, half = table.shape[1:]
+    group = 2 * LANES // pairs
+    cols = coefs.shape[0] // STEP
+    shape = (cols * group, 2 * LANES)
+    diagonal = (lax.broadcasted_iota(jnp.int32, shape, 0) & (group - 1)) == (
+        lax.broadcasted_iota(jnp.int32, shape, 1) // pairs
+    )
+    blank = jnp.zeros(shape, jnp.bfloat16)
+    for g, copy in enumerate(copies):
+        block = jnp.concatenate(
+            [coefs[c * STEP + g * group : c * STEP + (g + 1) * group] for c in range(cols)], axis=0
+        ).astype(jnp.bfloat16)
+        block = jnp.where(diagonal, jnp.concatenate([block, block], axis=1), blank)
+        copy.wait()
+        weights = table[g * group : (g + 1) * group].reshape(group * pairs, half)
+        got = jnp.dot(block, weights, preferred_element_type=jnp.float32)
+        for c in range(cols):
+            terms[pl.ds(c * STEP + g * group, group), :] = got[c * group : (c + 1) * group]
+
+
+def pack(terms, core, sent, kept):
+    rows = terms.shape[0]
+    part = rows // 4
+    lane_low = lax.broadcasted_iota(jnp.int32, (part, LANES), 1) < LANES // 2
+    for out, target in ((sent, 1 - core), (kept, core)):
+        first = pl.multiple_of(target * 3 * LANES, LANES)
+        out[:rows, :] = terms[:, pl.ds(first, 2 * LANES)].astype(out.dtype)
+    for j in range(2):
+        low = terms[pl.ds(2 * j * part, part), pl.ds(2 * LANES, LANES)]
+        high = terms[pl.ds((2 * j + 1) * part, part), pl.ds(2 * LANES, LANES)]
+        zeroth = jnp.where(lane_low, low, pltpu.roll(high, LANES // 2, 1))
+        other = jnp.where(lane_low, pltpu.roll(low, LANES // 2, 1), high)
+        for out, target in ((sent, 1 - core), (kept, core)):
+            out[rows:, j * LANES : (j + 1) * LANES] = jnp.where(target == 0, zeroth, other).astype(
+                out.dtype
+            )
+
+
+def far_kernel(block, row_count, cols, place_ref, kept_ref, mirror_ref, leg_ref, *refs):
+    sent, own, near_coefs, table, terms, sems = refs
+    lat = lax.axis_index("lat")
+    y, core = lat // 2, lat % 2
+    copies = fetch(block * STEP, 1 - y, leg_ref, table, sems)
+    tile, off = shift_of(block, row_count * cols)
+    lane = lax.broadcasted_iota(jnp.int32, (STEP, LANES), 1)
+    held = ((lane - off) & (LANES - 1)) // row_count
+    zero = jnp.zeros((STEP, LANES), jnp.bfloat16)
+    parts = []
+    for source in (kept_ref, mirror_ref):
+        for k in range(mirror_ref.shape[0]):
+            value = source[k, :, tile * LANES : (tile + 1) * LANES]
+            if off + row_count * cols > LANES:
+                value = jnp.where(
+                    lane >= off, value, source[k, :, (tile + 1) * LANES : (tile + 2) * LANES]
+                )
+            parts.append(
+                jnp.concatenate([jnp.where(held == c, value, zero) for c in range(cols)], axis=0)
+            )
+    both = jnp.dot(
+        jnp.concatenate(parts, axis=1), place_ref[...], preferred_element_type=jnp.float32
+    )
+    north, south = both[:, :LANES], both[:, LANES:]
+    even, odd = north + south, north - south
+    near_coefs[...] = jnp.where(y == 0, even, odd)
+    multiply(copies, jnp.where(y == 0, odd, even), table, terms)
+    pack(terms, core, sent, own)
+
+
+def near_kernel(block, coefs_ref, leg_ref, *refs):
+    sent, own, table, terms, sems = refs
+    lat = lax.axis_index("lat")
+    copies = fetch(block * STEP, lat // 2, leg_ref, table, sems)
+    multiply(copies, coefs_ref[...], table, terms)
+    pack(terms, lat % 2, sent, own)
+
+
+def final_kernel(slots, base, degrees, cols, table_ref, near_ref, far_ref, *refs):
+    out = refs[-1]
+    lat, me = lax.axis_index("lat"), lax.axis_index("wave")
+    first = lat % 2 == 0
+    half = degrees // 2
+    width = out.shape[2]
+    rows = STEP * cols
+    value = near_ref[...] + far_ref[...].astype(jnp.float32)
+    main0, main1 = value[:rows, :LANES], value[:rows, LANES:]
+    tails = []
+    for j in range(4):
+        tail = value[rows:, (j // 2) * LANES : (j // 2 + 1) * LANES]
+        tails.append(pltpu.roll(tail, LANES // 2, 1) if j % 2 else tail)
+    tail = jnp.concatenate(tails, axis=0)
+    lane_low = lax.broadcasted_iota(jnp.int32, (rows, LANES), 1) < LANES // 2
+    turn0, turn1 = pltpu.roll(main0, LANES // 2, 1), pltpu.roll(main1, LANES // 2, 1)
+    ordered = jnp.concatenate(
+        [
+            jnp.where(first, main0, jnp.where(lane_low, tail, turn0)),
+            jnp.where(first, main1, jnp.where(lane_low, turn0, turn1)),
+            jnp.where(first, tail, turn1),
+        ],
+        axis=1,
+    )
+    shape = (STEP, 3 * LANES)
+    degree = lat * width + lax.broadcasted_iota(jnp.int32, shape, 1)
+    offsets = jnp.where(degree < half, 2 * degree, 2 * (degree - half) + 1)
+    line = lax.broadcasted_iota(jnp.int32, shape, 0)
+    start = me * slots + base
+    limits = jnp.zeros(shape, jnp.int32)
+    for s in range(STEP):
+        limits = jnp.where(line == s, degrees - table_ref[start + s], limits)
+    inside = offsets < limits
+    for c in range(cols):
+        out[c] = jnp.where(inside, ordered[c * STEP : (c + 1) * STEP], 0.0)[:, :width]
+
+
+def packed(fourier, wave_table, legendre):
+    slots, pairs, degrees = legendre.shape
+    row_count, cols, waves = fourier.shape
+    wave_count, lat_count = lax.axis_size("wave"), lax.axis_size("lat")
+    width = degrees // lat_count
+    used = row_count * cols
+    params = pltpu.CompilerParams(vmem_limit_bytes=VMEM)
+    whole = pl.BlockSpec(memory_space=pltpu.VMEM)
+    anywhere = pl.BlockSpec(memory_space=pl.ANY)
+
+    message = -(-(slots // STEP) * used // LANES) * LANES
+    ordered = pl.pallas_call(
+        functools.partial(gather_kernel, slots),
+        out_shape=jax.ShapeDtypeStruct((wave_count, STEP, message), jnp.bfloat16),
+        in_specs=[whole, whole],
+        out_specs=whole,
+        scratch_shapes=[pltpu.VMEM((slots * wave_count, LANES), jnp.float32)],
+        compiler_params=params,
+        name="gather",
+    )(
+        wave_table.reshape(-1, LANES),
+        jnp.transpose(fourier, (1, 0, 2)).reshape(used, waves),
+    )
+    place = pl.pallas_call(
+        functools.partial(place_kernel, wave_count, lat_count, row_count, pairs),
+        out_shape=jax.ShapeDtypeStruct((wave_count * LANES, 2 * LANES), jnp.bfloat16),
+        out_specs=whole,
+        compiler_params=params,
+        name="place",
+    )()
+    arrived = lax.all_to_all(ordered, "wave", split_axis=0, concat_axis=0, tiled=True)
+    mirror = lax.ppermute(
+        arrived[wave_count // 2 :], "lat", [(lat, lat_count - 1 - lat) for lat in range(lat_count)]
+    )
+
+    rows = STEP * cols
+    shape = (rows + rows // 4, 2 * LANES)
+    group = 2 * LANES // pairs
+    core_route = [(lat, lat ^ 1) for lat in range(lat_count)]
+    y_route = [(lat, lat ^ 2) for lat in range(lat_count)]
+    scratch = [
+        pltpu.VMEM((STEP, pairs, degrees // 2), jnp.bfloat16),
+        pltpu.VMEM((rows, degrees // 2), jnp.float32),
+        pltpu.SemaphoreType.DMA((STEP // group,)),
+    ]
+    cost = pl.CostEstimate(flops=0, bytes_accessed=1024, transcendentals=0)
+    pair_of_sums = [
+        jax.ShapeDtypeStruct(shape, jnp.bfloat16),
+        jax.ShapeDtypeStruct(shape, jnp.float32),
+    ]
+    count = slots // STEP
+
+    def far(block, sources):
+        return pl.pallas_call(
+            functools.partial(far_kernel, block, row_count, cols),
+            out_shape=pair_of_sums + [jax.ShapeDtypeStruct((rows, LANES), jnp.float32)],
+            in_specs=[whole] * 3 + [anywhere],
+            out_specs=[whole] * 3,
+            scratch_shapes=scratch,
+            compiler_params=params,
+            cost_estimate=cost,
+            name="far",
+        )(place, *sources, legendre)
+
+    def near(block, coefs):
+        return pl.pallas_call(
+            functools.partial(near_kernel, block),
+            out_shape=pair_of_sums,
+            in_specs=[whole, anywhere],
+            out_specs=[whole] * 2,
+            scratch_shapes=scratch,
+            compiler_params=params,
+            cost_estimate=cost,
+            name="near",
+        )(coefs, legendre)
+
+    def settle(pair):
+        sent, kept = pair
+        return kept + lax.ppermute(sent, "lat", core_route).astype(jnp.float32)
+
+    def cross(pair):
+        summed = settle(pair).astype(jnp.bfloat16)
+        return summed, lax.ppermute(summed, "lat", y_route)
+
+    sources = (arrived, mirror)
+    crossed, settled = [], []
+    ahead = [far(block, sources) for block in range(min(2, count))]
+    for block in range(count):
+        *pair, coefs = ahead[block]
+        summed, far_sum = cross(pair)
+        crossed.append(far_sum)
+        ties = [summed] + settled[-1:]
+        coefs, ties = lax.optimization_barrier((coefs, ties))
+        pair = near(block, coefs)
+        settled.append(settle(pair))
+        if block + 2 < count:
+            sources, pair = lax.optimization_barrier((sources, pair))
+            ahead.append(far(block + 2, sources))
+
+    out = None
+    for block in range(count):
+        carried = [] if out is None else [out]
+        out = pl.pallas_call(
+            functools.partial(final_kernel, slots, block * STEP, degrees, cols),
+            grid_spec=pltpu.PrefetchScalarGridSpec(
+                num_scalar_prefetch=1,
+                grid=(1,),
+                in_specs=[whole] * 2 + [anywhere] * len(carried),
+                out_specs=pl.BlockSpec((cols, STEP, width), lambda g, table, at=block: (0, at, 0)),
+            ),
+            out_shape=jax.ShapeDtypeStruct((cols, slots, width), jnp.float32),
+            input_output_aliases={3: 0} if carried else {},
+            compiler_params=params,
+            cost_estimate=cost,
+            name="final",
+        )(wave_table, settled[block], crossed[block], *carried)
+    return jnp.transpose(out, (1, 0, 2))
+
+
+def local(fourier, wave_table, legendre):
+    slots, pairs, degrees = legendre.shape
+    row_count, cols, waves = fourier.shape
+    wave_count, lat_count = lax.axis_size("wave"), lax.axis_size("lat")
+    fits = (
+        lat_count == 4
+        and wave_count & (wave_count - 1) == 0
+        and slots % STEP == 0
+        and degrees // 2 == 5 * LANES
+        and row_count & (row_count - 1) == 0
+        and LANES // 4 % row_count == 0
+        and row_count * cols % (LANES // 4) == 0
+        and row_count * cols <= LANES
+        and pairs == row_count * wave_count // 2
+        and pairs * TILE == 2 * LANES
+        and waves % (2 * LANES) == 0
+    )
+    if not fits:
+        return plain(fourier, wave_table, legendre)
+    return packed(fourier, wave_table, legendre)
+
+
 def solution(mesh):
     in_specs = (P(("lat", "wave"), None, None), P(), P("wave", "lat", None))
     out_specs = P("wave", None, "lat")

time: 355 us -> 68 us (0.19); the launches traced: 351 us -> 67.6 us
  local copies, waits for them, and re-layouts: 209 us -> 1.66 us
  waiting for transfers between devices: 85.9 us -> 10.8 us
  Pallas kernels: 0 us -> 30.7 us
  other arithmetic: 17 us -> 0.54 us
  between operations: 13.5 us -> 0.21 us
  matrix products: 8.06 us -> 0 us
  starting transfers between devices: 1.59 us -> 7.73 us
    unnamed x7 -> x6, local copies, waits for them, and re-layouts: 199 us -> 1.65 us
    unnamed x2 -> x0, waiting for transfers between devices: 79.2 us -> none
    pallas_call x0 -> x17, Pallas kernels: none -> 30.7 us  [the longest x5 11.9 us: far(): pl.pallas_call(functools.partial(far_kernel, block, row_count, cols), out...]
    dot_general x2 -> x0, matrix products: 8.06 us -> none  [the longest x1 4.03 us: local(): jnp.einsum('mcp,mpk->mck', even_part, legendre[:, :, :half_degrees], pref...]
    unnamed x1 -> x0, other arithmetic: 6.61 us -> none
    ppermute x2 -> x16, starting transfers between devices: 1.59 us -> 7.73 us  [the longest x5 4.97 us: cross(): return (summed, lax.ppermute(summed, 'lat', y_route))]
    concatenate x1 -> x0, other arithmetic: 5.31 us -> none  [local(): partial_terms = jnp.concatenate([even_out, odd_out], axis=2)]
    gather x1 -> x0, local copies, waits for them, and re-layouts: 4.43 us -> none  [local(): ordered = jnp.take(fourier, wave_table, axis=2)]
  transfers between devices with their start and end apart: 3 -> 16, of which waited for: 3 -> 3; matrix products, arithmetic and copies ran while one was open for 0% -> 1% of each run, Pallas kernels for 0% -> 38%
where the time goes in v3:
time: 68 us; the launch traced here: 67.6 us
  Pallas kernels  30.7 us (45%)
  blocking collectives  16 us (24%)
  waiting for transfers between devices  10.8 us (16%)
  starting transfers between devices  7.73 us (11%)
  local copies, waits for them, and re-layouts  1.66 us (2%)
    all_to_all x1, blocking collectives, packed(): lax.all_to_all(ordered, 'wave', split_axis=0, concat_axis=0, tiled=True)  16 us
    pallas_call x5, Pallas kernels, far(): pl.pallas_call(functools.partial(far_kernel, block, row_count, cols), out...  11.9 us
    pallas_call x5, Pallas kernels, near(): pl.pallas_call(functools.partial(near_kernel, block), out_shape=pair_of_s...  9.76 us
    pallas_call x5, Pallas kernels, packed(): pl.pallas_call(functools.partial(final_kernel, slots, block * STEP, degre...  8.15 us
    ppermute x1, waiting for transfers between devices, packed(): lax.ppermute(arrived[wave_count // 2:], 'lat', [(lat, lat_count - 1 - lat...  5.54 us
    ppermute x5, starting transfers between devices, cross(): return (summed, lax.ppermute(summed, 'lat', y_route))  4.97 us
    ppermute x5, waiting for transfers between devices, cross(): return (summed, lax.ppermute(summed, 'lat', y_route))  4.08 us
    ppermute x10, starting transfers between devices, settle(): return kept + lax.ppermute(sent, 'lat', core_route).astype(jnp.float32)  2.69 us
  transfers between devices with their start and end apart: 16, of which 3 were waited for; matrix products, arithmetic and copies ran while one was open for 1% of the time, Pallas kernels for 38%

profile of v3, /device:TPU:0, one launch (start us, length us, event | category | flops | bytes accessed | tf_op | source)
XLA Modules:
  0.0 67.6 jit_solution(1907004582145730192)
XLA Ops:
  0.0 0.0 copy-start
  0.0 0.7 %copy-done = s32[1280]{0:T(1024)S(1)} copy-done((s32[1280]{0:T(1024)S(1)}, s32[1280]{0:T(1024)}, u32[]{:S(2)}) %copy-start) | copy-done | bytes 5144
  0.7 0.0 copy-start.2
  0.7 0.9 %copy-done.2 = bf16[8,12,1280]{2,0,1:T(8,128)(2,1)S(1)} copy-done((bf16[8,12,1280]{2,0,1:T(8,128)(2,1)S(1)}, bf16[8,12,1280]{2,0,1:T(8,128)(2,1)}, u32[]{:S(2)}) %copy-start.2) | copy-done | bytes 245784
  1.6 0.8 %gather.1 = bf16[8,32,512]{2,1,0:T(8,128)(2,1)S(1)} custom-call(s32[10,128]{1,0:T(8,128)S(1)} %bitcast.5, bf16[96,1280]{1,0:T(8,128)(2,1)S(1)} %bitcast.6), custom_call_target="tpu_custom_call" | custom-call | tf_op jit(solution)/shard_map/gather/pallas_call | solution.py:246
  2.4 16.0 %all_to_all.5.kept_ref = bf16[8,32,512]{2,1,0:T(8,128)(2,1)S(1)} all-to-all(bf16[8,32,512]{2,1,0:T(8,128)(2,1)S(1)} %gather.1), channel_id=1, replica_groups=mesh['lat'=4,'wave'=8] {'wave'}, dimensions={0} | all-to-all | bytes 524288 | tf_op jit(solution)/shard_map/all_to_all | solution.py:265
  18.4 0.1 collective-permute-start
  18.5 0.2 place.1.place_ref
  18.7 5.5 %collective-permute-done.mirror_ref = bf16[4,32,512]{2,1,0:T(8,128)(2,1)S(1)} collective-permute-done((bf16[4,32,512]{2,1,0:T(8,128)(2,1)S(1)}, bf16[4,32,512]{2,1,0:T(8,128)(2,1)S(1)}, u32[]{:S(2)}, u32[]{:S(2)}) %collective-permute-start) | collective-permute-done | bytes 131104 | tf_op jit(solution)/shard_map/ppermute | solution.py:266
  24.2 2.4 %far.5 = (bf16[480,256]{1,0:T(8,128)(2,1)S(1)}, f32[480,256]{1,0:T(8,128)S(1)}, f32[384,128]{1,0:T(8,128)S(1)}) custom-call(bf16[1024,256]{1,0:T(8,128)(2,1)S(1)} %place.1.place_ref, bf16[8,32,512]{2,1,0:T(8,128)(2,1)S(1)} %all_to_all.5.kept_ref, bf16[4,32,512]{2,1,0:T(8,128)(2,1)S(1)} %collective-permute-done.mirror_ref, bf16[160,32,1280]{2,1,0:T(8,128)(2,1)} %leg_ref.19), custom_call_target="tpu_custom_call" | custom-call | bytes 1024 | tf_op jit(solution)/shard_map/far/pallas_call | solution.py:288
  26.6 0.2 collective-permute-start.1
  26.8 2.4 %far.6 = (bf16[480,256]{1,0:T(8,128)(2,1)S(1)}, f32[480,256]{1,0:T(8,128)S(1)}, f32[384,128]{1,0:T(8,128)S(1)}) custom-call(bf16[1024,256]{1,0:T(8,128)(2,1)S(1)} %place.1.place_ref, bf16[8,32,512]{2,1,0:T(8,128)(2,1)S(1)} %all_to_all.5.kept_ref, bf16[4,32,512]{2,1,0:T(8,128)(2,1)S(1)} %collective-permute-done.mirror_ref, bf16[160,32,1280]{2,1,0:T(8,128)(2,1)} %leg_ref.19), custom_call_target="tpu_custom_call" | custom-call | bytes 1024 | tf_op jit(solution)/shard_map/far/pallas_call | solution.py:288
  29.1 0.5 collective-permute-start.2
  29.6 0.0 collective-permute-done.1
  29.6 0.1 add_convert_fusion.4
  29.7 0.7 %collective-permute-start.15 = (bf16[480,256]{1,0:T(8,128)(2,1)S(1)}, bf16[480,256]{1,0:T(8,128)(2,1)S(1)}, u32[]{:S(2)}, u32[]{:S(2)}) collective-permute-start(bf16[480,256]{1,0:T(8,128)(2,1)S(1)} %add_convert_fusion.4), channel_id=1, source_target_pairs={{0,16},{8,24},{16,0},{24,8},{1,17},{9,25},{17,1},{25,9},{2,18},{10... | collective-permute-start | bytes 737288 | tf_op jit(solution)/shard_map/ppermute | solution.py:317
  30.4 2.0 %near.5 = (bf16[480,256]{1,0:T(8,128)(2,1)S(1)}, f32[480,256]{1,0:T(8,128)S(1)}) custom-call(f32[384,128]{1,0:T(8,128)S(1)} %get-tuple-element.44.coefs_ref, bf16[160,32,1280]{2,1,0:T(8,128)(2,1)} %leg_ref.19), custom_call_target="tpu_custom_call" | custom-call | bytes 1024 | tf_op jit(solution)/shard_map/near/pallas_call | solution.py:300
  32.3 0.1 collective-permute-start.3
  32.4 0.0 collective-permute-done.2
  32.4 0.1 add_convert_fusion.3
  32.5 1.4 %collective-permute-start.14 = (bf16[480,256]{1,0:T(8,128)(2,1)S(1)}, bf16[480,256]{1,0:T(8,128)(2,1)S(1)}, u32[]{:S(2)}, u32[]{:S(2)}) collective-permute-start(bf16[480,256]{1,0:T(8,128)(2,1)S(1)} %add_convert_fusion.3), channel_id=1, source_target_pairs={{0,16},{8,24},{16,0},{24,8},{1,17},{9,25},{17,1},{25,9},{2,18},{10... | collective-permute-start | bytes 737288 | tf_op jit(solution)/shard_map/ppermute | solution.py:317
  33.9 2.4 %far.7 = (bf16[480,256]{1,0:T(8,128)(2,1)S(1)}, f32[480,256]{1,0:T(8,128)S(1)}, f32[384,128]{1,0:T(8,128)S(1)}) custom-call(bf16[1024,256]{1,0:T(8,128)(2,1)S(1)} %place.1.place_ref, bf16[8,32,512]{2,1,0:T(8,128)(2,1)S(1)} %all_to_all.5.kept_ref, bf16[4,32,512]{2,1,0:T(8,128)(2,1)S(1)} %collective-permute-done.mirror_ref, bf16[160,32,1280]{2,1,0:T(8,128)(2,1)} %leg_ref.19), custom_call_target="tpu_custom_call" | custom-call | bytes 1024 | tf_op jit(solution)/shard_map/far/pallas_call | solution.py:288
  36.3 0.3 collective-permute-start.4
  36.6 0.0 collective-permute-done.3
  36.6 2.0 %near.6 = (bf16[480,256]{1,0:T(8,128)(2,1)S(1)}, f32[480,256]{1,0:T(8,128)S(1)}) custom-call(f32[384,128]{1,0:T(8,128)S(1)} %get-tuple-element.52.coefs_ref, bf16[160,32,1280]{2,1,0:T(8,128)(2,1)} %leg_ref.19), custom_call_target="tpu_custom_call" | custom-call | bytes 1024 | tf_op jit(solution)/shard_map/near/pallas_call | solution.py:300
  38.6 0.4 collective-permute-start.5
  39.0 2.4 %far.9 = (bf16[480,256]{1,0:T(8,128)(2,1)S(1)}, f32[480,256]{1,0:T(8,128)S(1)}, f32[384,128]{1,0:T(8,128)S(1)}) custom-call(bf16[1024,256]{1,0:T(8,128)(2,1)S(1)} %place.1.place_ref, bf16[8,32,512]{2,1,0:T(8,128)(2,1)S(1)} %all_to_all.5.kept_ref, bf16[4,32,512]{2,1,0:T(8,128)(2,1)S(1)} %collective-permute-done.mirror_ref, bf16[160,32,1280]{2,1,0:T(8,128)(2,1)} %leg_ref.19), custom_call_target="tpu_custom_call" | custom-call | bytes 1024 | tf_op jit(solution)/shard_map/far/pallas_call | solution.py:288
  41.4 0.3 collective-permute-start.7
  41.6 0.0 collective-permute-done.4
  41.6 0.1 add_convert_fusion.2
  41.7 0.7 %collective-permute-start.13 = (bf16[480,256]{1,0:T(8,128)(2,1)S(1)}, bf16[480,256]{1,0:T(8,128)(2,1)S(1)}, u32[]{:S(2)}, u32[]{:S(2)}) collective-permute-start(bf16[480,256]{1,0:T(8,128)(2,1)S(1)} %add_convert_fusion.2), channel_id=1, source_target_pairs={{0,16},{8,24},{16,0},{24,8},{1,17},{9,25},{17,1},{25,9},{2,18},{10... | collective-permute-start | bytes 737288 | tf_op jit(solution)/shard_map/ppermute | solution.py:317
  42.4 0.0 collective-permute-done.5
  42.5 2.0 %near.7 = (bf16[480,256]{1,0:T(8,128)(2,1)S(1)}, f32[480,256]{1,0:T(8,128)S(1)}) custom-call(f32[384,128]{1,0:T(8,128)S(1)} %get-tuple-element.60.coefs_ref, bf16[160,32,1280]{2,1,0:T(8,128)(2,1)} %leg_ref.19), custom_call_target="tpu_custom_call" | custom-call | bytes 1024 | tf_op jit(solution)/shard_map/near/pallas_call | solution.py:300
  44.4 0.1 collective-permute-start.8
  44.5 0.0 collective-permute-done.7
  44.5 0.1 add_convert_fusion
  44.6 1.4 %collective-permute-start.12 = (bf16[480,256]{1,0:T(8,128)(2,1)S(1)}, bf16[480,256]{1,0:T(8,128)(2,1)S(1)}, u32[]{:S(2)}, u32[]{:S(2)}) collective-permute-start(bf16[480,256]{1,0:T(8,128)(2,1)S(1)} %add_convert_fusion), channel_id=1, source_target_pairs={{0,16},{8,24},{16,0},{24,8},{1,17},{9,25},{17,1},{25,9},{2,18},{10... | collective-permute-start | bytes 737288 | tf_op jit(solution)/shard_map/ppermute | solution.py:317
  46.0 2.4 %far.8 = (bf16[480,256]{1,0:T(8,128)(2,1)S(1)}, f32[480,256]{1,0:T(8,128)S(1)}, f32[384,128]{1,0:T(8,128)S(1)}) custom-call(bf16[1024,256]{1,0:T(8,128)(2,1)S(1)} %place.1.place_ref, bf16[8,32,512]{2,1,0:T(8,128)(2,1)S(1)} %all_to_all.5.kept_ref, bf16[4,32,512]{2,1,0:T(8,128)(2,1)S(1)} %collective-permute-done.mirror_ref, bf16[160,32,1280]{2,1,0:T(8,128)(2,1)} %leg_ref.19), custom_call_target="tpu_custom_call" | custom-call | bytes 1024 | tf_op jit(solution)/shard_map/far/pallas_call | solution.py:288
  48.4 0.0 collective-permute-done.8
  48.4 0.3 collective-permute-start.6
  48.7 2.0 %near.8 = (bf16[480,256]{1,0:T(8,128)(2,1)S(1)}, f32[480,256]{1,0:T(8,128)S(1)}) custom-call(f32[384,128]{1,0:T(8,128)S(1)} %get-tuple-element.71.coefs_ref, bf16[160,32,1280]{2,1,0:T(8,128)(2,1)} %leg_ref.19), custom_call_target="tpu_custom_call" | custom-call | bytes 1024 | tf_op jit(solution)/shard_map/near/pallas_call | solution.py:300
  50.7 0.0 collective-permute-done.6
  50.7 0.4 collective-permute-start.9
  51.0 0.1 add_convert_fusion.1
  51.1 1.2 %collective-permute-done.9 = bf16[480,256]{1,0:T(8,128)(2,1)S(1)} collective-permute-done((bf16[480,256]{1,0:T(8,128)(2,1)S(1)}, bf16[480,256]{1,0:T(8,128)(2,1)S(1)}, u32[]{:S(2)}, u32[]{:S(2)}) %collective-permute-start.9) | collective-permute-done | bytes 245792 | tf_op jit(solution)/shard_map/ppermute | solution.py:313
  52.3 0.0 copy-start.1
  52.3 2.0 %near.9 = (bf16[480,256]{1,0:T(8,128)(2,1)S(1)}, f32[480,256]{1,0:T(8,128)S(1)}) custom-call(f32[384,128]{1,0:T(8,128)S(1)} %get-tuple-element.74.coefs_ref, bf16[160,32,1280]{2,1,0:T(8,128)(2,1)} %leg_ref.19), custom_call_target="tpu_custom_call" | custom-call | bytes 1024 | tf_op jit(solution)/shard_map/near/pallas_call | solution.py:300
  54.3 0.4 collective-permute-start.10
  54.6 0.0 collective-permute-done.15.far_ref
  54.6 0.0 copy-done.1
  54.6 1.6 %final.5.refs_0_ = f32[12,160,320]{2,1,0:T(8,128)} custom-call(s32[1280]{0:T(1024)S(1)} %copy-done.1, f32[480,256]{1,0:T(8,128)S(1)} %convert_add_fusion.4.near_ref, bf16[480,256]{1,0:T(8,128)(2,1)S(1)} %collective-permute-done.15.far_ref), custom_call_target="tpu_custom_call" | custom-call | bytes 1024 | tf_op jit(solution)/shard_map/final/pallas_call | solution.py:337
  56.3 0.0 collective-permute-done.14.far_ref
  56.3 1.6 %final.6.refs_0_ = f32[12,160,320]{2,1,0:T(8,128)} custom-call(s32[1280]{0:T(1024)S(1)} %copy-done.1, f32[480,256]{1,0:T(8,128)S(1)} %convert_add_fusion.3.near_ref, bf16[480,256]{1,0:T(8,128)(2,1)S(1)} %collective-permute-done.14.far_ref, f32[12,160,320]{2,1,0:T(8,128)} %final.5.refs_0_), custom_call_target="tpu_custom_call", output_to_operand_aliasing={{}: (3, {})} | custom-call | bytes 1024 | tf_op jit(solution)/shard_map/final/pallas_call | solution.py:337
  57.9 0.7 collective-permute-start.11
  58.6 0.0 collective-permute-done.13.far_ref
  58.6 1.6 %final.7.refs_0_ = f32[12,160,320]{2,1,0:T(8,128)} custom-call(s32[1280]{0:T(1024)S(1)} %copy-done.1, f32[480,256]{1,0:T(8,128)S(1)} %convert_add_fusion.2.near_ref, bf16[480,256]{1,0:T(8,128)(2,1)S(1)} %collective-permute-done.13.far_ref, f32[12,160,320]{2,1,0:T(8,128)} %final.6.refs_0_), custom_call_target="tpu_custom_call", output_to_operand_aliasing={{}: (3, {})} | custom-call | bytes 1024 | tf_op jit(solution)/shard_map/final/pallas_call | solution.py:337
  60.2 0.0 collective-permute-done.12.far_ref
  60.2 1.6 %final.8.refs_0_ = f32[12,160,320]{2,1,0:T(8,128)} custom-call(s32[1280]{0:T(1024)S(1)} %copy-done.1, f32[480,256]{1,0:T(8,128)S(1)} %convert_add_fusion.1.near_ref, bf16[480,256]{1,0:T(8,128)(2,1)S(1)} %collective-permute-done.12.far_ref, f32[12,160,320]{2,1,0:T(8,128)} %final.7.refs_0_), custom_call_target="tpu_custom_call", output_to_operand_aliasing={{}: (3, {})} | custom-call | bytes 1024 | tf_op jit(solution)/shard_map/final/pallas_call | solution.py:337
  61.8 0.0 collective-permute-done.10
  61.8 0.1 convert_add_fusion.near_ref
  61.9 4.1 %collective-permute-done.11.far_ref = bf16[480,256]{1,0:T(8,128)(2,1)S(1)} collective-permute-done((bf16[480,256]{1,0:T(8,128)(2,1)S(1)}, bf16[480,256]{1,0:T(8,128)(2,1)S(1)}, u32[]{:S(2)}, u32[]{:S(2)}) %collective-permute-start.11) | collective-permute-done | bytes 245792 | tf_op jit(solution)/shard_map/ppermute | solution.py:317
  66.0 1.6 %final.9 = f32[12,160,320]{2,1,0:T(8,128)} custom-call(s32[1280]{0:T(1024)S(1)} %copy-done.1, f32[480,256]{1,0:T(8,128)S(1)} %convert_add_fusion.near_ref, bf16[480,256]{1,0:T(8,128)(2,1)S(1)} %collective-permute-done.11.far_ref, f32[12,160,320]{2,1,0:T(8,128)} %final.8.refs_0_), custom_call_target="tpu_custom_call", output_to_operand_aliasing={{}: (3, {})} | custom-call | bytes 1024 | tf_op jit(solution)/shard_map/final/pallas_call | solution.py:337
  (5 shorter events, 0.2 us)
Async XLA Ops:
  0.0 0.7 %copy-start = (s32[1280]{0:T(1024)S(1)}, s32[1280]{0:T(1024)}, u32[]{:S(2)}) copy-start(s32[1280]{0:T(1024)} %table_ref.9) | copy-start | bytes 15364
  0.7 0.9 %copy-start.2 = (bf16[8,12,1280]{2,0,1:T(8,128)(2,1)S(1)}, bf16[8,12,1280]{2,0,1:T(8,128)(2,1)}, u32[]{:S(2)}) copy-start(bf16[8,12,1280]{2,0,1:T(8,128)(2,1)} %param.3) | copy-start | bytes 737284
  18.4 5.8 %collective-permute-start = (bf16[4,32,512]{2,1,0:T(8,128)(2,1)S(1)}, bf16[4,32,512]{2,1,0:T(8,128)(2,1)S(1)}, u32[]{:S(2)}, u32[]{:S(2)}) collective-permute-start(bf16[4,32,512]{2,1,0:T(8,128)(2,1)S(1)} %slice.4), channel_id=1, source_target_pairs={{0,24},{8,16},{16,8},{24,0},{1,25},{9,17},{17,9},{25,1},{2,26},{10... | collective-permute-start | bytes 393224 | tf_op jit(solution)/shard_map/ppermute | solution.py:266
  26.6 3.0 %collective-permute-start.1 = (bf16[480,256]{1,0:T(8,128)(2,1)S(1)}, bf16[480,256]{1,0:T(8,128)(2,1)S(1)}, u32[]{:S(2)}, u32[]{:S(2)}) collective-permute-start(bf16[480,256]{1,0:T(8,128)(2,1)S(1)} %get-tuple-element.43), channel_id=1, source_target_pairs={{0,8},{8,0},{16,24},{24,16},{1,9},{9,1},{17,25},{25,17},{2,10},{10... | collective-permute-start | bytes 737288 | tf_op jit(solution)/shard_map/ppermute | solution.py:313
  29.1 3.3 %collective-permute-start.2 = (bf16[480,256]{1,0:T(8,128)(2,1)S(1)}, bf16[480,256]{1,0:T(8,128)(2,1)S(1)}, u32[]{:S(2)}, u32[]{:S(2)}) collective-permute-start(bf16[480,256]{1,0:T(8,128)(2,1)S(1)} %get-tuple-element.51), channel_id=1, source_target_pairs={{0,8},{8,0},{16,24},{24,16},{1,9},{9,1},{17,25},{25,17},{2,10},{10... | collective-permute-start | bytes 737288 | tf_op jit(solution)/shard_map/ppermute | solution.py:313
  29.7 25.0 %collective-permute-start.15 = (bf16[480,256]{1,0:T(8,128)(2,1)S(1)}, bf16[480,256]{1,0:T(8,128)(2,1)S(1)}, u32[]{:S(2)}, u32[]{:S(2)}) collective-permute-start(bf16[480,256]{1,0:T(8,128)(2,1)S(1)} %add_convert_fusion.4), channel_id=1, source_target_pairs={{0,16},{8,24},{16,0},{24,8},{1,17},{9,25},{17,1},{25,9},{2,18},{10... | collective-permute-start | bytes 737288 | tf_op jit(solution)/shard_map/ppermute | solution.py:317
  32.3 4.2 %collective-permute-start.3 = (bf16[480,256]{1,0:T(8,128)(2,1)S(1)}, bf16[480,256]{1,0:T(8,128)(2,1)S(1)}, u32[]{:S(2)}, u32[]{:S(2)}) collective-permute-start(bf16[480,256]{1,0:T(8,128)(2,1)S(1)} %get-tuple-element.45), channel_id=1, source_target_pairs={{0,8},{8,0},{16,24},{24,16},{1,9},{9,1},{17,25},{25,17},{2,10},{10... | collective-permute-start | bytes 737288 | tf_op jit(solution)/shard_map/ppermute | solution.py:313
  32.5 23.8 %collective-permute-start.14 = (bf16[480,256]{1,0:T(8,128)(2,1)S(1)}, bf16[480,256]{1,0:T(8,128)(2,1)S(1)}, u32[]{:S(2)}, u32[]{:S(2)}) collective-permute-start(bf16[480,256]{1,0:T(8,128)(2,1)S(1)} %add_convert_fusion.3), channel_id=1, source_target_pairs={{0,16},{8,24},{16,0},{24,8},{1,17},{9,25},{17,1},{25,9},{2,18},{10... | collective-permute-start | bytes 737288 | tf_op jit(solution)/shard_map/ppermute | solution.py:317
  36.3 5.3 %collective-permute-start.4 = (bf16[480,256]{1,0:T(8,128)(2,1)S(1)}, bf16[480,256]{1,0:T(8,128)(2,1)S(1)}, u32[]{:S(2)}, u32[]{:S(2)}) collective-permute-start(bf16[480,256]{1,0:T(8,128)(2,1)S(1)} %get-tuple-element.59), channel_id=1, source_target_pairs={{0,8},{8,0},{16,24},{24,16},{1,9},{9,1},{17,25},{25,17},{2,10},{10... | collective-permute-start | bytes 737288 | tf_op jit(solution)/shard_map/ppermute | solution.py:313
  38.6 3.8 %collective-permute-start.5 = (bf16[480,256]{1,0:T(8,128)(2,1)S(1)}, bf16[480,256]{1,0:T(8,128)(2,1)S(1)}, u32[]{:S(2)}, u32[]{:S(2)}) collective-permute-start(bf16[480,256]{1,0:T(8,128)(2,1)S(1)} %get-tuple-element.53), channel_id=1, source_target_pairs={{0,8},{8,0},{16,24},{24,16},{1,9},{9,1},{17,25},{25,17},{2,10},{10... | collective-permute-start | bytes 737288 | tf_op jit(solution)/shard_map/ppermute | solution.py:313
  41.4 3.1 %collective-permute-start.7 = (bf16[480,256]{1,0:T(8,128)(2,1)S(1)}, bf16[480,256]{1,0:T(8,128)(2,1)S(1)}, u32[]{:S(2)}, u32[]{:S(2)}) collective-permute-start(bf16[480,256]{1,0:T(8,128)(2,1)S(1)} %get-tuple-element.70), channel_id=1, source_target_pairs={{0,8},{8,0},{16,24},{24,16},{1,9},{9,1},{17,25},{25,17},{2,10},{10... | collective-permute-start | bytes 737288 | tf_op jit(solution)/shard_map/ppermute | solution.py:313
  41.7 16.9 %collective-permute-start.13 = (bf16[480,256]{1,0:T(8,128)(2,1)S(1)}, bf16[480,256]{1,0:T(8,128)(2,1)S(1)}, u32[]{:S(2)}, u32[]{:S(2)}) collective-permute-start(bf16[480,256]{1,0:T(8,128)(2,1)S(1)} %add_convert_fusion.2), channel_id=1, source_target_pairs={{0,16},{8,24},{16,0},{24,8},{1,17},{9,25},{17,1},{25,9},{2,18},{10... | collective-permute-start | bytes 737288 | tf_op jit(solution)/shard_map/ppermute | solution.py:317
  44.4 4.0 %collective-permute-start.8 = (bf16[480,256]{1,0:T(8,128)(2,1)S(1)}, bf16[480,256]{1,0:T(8,128)(2,1)S(1)}, u32[]{:S(2)}, u32[]{:S(2)}) collective-permute-start(bf16[480,256]{1,0:T(8,128)(2,1)S(1)} %get-tuple-element.61), channel_id=1, source_target_pairs={{0,8},{8,0},{16,24},{24,16},{1,9},{9,1},{17,25},{25,17},{2,10},{10... | collective-permute-start | bytes 737288 | tf_op jit(solution)/shard_map/ppermute | solution.py:313
  44.6 15.6 %collective-permute-start.12 = (bf16[480,256]{1,0:T(8,128)(2,1)S(1)}, bf16[480,256]{1,0:T(8,128)(2,1)S(1)}, u32[]{:S(2)}, u32[]{:S(2)}) collective-permute-start(bf16[480,256]{1,0:T(8,128)(2,1)S(1)} %add_convert_fusion), channel_id=1, source_target_pairs={{0,16},{8,24},{16,0},{24,8},{1,17},{9,25},{17,1},{25,9},{2,18},{10... | collective-permute-start | bytes 737288 | tf_op jit(solution)/shard_map/ppermute | solution.py:317
  48.4 2.3 %collective-permute-start.6 = (bf16[480,256]{1,0:T(8,128)(2,1)S(1)}, bf16[480,256]{1,0:T(8,128)(2,1)S(1)}, u32[]{:S(2)}, u32[]{:S(2)}) collective-permute-start(bf16[480,256]{1,0:T(8,128)(2,1)S(1)} %get-tuple-element.67), channel_id=1, source_target_pairs={{0,8},{8,0},{16,24},{24,16},{1,9},{9,1},{17,25},{25,17},{2,10},{10... | collective-permute-start | bytes 737288 | tf_op jit(solution)/shard_map/ppermute | solution.py:313
  50.7 1.6 %collective-permute-start.9 = (bf16[480,256]{1,0:T(8,128)(2,1)S(1)}, bf16[480,256]{1,0:T(8,128)(2,1)S(1)}, u32[]{:S(2)}, u32[]{:S(2)}) collective-permute-start(bf16[480,256]{1,0:T(8,128)(2,1)S(1)} %get-tuple-element.73), channel_id=1, source_target_pairs={{0,8},{8,0},{16,24},{24,16},{1,9},{9,1},{17,25},{25,17},{2,10},{10... | collective-permute-start | bytes 737288 | tf_op jit(solution)/shard_map/ppermute | solution.py:313
  52.3 2.3 %copy-start.1 = (s32[1280]{0:T(1024)S(1)}, s32[1280]{0:T(1024)}, u32[]{:S(2)}) copy-start(s32[1280]{0:T(1024)} %table_ref.9) | copy-start | bytes 15364
  54.3 7.6 %collective-permute-start.10 = (bf16[480,256]{1,0:T(8,128)(2,1)S(1)}, bf16[480,256]{1,0:T(8,128)(2,1)S(1)}, u32[]{:S(2)}, u32[]{:S(2)}) collective-permute-start(bf16[480,256]{1,0:T(8,128)(2,1)S(1)} %get-tuple-element.76), channel_id=1, source_target_pairs={{0,8},{8,0},{16,24},{24,16},{1,9},{9,1},{17,25},{25,17},{2,10},{10... | collective-permute-start | bytes 737288 | tf_op jit(solution)/shard_map/ppermute | solution.py:313
  57.9 8.1 %collective-permute-start.11 = (bf16[480,256]{1,0:T(8,128)(2,1)S(1)}, bf16[480,256]{1,0:T(8,128)(2,1)S(1)}, u32[]{:S(2)}, u32[]{:S(2)}) collective-permute-start(bf16[480,256]{1,0:T(8,128)(2,1)S(1)} %add_convert_fusion.1), channel_id=1, source_target_pairs={{0,16},{8,24},{16,0},{24,8},{1,17},{9,25},{17,1},{25,9},{2,18},{10... | collective-permute-start | bytes 737288 | tf_op jit(solution)/shard_map/ppermute | solution.py:317

commit v4 on v3

v4 whole, which is shorter than its diff:
```python
import functools

import jax
import jax.numpy as jnp
from jax import lax
from jax.experimental import pallas as pl
from jax.experimental.pallas import tpu as pltpu
from jax.sharding import PartitionSpec as P

LANES = 128
STEP = 32
TILE = 8
VMEM = 48 * 1024 * 1024


def partner(block, axis, stride):
    count = lax.axis_size(axis)
    route = []
    for low in range(count):
        high = low | 1 << stride
        if high != low and high < count:
            route += [(low, high), (high, low)]
    return lax.ppermute(block, axis, route)


def plain(fourier, wave_table, legendre):
    slot_count, pair_count, degree_count = legendre.shape
    lat_count = lax.axis_size("lat")
    half_degrees = degree_count // 2
    slice_width = degree_count // lat_count
    lat_index = lax.axis_index("lat")
    ordered = jnp.take(fourier, wave_table, axis=2)
    arrived = lax.all_to_all(ordered, "wave", split_axis=2, concat_axis=0, tiled=True)
    local_rows = jnp.transpose(arrived, (2, 1, 0))
    kept_rows = local_rows[:, :, :pair_count]
    received = local_rows[:, :, pair_count:]
    for bit_number in range(lat_count.bit_length() - 1):
        received = partner(received, "lat", bit_number)
    northern = lat_index < lat_count // 2
    north_rows = jnp.where(northern, kept_rows, received).astype(jnp.float32)
    south_rows = jnp.where(northern, jnp.flip(received, 2), jnp.flip(kept_rows, 2)).astype(
        jnp.float32
    )
    even_part = (north_rows + south_rows).astype(jnp.bfloat16)
    odd_part = (north_rows - south_rows).astype(jnp.bfloat16)
    my_waves = lax.dynamic_slice_in_dim(wave_table, lax.axis_index("wave") * slot_count, slot_count)
    even_out = jnp.einsum(
        "mcp,mpk->mck", even_part, legendre[:, :, :half_degrees], preferred_element_type=jnp.float32
    )
    odd_out = jnp.einsum(
        "mcp,mpk->mck", odd_part, legendre[:, :, half_degrees:], preferred_element_type=jnp.float32
    )
    partial_terms = jnp.concatenate([even_out, odd_out], axis=2)
    spectral = lax.psum_scatter(partial_terms, "lat", scatter_dimension=2, tiled=True)
    degree_slot = lat_index * slice_width + jnp.arange(slice_width, dtype=jnp.int32)
    offsets = jnp.where(
        degree_slot < half_degrees, 2 * degree_slot, 2 * (degree_slot - half_degrees) + 1
    )
    inside = offsets[None, None, :] < (degree_count - my_waves)[:, None, None]
    return jnp.where(inside, spectral, jnp.zeros_like(spectral))


def shift_of(block, used):
    return block * used // LANES, block * used % LANES


def gather_kernel(slots, low, table_ref, rows_ref, *refs):
    outs, turned = refs[:-1], refs[-1]
    me = lax.axis_index("wave")
    used, waves = rows_ref.shape
    rows = jnp.concatenate([rows_ref[...], jnp.zeros((LANES - used, waves), jnp.bfloat16)], axis=0)
    number = lax.broadcasted_iota(jnp.int32, (waves, LANES), 0)
    for j in range(0, table_ref.shape[0], 2):
        chosen = jnp.concatenate(
            [(number == table_ref[k : k + 1, :]).astype(jnp.bfloat16) for k in (j, j + 1)], axis=1
        )
        got = jnp.dot(rows, chosen, preferred_element_type=jnp.float32)
        turned[j * LANES : (j + 2) * LANES, :] = got.T
    lane = lax.broadcasted_iota(jnp.int32, (STEP, LANES), 1)
    for t, out in enumerate(outs):
        for u in range(low):
            begin = (me ^ (t * low + u)) * slots
            tiles = [jnp.zeros((STEP, LANES), jnp.float32)] * (out.shape[2] // LANES)
            for block in range(slots // STEP):
                tile, off = shift_of(block, used)
                value = turned[pl.ds(pl.multiple_of(begin + block * STEP, STEP), STEP), :]
                value = pltpu.roll(value, off, 1) if off else value
                tiles[tile] = jnp.where(lane >= off, value, tiles[tile])
                if off + used > LANES:
                    tiles[tile + 1] = jnp.where(lane < off + used - LANES, value, tiles[tile + 1])
            for k, tile in enumerate(tiles):
                out[u, :, k * LANES : (k + 1) * LANES] = tile.astype(jnp.bfloat16)


def place_kernel(turns, lat_count, row_count, pairs, degrees, table_ref, out, limits):
    northern = lax.axis_index("lat") < lat_count // 2
    me = lax.axis_index("wave")
    row = lax.broadcasted_iota(jnp.int32, (LANES, 2 * LANES), 0) & (row_count - 1)
    col = lax.broadcasted_iota(jnp.int32, (LANES, 2 * LANES), 1) & (pairs - 1 | LANES)
    half = len(turns) // 2
    for k, turn in enumerate(turns):
        source = me ^ turn
        ascending = (source < half) == northern
        position = (source % half) * row_count + row
        position = jnp.where(ascending, position, pairs - 1 - position)
        target = position + jnp.where(ascending, 0, LANES)
        out[k * LANES : (k + 1) * LANES, :] = (col == target).astype(jnp.bfloat16)
    slots = limits.shape[0]
    line = lax.broadcasted_iota(jnp.int32, (TILE, LANES), 0)
    for first in range(0, slots, TILE):
        value = jnp.zeros((TILE, LANES), jnp.int32)
        for s in range(TILE):
            value = jnp.where(line == s, degrees - table_ref[me * slots + first + s], value)
        limits[first : first + TILE, :] = value


def multiply(coefs, table, first, half, terms):
    pairs = table.shape[1]
    group = 2 * LANES // pairs
    cols = coefs.shape[0] // STEP
    shape = (cols * group, 2 * LANES)
    diagonal = (lax.broadcasted_iota(jnp.int32, shape, 0) & (group - 1)) == (
        lax.broadcasted_iota(jnp.int32, shape, 1) // pairs
    )
    blank = jnp.zeros(shape, jnp.bfloat16)
    for g in range(STEP // group):
        block = jnp.concatenate(
            [coefs[c * STEP + g * group : c * STEP + (g + 1) * group] for c in range(cols)], axis=0
        ).astype(jnp.bfloat16)
        block = jnp.where(diagonal, jnp.concatenate([block, block], axis=1), blank)
        weights = table[g * group : (g + 1) * group, :, pl.ds(first, half)]
        got = jnp.dot(
            block, weights.reshape(group * pairs, half), preferred_element_type=jnp.float32
        )
        for c in range(cols):
            terms[pl.ds(c * STEP + g * group, group), :] = got[c * group : (c + 1) * group]


def pack(terms, core, sent, kept):
    rows = terms.shape[0]
    part = rows // 4
    lane_low = lax.broadcasted_iota(jnp.int32, (part, LANES), 1) < LANES // 2
    for out, target in ((sent, 1 - core), (kept, core)):
        first = pl.multiple_of(target * 3 * LANES, LANES)
        out[:rows, :] = terms[:, pl.ds(first, 2 * LANES)].astype(out.dtype)
    for j in range(2):
        low = terms[pl.ds(2 * j * part, part), pl.ds(2 * LANES, LANES)]
        high = terms[pl.ds((2 * j + 1) * part, part), pl.ds(2 * LANES, LANES)]
        zeroth = jnp.where(lane_low, low, pltpu.roll(high, LANES // 2, 1))
        other = jnp.where(lane_low, pltpu.roll(low, LANES // 2, 1), high)
        for out, target in ((sent, 1 - core), (kept, core)):
            out[rows:, j * LANES : (j + 1) * LANES] = jnp.where(target == 0, zeroth, other).astype(
                out.dtype
            )


def product_kernel(block, row_count, cols, place_ref, leg_ref, *refs):
    sources = refs[:-8]
    far_sent, far_own, near_sent, near_own, table, far, near, sem = refs[-8:]
    half = far.shape[1]
    lat = lax.axis_index("lat")
    y, core = lat // 2, lat % 2
    copy = pltpu.make_async_copy(leg_ref.at[pl.ds(block * STEP, STEP)], table, sem)
    copy.start()
    tile, off = shift_of(block, row_count * cols)
    lane = lax.broadcasted_iota(jnp.int32, (STEP, LANES), 1)
    held = ((lane - off) & (LANES - 1)) // row_count
    zero = jnp.zeros((STEP, LANES), jnp.bfloat16)
    parts = []
    for source in sources:
        for k in range(source.shape[0]):
            value = source[k, :, tile * LANES : (tile + 1) * LANES]
            if off + row_count * cols > LANES:
                value = jnp.where(
                    lane >= off, value, source[k, :, (tile + 1) * LANES : (tile + 2) * LANES]
                )
            parts.append(
                jnp.concatenate([jnp.where(held == c, value, zero) for c in range(cols)], axis=0)
            )
    both = jnp.dot(
        jnp.concatenate(parts, axis=1), place_ref[...], preferred_element_type=jnp.float32
    )
    north, south = both[:, :LANES], both[:, LANES:]
    even, odd = north + south, north - south
    far_coefs, near_coefs = jnp.where(y == 0, odd, even), jnp.where(y == 0, even, odd)
    copy.wait()
    multiply(far_coefs, table, pl.multiple_of((1 - y) * half, LANES), half, far)
    multiply(near_coefs, table, pl.multiple_of(y * half, LANES), half, near)
    pack(far, core, far_sent, far_own)
    pack(near, core, near_sent, near_own)


def final_kernel(base, degrees, cols, limits_ref, near_ref, far_ref, *refs):
    out = refs[-1]
    lat = lax.axis_index("lat")
    first = lat % 2 == 0
    half = degrees // 2
    width = out.shape[2]
    rows = STEP * cols
    value = near_ref[...] + far_ref[...].astype(jnp.float32)
    main0, main1 = value[:rows, :LANES], value[:rows, LANES:]
    tails = []
    for j in range(4):
        tail = value[rows:, (j // 2) * LANES : (j // 2 + 1) * LANES]
        tails.append(pltpu.roll(tail, LANES // 2, 1) if j % 2 else tail)
    tail = jnp.concatenate(tails, axis=0)
    lane_low = lax.broadcasted_iota(jnp.int32, (rows, LANES), 1) < LANES // 2
    turn0, turn1 = pltpu.roll(main0, LANES // 2, 1), pltpu.roll(main1, LANES // 2, 1)
    ordered = jnp.concatenate(
        [
            jnp.where(first, main0, jnp.where(lane_low, tail, turn0)),
            jnp.where(first, main1, jnp.where(lane_low, turn0, turn1)),
            jnp.where(first, tail, turn1),
        ],
        axis=1,
    )
    shape = (STEP, 3 * LANES)
    degree = lat * width + lax.broadcasted_iota(jnp.int32, shape, 1)
    offsets = jnp.where(degree < half, 2 * degree, 2 * (degree - half) + 1)
    limits = limits_ref[base : base + STEP, :]
    limits = jnp.concatenate([limits] * 3, axis=1)
    inside = offsets < limits
    for c in range(cols):
        out[c] = jnp.where(inside, ordered[c * STEP : (c + 1) * STEP], 0.0)[:, :width]


def packed(fourier, wave_table, legendre):
    slots, pairs, degrees = legendre.shape
    row_count, cols, waves = fourier.shape
    wave_count, lat_count = lax.axis_size("wave"), lax.axis_size("lat")
    width = degrees // lat_count
    used = row_count * cols
    params = pltpu.CompilerParams(vmem_limit_bytes=VMEM)
    whole = pl.BlockSpec(memory_space=pltpu.VMEM)
    anywhere = pl.BlockSpec(memory_space=pl.ANY)

    message = -(-(slots // STEP) * used // LANES) * LANES
    low = 2
    high = wave_count // low
    ordered = pl.pallas_call(
        functools.partial(gather_kernel, slots, low),
        out_shape=[jax.ShapeDtypeStruct((low, STEP, message), jnp.bfloat16)] * high,
        in_specs=[whole, whole],
        out_specs=[whole] * high,
        scratch_shapes=[pltpu.VMEM((slots * wave_count, LANES), jnp.float32)],
        compiler_params=params,
        name="gather",
    )(
        wave_table.reshape(-1, LANES),
        jnp.transpose(fourier, (1, 0, 2)).reshape(used, waves),
    )
    turns = [
        t * low + u
        for u in range(low)
        for side in (0, 1)
        for t in range(side * high // 2, (side + 1) * high // 2)
    ]
    place, limits = pl.pallas_call(
        functools.partial(place_kernel, turns, lat_count, row_count, pairs, degrees),
        out_shape=[
            jax.ShapeDtypeStruct((wave_count * LANES, 2 * LANES), jnp.bfloat16),
            jax.ShapeDtypeStruct((slots, LANES), jnp.int32),
        ],
        in_specs=[pl.BlockSpec(memory_space=pltpu.SMEM)],
        out_specs=[whole] * 2,
        compiler_params=params,
        name="place",
    )(wave_table)

    passed = [ordered[0]] + [
        lax.ppermute(ordered[t], "wave", [(w, w ^ t * low) for w in range(wave_count)])
        for t in range(1, high)
    ]
    sources = []
    for u in range(low):
        for side in (0, 1):
            block = jnp.stack([passed[t][u] for t in range(side * high // 2, (side + 1) * high // 2)])
            route = []
            for lat in range(lat_count):
                for wave in range(wave_count):
                    began = (wave >= wave_count // 2) != (side == 1)
                    to = lat_count - 1 - lat if began else lat
                    route.append((lat * wave_count + wave, to * wave_count + (wave ^ u)))
            sources.append(lax.ppermute(block, ("lat", "wave"), route))

    rows = STEP * cols
    shape = (rows + rows // 4, 2 * LANES)
    core_route = [(lat, lat ^ 1) for lat in range(lat_count)]
    y_route = [(lat, lat ^ 2) for lat in range(lat_count)]
    scratch = [
        pltpu.VMEM((STEP, pairs, degrees), jnp.bfloat16),
        pltpu.VMEM((rows, degrees // 2), jnp.float32),
        pltpu.VMEM((rows, degrees // 2), jnp.float32),
        pltpu.SemaphoreType.DMA,
    ]
    cost = pl.CostEstimate(flops=0, bytes_accessed=1024, transcendentals=0)
    pair_of_sums = [
        jax.ShapeDtypeStruct(shape, jnp.bfloat16),
        jax.ShapeDtypeStruct(shape, jnp.float32),
    ]
    count = slots // STEP

    def settle(sent, kept):
        return kept + lax.ppermute(sent, "lat", core_route).astype(jnp.float32)

    crossed, settled = [], []
    ties = []
    for block in range(count):
        sources, ties = lax.optimization_barrier((sources, ties))
        far_sent, far_own, near_sent, near_own = pl.pallas_call(
            functools.partial(product_kernel, block, row_count, cols),
            out_shape=pair_of_sums * 2,
            in_specs=[whole, anywhere] + [whole] * len(sources),
            out_specs=[whole] * 4,
            scratch_shapes=scratch,
            compiler_params=params,
            cost_estimate=cost,
            name="product",
        )(place, legendre, *sources)
        summed = settle(far_sent, far_own).astype(jnp.bfloat16)
        ties = [summed] + settled[-1:]
        crossed.append(lax.ppermute(summed, "lat", y_route))
        settled.append(settle(near_sent, near_own))

    out = None
    for block in range(count):
        carried = [] if out is None else [out]
        out = pl.pallas_call(
            functools.partial(final_kernel, block * STEP, degrees, cols),
            grid=(1,),
            in_specs=[whole] * 3 + [anywhere] * len(carried),
            out_specs=pl.BlockSpec((cols, STEP, width), lambda g, at=block: (0, at, 0)),
            out_shape=jax.ShapeDtypeStruct((cols, slots, width), jnp.float32),
            input_output_aliases={3: 0} if carried else {},
            compiler_params=params,
            cost_estimate=cost,
            name="final",
        )(limits, settled[block], crossed[block], *carried)
    return jnp.transpose(out, (1, 0, 2))


def local(fourier, wave_table, legendre):
    slots, pairs, degrees = legendre.shape
    row_count, cols, waves = fourier.shape
    wave_count, lat_count = lax.axis_size("wave"), lax.axis_size("lat")
    fits = (
        lat_count == 4
        and wave_count & (wave_count - 1) == 0
        and slots % STEP == 0
        and degrees // 2 == 5 * LANES
        and row_count & (row_count - 1) == 0
        and LANES // 4 % row_count == 0
        and row_count * cols % (LANES // 4) == 0
        and row_count * cols <= LANES
        and pairs == row_count * wave_count // 2
        and pairs * TILE == 2 * LANES
        and waves % (2 * LANES) == 0
    )
    if not fits:
        return plain(fourier, wave_table, legendre)
    return packed(fourier, wave_table, legendre)


def solution(mesh):
    in_specs = (P(("lat", "wave"), None, None), P(), P("wave", "lat", None))
    out_specs = P("wave", None, "lat")
    return jax.shard_map(local, mesh=mesh, in_specs=in_specs, out_specs=out_specs, check_vma=False)
```

time: 68 us -> 59.8 us (0.88)
  blocking collectives: 16 us -> 0 us
  starting transfers between devices: 7.73 us -> 20.4 us
  Pallas kernels: 30.7 us -> 20.3 us
  waiting for transfers between devices: 10.8 us -> 16.3 us
    all_to_all x1 -> x0, blocking collectives: 16 us -> none  [packed(): lax.all_to_all(ordered, 'wave', split_axis=0, concat_axis=0, tiled=True)]
    ppermute x6 -> x12, starting transfers between devices: 5.04 us -> 17.6 us  [the longest x5 5.94 us: packed(): crossed.append(lax.ppermute(summed, 'lat', y_route))]
    pallas_call x17 -> x12, Pallas kernels: 30.7 us -> 20.3 us  [the longest x5 13.5 us: packed(): pl.pallas_call(functools.partial(product_kernel, block, row_count, cols),...]
    ppermute x6 -> x12, waiting for transfers between devices: 9.62 us -> 13.5 us  [the longest x5 5.7 us: packed(): crossed.append(lax.ppermute(summed, 'lat', y_route))]
    ppermute x10, waiting for transfers between devices: 1.18 us -> 2.88 us  [settle(): return kept + lax.ppermute(sent, 'lat', core_route).astype(jnp.float32)]
    unnamed x6 -> x4, local copies, waits for them, and re-layouts: 1.65 us -> 1.64 us
  transfers between devices with their start and end apart: 16 -> 22, of which waited for: 3 -> 10; matrix products, arithmetic and copies ran while one was open for 1% -> 1% of each run, Pallas kernels for 38% -> 26%
where the time goes in v4:
time: 59.8 us; the launch traced here: 59.5 us
  starting transfers between devices  20.4 us (34%)
  Pallas kernels  20.3 us (34%)
  waiting for transfers between devices  16.3 us (27%)
  local copies, waits for them, and re-layouts  1.66 us (3%)
    pallas_call x5, Pallas kernels, packed(): pl.pallas_call(functools.partial(product_kernel, block, row_count, cols),...  13.5 us
    ppermute x5, starting transfers between devices, packed(): crossed.append(lax.ppermute(summed, 'lat', y_route))  5.94 us
    ppermute x4, starting transfers between devices, packed(): sources.append(lax.ppermute(block, ('lat', 'wave'), route))  5.91 us
    ppermute x3, starting transfers between devices, packed(): lax.ppermute(ordered[t], 'wave', [(w, w ^ t * low) for w in range(wave_co...  5.76 us
    ppermute x5, waiting for transfers between devices, packed(): crossed.append(lax.ppermute(summed, 'lat', y_route))  5.7 us
    pallas_call x5, Pallas kernels, packed(): pl.pallas_call(functools.partial(final_kernel, block * STEP, degrees, col...  5.06 us
    ppermute x3, waiting for transfers between devices, packed(): lax.ppermute(ordered[t], 'wave', [(w, w ^ t * low) for w in range(wave_co...  4.95 us
    ppermute x10, waiting for transfers between devices, settle(): return kept + lax.ppermute(sent, 'lat', core_route).astype(jnp.float32)  2.88 us
  transfers between devices with their start and end apart: 22, of which 10 were waited for; matrix products, arithmetic and copies ran while one was open for 1% of the time, Pallas kernels for 26%

profile of v4, /device:TPU:0, one launch (start us, length us, event | category | flops | bytes accessed | tf_op | source)
XLA Modules:
  0.0 59.5 jit_solution(12843567978253372780)
XLA Ops:
  0.0 0.0 copy-start
  0.0 0.9 %copy-done = bf16[8,12,1280]{2,0,1:T(8,128)(2,1)S(1)} copy-done((bf16[8,12,1280]{2,0,1:T(8,128)(2,1)S(1)}, bf16[8,12,1280]{2,0,1:T(8,128)(2,1)}, u32[]{:S(2)}) %copy-start) | copy-done | bytes 245784
  0.9 0.7 %copy-done.1 = s32[1280]{0:T(1024)S(1)} copy-done((s32[1280]{0:T(1024)S(1)}, s32[1280]{0:T(1024)}, u32[]{:S(2)}) %copy-start.1) | copy-done | bytes 5144
  1.6 0.8 %gather.1 = (bf16[2,32,512]{2,1,0:T(8,128)(2,1)S(1)}, bf16[2,32,512]{2,1,0:T(8,128)(2,1)S(1)}, bf16[2,32,512]{2,1,0:T(8,128)(2,1)S(1)}, bf16[2,32,512]{2,1,0:T(8,128)(2,1)S(1)}) custom-call(s32[10,128]{1,0:T(8,128)S(1)} %bitcast.6, bf16[96,1280]{1,0:T(8,128)(2,1)S(1)} %bitcast.5), custom_call_target="tpu_custom_call" | custom-call | tf_op jit(solution)/shard_map/gather/pallas_call | solution.py:240
  2.5 5.1 %collective-permute-start.3 = (bf16[2,32,512]{2,1,0:T(8,128)(2,1)S(1)}, bf16[2,32,512]{2,1,0:T(8,128)(2,1)S(1)}, u32[]{:S(2)}, u32[]{:S(2)}) collective-permute-start(bf16[2,32,512]{2,1,0:T(8,128)(2,1)S(1)} %get-tuple-element.56), channel_id=1, source_target_pairs={{0,6},{1,7},{2,4},{3,5},{4,2},{5,3},{6,0},{7,1},{8,14},{9,15},{10,... | collective-permute-start | bytes 196616 | tf_op jit(solution)/shard_map/ppermute | solution.py:271
  7.6 0.0 collective-permute-start.2
  7.6 0.6 %collective-permute-start = (bf16[2,32,512]{2,1,0:T(8,128)(2,1)S(1)}, bf16[2,32,512]{2,1,0:T(8,128)(2,1)S(1)}, u32[]{:S(2)}, u32[]{:S(2)}) collective-permute-start(bf16[2,32,512]{2,1,0:T(8,128)(2,1)S(1)} %get-tuple-element.54), channel_id=1, source_target_pairs={{0,2},{1,3},{2,0},{3,1},{4,6},{5,7},{6,4},{7,5},{8,10},{9,11},{10,... | collective-permute-start | bytes 196616 | tf_op jit(solution)/shard_map/ppermute | solution.py:271
  8.2 1.9 %collective-permute-done.3 = bf16[2,32,512]{2,1,0:T(8,128)(2,1)S(1)} collective-permute-done((bf16[2,32,512]{2,1,0:T(8,128)(2,1)S(1)}, bf16[2,32,512]{2,1,0:T(8,128)(2,1)S(1)}, u32[]{:S(2)}, u32[]{:S(2)}) %collective-permute-start.3) | collective-permute-done | bytes 65568 | tf_op jit(solution)/shard_map/ppermute | solution.py:271
  10.2 3.0 %collective-permute-done.2 = bf16[2,32,512]{2,1,0:T(8,128)(2,1)S(1)} collective-permute-done((bf16[2,32,512]{2,1,0:T(8,128)(2,1)S(1)}, bf16[2,32,512]{2,1,0:T(8,128)(2,1)S(1)}, u32[]{:S(2)}, u32[]{:S(2)}) %collective-permute-start.2) | collective-permute-done | bytes 65568 | tf_op jit(solution)/shard_map/ppermute | solution.py:271
  13.2 2.9 %collective-permute-start.4 = (bf16[2,32,512]{2,1,0:T(8,128)(2,1)S(1)}, bf16[2,32,512]{2,1,0:T(8,128)(2,1)S(1)}, u32[]{:S(2)}, u32[]{:S(2)}) collective-permute-start(bf16[2,32,512]{2,1,0:T(8,128)(2,1)S(1)} %pad_maximum_fusion.1), channel_id=1, source_target_pairs={{0,24},{1,25},{2,26},{3,27},{4,4},{5,5},{6,6},{7,7},{8,16},{9,17},... | collective-permute-start | bytes 196616 | tf_op jit(solution)/shard_map/ppermute | solution.py:284
  16.1 1.8 %collective-permute-start.6 = (bf16[2,32,512]{2,1,0:T(8,128)(2,1)S(1)}, bf16[2,32,512]{2,1,0:T(8,128)(2,1)S(1)}, u32[]{:S(2)}, u32[]{:S(2)}) collective-permute-start(bf16[2,32,512]{2,1,0:T(8,128)(2,1)S(1)} %pad_maximum_fusion.3), channel_id=1, source_target_pairs={{0,25},{1,24},{2,27},{3,26},{4,5},{5,4},{6,7},{7,6},{8,17},{9,16},... | collective-permute-start | bytes 196616 | tf_op jit(solution)/shard_map/ppermute | solution.py:284
  17.9 0.0 collective-permute-done
  17.9 0.7 %collective-permute-start.1 = (bf16[2,32,512]{2,1,0:T(8,128)(2,1)S(1)}, bf16[2,32,512]{2,1,0:T(8,128)(2,1)S(1)}, u32[]{:S(2)}, u32[]{:S(2)}) collective-permute-start(bf16[2,32,512]{2,1,0:T(8,128)(2,1)S(1)} %pad_maximum_fusion), channel_id=1, source_target_pairs={{0,0},{1,1},{2,2},{3,3},{4,28},{5,29},{6,30},{7,31},{8,8},{9,9},{1... | collective-permute-start | bytes 196616 | tf_op jit(solution)/shard_map/ppermute | solution.py:284
  18.6 0.6 %collective-permute-start.5 = (bf16[2,32,512]{2,1,0:T(8,128)(2,1)S(1)}, bf16[2,32,512]{2,1,0:T(8,128)(2,1)S(1)}, u32[]{:S(2)}, u32[]{:S(2)}) collective-permute-start(bf16[2,32,512]{2,1,0:T(8,128)(2,1)S(1)} %pad_maximum_fusion.2), channel_id=1, source_target_pairs={{0,1},{1,0},{2,3},{3,2},{4,29},{5,28},{6,31},{7,30},{8,9},{9,8},{1... | collective-permute-start | bytes 196616 | tf_op jit(solution)/shard_map/ppermute | solution.py:284
  19.2 0.9 %place.1 = (bf16[1024,256]{1,0:T(8,128)(2,1)S(1)}, s32[160,128]{1,0:T(8,128)S(1)}) custom-call(s32[1280]{0:T(1024)S(1)} %copy-done.1), custom_call_target="tpu_custom_call" | custom-call | tf_op jit(solution)/shard_map/place/pallas_call | solution.py:258
  20.1 0.0 collective-permute-done.4.refs_1_
  20.1 0.6 %collective-permute-done.6.refs_3_ = bf16[2,32,512]{2,1,0:T(8,128)(2,1)S(1)} collective-permute-done((bf16[2,32,512]{2,1,0:T(8,128)(2,1)S(1)}, bf16[2,32,512]{2,1,0:T(8,128)(2,1)S(1)}, u32[]{:S(2)}, u32[]{:S(2)}) %collective-permute-start.6) | collective-permute-done | bytes 65568 | tf_op jit(solution)/shard_map/ppermute | solution.py:284
  20.8 0.0 collective-permute-done.1.refs_0_
  20.8 2.2 %collective-permute-done.5.refs_2_ = bf16[2,32,512]{2,1,0:T(8,128)(2,1)S(1)} collective-permute-done((bf16[2,32,512]{2,1,0:T(8,128)(2,1)S(1)}, bf16[2,32,512]{2,1,0:T(8,128)(2,1)S(1)}, u32[]{:S(2)}, u32[]{:S(2)}) %collective-permute-start.5) | collective-permute-done | bytes 65568 | tf_op jit(solution)/shard_map/ppermute | solution.py:284
  22.9 2.7 %product.5 = (bf16[480,256]{1,0:T(8,128)(2,1)S(1)}, f32[480,256]{1,0:T(8,128)S(1)}, bf16[480,256]{1,0:T(8,128)(2,1)S(1)}, f32[480,256]{1,0:T(8,128)S(1)}) custom-call(bf16[1024,256]{1,0:T(8,128)(2,1)S(1)} %get-tuple-element.52.place_ref, bf16[160,32,1280]{2,1,0:T(8,128)(2,1)} %leg_ref.9, bf16[2,32,512]{2,1,0:T(8,128)(2,1)S(1)} %collective-permute-done.1.refs_0_, ...), custom_call_target="tpu_custom_call" | custom-call | bytes 1024 | tf_op jit(solution)/shard_map/product/pallas_call | solution.py:310
  25.6 0.1 collective-permute-start.7
  25.7 0.5 collective-permute-start.9
  26.2 1.0 %collective-permute-done.7 = bf16[480,256]{1,0:T(8,128)(2,1)S(1)} collective-permute-done((bf16[480,256]{1,0:T(8,128)(2,1)S(1)}, bf16[480,256]{1,0:T(8,128)(2,1)S(1)}, u32[]{:S(2)}, u32[]{:S(2)}) %collective-permute-start.7) | collective-permute-done | bytes 245792 | tf_op jit(solution)/shard_map/ppermute | solution.py:304
  27.2 0.1 add_convert_fusion.4
  27.3 1.6 %collective-permute-start.21 = (bf16[480,256]{1,0:T(8,128)(2,1)S(1)}, bf16[480,256]{1,0:T(8,128)(2,1)S(1)}, u32[]{:S(2)}, u32[]{:S(2)}) collective-permute-start(bf16[480,256]{1,0:T(8,128)(2,1)S(1)} %add_convert_fusion.4), channel_id=1, source_target_pairs={{0,16},{8,24},{16,0},{24,8},{1,17},{9,25},{17,1},{25,9},{2,18},{10... | collective-permute-start | bytes 737288 | tf_op jit(solution)/shard_map/ppermute | solution.py:322
  28.9 2.7 %product.6 = (bf16[480,256]{1,0:T(8,128)(2,1)S(1)}, f32[480,256]{1,0:T(8,128)S(1)}, bf16[480,256]{1,0:T(8,128)(2,1)S(1)}, f32[480,256]{1,0:T(8,128)S(1)}) custom-call(bf16[1024,256]{1,0:T(8,128)(2,1)S(1)} %get-tuple-element.52.place_ref, bf16[160,32,1280]{2,1,0:T(8,128)(2,1)} %leg_ref.9, bf16[2,32,512]{2,1,0:T(8,128)(2,1)S(1)} %collective-permute-done.1.refs_0_, ...), custom_call_target="tpu_custom_call" | custom-call | bytes 1024 | tf_op jit(solution)/shard_map/product/pallas_call | solution.py:310
  31.6 0.1 collective-permute-start.11
  31.6 0.5 collective-permute-start.8
  32.1 0.0 collective-permute-done.9
  32.2 1.3 %collective-permute-done.8 = bf16[480,256]{1,0:T(8,128)(2,1)S(1)} collective-permute-done((bf16[480,256]{1,0:T(8,128)(2,1)S(1)}, bf16[480,256]{1,0:T(8,128)(2,1)S(1)}, u32[]{:S(2)}, u32[]{:S(2)}) %collective-permute-start.8) | collective-permute-done | bytes 245792 | tf_op jit(solution)/shard_map/ppermute | solution.py:304
  33.5 0.1 add_convert_fusion.3
  33.5 0.6 collective-permute-start.20
  34.1 2.7 %product.7 = (bf16[480,256]{1,0:T(8,128)(2,1)S(1)}, f32[480,256]{1,0:T(8,128)S(1)}, bf16[480,256]{1,0:T(8,128)(2,1)S(1)}, f32[480,256]{1,0:T(8,128)S(1)}) custom-call(bf16[1024,256]{1,0:T(8,128)(2,1)S(1)} %get-tuple-element.52.place_ref, bf16[160,32,1280]{2,1,0:T(8,128)(2,1)} %leg_ref.9, bf16[2,32,512]{2,1,0:T(8,128)(2,1)S(1)} %collective-permute-done.1.refs_0_, ...), custom_call_target="tpu_custom_call" | custom-call | bytes 1024 | tf_op jit(solution)/shard_map/product/pallas_call | solution.py:310
  36.8 0.1 collective-permute-start.13
  36.9 0.5 collective-permute-start.10
  37.4 0.0 collective-permute-done.21.far_ref
  37.4 1.0 %final.5.refs_0_ = f32[12,160,320]{2,1,0:T(8,128)} custom-call(s32[160,128]{1,0:T(8,128)S(1)} %get-tuple-element.51.limits_ref, f32[480,256]{1,0:T(8,128)S(1)} %convert_add_fusion.4.near_ref, bf16[480,256]{1,0:T(8,128)(2,1)S(1)} %collective-permute-done.21.far_ref), custom_call_target="tpu_custom_call" | custom-call | bytes 1024 | tf_op jit(solution)/shard_map/final/pallas_call | solution.py:328
  38.4 0.0 collective-permute-done.11
  38.5 0.3 collective-permute-done.10
  38.7 0.1 add_convert_fusion.2
  38.8 1.6 %collective-permute-start.19 = (bf16[480,256]{1,0:T(8,128)(2,1)S(1)}, bf16[480,256]{1,0:T(8,128)(2,1)S(1)}, u32[]{:S(2)}, u32[]{:S(2)}) collective-permute-start(bf16[480,256]{1,0:T(8,128)(2,1)S(1)} %add_convert_fusion.2), channel_id=1, source_target_pairs={{0,16},{8,24},{16,0},{24,8},{1,17},{9,25},{17,1},{25,9},{2,18},{10... | collective-permute-start | bytes 737288 | tf_op jit(solution)/shard_map/ppermute | solution.py:322
  40.4 2.7 %product.8 = (bf16[480,256]{1,0:T(8,128)(2,1)S(1)}, f32[480,256]{1,0:T(8,128)S(1)}, bf16[480,256]{1,0:T(8,128)(2,1)S(1)}, f32[480,256]{1,0:T(8,128)S(1)}) custom-call(bf16[1024,256]{1,0:T(8,128)(2,1)S(1)} %get-tuple-element.52.place_ref, bf16[160,32,1280]{2,1,0:T(8,128)(2,1)} %leg_ref.9, bf16[2,32,512]{2,1,0:T(8,128)(2,1)S(1)} %collective-permute-done.1.refs_0_, ...), custom_call_target="tpu_custom_call" | custom-call | bytes 1024 | tf_op jit(solution)/shard_map/product/pallas_call | solution.py:310
  43.1 0.1 collective-permute-start.17
  43.2 0.5 collective-permute-start.12
  43.7 0.0 collective-permute-done.20.far_ref
  43.7 1.0 %final.6.refs_0_ = f32[12,160,320]{2,1,0:T(8,128)} custom-call(s32[160,128]{1,0:T(8,128)S(1)} %get-tuple-element.51.limits_ref, f32[480,256]{1,0:T(8,128)S(1)} %convert_add_fusion.3.near_ref, bf16[480,256]{1,0:T(8,128)(2,1)S(1)} %collective-permute-done.20.far_ref, f32[12,160,320]{2,1,0:T(8,128)} %final.5.refs_0_), custom_call_target="tpu_custom_call", output_to_operand_aliasing={{}: (3, {})} | custom-call | bytes 1024 | tf_op jit(solution)/shard_map/final/pallas_call | solution.py:328
  44.7 0.0 collective-permute-done.13
  44.8 0.3 collective-permute-done.12
  45.0 0.1 add_convert_fusion.1
  45.1 0.6 collective-permute-start.18
  45.7 2.7 %product.9 = (bf16[480,256]{1,0:T(8,128)(2,1)S(1)}, f32[480,256]{1,0:T(8,128)S(1)}, bf16[480,256]{1,0:T(8,128)(2,1)S(1)}, f32[480,256]{1,0:T(8,128)S(1)}) custom-call(bf16[1024,256]{1,0:T(8,128)(2,1)S(1)} %get-tuple-element.52.place_ref, bf16[160,32,1280]{2,1,0:T(8,128)(2,1)} %leg_ref.9, bf16[2,32,512]{2,1,0:T(8,128)(2,1)S(1)} %collective-permute-done.1.refs_0_, ...), custom_call_target="tpu_custom_call" | custom-call | bytes 1024 | tf_op jit(solution)/shard_map/product/pallas_call | solution.py:310
  48.4 0.1 collective-permute-start.15
  48.4 0.5 collective-permute-start.14
  48.9 0.0 collective-permute-done.19.far_ref
  48.9 1.0 %final.7.refs_0_ = f32[12,160,320]{2,1,0:T(8,128)} custom-call(s32[160,128]{1,0:T(8,128)S(1)} %get-tuple-element.51.limits_ref, f32[480,256]{1,0:T(8,128)S(1)} %convert_add_fusion.2.near_ref, bf16[480,256]{1,0:T(8,128)(2,1)S(1)} %collective-permute-done.19.far_ref, f32[12,160,320]{2,1,0:T(8,128)} %final.6.refs_0_), custom_call_target="tpu_custom_call", output_to_operand_aliasing={{}: (3, {})} | custom-call | bytes 1024 | tf_op jit(solution)/shard_map/final/pallas_call | solution.py:328
  50.0 0.0 collective-permute-done.17
  50.0 0.0 collective-permute-done.15
  50.0 0.1 add_convert_fusion
  50.1 1.6 %collective-permute-start.16 = (bf16[480,256]{1,0:T(8,128)(2,1)S(1)}, bf16[480,256]{1,0:T(8,128)(2,1)S(1)}, u32[]{:S(2)}, u32[]{:S(2)}) collective-permute-start(bf16[480,256]{1,0:T(8,128)(2,1)S(1)} %add_convert_fusion), channel_id=1, source_target_pairs={{0,16},{8,24},{16,0},{24,8},{1,17},{9,25},{17,1},{25,9},{2,18},{10... | collective-permute-start | bytes 737288 | tf_op jit(solution)/shard_map/ppermute | solution.py:322
  51.7 1.8 %collective-permute-done.18.far_ref = bf16[480,256]{1,0:T(8,128)(2,1)S(1)} collective-permute-done((bf16[480,256]{1,0:T(8,128)(2,1)S(1)}, bf16[480,256]{1,0:T(8,128)(2,1)S(1)}, u32[]{:S(2)}, u32[]{:S(2)}) %collective-permute-start.18) | collective-permute-done | bytes 245792 | tf_op jit(solution)/shard_map/ppermute | solution.py:322
  53.5 1.0 %final.8.refs_0_ = f32[12,160,320]{2,1,0:T(8,128)} custom-call(s32[160,128]{1,0:T(8,128)S(1)} %get-tuple-element.51.limits_ref, f32[480,256]{1,0:T(8,128)S(1)} %convert_add_fusion.near_ref, bf16[480,256]{1,0:T(8,128)(2,1)S(1)} %collective-permute-done.18.far_ref, f32[12,160,320]{2,1,0:T(8,128)} %final.7.refs_0_), custom_call_target="tpu_custom_call", output_to_operand_aliasing={{}: (3, {})} | custom-call | bytes 1024 | tf_op jit(solution)/shard_map/final/pallas_call | solution.py:328
  54.5 0.0 collective-permute-done.14
  54.5 3.9 %collective-permute-done.16.far_ref = bf16[480,256]{1,0:T(8,128)(2,1)S(1)} collective-permute-done((bf16[480,256]{1,0:T(8,128)(2,1)S(1)}, bf16[480,256]{1,0:T(8,128)(2,1)S(1)}, u32[]{:S(2)}, u32[]{:S(2)}) %collective-permute-start.16) | collective-permute-done | bytes 245792 | tf_op jit(solution)/shard_map/ppermute | solution.py:322
  58.4 1.0 %final.9 = f32[12,160,320]{2,1,0:T(8,128)} custom-call(s32[160,128]{1,0:T(8,128)S(1)} %get-tuple-element.51.limits_ref, f32[480,256]{1,0:T(8,128)S(1)} %convert_add_fusion.1.near_ref, bf16[480,256]{1,0:T(8,128)(2,1)S(1)} %collective-permute-done.16.far_ref, f32[12,160,320]{2,1,0:T(8,128)} %final.8.refs_0_), custom_call_target="tpu_custom_call", output_to_operand_aliasing={{}: (3, {})} | custom-call | bytes 1024 | tf_op jit(solution)/shard_map/final/pallas_call | solution.py:328
  (14 shorter events, 0.3 us)
Async XLA Ops:
  0.0 0.9 %copy-start = (bf16[8,12,1280]{2,0,1:T(8,128)(2,1)S(1)}, bf16[8,12,1280]{2,0,1:T(8,128)(2,1)}, u32[]{:S(2)}) copy-start(bf16[8,12,1280]{2,0,1:T(8,128)(2,1)} %param.3) | copy-start | bytes 737284
  0.9 0.7 %copy-start.1 = (s32[1280]{0:T(1024)S(1)}, s32[1280]{0:T(1024)}, u32[]{:S(2)}) copy-start(s32[1280]{0:T(1024)} %table_ref.1) | copy-start | bytes 15364
  2.5 7.7 %collective-permute-start.3 = (bf16[2,32,512]{2,1,0:T(8,128)(2,1)S(1)}, bf16[2,32,512]{2,1,0:T(8,128)(2,1)S(1)}, u32[]{:S(2)}, u32[]{:S(2)}) collective-permute-start(bf16[2,32,512]{2,1,0:T(8,128)(2,1)S(1)} %get-tuple-element.56), channel_id=1, source_target_pairs={{0,6},{1,7},{2,4},{3,5},{4,2},{5,3},{6,0},{7,1},{8,14},{9,15},{10,... | collective-permute-start | bytes 196616 | tf_op jit(solution)/shard_map/ppermute | solution.py:271
  7.6 5.6 %collective-permute-start.2 = (bf16[2,32,512]{2,1,0:T(8,128)(2,1)S(1)}, bf16[2,32,512]{2,1,0:T(8,128)(2,1)S(1)}, u32[]{:S(2)}, u32[]{:S(2)}) collective-permute-start(bf16[2,32,512]{2,1,0:T(8,128)(2,1)S(1)} %get-tuple-element.55), channel_id=1, source_target_pairs={{0,4},{1,5},{2,6},{3,7},{4,0},{5,1},{6,2},{7,3},{8,12},{9,13},{10,... | collective-permute-start | bytes 196616 | tf_op jit(solution)/shard_map/ppermute | solution.py:271
  7.6 10.3 %collective-permute-start = (bf16[2,32,512]{2,1,0:T(8,128)(2,1)S(1)}, bf16[2,32,512]{2,1,0:T(8,128)(2,1)S(1)}, u32[]{:S(2)}, u32[]{:S(2)}) collective-permute-start(bf16[2,32,512]{2,1,0:T(8,128)(2,1)S(1)} %get-tuple-element.54), channel_id=1, source_target_pairs={{0,2},{1,3},{2,0},{3,1},{4,6},{5,7},{6,4},{7,5},{8,10},{9,11},{10,... | collective-permute-start | bytes 196616 | tf_op jit(solution)/shard_map/ppermute | solution.py:271
  13.2 6.9 %collective-permute-start.4 = (bf16[2,32,512]{2,1,0:T(8,128)(2,1)S(1)}, bf16[2,32,512]{2,1,0:T(8,128)(2,1)S(1)}, u32[]{:S(2)}, u32[]{:S(2)}) collective-permute-start(bf16[2,32,512]{2,1,0:T(8,128)(2,1)S(1)} %pad_maximum_fusion.1), channel_id=1, source_target_pairs={{0,24},{1,25},{2,26},{3,27},{4,4},{5,5},{6,6},{7,7},{8,16},{9,17},... | collective-permute-start | bytes 196616 | tf_op jit(solution)/shard_map/ppermute | solution.py:284
  16.1 4.7 %collective-permute-start.6 = (bf16[2,32,512]{2,1,0:T(8,128)(2,1)S(1)}, bf16[2,32,512]{2,1,0:T(8,128)(2,1)S(1)}, u32[]{:S(2)}, u32[]{:S(2)}) collective-permute-start(bf16[2,32,512]{2,1,0:T(8,128)(2,1)S(1)} %pad_maximum_fusion.3), channel_id=1, source_target_pairs={{0,25},{1,24},{2,27},{3,26},{4,5},{5,4},{6,7},{7,6},{8,17},{9,16},... | collective-permute-start | bytes 196616 | tf_op jit(solution)/shard_map/ppermute | solution.py:284
  17.9 2.9 %collective-permute-start.1 = (bf16[2,32,512]{2,1,0:T(8,128)(2,1)S(1)}, bf16[2,32,512]{2,1,0:T(8,128)(2,1)S(1)}, u32[]{:S(2)}, u32[]{:S(2)}) collective-permute-start(bf16[2,32,512]{2,1,0:T(8,128)(2,1)S(1)} %pad_maximum_fusion), channel_id=1, source_target_pairs={{0,0},{1,1},{2,2},{3,3},{4,28},{5,29},{6,30},{7,31},{8,8},{9,9},{1... | collective-permute-start | bytes 196616 | tf_op jit(solution)/shard_map/ppermute | solution.py:284
  18.6 4.3 %collective-permute-start.5 = (bf16[2,32,512]{2,1,0:T(8,128)(2,1)S(1)}, bf16[2,32,512]{2,1,0:T(8,128)(2,1)S(1)}, u32[]{:S(2)}, u32[]{:S(2)}) collective-permute-start(bf16[2,32,512]{2,1,0:T(8,128)(2,1)S(1)} %pad_maximum_fusion.2), channel_id=1, source_target_pairs={{0,1},{1,0},{2,3},{3,2},{4,29},{5,28},{6,31},{7,30},{8,9},{9,8},{1... | collective-permute-start | bytes 196616 | tf_op jit(solution)/shard_map/ppermute | solution.py:284
  25.6 1.6 %collective-permute-start.7 = (bf16[480,256]{1,0:T(8,128)(2,1)S(1)}, bf16[480,256]{1,0:T(8,128)(2,1)S(1)}, u32[]{:S(2)}, u32[]{:S(2)}) collective-permute-start(bf16[480,256]{1,0:T(8,128)(2,1)S(1)} %get-tuple-element.62), channel_id=1, source_target_pairs={{0,8},{8,0},{16,24},{24,16},{1,9},{9,1},{17,25},{25,17},{2,10},{10... | collective-permute-start | bytes 737288 | tf_op jit(solution)/shard_map/ppermute | solution.py:304
  25.7 6.4 %collective-permute-start.9 = (bf16[480,256]{1,0:T(8,128)(2,1)S(1)}, bf16[480,256]{1,0:T(8,128)(2,1)S(1)}, u32[]{:S(2)}, u32[]{:S(2)}) collective-permute-start(bf16[480,256]{1,0:T(8,128)(2,1)S(1)} %get-tuple-element.70), channel_id=1, source_target_pairs={{0,8},{8,0},{16,24},{24,16},{1,9},{9,1},{17,25},{25,17},{2,10},{10... | collective-permute-start | bytes 737288 | tf_op jit(solution)/shard_map/ppermute | solution.py:304
  27.3 10.1 %collective-permute-start.21 = (bf16[480,256]{1,0:T(8,128)(2,1)S(1)}, bf16[480,256]{1,0:T(8,128)(2,1)S(1)}, u32[]{:S(2)}, u32[]{:S(2)}) collective-permute-start(bf16[480,256]{1,0:T(8,128)(2,1)S(1)} %add_convert_fusion.4), channel_id=1, source_target_pairs={{0,16},{8,24},{16,0},{24,8},{1,17},{9,25},{17,1},{25,9},{2,18},{10... | collective-permute-start | bytes 737288 | tf_op jit(solution)/shard_map/ppermute | solution.py:322
  31.6 6.9 %collective-permute-start.11 = (bf16[480,256]{1,0:T(8,128)(2,1)S(1)}, bf16[480,256]{1,0:T(8,128)(2,1)S(1)}, u32[]{:S(2)}, u32[]{:S(2)}) collective-permute-start(bf16[480,256]{1,0:T(8,128)(2,1)S(1)} %get-tuple-element.78), channel_id=1, source_target_pairs={{0,8},{8,0},{16,24},{24,16},{1,9},{9,1},{17,25},{25,17},{2,10},{10... | collective-permute-start | bytes 737288 | tf_op jit(solution)/shard_map/ppermute | solution.py:304
  31.6 1.9 %collective-permute-start.8 = (bf16[480,256]{1,0:T(8,128)(2,1)S(1)}, bf16[480,256]{1,0:T(8,128)(2,1)S(1)}, u32[]{:S(2)}, u32[]{:S(2)}) collective-permute-start(bf16[480,256]{1,0:T(8,128)(2,1)S(1)} %get-tuple-element.68), channel_id=1, source_target_pairs={{0,8},{8,0},{16,24},{24,16},{1,9},{9,1},{17,25},{25,17},{2,10},{10... | collective-permute-start | bytes 737288 | tf_op jit(solution)/shard_map/ppermute | solution.py:304
  33.5 10.1 %collective-permute-start.20 = (bf16[480,256]{1,0:T(8,128)(2,1)S(1)}, bf16[480,256]{1,0:T(8,128)(2,1)S(1)}, u32[]{:S(2)}, u32[]{:S(2)}) collective-permute-start(bf16[480,256]{1,0:T(8,128)(2,1)S(1)} %add_convert_fusion.3), channel_id=1, source_target_pairs={{0,16},{8,24},{16,0},{24,8},{1,17},{9,25},{17,1},{25,9},{2,18},{10... | collective-permute-start | bytes 737288 | tf_op jit(solution)/shard_map/ppermute | solution.py:322
  36.8 7.9 %collective-permute-start.13 = (bf16[480,256]{1,0:T(8,128)(2,1)S(1)}, bf16[480,256]{1,0:T(8,128)(2,1)S(1)}, u32[]{:S(2)}, u32[]{:S(2)}) collective-permute-start(bf16[480,256]{1,0:T(8,128)(2,1)S(1)} %get-tuple-element.86), channel_id=1, source_target_pairs={{0,8},{8,0},{16,24},{24,16},{1,9},{9,1},{17,25},{25,17},{2,10},{10... | collective-permute-start | bytes 737288 | tf_op jit(solution)/shard_map/ppermute | solution.py:304
  36.9 1.9 %collective-permute-start.10 = (bf16[480,256]{1,0:T(8,128)(2,1)S(1)}, bf16[480,256]{1,0:T(8,128)(2,1)S(1)}, u32[]{:S(2)}, u32[]{:S(2)}) collective-permute-start(bf16[480,256]{1,0:T(8,128)(2,1)S(1)} %get-tuple-element.76), channel_id=1, source_target_pairs={{0,8},{8,0},{16,24},{24,16},{1,9},{9,1},{17,25},{25,17},{2,10},{10... | collective-permute-start | bytes 737288 | tf_op jit(solution)/shard_map/ppermute | solution.py:304
  38.8 10.1 %collective-permute-start.19 = (bf16[480,256]{1,0:T(8,128)(2,1)S(1)}, bf16[480,256]{1,0:T(8,128)(2,1)S(1)}, u32[]{:S(2)}, u32[]{:S(2)}) collective-permute-start(bf16[480,256]{1,0:T(8,128)(2,1)S(1)} %add_convert_fusion.2), channel_id=1, source_target_pairs={{0,16},{8,24},{16,0},{24,8},{1,17},{9,25},{17,1},{25,9},{2,18},{10... | collective-permute-start | bytes 737288 | tf_op jit(solution)/shard_map/ppermute | solution.py:322
  43.1 6.8 %collective-permute-start.17 = (bf16[480,256]{1,0:T(8,128)(2,1)S(1)}, bf16[480,256]{1,0:T(8,128)(2,1)S(1)}, u32[]{:S(2)}, u32[]{:S(2)}) collective-permute-start(bf16[480,256]{1,0:T(8,128)(2,1)S(1)} %get-tuple-element.96), channel_id=1, source_target_pairs={{0,8},{8,0},{16,24},{24,16},{1,9},{9,1},{17,25},{25,17},{2,10},{10... | collective-permute-start | bytes 737288 | tf_op jit(solution)/shard_map/ppermute | solution.py:304
  43.2 1.9 %collective-permute-start.12 = (bf16[480,256]{1,0:T(8,128)(2,1)S(1)}, bf16[480,256]{1,0:T(8,128)(2,1)S(1)}, u32[]{:S(2)}, u32[]{:S(2)}) collective-permute-start(bf16[480,256]{1,0:T(8,128)(2,1)S(1)} %get-tuple-element.84), channel_id=1, source_target_pairs={{0,8},{8,0},{16,24},{24,16},{1,9},{9,1},{17,25},{25,17},{2,10},{10... | collective-permute-start | bytes 737288 | tf_op jit(solution)/shard_map/ppermute | solution.py:304
  45.1 8.4 %collective-permute-start.18 = (bf16[480,256]{1,0:T(8,128)(2,1)S(1)}, bf16[480,256]{1,0:T(8,128)(2,1)S(1)}, u32[]{:S(2)}, u32[]{:S(2)}) collective-permute-start(bf16[480,256]{1,0:T(8,128)(2,1)S(1)} %add_convert_fusion.1), channel_id=1, source_target_pairs={{0,16},{8,24},{16,0},{24,8},{1,17},{9,25},{17,1},{25,9},{2,18},{10... | collective-permute-start | bytes 737288 | tf_op jit(solution)/shard_map/ppermute | solution.py:322
  48.4 1.7 %collective-permute-start.15 = (bf16[480,256]{1,0:T(8,128)(2,1)S(1)}, bf16[480,256]{1,0:T(8,128)(2,1)S(1)}, u32[]{:S(2)}, u32[]{:S(2)}) collective-permute-start(bf16[480,256]{1,0:T(8,128)(2,1)S(1)} %get-tuple-element.94), channel_id=1, source_target_pairs={{0,8},{8,0},{16,24},{24,16},{1,9},{9,1},{17,25},{25,17},{2,10},{10... | collective-permute-start | bytes 737288 | tf_op jit(solution)/shard_map/ppermute | solution.py:304
  48.4 6.0 %collective-permute-start.14 = (bf16[480,256]{1,0:T(8,128)(2,1)S(1)}, bf16[480,256]{1,0:T(8,128)(2,1)S(1)}, u32[]{:S(2)}, u32[]{:S(2)}) collective-permute-start(bf16[480,256]{1,0:T(8,128)(2,1)S(1)} %get-tuple-element.92), channel_id=1, source_target_pairs={{0,8},{8,0},{16,24},{24,16},{1,9},{9,1},{17,25},{25,17},{2,10},{10... | collective-permute-start | bytes 737288 | tf_op jit(solution)/shard_map/ppermute | solution.py:304
  50.1 8.4 %collective-permute-start.16 = (bf16[480,256]{1,0:T(8,128)(2,1)S(1)}, bf16[480,256]{1,0:T(8,128)(2,1)S(1)}, u32[]{:S(2)}, u32[]{:S(2)}) collective-permute-start(bf16[480,256]{1,0:T(8,128)(2,1)S(1)} %add_convert_fusion), channel_id=1, source_target_pairs={{0,16},{8,24},{16,0},{24,8},{1,17},{9,25},{17,1},{25,9},{2,18},{10... | collective-permute-start | bytes 737288 | tf_op jit(solution)/shard_map/ppermute | solution.py:322

commit v5 on v4

--- a/solution.py
+++ b/solution.py
@@ -10,7 +10,7 @@
 LANES = 128
 STEP = 32
 TILE = 8
-VMEM = 48 * 1024 * 1024
+VMEM = 20 * 1024 * 1024
 
 
 def partner(block, axis, stride):
@@ -92,7 +92,7 @@
                 out[u, :, k * LANES : (k + 1) * LANES] = tile.astype(jnp.bfloat16)
 
 
-def place_kernel(turns, lat_count, row_count, pairs, degrees, table_ref, out, limits):
+def place_kernel(turns, lat_count, row_count, pairs, degrees, table_ref, leg_ref, out, limits):
     northern = lax.axis_index("lat") < lat_count // 2
     me = lax.axis_index("wave")
     row = lax.broadcasted_iota(jnp.int32, (LANES, 2 * LANES), 0) & (row_count - 1)
@@ -155,13 +155,12 @@
 
 
 def product_kernel(block, row_count, cols, place_ref, leg_ref, *refs):
-    sources = refs[:-8]
-    far_sent, far_own, near_sent, near_own, table, far, near, sem = refs[-8:]
+    sources = refs[:-6]
+    far_sent, far_own, near_sent, near_own, far, near = refs[-6:]
     half = far.shape[1]
+    table = leg_ref.at[block * STEP : (block + 1) * STEP]
     lat = lax.axis_index("lat")
     y, core = lat // 2, lat % 2
-    copy = pltpu.make_async_copy(leg_ref.at[pl.ds(block * STEP, STEP)], table, sem)
-    copy.start()
     tile, off = shift_of(block, row_count * cols)
     lane = lax.broadcasted_iota(jnp.int32, (STEP, LANES), 1)
     held = ((lane - off) & (LANES - 1)) // row_count
@@ -183,7 +182,6 @@
     north, south = both[:, :LANES], both[:, LANES:]
     even, odd = north + south, north - south
     far_coefs, near_coefs = jnp.where(y == 0, odd, even), jnp.where(y == 0, even, odd)
-    copy.wait()
     multiply(far_coefs, table, pl.multiple_of((1 - y) * half, LANES), half, far)
     multiply(near_coefs, table, pl.multiple_of(y * half, LANES), half, near)
     pack(far, core, far_sent, far_own)
@@ -261,11 +259,11 @@
             jax.ShapeDtypeStruct((wave_count * LANES, 2 * LANES), jnp.bfloat16),
             jax.ShapeDtypeStruct((slots, LANES), jnp.int32),
         ],
-        in_specs=[pl.BlockSpec(memory_space=pltpu.SMEM)],
+        in_specs=[pl.BlockSpec(memory_space=pltpu.SMEM), anywhere],
         out_specs=[whole] * 2,
         compiler_params=params,
         name="place",
-    )(wave_table)
+    )(wave_table, legendre)
 
     passed = [ordered[0]] + [
         lax.ppermute(ordered[t], "wave", [(w, w ^ t * low) for w in range(wave_count)])
@@ -281,6 +279,7 @@
                     began = (wave >= wave_count // 2) != (side == 1)
                     to = lat_count - 1 - lat if began else lat
                     route.append((lat * wave_count + wave, to * wave_count + (wave ^ u)))
+            block, place = lax.optimization_barrier((block, place))
             sources.append(lax.ppermute(block, ("lat", "wave"), route))
 
     rows = STEP * cols
@@ -288,10 +287,8 @@
     core_route = [(lat, lat ^ 1) for lat in range(lat_count)]
     y_route = [(lat, lat ^ 2) for lat in range(lat_count)]
     scratch = [
-        pltpu.VMEM((STEP, pairs, degrees), jnp.bfloat16),
         pltpu.VMEM((rows, degrees // 2), jnp.float32),
         pltpu.VMEM((rows, degrees // 2), jnp.float32),
-        pltpu.SemaphoreType.DMA,
     ]
     cost = pl.CostEstimate(flops=0, bytes_accessed=1024, transcendentals=0)
     pair_of_sums = [
@@ -310,7 +307,7 @@
         far_sent, far_own, near_sent, near_own = pl.pallas_call(
             functools.partial(product_kernel, block, row_count, cols),
             out_shape=pair_of_sums * 2,
-            in_specs=[whole, anywhere] + [whole] * len(sources),
+            in_specs=[whole] * (2 + len(sources)),
             out_specs=[whole] * 4,
             scratch_shapes=scratch,
             compiler_params=params,

time: 59.8 us -> 56 us (0.936)
  Pallas kernels: 20.3 us -> 13.9 us
  local copies, waits for them, and re-layouts: 1.66 us -> 6.39 us
  waiting for transfers between devices: 16.3 us -> 12.9 us
  starting transfers between devices: 20.4 us -> 21.8 us
    pallas_call x5, Pallas kernels: 13.5 us -> 7.09 us  [packed(): pl.pallas_call(functools.partial(product_kernel, block, row_count, cols),...]
    unnamed x4 -> x8, local copies, waits for them, and re-layouts: 1.64 us -> 6.36 us
    ppermute x3, waiting for transfers between devices: 4.95 us -> 0.35 us  [packed(): lax.ppermute(ordered[t], 'wave', [(w, w ^ t * low) for w in range(wave_co...]
    ppermute x5, waiting for transfers between devices: 5.7 us -> 8.41 us  [packed(): crossed.append(lax.ppermute(summed, 'lat', y_route))]
    ppermute x5, starting transfers between devices: 5.94 us -> 6.99 us  [packed(): crossed.append(lax.ppermute(summed, 'lat', y_route))]
    ppermute x4, waiting for transfers between devices: 2.81 us -> 1.76 us  [packed(): sources.append(lax.ppermute(block, ('lat', 'wave'), route))]
    ppermute x10, starting transfers between devices: 2.84 us -> 3.53 us  [settle(): return kept + lax.ppermute(sent, 'lat', core_route).astype(jnp.float32)]
  transfers between devices with their start and end apart: 22 -> 22, of which waited for: 10 -> 10; matrix products, arithmetic and copies ran while one was open for 1% -> 1% of each run, Pallas kernels for 26% -> 19%
where the time goes in v5:
time: 56 us; the launch traced here: 55.8 us
  starting transfers between devices  21.8 us (39%)
  Pallas kernels  13.9 us (25%)
  waiting for transfers between devices  12.9 us (23%)
  local copies, waits for them, and re-layouts  6.39 us (11%)
  other arithmetic  0.62 us (1%)
    ppermute x5, waiting for transfers between devices, packed(): crossed.append(lax.ppermute(summed, 'lat', y_route))  8.41 us
    pallas_call x5, Pallas kernels, packed(): pl.pallas_call(functools.partial(product_kernel, block, row_count, cols),...  7.09 us
    ppermute x5, starting transfers between devices, packed(): crossed.append(lax.ppermute(summed, 'lat', y_route))  6.99 us
    unnamed x8, local copies, waits for them, and re-layouts  6.36 us
    ppermute x3, starting transfers between devices, packed(): lax.ppermute(ordered[t], 'wave', [(w, w ^ t * low) for w in range(wave_co...  5.68 us
    ppermute x4, starting transfers between devices, packed(): sources.append(lax.ppermute(block, ('lat', 'wave'), route))  5.55 us
    pallas_call x5, Pallas kernels, packed(): pl.pallas_call(functools.partial(final_kernel, block * STEP, degrees, col...  5.06 us
    ppermute x10, starting transfers between devices, settle(): return kept + lax.ppermute(sent, 'lat', core_route).astype(jnp.float32)  3.53 us
  transfers between devices with their start and end apart: 22, of which 10 were waited for; matrix products, arithmetic and copies ran while one was open for 1% of the time, Pallas kernels for 19%

profile of v5, /device:TPU:0, one launch (start us, length us, event | category | flops | bytes accessed | tf_op | source)
XLA Modules:
  0.0 55.8 jit_solution(1640235710168929061)
XLA Ops:
  0.0 0.9 %copy-done.2 = bf16[8,12,1280]{2,0,1:T(8,128)(2,1)S(1)} copy-done((bf16[8,12,1280]{2,0,1:T(8,128)(2,1)S(1)}, bf16[8,12,1280]{2,0,1:T(8,128)(2,1)}, u32[]{:S(2)}) %copy-start.2) | copy-done | bytes 245784
  0.9 0.7 %copy-done.3 = s32[1280]{0:T(1024)S(1)} copy-done((s32[1280]{0:T(1024)S(1)}, s32[1280]{0:T(1024)}, u32[]{:S(2)}) %copy-start.3) | copy-done | bytes 5144
  1.6 0.8 %gather.1 = (bf16[2,32,512]{2,1,0:T(8,128)(2,1)S(1)}, bf16[2,32,512]{2,1,0:T(8,128)(2,1)S(1)}, bf16[2,32,512]{2,1,0:T(8,128)(2,1)S(1)}, bf16[2,32,512]{2,1,0:T(8,128)(2,1)S(1)}) custom-call(s32[10,128]{1,0:T(8,128)S(1)} %bitcast.6, bf16[96,1280]{1,0:T(8,128)(2,1)S(1)} %bitcast.5), custom_call_target="tpu_custom_call" | custom-call | tf_op jit(solution)/shard_map/gather/pallas_call | solution.py:238
  2.5 3.1 %collective-permute-start.2 = (bf16[2,32,512]{2,1,0:T(8,128)(2,1)S(1)}, bf16[2,32,512]{2,1,0:T(8,128)(2,1)S(1)}, u32[]{:S(2)}, u32[]{:S(2)}) collective-permute-start(bf16[2,32,512]{2,1,0:T(8,128)(2,1)S(1)} %get-tuple-element.63), channel_id=1, source_target_pairs={{0,2},{1,3},{2,0},{3,1},{4,6},{5,7},{6,4},{7,5},{8,10},{9,11},{10,... | collective-permute-start | bytes 196616 | tf_op jit(solution)/shard_map/ppermute | solution.py:269
  5.6 2.6 %collective-permute-start = (bf16[2,32,512]{2,1,0:T(8,128)(2,1)S(1)}, bf16[2,32,512]{2,1,0:T(8,128)(2,1)S(1)}, u32[]{:S(2)}, u32[]{:S(2)}) collective-permute-start(bf16[2,32,512]{2,1,0:T(8,128)(2,1)S(1)} %get-tuple-element.60), channel_id=1, source_target_pairs={{0,4},{1,5},{2,6},{3,7},{4,0},{5,1},{6,2},{7,3},{8,12},{9,13},{10,... | collective-permute-start | bytes 196616 | tf_op jit(solution)/shard_map/ppermute | solution.py:269
  8.1 0.0 collective-permute-start.1
  8.2 0.0 copy-start
  8.2 4.7 %copy-done = bf16[160,32,1280]{2,1,0:T(8,128)(2,1)S(1)} copy-done((bf16[160,32,1280]{2,1,0:T(8,128)(2,1)S(1)}, bf16[160,32,1280]{2,1,0:T(8,128)(2,1)}, u32[]{:S(2)}) %copy-start) | copy-done | bytes 13107224
  12.9 0.9 %place.1 = (bf16[1024,256]{1,0:T(8,128)(2,1)S(1)}, s32[160,128]{1,0:T(8,128)S(1)}) custom-call(s32[1280]{0:T(1024)S(1)} %copy-done.3, bf16[160,32,1280]{2,1,0:T(8,128)(2,1)S(1)} %copy-done), custom_call_target="tpu_custom_call" | custom-call | tf_op jit(solution)/shard_map/place/pallas_call | solution.py:256
  13.8 0.0 collective-permute-done.2
  13.8 0.0 collective-permute-done
  13.9 0.3 collective-permute-done.1
  14.2 1.1 %collective-permute-start.6 = (bf16[2,32,512]{2,1,0:T(8,128)(2,1)S(1)}, bf16[2,32,512]{2,1,0:T(8,128)(2,1)S(1)}, u32[]{:S(2)}, u32[]{:S(2)}) collective-permute-start(bf16[2,32,512]{2,1,0:T(8,128)(2,1)S(1)} %get-tuple-element.72), channel_id=1, source_target_pairs={{0,25},{1,24},{2,27},{3,26},{4,5},{5,4},{6,7},{7,6},{8,17},{9,16},... | collective-permute-start | bytes 196616 | tf_op jit(solution)/shard_map/ppermute | solution.py:283
  15.3 0.6 %collective-permute-start.5 = (bf16[2,32,512]{2,1,0:T(8,128)(2,1)S(1)}, bf16[2,32,512]{2,1,0:T(8,128)(2,1)S(1)}, u32[]{:S(2)}, u32[]{:S(2)}) collective-permute-start(bf16[2,32,512]{2,1,0:T(8,128)(2,1)S(1)} %get-tuple-element.71), channel_id=1, source_target_pairs={{0,1},{1,0},{2,3},{3,2},{4,29},{5,28},{6,31},{7,30},{8,9},{9,8},{1... | collective-permute-start | bytes 196616 | tf_op jit(solution)/shard_map/ppermute | solution.py:283
  15.9 3.3 %collective-permute-start.4 = (bf16[2,32,512]{2,1,0:T(8,128)(2,1)S(1)}, bf16[2,32,512]{2,1,0:T(8,128)(2,1)S(1)}, u32[]{:S(2)}, u32[]{:S(2)}) collective-permute-start(bf16[2,32,512]{2,1,0:T(8,128)(2,1)S(1)} %get-tuple-element.70), channel_id=1, source_target_pairs={{0,24},{1,25},{2,26},{3,27},{4,4},{5,5},{6,6},{7,7},{8,16},{9,17},... | collective-permute-start | bytes 196616 | tf_op jit(solution)/shard_map/ppermute | solution.py:283
  19.1 0.7 %collective-permute-start.3 = (bf16[2,32,512]{2,1,0:T(8,128)(2,1)S(1)}, bf16[2,32,512]{2,1,0:T(8,128)(2,1)S(1)}, u32[]{:S(2)}, u32[]{:S(2)}) collective-permute-start(bf16[2,32,512]{2,1,0:T(8,128)(2,1)S(1)} %get-tuple-element.69), channel_id=1, source_target_pairs={{0,0},{1,1},{2,2},{3,3},{4,28},{5,29},{6,30},{7,31},{8,8},{9,9},{1... | collective-permute-start | bytes 196616 | tf_op jit(solution)/shard_map/ppermute | solution.py:283
  19.8 0.0 collective-permute-done.6.refs_3_
  19.8 0.1 collective-permute-done.5.refs_2_
  19.9 1.7 %collective-permute-done.4.refs_1_ = bf16[2,32,512]{2,1,0:T(8,128)(2,1)S(1)} collective-permute-done((bf16[2,32,512]{2,1,0:T(8,128)(2,1)S(1)}, bf16[2,32,512]{2,1,0:T(8,128)(2,1)S(1)}, u32[]{:S(2)}, u32[]{:S(2)}) %collective-permute-start.4) | collective-permute-done | bytes 65568 | tf_op jit(solution)/shard_map/ppermute | solution.py:283
  21.6 0.0 collective-permute-done.3.refs_0_
  21.6 1.4 %product.5 = (bf16[480,256]{1,0:T(8,128)(2,1)S(1)}, f32[480,256]{1,0:T(8,128)S(1)}, bf16[480,256]{1,0:T(8,128)(2,1)S(1)}, f32[480,256]{1,0:T(8,128)S(1)}) custom-call(bf16[1024,256]{1,0:T(8,128)(2,1)S(1)} %get-tuple-element.68.place_ref, bf16[160,32,1280]{2,1,0:T(8,128)(2,1)S(1)} %copy-done.1, bf16[2,32,512]{2,1,0:T(8,128)(2,1)S(1)} %collective-permute-done.3.refs_0_, ...), custom_call_target="tpu_custom_call" | custom-call | bytes 1024 | tf_op jit(solution)/shard_map/product/pallas_call | solution.py:307
  23.0 1.2 %collective-permute-start.7 = (bf16[480,256]{1,0:T(8,128)(2,1)S(1)}, bf16[480,256]{1,0:T(8,128)(2,1)S(1)}, u32[]{:S(2)}, u32[]{:S(2)}) collective-permute-start(bf16[480,256]{1,0:T(8,128)(2,1)S(1)} %get-tuple-element.78), channel_id=1, source_target_pairs={{0,8},{8,0},{16,24},{24,16},{1,9},{9,1},{17,25},{25,17},{2,10},{10... | collective-permute-start | bytes 737288 | tf_op jit(solution)/shard_map/ppermute | solution.py:301
  24.2 0.1 collective-permute-start.9
  24.3 1.1 %collective-permute-done.7 = bf16[480,256]{1,0:T(8,128)(2,1)S(1)} collective-permute-done((bf16[480,256]{1,0:T(8,128)(2,1)S(1)}, bf16[480,256]{1,0:T(8,128)(2,1)S(1)}, u32[]{:S(2)}, u32[]{:S(2)}) %collective-permute-start.7) | collective-permute-done | bytes 245792 | tf_op jit(solution)/shard_map/ppermute | solution.py:301
  25.3 0.1 add_convert_fusion.4
  25.4 1.5 %collective-permute-start.21 = (bf16[480,256]{1,0:T(8,128)(2,1)S(1)}, bf16[480,256]{1,0:T(8,128)(2,1)S(1)}, u32[]{:S(2)}, u32[]{:S(2)}) collective-permute-start(bf16[480,256]{1,0:T(8,128)(2,1)S(1)} %add_convert_fusion.4), channel_id=1, source_target_pairs={{0,16},{8,24},{16,0},{24,8},{1,17},{9,25},{17,1},{25,9},{2,18},{10... | collective-permute-start | bytes 737288 | tf_op jit(solution)/shard_map/ppermute | solution.py:319
  26.9 1.4 %product.6 = (bf16[480,256]{1,0:T(8,128)(2,1)S(1)}, f32[480,256]{1,0:T(8,128)S(1)}, bf16[480,256]{1,0:T(8,128)(2,1)S(1)}, f32[480,256]{1,0:T(8,128)S(1)}) custom-call(bf16[1024,256]{1,0:T(8,128)(2,1)S(1)} %get-tuple-element.68.place_ref, bf16[160,32,1280]{2,1,0:T(8,128)(2,1)S(1)} %copy-done.1, bf16[2,32,512]{2,1,0:T(8,128)(2,1)S(1)} %collective-permute-done.3.refs_0_, ...), custom_call_target="tpu_custom_call" | custom-call | bytes 1024 | tf_op jit(solution)/shard_map/product/pallas_call | solution.py:307
  28.4 0.1 collective-permute-start.11
  28.4 0.5 collective-permute-start.8
  28.9 0.0 collective-permute-done.9
  29.0 1.3 %collective-permute-done.8 = bf16[480,256]{1,0:T(8,128)(2,1)S(1)} collective-permute-done((bf16[480,256]{1,0:T(8,128)(2,1)S(1)}, bf16[480,256]{1,0:T(8,128)(2,1)S(1)}, u32[]{:S(2)}, u32[]{:S(2)}) %collective-permute-start.8) | collective-permute-done | bytes 245792 | tf_op jit(solution)/shard_map/ppermute | solution.py:301
  30.3 0.1 add_convert_fusion.3
  30.3 0.7 %collective-permute-start.20 = (bf16[480,256]{1,0:T(8,128)(2,1)S(1)}, bf16[480,256]{1,0:T(8,128)(2,1)S(1)}, u32[]{:S(2)}, u32[]{:S(2)}) collective-permute-start(bf16[480,256]{1,0:T(8,128)(2,1)S(1)} %add_convert_fusion.3), channel_id=1, source_target_pairs={{0,16},{8,24},{16,0},{24,8},{1,17},{9,25},{17,1},{25,9},{2,18},{10... | collective-permute-start | bytes 737288 | tf_op jit(solution)/shard_map/ppermute | solution.py:319
  31.0 1.4 %product.7 = (bf16[480,256]{1,0:T(8,128)(2,1)S(1)}, f32[480,256]{1,0:T(8,128)S(1)}, bf16[480,256]{1,0:T(8,128)(2,1)S(1)}, f32[480,256]{1,0:T(8,128)S(1)}) custom-call(bf16[1024,256]{1,0:T(8,128)(2,1)S(1)} %get-tuple-element.68.place_ref, bf16[160,32,1280]{2,1,0:T(8,128)(2,1)S(1)} %copy-done.1, bf16[2,32,512]{2,1,0:T(8,128)(2,1)S(1)} %collective-permute-done.3.refs_0_, ...), custom_call_target="tpu_custom_call" | custom-call | bytes 1024 | tf_op jit(solution)/shard_map/product/pallas_call | solution.py:307
  32.4 0.1 collective-permute-start.13
  32.5 0.5 collective-permute-start.10
  33.0 1.2 %collective-permute-done.21.far_ref = bf16[480,256]{1,0:T(8,128)(2,1)S(1)} collective-permute-done((bf16[480,256]{1,0:T(8,128)(2,1)S(1)}, bf16[480,256]{1,0:T(8,128)(2,1)S(1)}, u32[]{:S(2)}, u32[]{:S(2)}) %collective-permute-start.21) | collective-permute-done | bytes 245792 | tf_op jit(solution)/shard_map/ppermute | solution.py:319
  34.2 1.0 %final.5.refs_0_ = f32[12,160,320]{2,1,0:T(8,128)} custom-call(s32[160,128]{1,0:T(8,128)S(1)} %get-tuple-element.59.limits_ref, f32[480,256]{1,0:T(8,128)S(1)} %convert_add_fusion.4.near_ref, bf16[480,256]{1,0:T(8,128)(2,1)S(1)} %collective-permute-done.21.far_ref), custom_call_target="tpu_custom_call" | custom-call | bytes 1024 | tf_op jit(solution)/shard_map/final/pallas_call | solution.py:325
  35.2 0.0 collective-permute-done.11
  35.2 0.1 convert_add_fusion.3.near_ref
  35.3 0.0 collective-permute-done.10
  35.3 0.1 add_convert_fusion.2
  35.4 1.6 %collective-permute-start.19 = (bf16[480,256]{1,0:T(8,128)(2,1)S(1)}, bf16[480,256]{1,0:T(8,128)(2,1)S(1)}, u32[]{:S(2)}, u32[]{:S(2)}) collective-permute-start(bf16[480,256]{1,0:T(8,128)(2,1)S(1)} %add_convert_fusion.2), channel_id=1, source_target_pairs={{0,16},{8,24},{16,0},{24,8},{1,17},{9,25},{17,1},{25,9},{2,18},{10... | collective-permute-start | bytes 737288 | tf_op jit(solution)/shard_map/ppermute | solution.py:319
  37.0 1.4 %product.8 = (bf16[480,256]{1,0:T(8,128)(2,1)S(1)}, f32[480,256]{1,0:T(8,128)S(1)}, bf16[480,256]{1,0:T(8,128)(2,1)S(1)}, f32[480,256]{1,0:T(8,128)S(1)}) custom-call(bf16[1024,256]{1,0:T(8,128)(2,1)S(1)} %get-tuple-element.68.place_ref, bf16[160,32,1280]{2,1,0:T(8,128)(2,1)S(1)} %copy-done.1, bf16[2,32,512]{2,1,0:T(8,128)(2,1)S(1)} %collective-permute-done.3.refs_0_, ...), custom_call_target="tpu_custom_call" | custom-call | bytes 1024 | tf_op jit(solution)/shard_map/product/pallas_call | solution.py:307
  38.4 0.1 collective-permute-start.17
  38.5 0.5 collective-permute-start.12
  39.0 0.5 collective-permute-done.20.far_ref
  39.5 1.0 %final.6.refs_0_ = f32[12,160,320]{2,1,0:T(8,128)} custom-call(s32[160,128]{1,0:T(8,128)S(1)} %get-tuple-element.59.limits_ref, f32[480,256]{1,0:T(8,128)S(1)} %convert_add_fusion.3.near_ref, bf16[480,256]{1,0:T(8,128)(2,1)S(1)} %collective-permute-done.20.far_ref, f32[12,160,320]{2,1,0:T(8,128)} %final.5.refs_0_), custom_call_target="tpu_custom_call", output_to_operand_aliasing={{}: (3, {})} | custom-call | bytes 1024 | tf_op jit(solution)/shard_map/final/pallas_call | solution.py:325
  40.5 0.0 collective-permute-done.13
  40.5 0.0 collective-permute-done.12
  40.5 0.1 add_convert_fusion.1
  40.6 1.6 %collective-permute-start.18 = (bf16[480,256]{1,0:T(8,128)(2,1)S(1)}, bf16[480,256]{1,0:T(8,128)(2,1)S(1)}, u32[]{:S(2)}, u32[]{:S(2)}) collective-permute-start(bf16[480,256]{1,0:T(8,128)(2,1)S(1)} %add_convert_fusion.1), channel_id=1, source_target_pairs={{0,16},{8,24},{16,0},{24,8},{1,17},{9,25},{17,1},{25,9},{2,18},{10... | collective-permute-start | bytes 737288 | tf_op jit(solution)/shard_map/ppermute | solution.py:319
  42.2 1.4 %product.9 = (bf16[480,256]{1,0:T(8,128)(2,1)S(1)}, f32[480,256]{1,0:T(8,128)S(1)}, bf16[480,256]{1,0:T(8,128)(2,1)S(1)}, f32[480,256]{1,0:T(8,128)S(1)}) custom-call(bf16[1024,256]{1,0:T(8,128)(2,1)S(1)} %get-tuple-element.68.place_ref, bf16[160,32,1280]{2,1,0:T(8,128)(2,1)S(1)} %copy-done.1, bf16[2,32,512]{2,1,0:T(8,128)(2,1)S(1)} %collective-permute-done.3.refs_0_, ...), custom_call_target="tpu_custom_call" | custom-call | bytes 1024 | tf_op jit(solution)/shard_map/product/pallas_call | solution.py:307
  43.6 0.1 collective-permute-start.15
  43.7 0.5 collective-permute-start.14
  44.2 0.5 collective-permute-done.19.far_ref
  44.7 1.0 %final.7.refs_0_ = f32[12,160,320]{2,1,0:T(8,128)} custom-call(s32[160,128]{1,0:T(8,128)S(1)} %get-tuple-element.59.limits_ref, f32[480,256]{1,0:T(8,128)S(1)} %convert_add_fusion.2.near_ref, bf16[480,256]{1,0:T(8,128)(2,1)S(1)} %collective-permute-done.19.far_ref, f32[12,160,320]{2,1,0:T(8,128)} %final.6.refs_0_), custom_call_target="tpu_custom_call", output_to_operand_aliasing={{}: (3, {})} | custom-call | bytes 1024 | tf_op jit(solution)/shard_map/final/pallas_call | solution.py:325
  45.7 0.1 convert_add_fusion.near_ref
  45.8 0.1 add_convert_fusion
  45.9 1.6 %collective-permute-start.16 = (bf16[480,256]{1,0:T(8,128)(2,1)S(1)}, bf16[480,256]{1,0:T(8,128)(2,1)S(1)}, u32[]{:S(2)}, u32[]{:S(2)}) collective-permute-start(bf16[480,256]{1,0:T(8,128)(2,1)S(1)} %add_convert_fusion), channel_id=1, source_target_pairs={{0,16},{8,24},{16,0},{24,8},{1,17},{9,25},{17,1},{25,9},{2,18},{10... | collective-permute-start | bytes 737288 | tf_op jit(solution)/shard_map/ppermute | solution.py:319
  47.5 2.5 %collective-permute-done.18.far_ref = bf16[480,256]{1,0:T(8,128)(2,1)S(1)} collective-permute-done((bf16[480,256]{1,0:T(8,128)(2,1)S(1)}, bf16[480,256]{1,0:T(8,128)(2,1)S(1)}, u32[]{:S(2)}, u32[]{:S(2)}) %collective-permute-start.18) | collective-permute-done | bytes 245792 | tf_op jit(solution)/shard_map/ppermute | solution.py:319
  50.0 1.0 %final.8.refs_0_ = f32[12,160,320]{2,1,0:T(8,128)} custom-call(s32[160,128]{1,0:T(8,128)S(1)} %get-tuple-element.59.limits_ref, f32[480,256]{1,0:T(8,128)S(1)} %convert_add_fusion.near_ref, bf16[480,256]{1,0:T(8,128)(2,1)S(1)} %collective-permute-done.18.far_ref, f32[12,160,320]{2,1,0:T(8,128)} %final.7.refs_0_), custom_call_target="tpu_custom_call", output_to_operand_aliasing={{}: (3, {})} | custom-call | bytes 1024 | tf_op jit(solution)/shard_map/final/pallas_call | solution.py:325
  51.1 3.7 %collective-permute-done.16.far_ref = bf16[480,256]{1,0:T(8,128)(2,1)S(1)} collective-permute-done((bf16[480,256]{1,0:T(8,128)(2,1)S(1)}, bf16[480,256]{1,0:T(8,128)(2,1)S(1)}, u32[]{:S(2)}, u32[]{:S(2)}) %collective-permute-start.16) | collective-permute-done | bytes 245792 | tf_op jit(solution)/shard_map/ppermute | solution.py:319
  54.8 1.0 %final.9 = f32[12,160,320]{2,1,0:T(8,128)} custom-call(s32[160,128]{1,0:T(8,128)S(1)} %get-tuple-element.59.limits_ref, f32[480,256]{1,0:T(8,128)S(1)} %convert_add_fusion.1.near_ref, bf16[480,256]{1,0:T(8,128)(2,1)S(1)} %collective-permute-done.16.far_ref, f32[12,160,320]{2,1,0:T(8,128)} %final.8.refs_0_), custom_call_target="tpu_custom_call", output_to_operand_aliasing={{}: (3, {})} | custom-call | bytes 1024 | tf_op jit(solution)/shard_map/final/pallas_call | solution.py:325
  (16 shorter events, 0.2 us)
Async XLA Ops:
  0.0 0.9 %copy-start.2 = (bf16[8,12,1280]{2,0,1:T(8,128)(2,1)S(1)}, bf16[8,12,1280]{2,0,1:T(8,128)(2,1)}, u32[]{:S(2)}) copy-start(bf16[8,12,1280]{2,0,1:T(8,128)(2,1)} %param.3) | copy-start | bytes 737284
  0.9 0.7 %copy-start.3 = (s32[1280]{0:T(1024)S(1)}, s32[1280]{0:T(1024)}, u32[]{:S(2)}) copy-start(s32[1280]{0:T(1024)} %table_ref.1) | copy-start | bytes 15364
  2.5 11.3 %collective-permute-start.2 = (bf16[2,32,512]{2,1,0:T(8,128)(2,1)S(1)}, bf16[2,32,512]{2,1,0:T(8,128)(2,1)S(1)}, u32[]{:S(2)}, u32[]{:S(2)}) collective-permute-start(bf16[2,32,512]{2,1,0:T(8,128)(2,1)S(1)} %get-tuple-element.63), channel_id=1, source_target_pairs={{0,2},{1,3},{2,0},{3,1},{4,6},{5,7},{6,4},{7,5},{8,10},{9,11},{10,... | collective-permute-start | bytes 196616 | tf_op jit(solution)/shard_map/ppermute | solution.py:269
  5.6 8.3 %collective-permute-start = (bf16[2,32,512]{2,1,0:T(8,128)(2,1)S(1)}, bf16[2,32,512]{2,1,0:T(8,128)(2,1)S(1)}, u32[]{:S(2)}, u32[]{:S(2)}) collective-permute-start(bf16[2,32,512]{2,1,0:T(8,128)(2,1)S(1)} %get-tuple-element.60), channel_id=1, source_target_pairs={{0,4},{1,5},{2,6},{3,7},{4,0},{5,1},{6,2},{7,3},{8,12},{9,13},{10,... | collective-permute-start | bytes 196616 | tf_op jit(solution)/shard_map/ppermute | solution.py:269
  8.1 6.1 %collective-permute-start.1 = (bf16[2,32,512]{2,1,0:T(8,128)(2,1)S(1)}, bf16[2,32,512]{2,1,0:T(8,128)(2,1)S(1)}, u32[]{:S(2)}, u32[]{:S(2)}) collective-permute-start(bf16[2,32,512]{2,1,0:T(8,128)(2,1)S(1)} %get-tuple-element.61), channel_id=1, source_target_pairs={{0,6},{1,7},{2,4},{3,5},{4,2},{5,3},{6,0},{7,1},{8,14},{9,15},{10,... | collective-permute-start | bytes 196616 | tf_op jit(solution)/shard_map/ppermute | solution.py:269
  8.2 4.7 %copy-start = (bf16[160,32,1280]{2,1,0:T(8,128)(2,1)S(1)}, bf16[160,32,1280]{2,1,0:T(8,128)(2,1)}, u32[]{:S(2)}) copy-start(bf16[160,32,1280]{2,1,0:T(8,128)(2,1)} %leg_ref.11) | copy-start | bytes 39321604
  12.9 8.7 %copy-start.1 = (bf16[160,32,1280]{2,1,0:T(8,128)(2,1)S(1)}, bf16[160,32,1280]{2,1,0:T(8,128)(2,1)}, u32[]{:S(2)}) copy-start(bf16[160,32,1280]{2,1,0:T(8,128)(2,1)} %leg_ref.11) | copy-start | bytes 39321604
  14.2 5.6 %collective-permute-start.6 = (bf16[2,32,512]{2,1,0:T(8,128)(2,1)S(1)}, bf16[2,32,512]{2,1,0:T(8,128)(2,1)S(1)}, u32[]{:S(2)}, u32[]{:S(2)}) collective-permute-start(bf16[2,32,512]{2,1,0:T(8,128)(2,1)S(1)} %get-tuple-element.72), channel_id=1, source_target_pairs={{0,25},{1,24},{2,27},{3,26},{4,5},{5,4},{6,7},{7,6},{8,17},{9,16},... | collective-permute-start | bytes 196616 | tf_op jit(solution)/shard_map/ppermute | solution.py:283
  15.3 4.6 %collective-permute-start.5 = (bf16[2,32,512]{2,1,0:T(8,128)(2,1)S(1)}, bf16[2,32,512]{2,1,0:T(8,128)(2,1)S(1)}, u32[]{:S(2)}, u32[]{:S(2)}) collective-permute-start(bf16[2,32,512]{2,1,0:T(8,128)(2,1)S(1)} %get-tuple-element.71), channel_id=1, source_target_pairs={{0,1},{1,0},{2,3},{3,2},{4,29},{5,28},{6,31},{7,30},{8,9},{9,8},{1... | collective-permute-start | bytes 196616 | tf_op jit(solution)/shard_map/ppermute | solution.py:283
  15.9 5.7 %collective-permute-start.4 = (bf16[2,32,512]{2,1,0:T(8,128)(2,1)S(1)}, bf16[2,32,512]{2,1,0:T(8,128)(2,1)S(1)}, u32[]{:S(2)}, u32[]{:S(2)}) collective-permute-start(bf16[2,32,512]{2,1,0:T(8,128)(2,1)S(1)} %get-tuple-element.70), channel_id=1, source_target_pairs={{0,24},{1,25},{2,26},{3,27},{4,4},{5,5},{6,6},{7,7},{8,16},{9,17},... | collective-permute-start | bytes 196616 | tf_op jit(solution)/shard_map/ppermute | solution.py:283
  19.1 2.4 %collective-permute-start.3 = (bf16[2,32,512]{2,1,0:T(8,128)(2,1)S(1)}, bf16[2,32,512]{2,1,0:T(8,128)(2,1)S(1)}, u32[]{:S(2)}, u32[]{:S(2)}) collective-permute-start(bf16[2,32,512]{2,1,0:T(8,128)(2,1)S(1)} %get-tuple-element.69), channel_id=1, source_target_pairs={{0,0},{1,1},{2,2},{3,3},{4,28},{5,29},{6,30},{7,31},{8,8},{9,9},{1... | collective-permute-start | bytes 196616 | tf_op jit(solution)/shard_map/ppermute | solution.py:283
  23.0 2.3 %collective-permute-start.7 = (bf16[480,256]{1,0:T(8,128)(2,1)S(1)}, bf16[480,256]{1,0:T(8,128)(2,1)S(1)}, u32[]{:S(2)}, u32[]{:S(2)}) collective-permute-start(bf16[480,256]{1,0:T(8,128)(2,1)S(1)} %get-tuple-element.78), channel_id=1, source_target_pairs={{0,8},{8,0},{16,24},{24,16},{1,9},{9,1},{17,25},{25,17},{2,10},{10... | collective-permute-start | bytes 737288 | tf_op jit(solution)/shard_map/ppermute | solution.py:301
  24.2 4.7 %collective-permute-start.9 = (bf16[480,256]{1,0:T(8,128)(2,1)S(1)}, bf16[480,256]{1,0:T(8,128)(2,1)S(1)}, u32[]{:S(2)}, u32[]{:S(2)}) collective-permute-start(bf16[480,256]{1,0:T(8,128)(2,1)S(1)} %get-tuple-element.86), channel_id=1, source_target_pairs={{0,8},{8,0},{16,24},{24,16},{1,9},{9,1},{17,25},{25,17},{2,10},{10... | collective-permute-start | bytes 737288 | tf_op jit(solution)/shard_map/ppermute | solution.py:301
  25.4 8.8 %collective-permute-start.21 = (bf16[480,256]{1,0:T(8,128)(2,1)S(1)}, bf16[480,256]{1,0:T(8,128)(2,1)S(1)}, u32[]{:S(2)}, u32[]{:S(2)}) collective-permute-start(bf16[480,256]{1,0:T(8,128)(2,1)S(1)} %add_convert_fusion.4), channel_id=1, source_target_pairs={{0,16},{8,24},{16,0},{24,8},{1,17},{9,25},{17,1},{25,9},{2,18},{10... | collective-permute-start | bytes 737288 | tf_op jit(solution)/shard_map/ppermute | solution.py:319
  28.4 6.9 %collective-permute-start.11 = (bf16[480,256]{1,0:T(8,128)(2,1)S(1)}, bf16[480,256]{1,0:T(8,128)(2,1)S(1)}, u32[]{:S(2)}, u32[]{:S(2)}) collective-permute-start(bf16[480,256]{1,0:T(8,128)(2,1)S(1)} %get-tuple-element.94), channel_id=1, source_target_pairs={{0,8},{8,0},{16,24},{24,16},{1,9},{9,1},{17,25},{25,17},{2,10},{10... | collective-permute-start | bytes 737288 | tf_op jit(solution)/shard_map/ppermute | solution.py:301
  28.4 1.9 %collective-permute-start.8 = (bf16[480,256]{1,0:T(8,128)(2,1)S(1)}, bf16[480,256]{1,0:T(8,128)(2,1)S(1)}, u32[]{:S(2)}, u32[]{:S(2)}) collective-permute-start(bf16[480,256]{1,0:T(8,128)(2,1)S(1)} %get-tuple-element.84), channel_id=1, source_target_pairs={{0,8},{8,0},{16,24},{24,16},{1,9},{9,1},{17,25},{25,17},{2,10},{10... | collective-permute-start | bytes 737288 | tf_op jit(solution)/shard_map/ppermute | solution.py:301
  30.3 9.1 %collective-permute-start.20 = (bf16[480,256]{1,0:T(8,128)(2,1)S(1)}, bf16[480,256]{1,0:T(8,128)(2,1)S(1)}, u32[]{:S(2)}, u32[]{:S(2)}) collective-permute-start(bf16[480,256]{1,0:T(8,128)(2,1)S(1)} %add_convert_fusion.3), channel_id=1, source_target_pairs={{0,16},{8,24},{16,0},{24,8},{1,17},{9,25},{17,1},{25,9},{2,18},{10... | collective-permute-start | bytes 737288 | tf_op jit(solution)/shard_map/ppermute | solution.py:319
  32.4 8.1 %collective-permute-start.13 = (bf16[480,256]{1,0:T(8,128)(2,1)S(1)}, bf16[480,256]{1,0:T(8,128)(2,1)S(1)}, u32[]{:S(2)}, u32[]{:S(2)}) collective-permute-start(bf16[480,256]{1,0:T(8,128)(2,1)S(1)} %get-tuple-element.102), channel_id=1, source_target_pairs={{0,8},{8,0},{16,24},{24,16},{1,9},{9,1},{17,25},{25,17},{2,10},{10... | collective-permute-start | bytes 737288 | tf_op jit(solution)/shard_map/ppermute | solution.py:301
  32.5 2.8 %collective-permute-start.10 = (bf16[480,256]{1,0:T(8,128)(2,1)S(1)}, bf16[480,256]{1,0:T(8,128)(2,1)S(1)}, u32[]{:S(2)}, u32[]{:S(2)}) collective-permute-start(bf16[480,256]{1,0:T(8,128)(2,1)S(1)} %get-tuple-element.92), channel_id=1, source_target_pairs={{0,8},{8,0},{16,24},{24,16},{1,9},{9,1},{17,25},{25,17},{2,10},{10... | collective-permute-start | bytes 737288 | tf_op jit(solution)/shard_map/ppermute | solution.py:301
  35.4 9.4 %collective-permute-start.19 = (bf16[480,256]{1,0:T(8,128)(2,1)S(1)}, bf16[480,256]{1,0:T(8,128)(2,1)S(1)}, u32[]{:S(2)}, u32[]{:S(2)}) collective-permute-start(bf16[480,256]{1,0:T(8,128)(2,1)S(1)} %add_convert_fusion.2), channel_id=1, source_target_pairs={{0,16},{8,24},{16,0},{24,8},{1,17},{9,25},{17,1},{25,9},{2,18},{10... | collective-permute-start | bytes 737288 | tf_op jit(solution)/shard_map/ppermute | solution.py:319
  38.4 7.4 %collective-permute-start.17 = (bf16[480,256]{1,0:T(8,128)(2,1)S(1)}, bf16[480,256]{1,0:T(8,128)(2,1)S(1)}, u32[]{:S(2)}, u32[]{:S(2)}) collective-permute-start(bf16[480,256]{1,0:T(8,128)(2,1)S(1)} %get-tuple-element.112), channel_id=1, source_target_pairs={{0,8},{8,0},{16,24},{24,16},{1,9},{9,1},{17,25},{25,17},{2,10},{10... | collective-permute-start | bytes 737288 | tf_op jit(solution)/shard_map/ppermute | solution.py:301
  38.5 2.1 %collective-permute-start.12 = (bf16[480,256]{1,0:T(8,128)(2,1)S(1)}, bf16[480,256]{1,0:T(8,128)(2,1)S(1)}, u32[]{:S(2)}, u32[]{:S(2)}) collective-permute-start(bf16[480,256]{1,0:T(8,128)(2,1)S(1)} %get-tuple-element.100), channel_id=1, source_target_pairs={{0,8},{8,0},{16,24},{24,16},{1,9},{9,1},{17,25},{25,17},{2,10},{10... | collective-permute-start | bytes 737288 | tf_op jit(solution)/shard_map/ppermute | solution.py:301
  40.6 9.4 %collective-permute-start.18 = (bf16[480,256]{1,0:T(8,128)(2,1)S(1)}, bf16[480,256]{1,0:T(8,128)(2,1)S(1)}, u32[]{:S(2)}, u32[]{:S(2)}) collective-permute-start(bf16[480,256]{1,0:T(8,128)(2,1)S(1)} %add_convert_fusion.1), channel_id=1, source_target_pairs={{0,16},{8,24},{16,0},{24,8},{1,17},{9,25},{17,1},{25,9},{2,18},{10... | collective-permute-start | bytes 737288 | tf_op jit(solution)/shard_map/ppermute | solution.py:319
  43.6 2.2 %collective-permute-start.15 = (bf16[480,256]{1,0:T(8,128)(2,1)S(1)}, bf16[480,256]{1,0:T(8,128)(2,1)S(1)}, u32[]{:S(2)}, u32[]{:S(2)}) collective-permute-start(bf16[480,256]{1,0:T(8,128)(2,1)S(1)} %get-tuple-element.110), channel_id=1, source_target_pairs={{0,8},{8,0},{16,24},{24,16},{1,9},{9,1},{17,25},{25,17},{2,10},{10... | collective-permute-start | bytes 737288 | tf_op jit(solution)/shard_map/ppermute | solution.py:301
  43.7 7.3 %collective-permute-start.14 = (bf16[480,256]{1,0:T(8,128)(2,1)S(1)}, bf16[480,256]{1,0:T(8,128)(2,1)S(1)}, u32[]{:S(2)}, u32[]{:S(2)}) collective-permute-start(bf16[480,256]{1,0:T(8,128)(2,1)S(1)} %get-tuple-element.108), channel_id=1, source_target_pairs={{0,8},{8,0},{16,24},{24,16},{1,9},{9,1},{17,25},{25,17},{2,10},{10... | collective-permute-start | bytes 737288 | tf_op jit(solution)/shard_map/ppermute | solution.py:301
  45.9 8.9 %collective-permute-start.16 = (bf16[480,256]{1,0:T(8,128)(2,1)S(1)}, bf16[480,256]{1,0:T(8,128)(2,1)S(1)}, u32[]{:S(2)}, u32[]{:S(2)}) collective-permute-start(bf16[480,256]{1,0:T(8,128)(2,1)S(1)} %add_convert_fusion), channel_id=1, source_target_pairs={{0,16},{8,24},{16,0},{24,8},{1,17},{9,25},{17,1},{25,9},{2,18},{10... | collective-permute-start | bytes 737288 | tf_op jit(solution)/shard_map/ppermute | solution.py:319

commit v6 on v5

--- a/solution.py
+++ b/solution.py
@@ -64,7 +64,7 @@
     return block * used // LANES, block * used % LANES
 
 
-def gather_kernel(slots, low, table_ref, rows_ref, *refs):
+def gather_kernel(slots, table_ref, rows_ref, *refs):
     outs, turned = refs[:-1], refs[-1]
     me = lax.axis_index("wave")
     used, waves = rows_ref.shape
@@ -78,8 +78,8 @@
         turned[j * LANES : (j + 2) * LANES, :] = got.T
     lane = lax.broadcasted_iota(jnp.int32, (STEP, LANES), 1)
     for t, out in enumerate(outs):
-        for u in range(low):
-            begin = (me ^ (t * low + u)) * slots
+        for u in range(out.shape[0]):
+            begin = (me ^ (t * out.shape[0] + u)) * slots
             tiles = [jnp.zeros((STEP, LANES), jnp.float32)] * (out.shape[2] // LANES)
             for block in range(slots // STEP):
                 tile, off = shift_of(block, used)
@@ -233,13 +233,12 @@
     anywhere = pl.BlockSpec(memory_space=pl.ANY)
 
     message = -(-(slots // STEP) * used // LANES) * LANES
-    low = 2
-    high = wave_count // low
+    upper = wave_count // 2
     ordered = pl.pallas_call(
-        functools.partial(gather_kernel, slots, low),
-        out_shape=[jax.ShapeDtypeStruct((low, STEP, message), jnp.bfloat16)] * high,
+        functools.partial(gather_kernel, slots),
+        out_shape=[jax.ShapeDtypeStruct((upper, STEP, message), jnp.bfloat16)] * 2,
         in_specs=[whole, whole],
-        out_specs=[whole] * high,
+        out_specs=[whole] * 2,
         scratch_shapes=[pltpu.VMEM((slots * wave_count, LANES), jnp.float32)],
         compiler_params=params,
         name="gather",
@@ -247,40 +246,34 @@
         wave_table.reshape(-1, LANES),
         jnp.transpose(fourier, (1, 0, 2)).reshape(used, waves),
     )
-    turns = [
-        t * low + u
-        for u in range(low)
-        for side in (0, 1)
-        for t in range(side * high // 2, (side + 1) * high // 2)
-    ]
+    turns = [u + side * upper for u in range(upper) for side in (0, 1)]
     place, limits = pl.pallas_call(
         functools.partial(place_kernel, turns, lat_count, row_count, pairs, degrees),
         out_shape=[
             jax.ShapeDtypeStruct((wave_count * LANES, 2 * LANES), jnp.bfloat16),
             jax.ShapeDtypeStruct((slots, LANES), jnp.int32),
         ],
-        in_specs=[pl.BlockSpec(memory_space=pltpu.SMEM), anywhere],
+        in_specs=[pl.BlockSpec(memory_space=pltpu.SMEM), whole],
         out_specs=[whole] * 2,
         compiler_params=params,
         name="place",
     )(wave_table, legendre)
 
-    passed = [ordered[0]] + [
-        lax.ppermute(ordered[t], "wave", [(w, w ^ t * low) for w in range(wave_count)])
-        for t in range(1, high)
-    ]
+    passed = []
+    for side in (0, 1):
+        route = []
+        for lat in range(lat_count):
+            for wave in range(wave_count):
+                to = lat if wave < upper else lat_count - 1 - lat
+                route.append((lat * wave_count + wave, to * wave_count + (wave ^ side * upper)))
+        passed.append(lax.ppermute(ordered[side], ("lat", "wave"), route))
     sources = []
-    for u in range(low):
-        for side in (0, 1):
-            block = jnp.stack([passed[t][u] for t in range(side * high // 2, (side + 1) * high // 2)])
-            route = []
-            for lat in range(lat_count):
-                for wave in range(wave_count):
-                    began = (wave >= wave_count // 2) != (side == 1)
-                    to = lat_count - 1 - lat if began else lat
-                    route.append((lat * wave_count + wave, to * wave_count + (wave ^ u)))
-            block, place = lax.optimization_barrier((block, place))
-            sources.append(lax.ppermute(block, ("lat", "wave"), route))
+    for u in range(upper):
+        block = jnp.stack([passed[0][u], passed[1][u]])
+        block, place = lax.optimization_barrier((block, place))
+        if u:
+            block = lax.ppermute(block, "wave", [(w, w ^ u) for w in range(wave_count)])
+        sources.append(block)
 
     rows = STEP * cols
     shape = (rows + rows // 4, 2 * LANES)

time: 56 us -> 57.2 us (1.021)
  waiting for transfers between devices: 12.9 us -> 14.4 us
    ppermute x7 -> x5, waiting for transfers between devices: 2.11 us -> 5.07 us  [the longest x3 3.73 us: packed(): block = lax.ppermute(block, 'wave', [(w, w ^ u) for w in range(wave_count)])]
    ppermute x5, waiting for transfers between devices: 8.41 us -> 6.97 us  [packed(): crossed.append(lax.ppermute(summed, 'lat', y_route))]
    ppermute x5, starting transfers between devices: 6.99 us -> 8.21 us  [packed(): crossed.append(lax.ppermute(summed, 'lat', y_route))]
    ppermute x7 -> x5, starting transfers between devices: 11.2 us -> 10.5 us  [the longest x2 6.97 us: packed(): passed.append(lax.ppermute(ordered[side], ('lat', 'wave'), route))]
    ppermute x10, starting transfers between devices: 3.53 us -> 2.84 us  [settle(): return kept + lax.ppermute(sent, 'lat', core_route).astype(jnp.float32)]
  transfers between devices with their start and end apart: 22 -> 20, of which waited for: 10 -> 11; matrix products, arithmetic and copies ran while one was open for 1% -> 1% of each run, Pallas kernels for 19% -> 19%
where the time goes in v6:
time: 57.2 us; the launch traced here: 57 us
  starting transfers between devices  21.6 us (38%)
  waiting for transfers between devices  14.4 us (25%)
  Pallas kernels  13.9 us (24%)
  local copies, waits for them, and re-layouts  6.39 us (11%)
    ppermute x5, starting transfers between devices, packed(): crossed.append(lax.ppermute(summed, 'lat', y_route))  8.21 us
    pallas_call x5, Pallas kernels, packed(): pl.pallas_call(functools.partial(product_kernel, block, row_count, cols),...  7.09 us
    ppermute x5, waiting for transfers between devices, packed(): crossed.append(lax.ppermute(summed, 'lat', y_route))  6.97 us
    ppermute x2, starting transfers between devices, packed(): passed.append(lax.ppermute(ordered[side], ('lat', 'wave'), route))  6.97 us
    unnamed x8, local copies, waits for them, and re-layouts  6.37 us
    pallas_call x5, Pallas kernels, packed(): pl.pallas_call(functools.partial(final_kernel, block * STEP, degrees, col...  5.09 us
    ppermute x3, waiting for transfers between devices, packed(): block = lax.ppermute(block, 'wave', [(w, w ^ u) for w in range(wave_count)])  3.73 us
    ppermute x3, starting transfers between devices, packed(): block = lax.ppermute(block, 'wave', [(w, w ^ u) for w in range(wave_count)])  3.55 us
  transfers between devices with their start and end apart: 20, of which 11 were waited for; matrix products, arithmetic and copies ran while one was open for 1% of the time, Pallas kernels for 19%

profile of v6, /device:TPU:0, one launch (start us, length us, event | category | flops | bytes accessed | tf_op | source)
XLA Modules:
  0.0 57.0 jit_solution(7538405867412138082)
XLA Ops:
  0.0 0.0 copy-start.2
  0.0 0.9 %copy-done.2 = bf16[8,12,1280]{2,0,1:T(8,128)(2,1)S(1)} copy-done((bf16[8,12,1280]{2,0,1:T(8,128)(2,1)S(1)}, bf16[8,12,1280]{2,0,1:T(8,128)(2,1)}, u32[]{:S(2)}) %copy-start.2) | copy-done | bytes 245784
  0.9 0.0 copy-start.3
  0.9 0.7 %copy-done.3 = s32[1280]{0:T(1024)S(1)} copy-done((s32[1280]{0:T(1024)S(1)}, s32[1280]{0:T(1024)}, u32[]{:S(2)}) %copy-start.3) | copy-done | bytes 5144
  1.6 0.8 %gather.1 = (bf16[4,32,512]{2,1,0:T(8,128)(2,1)S(1)}, bf16[4,32,512]{2,1,0:T(8,128)(2,1)S(1)}) custom-call(s32[10,128]{1,0:T(8,128)S(1)} %bitcast.6, bf16[96,1280]{1,0:T(8,128)(2,1)S(1)} %bitcast.5), custom_call_target="tpu_custom_call" | custom-call | tf_op jit(solution)/shard_map/gather/pallas_call | solution.py:237
  2.5 0.7 %collective-permute-start = (bf16[4,32,512]{2,1,0:T(8,128)(2,1)S(1)}, bf16[4,32,512]{2,1,0:T(8,128)(2,1)S(1)}, u32[]{:S(2)}, u32[]{:S(2)}) collective-permute-start(bf16[4,32,512]{2,1,0:T(8,128)(2,1)S(1)} %get-tuple-element.58), channel_id=1, source_target_pairs={{0,0},{1,1},{2,2},{3,3},{4,28},{5,29},{6,30},{7,31},{8,8},{9,9},{1... | collective-permute-start | bytes 393224 | tf_op jit(solution)/shard_map/ppermute | solution.py:269
  3.1 6.3 %collective-permute-start.1 = (bf16[4,32,512]{2,1,0:T(8,128)(2,1)S(1)}, bf16[4,32,512]{2,1,0:T(8,128)(2,1)S(1)}, u32[]{:S(2)}, u32[]{:S(2)}) collective-permute-start(bf16[4,32,512]{2,1,0:T(8,128)(2,1)S(1)} %get-tuple-element.59), channel_id=1, source_target_pairs={{0,4},{1,5},{2,6},{3,7},{4,24},{5,25},{6,26},{7,27},{8,12},{9,13},... | collective-permute-start | bytes 393224 | tf_op jit(solution)/shard_map/ppermute | solution.py:269
  9.4 0.0 copy-start
  9.4 4.7 %copy-done = bf16[160,32,1280]{2,1,0:T(8,128)(2,1)S(1)} copy-done((bf16[160,32,1280]{2,1,0:T(8,128)(2,1)S(1)}, bf16[160,32,1280]{2,1,0:T(8,128)(2,1)}, u32[]{:S(2)}) %copy-start) | copy-done | bytes 13107224
  14.2 0.9 %place.1 = (bf16[1024,256]{1,0:T(8,128)(2,1)S(1)}, s32[160,128]{1,0:T(8,128)S(1)}) custom-call(s32[1280]{0:T(1024)S(1)} %copy-done.3, bf16[160,32,1280]{2,1,0:T(8,128)(2,1)S(1)} %copy-done), custom_call_target="tpu_custom_call" | custom-call | tf_op jit(solution)/shard_map/place/pallas_call | solution.py:250
  15.1 0.0 collective-permute-done
  15.1 1.3 %collective-permute-done.1 = bf16[4,32,512]{2,1,0:T(8,128)(2,1)S(1)} collective-permute-done((bf16[4,32,512]{2,1,0:T(8,128)(2,1)S(1)}, bf16[4,32,512]{2,1,0:T(8,128)(2,1)S(1)}, u32[]{:S(2)}, u32[]{:S(2)}) %collective-permute-start.1) | collective-permute-done | bytes 131104 | tf_op jit(solution)/shard_map/ppermute | solution.py:269
  16.5 1.9 %collective-permute-start.4 = (bf16[2,32,512]{2,1,0:T(8,128)(2,1)S(1)}, bf16[2,32,512]{2,1,0:T(8,128)(2,1)S(1)}, u32[]{:S(2)}, u32[]{:S(2)}) collective-permute-start(bf16[2,32,512]{2,1,0:T(8,128)(2,1)S(1)} %get-tuple-element.68), channel_id=1, source_target_pairs={{0,3},{1,2},{2,1},{3,0},{4,7},{5,6},{6,5},{7,4},{8,11},{9,10},{10,... | collective-permute-start | bytes 196616 | tf_op jit(solution)/shard_map/ppermute | solution.py:275
  18.4 1.1 %collective-permute-start.3 = (bf16[2,32,512]{2,1,0:T(8,128)(2,1)S(1)}, bf16[2,32,512]{2,1,0:T(8,128)(2,1)S(1)}, u32[]{:S(2)}, u32[]{:S(2)}) collective-permute-start(bf16[2,32,512]{2,1,0:T(8,128)(2,1)S(1)} %get-tuple-element.67), channel_id=1, source_target_pairs={{0,2},{1,3},{2,0},{3,1},{4,6},{5,7},{6,4},{7,5},{8,10},{9,11},{10,... | collective-permute-start | bytes 196616 | tf_op jit(solution)/shard_map/ppermute | solution.py:275
  19.5 0.5 collective-permute-start.2
  20.1 2.3 %collective-permute-done.4.refs_3_ = bf16[2,32,512]{2,1,0:T(8,128)(2,1)S(1)} collective-permute-done((bf16[2,32,512]{2,1,0:T(8,128)(2,1)S(1)}, bf16[2,32,512]{2,1,0:T(8,128)(2,1)S(1)}, u32[]{:S(2)}, u32[]{:S(2)}) %collective-permute-start.4) | collective-permute-done | bytes 65568 | tf_op jit(solution)/shard_map/ppermute | solution.py:275
  22.4 0.6 %collective-permute-done.3.refs_2_ = bf16[2,32,512]{2,1,0:T(8,128)(2,1)S(1)} collective-permute-done((bf16[2,32,512]{2,1,0:T(8,128)(2,1)S(1)}, bf16[2,32,512]{2,1,0:T(8,128)(2,1)S(1)}, u32[]{:S(2)}, u32[]{:S(2)}) %collective-permute-start.3) | collective-permute-done | bytes 65568 | tf_op jit(solution)/shard_map/ppermute | solution.py:275
  23.0 0.8 %collective-permute-done.2.refs_1_ = bf16[2,32,512]{2,1,0:T(8,128)(2,1)S(1)} collective-permute-done((bf16[2,32,512]{2,1,0:T(8,128)(2,1)S(1)}, bf16[2,32,512]{2,1,0:T(8,128)(2,1)S(1)}, u32[]{:S(2)}, u32[]{:S(2)}) %collective-permute-start.2) | collective-permute-done | bytes 65568 | tf_op jit(solution)/shard_map/ppermute | solution.py:275
  23.8 0.0 copy-done.1
  23.8 1.4 %product.5 = (bf16[480,256]{1,0:T(8,128)(2,1)S(1)}, f32[480,256]{1,0:T(8,128)S(1)}, bf16[480,256]{1,0:T(8,128)(2,1)S(1)}, f32[480,256]{1,0:T(8,128)S(1)}) custom-call(bf16[1024,256]{1,0:T(8,128)(2,1)S(1)} %get-tuple-element.64.place_ref, bf16[160,32,1280]{2,1,0:T(8,128)(2,1)S(1)} %copy-done.1, bf16[2,32,512]{2,1,0:T(8,128)(2,1)S(1)} %get-tuple-element.99.refs_0_, ...), custom_call_target="tpu_custom_call" | custom-call | bytes 1024 | tf_op jit(solution)/shard_map/product/pallas_call | solution.py:300
  25.2 0.1 collective-permute-start.5
  25.3 0.5 collective-permute-start.7
  25.8 1.0 %collective-permute-done.5 = bf16[480,256]{1,0:T(8,128)(2,1)S(1)} collective-permute-done((bf16[480,256]{1,0:T(8,128)(2,1)S(1)}, bf16[480,256]{1,0:T(8,128)(2,1)S(1)}, u32[]{:S(2)}, u32[]{:S(2)}) %collective-permute-start.5) | collective-permute-done | bytes 245792 | tf_op jit(solution)/shard_map/ppermute | solution.py:294
  26.8 0.1 add_convert_fusion.4
  26.8 1.7 %collective-permute-start.19 = (bf16[480,256]{1,0:T(8,128)(2,1)S(1)}, bf16[480,256]{1,0:T(8,128)(2,1)S(1)}, u32[]{:S(2)}, u32[]{:S(2)}) collective-permute-start(bf16[480,256]{1,0:T(8,128)(2,1)S(1)} %add_convert_fusion.4), channel_id=1, source_target_pairs={{0,16},{8,24},{16,0},{24,8},{1,17},{9,25},{17,1},{25,9},{2,18},{10... | collective-permute-start | bytes 737288 | tf_op jit(solution)/shard_map/ppermute | solution.py:312
  28.5 1.4 %product.6 = (bf16[480,256]{1,0:T(8,128)(2,1)S(1)}, f32[480,256]{1,0:T(8,128)S(1)}, bf16[480,256]{1,0:T(8,128)(2,1)S(1)}, f32[480,256]{1,0:T(8,128)S(1)}) custom-call(bf16[1024,256]{1,0:T(8,128)(2,1)S(1)} %get-tuple-element.64.place_ref, bf16[160,32,1280]{2,1,0:T(8,128)(2,1)S(1)} %copy-done.1, bf16[2,32,512]{2,1,0:T(8,128)(2,1)S(1)} %get-tuple-element.99.refs_0_, ...), custom_call_target="tpu_custom_call" | custom-call | bytes 1024 | tf_op jit(solution)/shard_map/product/pallas_call | solution.py:300
  29.9 0.1 collective-permute-start.9
  30.0 0.5 collective-permute-start.6
  30.5 0.0 collective-permute-done.7
  30.6 1.3 %collective-permute-done.6 = bf16[480,256]{1,0:T(8,128)(2,1)S(1)} collective-permute-done((bf16[480,256]{1,0:T(8,128)(2,1)S(1)}, bf16[480,256]{1,0:T(8,128)(2,1)S(1)}, u32[]{:S(2)}, u32[]{:S(2)}) %collective-permute-start.6) | collective-permute-done | bytes 245792 | tf_op jit(solution)/shard_map/ppermute | solution.py:294
  31.9 0.1 add_convert_fusion.3
  31.9 0.5 collective-permute-start.18
  32.4 1.4 %product.7 = (bf16[480,256]{1,0:T(8,128)(2,1)S(1)}, f32[480,256]{1,0:T(8,128)S(1)}, bf16[480,256]{1,0:T(8,128)(2,1)S(1)}, f32[480,256]{1,0:T(8,128)S(1)}) custom-call(bf16[1024,256]{1,0:T(8,128)(2,1)S(1)} %get-tuple-element.64.place_ref, bf16[160,32,1280]{2,1,0:T(8,128)(2,1)S(1)} %copy-done.1, bf16[2,32,512]{2,1,0:T(8,128)(2,1)S(1)} %get-tuple-element.99.refs_0_, ...), custom_call_target="tpu_custom_call" | custom-call | bytes 1024 | tf_op jit(solution)/shard_map/product/pallas_call | solution.py:300
  33.8 0.1 collective-permute-start.11
  33.9 0.5 collective-permute-start.8
  34.4 0.6 %collective-permute-done.19.far_ref = bf16[480,256]{1,0:T(8,128)(2,1)S(1)} collective-permute-done((bf16[480,256]{1,0:T(8,128)(2,1)S(1)}, bf16[480,256]{1,0:T(8,128)(2,1)S(1)}, u32[]{:S(2)}, u32[]{:S(2)}) %collective-permute-start.19) | collective-permute-done | bytes 245792 | tf_op jit(solution)/shard_map/ppermute | solution.py:312
  35.0 1.0 %final.5.refs_0_ = f32[12,160,320]{2,1,0:T(8,128)} custom-call(s32[160,128]{1,0:T(8,128)S(1)} %get-tuple-element.57.limits_ref, f32[480,256]{1,0:T(8,128)S(1)} %convert_add_fusion.4.near_ref, bf16[480,256]{1,0:T(8,128)(2,1)S(1)} %collective-permute-done.19.far_ref), custom_call_target="tpu_custom_call" | custom-call | bytes 1024 | tf_op jit(solution)/shard_map/final/pallas_call | solution.py:318
  36.0 0.0 collective-permute-done.9
  36.1 0.0 collective-permute-done.8
  36.1 0.1 add_convert_fusion.2
  36.2 2.3 %collective-permute-start.17 = (bf16[480,256]{1,0:T(8,128)(2,1)S(1)}, bf16[480,256]{1,0:T(8,128)(2,1)S(1)}, u32[]{:S(2)}, u32[]{:S(2)}) collective-permute-start(bf16[480,256]{1,0:T(8,128)(2,1)S(1)} %add_convert_fusion.2), channel_id=1, source_target_pairs={{0,16},{8,24},{16,0},{24,8},{1,17},{9,25},{17,1},{25,9},{2,18},{10... | collective-permute-start | bytes 737288 | tf_op jit(solution)/shard_map/ppermute | solution.py:312
  38.5 1.4 %product.8 = (bf16[480,256]{1,0:T(8,128)(2,1)S(1)}, f32[480,256]{1,0:T(8,128)S(1)}, bf16[480,256]{1,0:T(8,128)(2,1)S(1)}, f32[480,256]{1,0:T(8,128)S(1)}) custom-call(bf16[1024,256]{1,0:T(8,128)(2,1)S(1)} %get-tuple-element.64.place_ref, bf16[160,32,1280]{2,1,0:T(8,128)(2,1)S(1)} %copy-done.1, bf16[2,32,512]{2,1,0:T(8,128)(2,1)S(1)} %get-tuple-element.99.refs_0_, ...), custom_call_target="tpu_custom_call" | custom-call | bytes 1024 | tf_op jit(solution)/shard_map/product/pallas_call | solution.py:300
  39.9 0.1 collective-permute-start.15
  40.0 0.5 collective-permute-start.10
  40.5 0.3 collective-permute-done.18.far_ref
  40.8 1.0 %final.6.refs_0_ = f32[12,160,320]{2,1,0:T(8,128)} custom-call(s32[160,128]{1,0:T(8,128)S(1)} %get-tuple-element.57.limits_ref, f32[480,256]{1,0:T(8,128)S(1)} %convert_add_fusion.3.near_ref, bf16[480,256]{1,0:T(8,128)(2,1)S(1)} %collective-permute-done.18.far_ref, f32[12,160,320]{2,1,0:T(8,128)} %final.5.refs_0_), custom_call_target="tpu_custom_call", output_to_operand_aliasing={{}: (3, {})} | custom-call | bytes 1024 | tf_op jit(solution)/shard_map/final/pallas_call | solution.py:318
  41.8 0.0 collective-permute-done.11
  41.9 0.0 collective-permute-done.10
  41.9 0.1 add_convert_fusion.1
  41.9 1.9 %collective-permute-start.16 = (bf16[480,256]{1,0:T(8,128)(2,1)S(1)}, bf16[480,256]{1,0:T(8,128)(2,1)S(1)}, u32[]{:S(2)}, u32[]{:S(2)}) collective-permute-start(bf16[480,256]{1,0:T(8,128)(2,1)S(1)} %add_convert_fusion.1), channel_id=1, source_target_pairs={{0,16},{8,24},{16,0},{24,8},{1,17},{9,25},{17,1},{25,9},{2,18},{10... | collective-permute-start | bytes 737288 | tf_op jit(solution)/shard_map/ppermute | solution.py:312
  43.8 1.4 %product.9 = (bf16[480,256]{1,0:T(8,128)(2,1)S(1)}, f32[480,256]{1,0:T(8,128)S(1)}, bf16[480,256]{1,0:T(8,128)(2,1)S(1)}, f32[480,256]{1,0:T(8,128)S(1)}) custom-call(bf16[1024,256]{1,0:T(8,128)(2,1)S(1)} %get-tuple-element.64.place_ref, bf16[160,32,1280]{2,1,0:T(8,128)(2,1)S(1)} %copy-done.1, bf16[2,32,512]{2,1,0:T(8,128)(2,1)S(1)} %get-tuple-element.99.refs_0_, ...), custom_call_target="tpu_custom_call" | custom-call | bytes 1024 | tf_op jit(solution)/shard_map/product/pallas_call | solution.py:300
  45.2 0.1 collective-permute-start.13
  45.3 0.5 collective-permute-start.12
  45.8 0.3 collective-permute-done.17.far_ref
  46.0 1.0 %final.7.refs_0_ = f32[12,160,320]{2,1,0:T(8,128)} custom-call(s32[160,128]{1,0:T(8,128)S(1)} %get-tuple-element.57.limits_ref, f32[480,256]{1,0:T(8,128)S(1)} %convert_add_fusion.2.near_ref, bf16[480,256]{1,0:T(8,128)(2,1)S(1)} %collective-permute-done.17.far_ref, f32[12,160,320]{2,1,0:T(8,128)} %final.6.refs_0_), custom_call_target="tpu_custom_call", output_to_operand_aliasing={{}: (3, {})} | custom-call | bytes 1024 | tf_op jit(solution)/shard_map/final/pallas_call | solution.py:318
  47.1 0.0 collective-permute-done.15
  47.1 0.0 collective-permute-done.13
  47.1 0.1 add_convert_fusion
  47.2 1.9 %collective-permute-start.14 = (bf16[480,256]{1,0:T(8,128)(2,1)S(1)}, bf16[480,256]{1,0:T(8,128)(2,1)S(1)}, u32[]{:S(2)}, u32[]{:S(2)}) collective-permute-start(bf16[480,256]{1,0:T(8,128)(2,1)S(1)} %add_convert_fusion), channel_id=1, source_target_pairs={{0,16},{8,24},{16,0},{24,8},{1,17},{9,25},{17,1},{25,9},{2,18},{10... | collective-permute-start | bytes 737288 | tf_op jit(solution)/shard_map/ppermute | solution.py:312
  49.0 2.3 %collective-permute-done.16.far_ref = bf16[480,256]{1,0:T(8,128)(2,1)S(1)} collective-permute-done((bf16[480,256]{1,0:T(8,128)(2,1)S(1)}, bf16[480,256]{1,0:T(8,128)(2,1)S(1)}, u32[]{:S(2)}, u32[]{:S(2)}) %collective-permute-start.16) | collective-permute-done | bytes 245792 | tf_op jit(solution)/shard_map/ppermute | solution.py:312
  51.3 1.0 %final.8.refs_0_ = f32[12,160,320]{2,1,0:T(8,128)} custom-call(s32[160,128]{1,0:T(8,128)S(1)} %get-tuple-element.57.limits_ref, f32[480,256]{1,0:T(8,128)S(1)} %convert_add_fusion.near_ref, bf16[480,256]{1,0:T(8,128)(2,1)S(1)} %collective-permute-done.16.far_ref, f32[12,160,320]{2,1,0:T(8,128)} %final.7.refs_0_), custom_call_target="tpu_custom_call", output_to_operand_aliasing={{}: (3, {})} | custom-call | bytes 1024 | tf_op jit(solution)/shard_map/final/pallas_call | solution.py:318
  52.3 0.0 collective-permute-done.12
  52.4 3.6 %collective-permute-done.14.far_ref = bf16[480,256]{1,0:T(8,128)(2,1)S(1)} collective-permute-done((bf16[480,256]{1,0:T(8,128)(2,1)S(1)}, bf16[480,256]{1,0:T(8,128)(2,1)S(1)}, u32[]{:S(2)}, u32[]{:S(2)}) %collective-permute-start.14) | collective-permute-done | bytes 245792 | tf_op jit(solution)/shard_map/ppermute | solution.py:312
  56.0 1.0 %final.9 = f32[12,160,320]{2,1,0:T(8,128)} custom-call(s32[160,128]{1,0:T(8,128)S(1)} %get-tuple-element.57.limits_ref, f32[480,256]{1,0:T(8,128)S(1)} %convert_add_fusion.1.near_ref, bf16[480,256]{1,0:T(8,128)(2,1)S(1)} %collective-permute-done.14.far_ref, f32[12,160,320]{2,1,0:T(8,128)} %final.8.refs_0_), custom_call_target="tpu_custom_call", output_to_operand_aliasing={{}: (3, {})} | custom-call | bytes 1024 | tf_op jit(solution)/shard_map/final/pallas_call | solution.py:318
  (10 shorter events, 0.3 us)
Async XLA Ops:
  0.0 0.9 %copy-start.2 = (bf16[8,12,1280]{2,0,1:T(8,128)(2,1)S(1)}, bf16[8,12,1280]{2,0,1:T(8,128)(2,1)}, u32[]{:S(2)}) copy-start(bf16[8,12,1280]{2,0,1:T(8,128)(2,1)} %param.3) | copy-start | bytes 737284
  0.9 0.7 %copy-start.3 = (s32[1280]{0:T(1024)S(1)}, s32[1280]{0:T(1024)}, u32[]{:S(2)}) copy-start(s32[1280]{0:T(1024)} %table_ref.1) | copy-start | bytes 15364
  2.5 12.6 %collective-permute-start = (bf16[4,32,512]{2,1,0:T(8,128)(2,1)S(1)}, bf16[4,32,512]{2,1,0:T(8,128)(2,1)S(1)}, u32[]{:S(2)}, u32[]{:S(2)}) collective-permute-start(bf16[4,32,512]{2,1,0:T(8,128)(2,1)S(1)} %get-tuple-element.58), channel_id=1, source_target_pairs={{0,0},{1,1},{2,2},{3,3},{4,28},{5,29},{6,30},{7,31},{8,8},{9,9},{1... | collective-permute-start | bytes 393224 | tf_op jit(solution)/shard_map/ppermute | solution.py:269
  3.1 13.3 %collective-permute-start.1 = (bf16[4,32,512]{2,1,0:T(8,128)(2,1)S(1)}, bf16[4,32,512]{2,1,0:T(8,128)(2,1)S(1)}, u32[]{:S(2)}, u32[]{:S(2)}) collective-permute-start(bf16[4,32,512]{2,1,0:T(8,128)(2,1)S(1)} %get-tuple-element.59), channel_id=1, source_target_pairs={{0,4},{1,5},{2,6},{3,7},{4,24},{5,25},{6,26},{7,27},{8,12},{9,13},... | collective-permute-start | bytes 393224 | tf_op jit(solution)/shard_map/ppermute | solution.py:269
  9.4 4.7 %copy-start = (bf16[160,32,1280]{2,1,0:T(8,128)(2,1)S(1)}, bf16[160,32,1280]{2,1,0:T(8,128)(2,1)}, u32[]{:S(2)}) copy-start(bf16[160,32,1280]{2,1,0:T(8,128)(2,1)} %leg_ref.11) | copy-start | bytes 39321604
  14.2 9.6 %copy-start.1 = (bf16[160,32,1280]{2,1,0:T(8,128)(2,1)S(1)}, bf16[160,32,1280]{2,1,0:T(8,128)(2,1)}, u32[]{:S(2)}) copy-start(bf16[160,32,1280]{2,1,0:T(8,128)(2,1)} %leg_ref.11) | copy-start | bytes 39321604
  16.5 5.9 %collective-permute-start.4 = (bf16[2,32,512]{2,1,0:T(8,128)(2,1)S(1)}, bf16[2,32,512]{2,1,0:T(8,128)(2,1)S(1)}, u32[]{:S(2)}, u32[]{:S(2)}) collective-permute-start(bf16[2,32,512]{2,1,0:T(8,128)(2,1)S(1)} %get-tuple-element.68), channel_id=1, source_target_pairs={{0,3},{1,2},{2,1},{3,0},{4,7},{5,6},{6,5},{7,4},{8,11},{9,10},{10,... | collective-permute-start | bytes 196616 | tf_op jit(solution)/shard_map/ppermute | solution.py:275
  18.4 4.6 %collective-permute-start.3 = (bf16[2,32,512]{2,1,0:T(8,128)(2,1)S(1)}, bf16[2,32,512]{2,1,0:T(8,128)(2,1)S(1)}, u32[]{:S(2)}, u32[]{:S(2)}) collective-permute-start(bf16[2,32,512]{2,1,0:T(8,128)(2,1)S(1)} %get-tuple-element.67), channel_id=1, source_target_pairs={{0,2},{1,3},{2,0},{3,1},{4,6},{5,7},{6,4},{7,5},{8,10},{9,11},{10,... | collective-permute-start | bytes 196616 | tf_op jit(solution)/shard_map/ppermute | solution.py:275
  19.5 4.3 %collective-permute-start.2 = (bf16[2,32,512]{2,1,0:T(8,128)(2,1)S(1)}, bf16[2,32,512]{2,1,0:T(8,128)(2,1)S(1)}, u32[]{:S(2)}, u32[]{:S(2)}) collective-permute-start(bf16[2,32,512]{2,1,0:T(8,128)(2,1)S(1)} %get-tuple-element.66), channel_id=1, source_target_pairs={{0,1},{1,0},{2,3},{3,2},{4,5},{5,4},{6,7},{7,6},{8,9},{9,8},{10,11... | collective-permute-start | bytes 196616 | tf_op jit(solution)/shard_map/ppermute | solution.py:275
  25.2 1.6 %collective-permute-start.5 = (bf16[480,256]{1,0:T(8,128)(2,1)S(1)}, bf16[480,256]{1,0:T(8,128)(2,1)S(1)}, u32[]{:S(2)}, u32[]{:S(2)}) collective-permute-start(bf16[480,256]{1,0:T(8,128)(2,1)S(1)} %get-tuple-element.74), channel_id=1, source_target_pairs={{0,8},{8,0},{16,24},{24,16},{1,9},{9,1},{17,25},{25,17},{2,10},{10... | collective-permute-start | bytes 737288 | tf_op jit(solution)/shard_map/ppermute | solution.py:294
  25.3 5.2 %collective-permute-start.7 = (bf16[480,256]{1,0:T(8,128)(2,1)S(1)}, bf16[480,256]{1,0:T(8,128)(2,1)S(1)}, u32[]{:S(2)}, u32[]{:S(2)}) collective-permute-start(bf16[480,256]{1,0:T(8,128)(2,1)S(1)} %get-tuple-element.82), channel_id=1, source_target_pairs={{0,8},{8,0},{16,24},{24,16},{1,9},{9,1},{17,25},{25,17},{2,10},{10... | collective-permute-start | bytes 737288 | tf_op jit(solution)/shard_map/ppermute | solution.py:294
  26.8 8.2 %collective-permute-start.19 = (bf16[480,256]{1,0:T(8,128)(2,1)S(1)}, bf16[480,256]{1,0:T(8,128)(2,1)S(1)}, u32[]{:S(2)}, u32[]{:S(2)}) collective-permute-start(bf16[480,256]{1,0:T(8,128)(2,1)S(1)} %add_convert_fusion.4), channel_id=1, source_target_pairs={{0,16},{8,24},{16,0},{24,8},{1,17},{9,25},{17,1},{25,9},{2,18},{10... | collective-permute-start | bytes 737288 | tf_op jit(solution)/shard_map/ppermute | solution.py:312
  29.9 6.1 %collective-permute-start.9 = (bf16[480,256]{1,0:T(8,128)(2,1)S(1)}, bf16[480,256]{1,0:T(8,128)(2,1)S(1)}, u32[]{:S(2)}, u32[]{:S(2)}) collective-permute-start(bf16[480,256]{1,0:T(8,128)(2,1)S(1)} %get-tuple-element.90), channel_id=1, source_target_pairs={{0,8},{8,0},{16,24},{24,16},{1,9},{9,1},{17,25},{25,17},{2,10},{10... | collective-permute-start | bytes 737288 | tf_op jit(solution)/shard_map/ppermute | solution.py:294
  30.0 1.9 %collective-permute-start.6 = (bf16[480,256]{1,0:T(8,128)(2,1)S(1)}, bf16[480,256]{1,0:T(8,128)(2,1)S(1)}, u32[]{:S(2)}, u32[]{:S(2)}) collective-permute-start(bf16[480,256]{1,0:T(8,128)(2,1)S(1)} %get-tuple-element.80), channel_id=1, source_target_pairs={{0,8},{8,0},{16,24},{24,16},{1,9},{9,1},{17,25},{25,17},{2,10},{10... | collective-permute-start | bytes 737288 | tf_op jit(solution)/shard_map/ppermute | solution.py:294
  31.9 8.9 %collective-permute-start.18 = (bf16[480,256]{1,0:T(8,128)(2,1)S(1)}, bf16[480,256]{1,0:T(8,128)(2,1)S(1)}, u32[]{:S(2)}, u32[]{:S(2)}) collective-permute-start(bf16[480,256]{1,0:T(8,128)(2,1)S(1)} %add_convert_fusion.3), channel_id=1, source_target_pairs={{0,16},{8,24},{16,0},{24,8},{1,17},{9,25},{17,1},{25,9},{2,18},{10... | collective-permute-start | bytes 737288 | tf_op jit(solution)/shard_map/ppermute | solution.py:312
  33.8 8.0 %collective-permute-start.11 = (bf16[480,256]{1,0:T(8,128)(2,1)S(1)}, bf16[480,256]{1,0:T(8,128)(2,1)S(1)}, u32[]{:S(2)}, u32[]{:S(2)}) collective-permute-start(bf16[480,256]{1,0:T(8,128)(2,1)S(1)} %get-tuple-element.98), channel_id=1, source_target_pairs={{0,8},{8,0},{16,24},{24,16},{1,9},{9,1},{17,25},{25,17},{2,10},{10... | collective-permute-start | bytes 737288 | tf_op jit(solution)/shard_map/ppermute | solution.py:294
  33.9 2.2 %collective-permute-start.8 = (bf16[480,256]{1,0:T(8,128)(2,1)S(1)}, bf16[480,256]{1,0:T(8,128)(2,1)S(1)}, u32[]{:S(2)}, u32[]{:S(2)}) collective-permute-start(bf16[480,256]{1,0:T(8,128)(2,1)S(1)} %get-tuple-element.88), channel_id=1, source_target_pairs={{0,8},{8,0},{16,24},{24,16},{1,9},{9,1},{17,25},{25,17},{2,10},{10... | collective-permute-start | bytes 737288 | tf_op jit(solution)/shard_map/ppermute | solution.py:294
  36.2 9.9 %collective-permute-start.17 = (bf16[480,256]{1,0:T(8,128)(2,1)S(1)}, bf16[480,256]{1,0:T(8,128)(2,1)S(1)}, u32[]{:S(2)}, u32[]{:S(2)}) collective-permute-start(bf16[480,256]{1,0:T(8,128)(2,1)S(1)} %add_convert_fusion.2), channel_id=1, source_target_pairs={{0,16},{8,24},{16,0},{24,8},{1,17},{9,25},{17,1},{25,9},{2,18},{10... | collective-permute-start | bytes 737288 | tf_op jit(solution)/shard_map/ppermute | solution.py:312
  39.9 7.1 %collective-permute-start.15 = (bf16[480,256]{1,0:T(8,128)(2,1)S(1)}, bf16[480,256]{1,0:T(8,128)(2,1)S(1)}, u32[]{:S(2)}, u32[]{:S(2)}) collective-permute-start(bf16[480,256]{1,0:T(8,128)(2,1)S(1)} %get-tuple-element.108), channel_id=1, source_target_pairs={{0,8},{8,0},{16,24},{24,16},{1,9},{9,1},{17,25},{25,17},{2,10},{10... | collective-permute-start | bytes 737288 | tf_op jit(solution)/shard_map/ppermute | solution.py:294
  40.0 1.9 %collective-permute-start.10 = (bf16[480,256]{1,0:T(8,128)(2,1)S(1)}, bf16[480,256]{1,0:T(8,128)(2,1)S(1)}, u32[]{:S(2)}, u32[]{:S(2)}) collective-permute-start(bf16[480,256]{1,0:T(8,128)(2,1)S(1)} %get-tuple-element.96), channel_id=1, source_target_pairs={{0,8},{8,0},{16,24},{24,16},{1,9},{9,1},{17,25},{25,17},{2,10},{10... | collective-permute-start | bytes 737288 | tf_op jit(solution)/shard_map/ppermute | solution.py:294
  41.9 9.4 %collective-permute-start.16 = (bf16[480,256]{1,0:T(8,128)(2,1)S(1)}, bf16[480,256]{1,0:T(8,128)(2,1)S(1)}, u32[]{:S(2)}, u32[]{:S(2)}) collective-permute-start(bf16[480,256]{1,0:T(8,128)(2,1)S(1)} %add_convert_fusion.1), channel_id=1, source_target_pairs={{0,16},{8,24},{16,0},{24,8},{1,17},{9,25},{17,1},{25,9},{2,18},{10... | collective-permute-start | bytes 737288 | tf_op jit(solution)/shard_map/ppermute | solution.py:312
  45.2 1.9 %collective-permute-start.13 = (bf16[480,256]{1,0:T(8,128)(2,1)S(1)}, bf16[480,256]{1,0:T(8,128)(2,1)S(1)}, u32[]{:S(2)}, u32[]{:S(2)}) collective-permute-start(bf16[480,256]{1,0:T(8,128)(2,1)S(1)} %get-tuple-element.106), channel_id=1, source_target_pairs={{0,8},{8,0},{16,24},{24,16},{1,9},{9,1},{17,25},{25,17},{2,10},{10... | collective-permute-start | bytes 737288 | tf_op jit(solution)/shard_map/ppermute | solution.py:294
  45.3 7.0 %collective-permute-start.12 = (bf16[480,256]{1,0:T(8,128)(2,1)S(1)}, bf16[480,256]{1,0:T(8,128)(2,1)S(1)}, u32[]{:S(2)}, u32[]{:S(2)}) collective-permute-start(bf16[480,256]{1,0:T(8,128)(2,1)S(1)} %get-tuple-element.104), channel_id=1, source_target_pairs={{0,8},{8,0},{16,24},{24,16},{1,9},{9,1},{17,25},{25,17},{2,10},{10... | collective-permute-start | bytes 737288 | tf_op jit(solution)/shard_map/ppermute | solution.py:294
  47.2 8.8 %collective-permute-start.14 = (bf16[480,256]{1,0:T(8,128)(2,1)S(1)}, bf16[480,256]{1,0:T(8,128)(2,1)S(1)}, u32[]{:S(2)}, u32[]{:S(2)}) collective-permute-start(bf16[480,256]{1,0:T(8,128)(2,1)S(1)} %add_convert_fusion), channel_id=1, source_target_pairs={{0,16},{8,24},{16,0},{24,8},{1,17},{9,25},{17,1},{25,9},{2,18},{10... | collective-permute-start | bytes 737288 | tf_op jit(solution)/shard_map/ppermute | solution.py:312

commit v7 on v5

--- a/solution.py
+++ b/solution.py
@@ -10,7 +10,7 @@
 LANES = 128
 STEP = 32
 TILE = 8
-VMEM = 20 * 1024 * 1024
+VMEM = 32 * 1024 * 1024
 
 
 def partner(block, axis, stride):
@@ -92,7 +92,7 @@
                 out[u, :, k * LANES : (k + 1) * LANES] = tile.astype(jnp.bfloat16)
 
 
-def place_kernel(turns, lat_count, row_count, pairs, degrees, table_ref, leg_ref, out, limits):
+def place_kernel(turns, lat_count, row_count, pairs, degrees, table_ref, out, limits):
     northern = lax.axis_index("lat") < lat_count // 2
     me = lax.axis_index("wave")
     row = lax.broadcasted_iota(jnp.int32, (LANES, 2 * LANES), 0) & (row_count - 1)
@@ -158,7 +158,6 @@
     sources = refs[:-6]
     far_sent, far_own, near_sent, near_own, far, near = refs[-6:]
     half = far.shape[1]
-    table = leg_ref.at[block * STEP : (block + 1) * STEP]
     lat = lax.axis_index("lat")
     y, core = lat // 2, lat % 2
     tile, off = shift_of(block, row_count * cols)
@@ -182,8 +181,8 @@
     north, south = both[:, :LANES], both[:, LANES:]
     even, odd = north + south, north - south
     far_coefs, near_coefs = jnp.where(y == 0, odd, even), jnp.where(y == 0, even, odd)
-    multiply(far_coefs, table, pl.multiple_of((1 - y) * half, LANES), half, far)
-    multiply(near_coefs, table, pl.multiple_of(y * half, LANES), half, near)
+    multiply(far_coefs, leg_ref, pl.multiple_of((1 - y) * half, LANES), half, far)
+    multiply(near_coefs, leg_ref, pl.multiple_of(y * half, LANES), half, near)
     pack(far, core, far_sent, far_own)
     pack(near, core, near_sent, near_own)
 
@@ -259,16 +258,19 @@
             jax.ShapeDtypeStruct((wave_count * LANES, 2 * LANES), jnp.bfloat16),
             jax.ShapeDtypeStruct((slots, LANES), jnp.int32),
         ],
-        in_specs=[pl.BlockSpec(memory_space=pltpu.SMEM), anywhere],
+        in_specs=[pl.BlockSpec(memory_space=pltpu.SMEM)],
         out_specs=[whole] * 2,
         compiler_params=params,
         name="place",
-    )(wave_table, legendre)
+    )(wave_table)
 
     passed = [ordered[0]] + [
         lax.ppermute(ordered[t], "wave", [(w, w ^ t * low) for w in range(wave_count)])
         for t in range(1, high)
     ]
+    count = slots // STEP
+    early = count - count // 2
+    tables = [legendre[block * STEP : (block + 1) * STEP] for block in range(early)]
     sources = []
     for u in range(low):
         for side in (0, 1):
@@ -279,8 +281,13 @@
                     began = (wave >= wave_count // 2) != (side == 1)
                     to = lat_count - 1 - lat if began else lat
                     route.append((lat * wave_count + wave, to * wave_count + (wave ^ u)))
-            block, place = lax.optimization_barrier((block, place))
+            block, tables = lax.optimization_barrier((block, tables))
+            if side == 0 and u == 0:
+                later, block = lax.optimization_barrier((legendre, block))
             sources.append(lax.ppermute(block, ("lat", "wave"), route))
+
+    tables += [later[block * STEP : (block + 1) * STEP] for block in range(early, count)]
+    sources, tables = lax.optimization_barrier((sources, tables))
 
     rows = STEP * cols
     shape = (rows + rows // 4, 2 * LANES)
@@ -295,8 +302,6 @@
         jax.ShapeDtypeStruct(shape, jnp.bfloat16),
         jax.ShapeDtypeStruct(shape, jnp.float32),
     ]
-    count = slots // STEP
-
     def settle(sent, kept):
         return kept + lax.ppermute(sent, "lat", core_route).astype(jnp.float32)
 
@@ -313,7 +318,7 @@
             compiler_params=params,
             cost_estimate=cost,
             name="product",
-        )(place, legendre, *sources)
+        )(place, tables[block], *sources)
         summed = settle(far_sent, far_own).astype(jnp.bfloat16)
         ties = [summed] + settled[-1:]
         crossed.append(lax.ppermute(summed, "lat", y_route))

time: 56 us -> 56.3 us (level)
  local copies, waits for them, and re-layouts: 6.39 us -> 8.23 us
  starting transfers between devices: 21.8 us -> 21 us
  waiting for transfers between devices: 12.9 us -> 12.1 us
    slice x0 -> x2, local copies, waits for them, and re-layouts: none -> 6.56 us  [the longest x1 3.69 us: packed(): legendre[block * STEP:(block + 1) * STEP]]
    unnamed x8 -> x4, local copies, waits for them, and re-layouts: 6.36 us -> 1.64 us
    ppermute x4, waiting for transfers between devices: 1.76 us -> 0.01 us  [packed(): sources.append(lax.ppermute(block, ('lat', 'wave'), route))]
    ppermute x3, waiting for transfers between devices: 0.35 us -> 1.39 us  [packed(): lax.ppermute(ordered[t], 'wave', [(w, w ^ t * low) for w in range(wave_co...]
    ppermute x10, starting transfers between devices: 3.53 us -> 2.85 us  [settle(): return kept + lax.ppermute(sent, 'lat', core_route).astype(jnp.float32)]
  transfers between devices with their start and end apart: 22 -> 22, of which waited for: 10 -> 8; matrix products, arithmetic and copies ran while one was open for 1% -> 13% of each run, Pallas kernels for 19% -> 19%
where the time goes in v7:
time: 56.3 us; the launch traced here: 56.1 us
  starting transfers between devices  21 us (37%)
  Pallas kernels  13.9 us (25%)
  waiting for transfers between devices  12.1 us (21%)
  local copies, waits for them, and re-layouts  8.23 us (15%)
    ppermute x5, waiting for transfers between devices, packed(): crossed.append(lax.ppermute(summed, 'lat', y_route))  8.73 us
    pallas_call x5, Pallas kernels, packed(): pl.pallas_call(functools.partial(product_kernel, block, row_count, cols),...  7.1 us
    ppermute x5, starting transfers between devices, packed(): crossed.append(lax.ppermute(summed, 'lat', y_route))  6.95 us
    ppermute x3, starting transfers between devices, packed(): lax.ppermute(ordered[t], 'wave', [(w, w ^ t * low) for w in range(wave_co...  5.68 us
    ppermute x4, starting transfers between devices, packed(): sources.append(lax.ppermute(block, ('lat', 'wave'), route))  5.55 us
    pallas_call x5, Pallas kernels, packed(): pl.pallas_call(functools.partial(final_kernel, block * STEP, degrees, col...  5.06 us
    slice x1, local copies, waits for them, and re-layouts, packed(): legendre[block * STEP:(block + 1) * STEP]  3.69 us
    slice x1, local copies, waits for them, and re-layouts, packed(): later[block * STEP:(block + 1) * STEP]  2.88 us
  transfers between devices with their start and end apart: 22, of which 8 were waited for; matrix products, arithmetic and copies ran while one was open for 13% of the time, Pallas kernels for 19%

profile of v7, /device:TPU:0, one launch (start us, length us, event | category | flops | bytes accessed | tf_op | source)
XLA Modules:
  0.0 56.1 jit_solution(11063957184131535742)
XLA Ops:
  0.0 0.9 %copy-done = bf16[8,12,1280]{2,0,1:T(8,128)(2,1)S(1)} copy-done((bf16[8,12,1280]{2,0,1:T(8,128)(2,1)S(1)}, bf16[8,12,1280]{2,0,1:T(8,128)(2,1)}, u32[]{:S(2)}) %copy-start) | copy-done | bytes 245784
  0.9 0.7 %copy-done.1 = s32[1280]{0:T(1024)S(1)} copy-done((s32[1280]{0:T(1024)S(1)}, s32[1280]{0:T(1024)}, u32[]{:S(2)}) %copy-start.1) | copy-done | bytes 5144
  1.6 0.8 %gather.1 = (bf16[2,32,512]{2,1,0:T(8,128)(2,1)S(1)}, bf16[2,32,512]{2,1,0:T(8,128)(2,1)S(1)}, bf16[2,32,512]{2,1,0:T(8,128)(2,1)S(1)}, bf16[2,32,512]{2,1,0:T(8,128)(2,1)S(1)}) custom-call(s32[10,128]{1,0:T(8,128)S(1)} %bitcast.6, bf16[96,1280]{1,0:T(8,128)(2,1)S(1)} %bitcast.5), custom_call_target="tpu_custom_call" | custom-call | tf_op jit(solution)/shard_map/gather/pallas_call | solution.py:237
  2.5 3.1 %collective-permute-start = (bf16[2,32,512]{2,1,0:T(8,128)(2,1)S(1)}, bf16[2,32,512]{2,1,0:T(8,128)(2,1)S(1)}, u32[]{:S(2)}, u32[]{:S(2)}) collective-permute-start(bf16[2,32,512]{2,1,0:T(8,128)(2,1)S(1)} %get-tuple-element.81), channel_id=1, source_target_pairs={{0,2},{1,3},{2,0},{3,1},{4,6},{5,7},{6,4},{7,5},{8,10},{9,11},{10,... | collective-permute-start | bytes 196616 | tf_op jit(solution)/shard_map/ppermute | solution.py:268
  5.6 2.6 %collective-permute-start.2 = (bf16[2,32,512]{2,1,0:T(8,128)(2,1)S(1)}, bf16[2,32,512]{2,1,0:T(8,128)(2,1)S(1)}, u32[]{:S(2)}, u32[]{:S(2)}) collective-permute-start(bf16[2,32,512]{2,1,0:T(8,128)(2,1)S(1)} %get-tuple-element.84), channel_id=1, source_target_pairs={{0,4},{1,5},{2,6},{3,7},{4,0},{5,1},{6,2},{7,3},{8,12},{9,13},{10,... | collective-permute-start | bytes 196616 | tf_op jit(solution)/shard_map/ppermute | solution.py:268
  8.1 0.0 collective-permute-start.3
  8.1 3.7 %fusion.1 = (bf16[32,32,1280]{2,1,0:T(8,128)(2,1)S(1)}, bf16[32,32,1280]{2,1,0:T(8,128)(2,1)S(1)}, bf16[32,32,1280]{2,1,0:T(8,128)(2,1)S(1)}) fusion(bf16[160,32,1280]{2,1,0:T(8,128)(2,1)} %param.5), kind=kLoop, calls=%fused_computation.15 | loop fusion | bytes 15728640 | tf_op jit(solution)/shard_map/slice | solution.py:273
  11.9 0.9 %place.1 = (bf16[1024,256]{1,0:T(8,128)(2,1)S(1)}, s32[160,128]{1,0:T(8,128)S(1)}) custom-call(s32[1280]{0:T(1024)S(1)} %copy-done.1), custom_call_target="tpu_custom_call" | custom-call | tf_op jit(solution)/shard_map/place/pallas_call | solution.py:255
  12.8 0.0 collective-permute-done
  12.8 0.0 collective-permute-done.2
  12.8 1.4 %collective-permute-done.3 = bf16[2,32,512]{2,1,0:T(8,128)(2,1)S(1)} collective-permute-done((bf16[2,32,512]{2,1,0:T(8,128)(2,1)S(1)}, bf16[2,32,512]{2,1,0:T(8,128)(2,1)S(1)}, u32[]{:S(2)}, u32[]{:S(2)}) %collective-permute-start.3) | collective-permute-done | bytes 65568 | tf_op jit(solution)/shard_map/ppermute | solution.py:268
  14.2 0.3 collective-permute-start.6
  14.6 1.3 %collective-permute-start.5 = (bf16[2,32,512]{2,1,0:T(8,128)(2,1)S(1)}, bf16[2,32,512]{2,1,0:T(8,128)(2,1)S(1)}, u32[]{:S(2)}, u32[]{:S(2)}) collective-permute-start(bf16[2,32,512]{2,1,0:T(8,128)(2,1)S(1)} %get-tuple-element.93), channel_id=1, source_target_pairs={{0,1},{1,0},{2,3},{3,2},{4,29},{5,28},{6,31},{7,30},{8,9},{9,8},{1... | collective-permute-start | bytes 196616 | tf_op jit(solution)/shard_map/ppermute | solution.py:287
  15.9 3.3 %collective-permute-start.4 = (bf16[2,32,512]{2,1,0:T(8,128)(2,1)S(1)}, bf16[2,32,512]{2,1,0:T(8,128)(2,1)S(1)}, u32[]{:S(2)}, u32[]{:S(2)}) collective-permute-start(bf16[2,32,512]{2,1,0:T(8,128)(2,1)S(1)} %get-tuple-element.89), channel_id=1, source_target_pairs={{0,24},{1,25},{2,26},{3,27},{4,4},{5,5},{6,6},{7,7},{8,16},{9,17},... | collective-permute-start | bytes 196616 | tf_op jit(solution)/shard_map/ppermute | solution.py:287
  19.1 0.7 %collective-permute-start.1 = (bf16[2,32,512]{2,1,0:T(8,128)(2,1)S(1)}, bf16[2,32,512]{2,1,0:T(8,128)(2,1)S(1)}, u32[]{:S(2)}, u32[]{:S(2)}) collective-permute-start(bf16[2,32,512]{2,1,0:T(8,128)(2,1)S(1)} %get-tuple-element.83), channel_id=1, source_target_pairs={{0,0},{1,1},{2,2},{3,3},{4,28},{5,29},{6,30},{7,31},{8,8},{9,9},{1... | collective-permute-start | bytes 196616 | tf_op jit(solution)/shard_map/ppermute | solution.py:287
  19.8 2.9 %fusion = (bf16[32,32,1280]{2,1,0:T(8,128)(2,1)S(1)}, bf16[32,32,1280]{2,1,0:T(8,128)(2,1)S(1)}) fusion(bf16[160,32,1280]{2,1,0:T(8,128)(2,1)} %param.5), kind=kLoop, calls=%fused_computation.14 | loop fusion | bytes 10485760 | tf_op jit(solution)/shard_map/slice | solution.py:289
  22.7 0.0 collective-permute-done.6.refs_3_
  22.7 0.0 collective-permute-done.5.refs_2_
  22.7 0.0 collective-permute-done.4.refs_1_
  22.7 0.0 collective-permute-done.1.refs_0_
  22.7 1.4 %product.5 = (bf16[480,256]{1,0:T(8,128)(2,1)S(1)}, f32[480,256]{1,0:T(8,128)S(1)}, bf16[480,256]{1,0:T(8,128)(2,1)S(1)}, f32[480,256]{1,0:T(8,128)S(1)}) custom-call(bf16[1024,256]{1,0:T(8,128)(2,1)S(1)} %get-tuple-element.79.place_ref, bf16[32,32,1280]{2,1,0:T(8,128)(2,1)S(1)} %get-tuple-element.111.leg_ref, ...), custom_call_target="tpu_custom_call" | custom-call | bytes 1024 | tf_op jit(solution)/shard_map/product/pallas_call | solution.py:312
  24.2 0.3 collective-permute-start.7
  24.5 0.2 collective-permute-start.9
  24.7 1.0 %collective-permute-done.7 = bf16[480,256]{1,0:T(8,128)(2,1)S(1)} collective-permute-done((bf16[480,256]{1,0:T(8,128)(2,1)S(1)}, bf16[480,256]{1,0:T(8,128)(2,1)S(1)}, u32[]{:S(2)}, u32[]{:S(2)}) %collective-permute-start.7) | collective-permute-done | bytes 245792 | tf_op jit(solution)/shard_map/ppermute | solution.py:306
  25.7 0.1 add_convert_fusion.4
  25.8 1.6 %collective-permute-start.21 = (bf16[480,256]{1,0:T(8,128)(2,1)S(1)}, bf16[480,256]{1,0:T(8,128)(2,1)S(1)}, u32[]{:S(2)}, u32[]{:S(2)}) collective-permute-start(bf16[480,256]{1,0:T(8,128)(2,1)S(1)} %add_convert_fusion.4), channel_id=1, source_target_pairs={{0,16},{8,24},{16,0},{24,8},{1,17},{9,25},{17,1},{25,9},{2,18},{10... | collective-permute-start | bytes 737288 | tf_op jit(solution)/shard_map/ppermute | solution.py:324
  27.4 1.4 %product.6 = (bf16[480,256]{1,0:T(8,128)(2,1)S(1)}, f32[480,256]{1,0:T(8,128)S(1)}, bf16[480,256]{1,0:T(8,128)(2,1)S(1)}, f32[480,256]{1,0:T(8,128)S(1)}) custom-call(bf16[1024,256]{1,0:T(8,128)(2,1)S(1)} %get-tuple-element.79.place_ref, bf16[32,32,1280]{2,1,0:T(8,128)(2,1)S(1)} %get-tuple-element.118.leg_ref, ...), custom_call_target="tpu_custom_call" | custom-call | bytes 1024 | tf_op jit(solution)/shard_map/product/pallas_call | solution.py:312
  28.8 0.1 collective-permute-start.8
  28.9 0.5 collective-permute-start.11
  29.4 0.0 collective-permute-done.9
  29.4 0.9 %collective-permute-done.8 = bf16[480,256]{1,0:T(8,128)(2,1)S(1)} collective-permute-done((bf16[480,256]{1,0:T(8,128)(2,1)S(1)}, bf16[480,256]{1,0:T(8,128)(2,1)S(1)}, u32[]{:S(2)}, u32[]{:S(2)}) %collective-permute-start.8) | collective-permute-done | bytes 245792 | tf_op jit(solution)/shard_map/ppermute | solution.py:306
  30.4 0.1 add_convert_fusion.3
  30.4 0.6 %collective-permute-start.20 = (bf16[480,256]{1,0:T(8,128)(2,1)S(1)}, bf16[480,256]{1,0:T(8,128)(2,1)S(1)}, u32[]{:S(2)}, u32[]{:S(2)}) collective-permute-start(bf16[480,256]{1,0:T(8,128)(2,1)S(1)} %add_convert_fusion.3), channel_id=1, source_target_pairs={{0,16},{8,24},{16,0},{24,8},{1,17},{9,25},{17,1},{25,9},{2,18},{10... | collective-permute-start | bytes 737288 | tf_op jit(solution)/shard_map/ppermute | solution.py:324
  31.0 1.4 %product.7 = (bf16[480,256]{1,0:T(8,128)(2,1)S(1)}, f32[480,256]{1,0:T(8,128)S(1)}, bf16[480,256]{1,0:T(8,128)(2,1)S(1)}, f32[480,256]{1,0:T(8,128)S(1)}) custom-call(bf16[1024,256]{1,0:T(8,128)(2,1)S(1)} %get-tuple-element.79.place_ref, bf16[32,32,1280]{2,1,0:T(8,128)(2,1)S(1)} %get-tuple-element.127.leg_ref, ...), custom_call_target="tpu_custom_call" | custom-call | bytes 1024 | tf_op jit(solution)/shard_map/product/pallas_call | solution.py:312
  32.4 0.1 collective-permute-start.10
  32.5 0.5 collective-permute-start.13
  33.0 1.6 %collective-permute-done.21.far_ref = bf16[480,256]{1,0:T(8,128)(2,1)S(1)} collective-permute-done((bf16[480,256]{1,0:T(8,128)(2,1)S(1)}, bf16[480,256]{1,0:T(8,128)(2,1)S(1)}, u32[]{:S(2)}, u32[]{:S(2)}) %collective-permute-start.21) | collective-permute-done | bytes 245792 | tf_op jit(solution)/shard_map/ppermute | solution.py:324
  34.7 1.0 %final.5.refs_0_ = f32[12,160,320]{2,1,0:T(8,128)} custom-call(s32[160,128]{1,0:T(8,128)S(1)} %get-tuple-element.78.limits_ref, f32[480,256]{1,0:T(8,128)S(1)} %convert_add_fusion.4.near_ref, bf16[480,256]{1,0:T(8,128)(2,1)S(1)} %collective-permute-done.21.far_ref), custom_call_target="tpu_custom_call" | custom-call | bytes 1024 | tf_op jit(solution)/shard_map/final/pallas_call | solution.py:330
  35.7 0.0 collective-permute-done.11
  35.7 0.0 collective-permute-done.10
  35.7 0.1 add_convert_fusion.2
  35.8 1.6 %collective-permute-start.19 = (bf16[480,256]{1,0:T(8,128)(2,1)S(1)}, bf16[480,256]{1,0:T(8,128)(2,1)S(1)}, u32[]{:S(2)}, u32[]{:S(2)}) collective-permute-start(bf16[480,256]{1,0:T(8,128)(2,1)S(1)} %add_convert_fusion.2), channel_id=1, source_target_pairs={{0,16},{8,24},{16,0},{24,8},{1,17},{9,25},{17,1},{25,9},{2,18},{10... | collective-permute-start | bytes 737288 | tf_op jit(solution)/shard_map/ppermute | solution.py:324
  37.4 1.4 %product.8 = (bf16[480,256]{1,0:T(8,128)(2,1)S(1)}, f32[480,256]{1,0:T(8,128)S(1)}, bf16[480,256]{1,0:T(8,128)(2,1)S(1)}, f32[480,256]{1,0:T(8,128)S(1)}) custom-call(bf16[1024,256]{1,0:T(8,128)(2,1)S(1)} %get-tuple-element.79.place_ref, bf16[32,32,1280]{2,1,0:T(8,128)(2,1)S(1)} %get-tuple-element.136.leg_ref, ...), custom_call_target="tpu_custom_call" | custom-call | bytes 1024 | tf_op jit(solution)/shard_map/product/pallas_call | solution.py:312
  38.8 0.1 collective-permute-start.12
  38.9 0.5 collective-permute-start.17
  39.4 0.5 collective-permute-done.20.far_ref
  39.9 1.0 %final.6.refs_0_ = f32[12,160,320]{2,1,0:T(8,128)} custom-call(s32[160,128]{1,0:T(8,128)S(1)} %get-tuple-element.78.limits_ref, f32[480,256]{1,0:T(8,128)S(1)} %convert_add_fusion.3.near_ref, bf16[480,256]{1,0:T(8,128)(2,1)S(1)} %collective-permute-done.20.far_ref, f32[12,160,320]{2,1,0:T(8,128)} %final.5.refs_0_), custom_call_target="tpu_custom_call", output_to_operand_aliasing={{}: (3, {})} | custom-call | bytes 1024 | tf_op jit(solution)/shard_map/final/pallas_call | solution.py:330
  41.0 0.0 collective-permute-done.12
  41.0 0.1 add_convert_fusion.1
  41.1 1.6 %collective-permute-start.18 = (bf16[480,256]{1,0:T(8,128)(2,1)S(1)}, bf16[480,256]{1,0:T(8,128)(2,1)S(1)}, u32[]{:S(2)}, u32[]{:S(2)}) collective-permute-start(bf16[480,256]{1,0:T(8,128)(2,1)S(1)} %add_convert_fusion.1), channel_id=1, source_target_pairs={{0,16},{8,24},{16,0},{24,8},{1,17},{9,25},{17,1},{25,9},{2,18},{10... | collective-permute-start | bytes 737288 | tf_op jit(solution)/shard_map/ppermute | solution.py:324
  42.7 1.4 %product.9 = (bf16[480,256]{1,0:T(8,128)(2,1)S(1)}, f32[480,256]{1,0:T(8,128)S(1)}, bf16[480,256]{1,0:T(8,128)(2,1)S(1)}, f32[480,256]{1,0:T(8,128)S(1)}) custom-call(bf16[1024,256]{1,0:T(8,128)(2,1)S(1)} %get-tuple-element.79.place_ref, bf16[32,32,1280]{2,1,0:T(8,128)(2,1)S(1)} %get-tuple-element.102.leg_ref, ...), custom_call_target="tpu_custom_call" | custom-call | bytes 1024 | tf_op jit(solution)/shard_map/product/pallas_call | solution.py:312
  44.1 0.1 collective-permute-start.14
  44.2 0.5 collective-permute-start.15
  44.7 0.5 collective-permute-done.19.far_ref
  45.2 1.0 %final.7.refs_0_ = f32[12,160,320]{2,1,0:T(8,128)} custom-call(s32[160,128]{1,0:T(8,128)S(1)} %get-tuple-element.78.limits_ref, f32[480,256]{1,0:T(8,128)S(1)} %convert_add_fusion.2.near_ref, bf16[480,256]{1,0:T(8,128)(2,1)S(1)} %collective-permute-done.19.far_ref, f32[12,160,320]{2,1,0:T(8,128)} %final.6.refs_0_), custom_call_target="tpu_custom_call", output_to_operand_aliasing={{}: (3, {})} | custom-call | bytes 1024 | tf_op jit(solution)/shard_map/final/pallas_call | solution.py:330
  46.2 0.0 collective-permute-done.17
  46.3 0.1 add_convert_fusion
  46.3 1.6 %collective-permute-start.16 = (bf16[480,256]{1,0:T(8,128)(2,1)S(1)}, bf16[480,256]{1,0:T(8,128)(2,1)S(1)}, u32[]{:S(2)}, u32[]{:S(2)}) collective-permute-start(bf16[480,256]{1,0:T(8,128)(2,1)S(1)} %add_convert_fusion), channel_id=1, source_target_pairs={{0,16},{8,24},{16,0},{24,8},{1,17},{9,25},{17,1},{25,9},{2,18},{10... | collective-permute-start | bytes 737288 | tf_op jit(solution)/shard_map/ppermute | solution.py:324
  47.9 2.5 %collective-permute-done.18.far_ref = bf16[480,256]{1,0:T(8,128)(2,1)S(1)} collective-permute-done((bf16[480,256]{1,0:T(8,128)(2,1)S(1)}, bf16[480,256]{1,0:T(8,128)(2,1)S(1)}, u32[]{:S(2)}, u32[]{:S(2)}) %collective-permute-start.18) | collective-permute-done | bytes 245792 | tf_op jit(solution)/shard_map/ppermute | solution.py:324
  50.5 1.0 %final.8.refs_0_ = f32[12,160,320]{2,1,0:T(8,128)} custom-call(s32[160,128]{1,0:T(8,128)S(1)} %get-tuple-element.78.limits_ref, f32[480,256]{1,0:T(8,128)S(1)} %convert_add_fusion.near_ref, bf16[480,256]{1,0:T(8,128)(2,1)S(1)} %collective-permute-done.18.far_ref, f32[12,160,320]{2,1,0:T(8,128)} %final.7.refs_0_), custom_call_target="tpu_custom_call", output_to_operand_aliasing={{}: (3, {})} | custom-call | bytes 1024 | tf_op jit(solution)/shard_map/final/pallas_call | solution.py:330
  51.5 0.0 collective-permute-done.14
  51.5 0.1 convert_add_fusion.1.near_ref
  51.5 3.5 %collective-permute-done.16.far_ref = bf16[480,256]{1,0:T(8,128)(2,1)S(1)} collective-permute-done((bf16[480,256]{1,0:T(8,128)(2,1)S(1)}, bf16[480,256]{1,0:T(8,128)(2,1)S(1)}, u32[]{:S(2)}, u32[]{:S(2)}) %collective-permute-start.16) | collective-permute-done | bytes 245792 | tf_op jit(solution)/shard_map/ppermute | solution.py:324
  55.1 1.0 %final.9 = f32[12,160,320]{2,1,0:T(8,128)} custom-call(s32[160,128]{1,0:T(8,128)S(1)} %get-tuple-element.78.limits_ref, f32[480,256]{1,0:T(8,128)S(1)} %convert_add_fusion.1.near_ref, bf16[480,256]{1,0:T(8,128)(2,1)S(1)} %collective-permute-done.16.far_ref, f32[12,160,320]{2,1,0:T(8,128)} %final.8.refs_0_), custom_call_target="tpu_custom_call", output_to_operand_aliasing={{}: (3, {})} | custom-call | bytes 1024 | tf_op jit(solution)/shard_map/final/pallas_call | solution.py:330
  (14 shorter events, 0.3 us)
Async XLA Ops:
  0.0 0.9 %copy-start = (bf16[8,12,1280]{2,0,1:T(8,128)(2,1)S(1)}, bf16[8,12,1280]{2,0,1:T(8,128)(2,1)}, u32[]{:S(2)}) copy-start(bf16[8,12,1280]{2,0,1:T(8,128)(2,1)} %param.3) | copy-start | bytes 737284
  0.9 0.7 %copy-start.1 = (s32[1280]{0:T(1024)S(1)}, s32[1280]{0:T(1024)}, u32[]{:S(2)}) copy-start(s32[1280]{0:T(1024)} %table_ref.1) | copy-start | bytes 15364
  2.5 10.3 %collective-permute-start = (bf16[2,32,512]{2,1,0:T(8,128)(2,1)S(1)}, bf16[2,32,512]{2,1,0:T(8,128)(2,1)S(1)}, u32[]{:S(2)}, u32[]{:S(2)}) collective-permute-start(bf16[2,32,512]{2,1,0:T(8,128)(2,1)S(1)} %get-tuple-element.81), channel_id=1, source_target_pairs={{0,2},{1,3},{2,0},{3,1},{4,6},{5,7},{6,4},{7,5},{8,10},{9,11},{10,... | collective-permute-start | bytes 196616 | tf_op jit(solution)/shard_map/ppermute | solution.py:268
  5.6 7.3 %collective-permute-start.2 = (bf16[2,32,512]{2,1,0:T(8,128)(2,1)S(1)}, bf16[2,32,512]{2,1,0:T(8,128)(2,1)S(1)}, u32[]{:S(2)}, u32[]{:S(2)}) collective-permute-start(bf16[2,32,512]{2,1,0:T(8,128)(2,1)S(1)} %get-tuple-element.84), channel_id=1, source_target_pairs={{0,4},{1,5},{2,6},{3,7},{4,0},{5,1},{6,2},{7,3},{8,12},{9,13},{10,... | collective-permute-start | bytes 196616 | tf_op jit(solution)/shard_map/ppermute | solution.py:268
  8.1 6.1 %collective-permute-start.3 = (bf16[2,32,512]{2,1,0:T(8,128)(2,1)S(1)}, bf16[2,32,512]{2,1,0:T(8,128)(2,1)S(1)}, u32[]{:S(2)}, u32[]{:S(2)}) collective-permute-start(bf16[2,32,512]{2,1,0:T(8,128)(2,1)S(1)} %get-tuple-element.85), channel_id=1, source_target_pairs={{0,6},{1,7},{2,4},{3,5},{4,2},{5,3},{6,0},{7,1},{8,14},{9,15},{10,... | collective-permute-start | bytes 196616 | tf_op jit(solution)/shard_map/ppermute | solution.py:268
  14.2 8.5 %collective-permute-start.6 = (bf16[2,32,512]{2,1,0:T(8,128)(2,1)S(1)}, bf16[2,32,512]{2,1,0:T(8,128)(2,1)S(1)}, u32[]{:S(2)}, u32[]{:S(2)}) collective-permute-start(bf16[2,32,512]{2,1,0:T(8,128)(2,1)S(1)} %get-tuple-element.97), channel_id=1, source_target_pairs={{0,25},{1,24},{2,27},{3,26},{4,5},{5,4},{6,7},{7,6},{8,17},{9,16},... | collective-permute-start | bytes 196616 | tf_op jit(solution)/shard_map/ppermute | solution.py:287
  14.6 8.1 %collective-permute-start.5 = (bf16[2,32,512]{2,1,0:T(8,128)(2,1)S(1)}, bf16[2,32,512]{2,1,0:T(8,128)(2,1)S(1)}, u32[]{:S(2)}, u32[]{:S(2)}) collective-permute-start(bf16[2,32,512]{2,1,0:T(8,128)(2,1)S(1)} %get-tuple-element.93), channel_id=1, source_target_pairs={{0,1},{1,0},{2,3},{3,2},{4,29},{5,28},{6,31},{7,30},{8,9},{9,8},{1... | collective-permute-start | bytes 196616 | tf_op jit(solution)/shard_map/ppermute | solution.py:287
  15.9 6.8 %collective-permute-start.4 = (bf16[2,32,512]{2,1,0:T(8,128)(2,1)S(1)}, bf16[2,32,512]{2,1,0:T(8,128)(2,1)S(1)}, u32[]{:S(2)}, u32[]{:S(2)}) collective-permute-start(bf16[2,32,512]{2,1,0:T(8,128)(2,1)S(1)} %get-tuple-element.89), channel_id=1, source_target_pairs={{0,24},{1,25},{2,26},{3,27},{4,4},{5,5},{6,6},{7,7},{8,16},{9,17},... | collective-permute-start | bytes 196616 | tf_op jit(solution)/shard_map/ppermute | solution.py:287
  19.1 3.6 %collective-permute-start.1 = (bf16[2,32,512]{2,1,0:T(8,128)(2,1)S(1)}, bf16[2,32,512]{2,1,0:T(8,128)(2,1)S(1)}, u32[]{:S(2)}, u32[]{:S(2)}) collective-permute-start(bf16[2,32,512]{2,1,0:T(8,128)(2,1)S(1)} %get-tuple-element.83), channel_id=1, source_target_pairs={{0,0},{1,1},{2,2},{3,3},{4,28},{5,29},{6,30},{7,31},{8,8},{9,9},{1... | collective-permute-start | bytes 196616 | tf_op jit(solution)/shard_map/ppermute | solution.py:287
  24.2 1.6 %collective-permute-start.7 = (bf16[480,256]{1,0:T(8,128)(2,1)S(1)}, bf16[480,256]{1,0:T(8,128)(2,1)S(1)}, u32[]{:S(2)}, u32[]{:S(2)}) collective-permute-start(bf16[480,256]{1,0:T(8,128)(2,1)S(1)} %get-tuple-element.113), channel_id=1, source_target_pairs={{0,8},{8,0},{16,24},{24,16},{1,9},{9,1},{17,25},{25,17},{2,10},{10... | collective-permute-start | bytes 737288 | tf_op jit(solution)/shard_map/ppermute | solution.py:306
  24.5 4.9 %collective-permute-start.9 = (bf16[480,256]{1,0:T(8,128)(2,1)S(1)}, bf16[480,256]{1,0:T(8,128)(2,1)S(1)}, u32[]{:S(2)}, u32[]{:S(2)}) collective-permute-start(bf16[480,256]{1,0:T(8,128)(2,1)S(1)} %get-tuple-element.122), channel_id=1, source_target_pairs={{0,8},{8,0},{16,24},{24,16},{1,9},{9,1},{17,25},{25,17},{2,10},{10... | collective-permute-start | bytes 737288 | tf_op jit(solution)/shard_map/ppermute | solution.py:306
  25.8 8.9 %collective-permute-start.21 = (bf16[480,256]{1,0:T(8,128)(2,1)S(1)}, bf16[480,256]{1,0:T(8,128)(2,1)S(1)}, u32[]{:S(2)}, u32[]{:S(2)}) collective-permute-start(bf16[480,256]{1,0:T(8,128)(2,1)S(1)} %add_convert_fusion.4), channel_id=1, source_target_pairs={{0,16},{8,24},{16,0},{24,8},{1,17},{9,25},{17,1},{25,9},{2,18},{10... | collective-permute-start | bytes 737288 | tf_op jit(solution)/shard_map/ppermute | solution.py:324
  28.8 1.6 %collective-permute-start.8 = (bf16[480,256]{1,0:T(8,128)(2,1)S(1)}, bf16[480,256]{1,0:T(8,128)(2,1)S(1)}, u32[]{:S(2)}, u32[]{:S(2)}) collective-permute-start(bf16[480,256]{1,0:T(8,128)(2,1)S(1)} %get-tuple-element.120), channel_id=1, source_target_pairs={{0,8},{8,0},{16,24},{24,16},{1,9},{9,1},{17,25},{25,17},{2,10},{10... | collective-permute-start | bytes 737288 | tf_op jit(solution)/shard_map/ppermute | solution.py:306
  28.9 6.8 %collective-permute-start.11 = (bf16[480,256]{1,0:T(8,128)(2,1)S(1)}, bf16[480,256]{1,0:T(8,128)(2,1)S(1)}, u32[]{:S(2)}, u32[]{:S(2)}) collective-permute-start(bf16[480,256]{1,0:T(8,128)(2,1)S(1)} %get-tuple-element.131), channel_id=1, source_target_pairs={{0,8},{8,0},{16,24},{24,16},{1,9},{9,1},{17,25},{25,17},{2,10},{10... | collective-permute-start | bytes 737288 | tf_op jit(solution)/shard_map/ppermute | solution.py:306
  30.4 9.5 %collective-permute-start.20 = (bf16[480,256]{1,0:T(8,128)(2,1)S(1)}, bf16[480,256]{1,0:T(8,128)(2,1)S(1)}, u32[]{:S(2)}, u32[]{:S(2)}) collective-permute-start(bf16[480,256]{1,0:T(8,128)(2,1)S(1)} %add_convert_fusion.3), channel_id=1, source_target_pairs={{0,16},{8,24},{16,0},{24,8},{1,17},{9,25},{17,1},{25,9},{2,18},{10... | collective-permute-start | bytes 737288 | tf_op jit(solution)/shard_map/ppermute | solution.py:324
  32.4 3.3 %collective-permute-start.10 = (bf16[480,256]{1,0:T(8,128)(2,1)S(1)}, bf16[480,256]{1,0:T(8,128)(2,1)S(1)}, u32[]{:S(2)}, u32[]{:S(2)}) collective-permute-start(bf16[480,256]{1,0:T(8,128)(2,1)S(1)} %get-tuple-element.129), channel_id=1, source_target_pairs={{0,8},{8,0},{16,24},{24,16},{1,9},{9,1},{17,25},{25,17},{2,10},{10... | collective-permute-start | bytes 737288 | tf_op jit(solution)/shard_map/ppermute | solution.py:306
  32.5 8.4 %collective-permute-start.13 = (bf16[480,256]{1,0:T(8,128)(2,1)S(1)}, bf16[480,256]{1,0:T(8,128)(2,1)S(1)}, u32[]{:S(2)}, u32[]{:S(2)}) collective-permute-start(bf16[480,256]{1,0:T(8,128)(2,1)S(1)} %get-tuple-element.140), channel_id=1, source_target_pairs={{0,8},{8,0},{16,24},{24,16},{1,9},{9,1},{17,25},{25,17},{2,10},{10... | collective-permute-start | bytes 737288 | tf_op jit(solution)/shard_map/ppermute | solution.py:306
  35.8 9.4 %collective-permute-start.19 = (bf16[480,256]{1,0:T(8,128)(2,1)S(1)}, bf16[480,256]{1,0:T(8,128)(2,1)S(1)}, u32[]{:S(2)}, u32[]{:S(2)}) collective-permute-start(bf16[480,256]{1,0:T(8,128)(2,1)S(1)} %add_convert_fusion.2), channel_id=1, source_target_pairs={{0,16},{8,24},{16,0},{24,8},{1,17},{9,25},{17,1},{25,9},{2,18},{10... | collective-permute-start | bytes 737288 | tf_op jit(solution)/shard_map/ppermute | solution.py:324
  38.8 2.2 %collective-permute-start.12 = (bf16[480,256]{1,0:T(8,128)(2,1)S(1)}, bf16[480,256]{1,0:T(8,128)(2,1)S(1)}, u32[]{:S(2)}, u32[]{:S(2)}) collective-permute-start(bf16[480,256]{1,0:T(8,128)(2,1)S(1)} %get-tuple-element.138), channel_id=1, source_target_pairs={{0,8},{8,0},{16,24},{24,16},{1,9},{9,1},{17,25},{25,17},{2,10},{10... | collective-permute-start | bytes 737288 | tf_op jit(solution)/shard_map/ppermute | solution.py:306
  38.9 7.3 %collective-permute-start.17 = (bf16[480,256]{1,0:T(8,128)(2,1)S(1)}, bf16[480,256]{1,0:T(8,128)(2,1)S(1)}, u32[]{:S(2)}, u32[]{:S(2)}) collective-permute-start(bf16[480,256]{1,0:T(8,128)(2,1)S(1)} %get-tuple-element.150), channel_id=1, source_target_pairs={{0,8},{8,0},{16,24},{24,16},{1,9},{9,1},{17,25},{25,17},{2,10},{10... | collective-permute-start | bytes 737288 | tf_op jit(solution)/shard_map/ppermute | solution.py:306
  41.1 9.4 %collective-permute-start.18 = (bf16[480,256]{1,0:T(8,128)(2,1)S(1)}, bf16[480,256]{1,0:T(8,128)(2,1)S(1)}, u32[]{:S(2)}, u32[]{:S(2)}) collective-permute-start(bf16[480,256]{1,0:T(8,128)(2,1)S(1)} %add_convert_fusion.1), channel_id=1, source_target_pairs={{0,16},{8,24},{16,0},{24,8},{1,17},{9,25},{17,1},{25,9},{2,18},{10... | collective-permute-start | bytes 737288 | tf_op jit(solution)/shard_map/ppermute | solution.py:324
  44.1 7.4 %collective-permute-start.14 = (bf16[480,256]{1,0:T(8,128)(2,1)S(1)}, bf16[480,256]{1,0:T(8,128)(2,1)S(1)}, u32[]{:S(2)}, u32[]{:S(2)}) collective-permute-start(bf16[480,256]{1,0:T(8,128)(2,1)S(1)} %get-tuple-element.146), channel_id=1, source_target_pairs={{0,8},{8,0},{16,24},{24,16},{1,9},{9,1},{17,25},{25,17},{2,10},{10... | collective-permute-start | bytes 737288 | tf_op jit(solution)/shard_map/ppermute | solution.py:306
  44.2 2.1 %collective-permute-start.15 = (bf16[480,256]{1,0:T(8,128)(2,1)S(1)}, bf16[480,256]{1,0:T(8,128)(2,1)S(1)}, u32[]{:S(2)}, u32[]{:S(2)}) collective-permute-start(bf16[480,256]{1,0:T(8,128)(2,1)S(1)} %get-tuple-element.148), channel_id=1, source_target_pairs={{0,8},{8,0},{16,24},{24,16},{1,9},{9,1},{17,25},{25,17},{2,10},{10... | collective-permute-start | bytes 737288 | tf_op jit(solution)/shard_map/ppermute | solution.py:306
  46.3 8.7 %collective-permute-start.16 = (bf16[480,256]{1,0:T(8,128)(2,1)S(1)}, bf16[480,256]{1,0:T(8,128)(2,1)S(1)}, u32[]{:S(2)}, u32[]{:S(2)}) collective-permute-start(bf16[480,256]{1,0:T(8,128)(2,1)S(1)} %add_convert_fusion), channel_id=1, source_target_pairs={{0,16},{8,24},{16,0},{24,8},{1,17},{9,25},{17,1},{25,9},{2,18},{10... | collective-permute-start | bytes 737288 | tf_op jit(solution)/shard_map/ppermute | solution.py:324

commit v8 on v5

--- a/solution.py
+++ b/solution.py
@@ -92,16 +92,19 @@
                 out[u, :, k * LANES : (k + 1) * LANES] = tile.astype(jnp.bfloat16)
 
 
-def place_kernel(turns, lat_count, row_count, pairs, degrees, table_ref, leg_ref, out, limits):
+def touch_kernel(leg_ref, out):
+    out[...] = leg_ref[0, : out.shape[0], : out.shape[1]]
+
+
+def place_kernel(turns, lat_count, row_count, pairs, degrees, table_ref, token_ref, out, limits):
     northern = lax.axis_index("lat") < lat_count // 2
     me = lax.axis_index("wave")
     row = lax.broadcasted_iota(jnp.int32, (LANES, 2 * LANES), 0) & (row_count - 1)
     col = lax.broadcasted_iota(jnp.int32, (LANES, 2 * LANES), 1) & (pairs - 1 | LANES)
-    half = len(turns) // 2
-    for k, turn in enumerate(turns):
-        source = me ^ turn
-        ascending = (source < half) == northern
-        position = (source % half) * row_count + row
+    half = len(turns)
+    for k in range(2 * half):
+        ascending = northern if k < half else jnp.logical_not(northern)
+        position = ((me ^ turns[k % half]) % half) * row_count + row
         position = jnp.where(ascending, position, pairs - 1 - position)
         target = position + jnp.where(ascending, 0, LANES)
         out[k * LANES : (k + 1) * LANES, :] = (col == target).astype(jnp.bfloat16)
@@ -247,40 +250,49 @@
         wave_table.reshape(-1, LANES),
         jnp.transpose(fourier, (1, 0, 2)).reshape(used, waves),
     )
-    turns = [
-        t * low + u
-        for u in range(low)
-        for side in (0, 1)
-        for t in range(side * high // 2, (side + 1) * high // 2)
+    token = pl.pallas_call(
+        touch_kernel,
+        out_shape=jax.ShapeDtypeStruct((2 * TILE, LANES), legendre.dtype),
+        in_specs=[whole],
+        out_specs=whole,
+        compiler_params=params,
+        name="touch",
+    )(legendre)
+    turns = [t * low + u for u in range(low) for t in range(high // 2)]
+    passed = [ordered[0]] + [
+        lax.ppermute(ordered[t], "wave", [(w, w ^ t * low) for w in range(wave_count)])
+        for t in range(1, high)
     ]
+    lower = lax.axis_index("wave") < wave_count // 2
+    sources = []
+    for mirrored in (False, True):
+        for u in range(low):
+            sides = [
+                jnp.stack([passed[t][u] for t in range(side * high // 2, (side + 1) * high // 2)])
+                for side in (0, 1)
+            ]
+            block = jnp.where(lower != mirrored, sides[0], sides[1])
+            block, token = lax.optimization_barrier((block, token))
+            route = []
+            for lat in range(lat_count):
+                for wave in range(wave_count):
+                    to = lat_count - 1 - lat if mirrored else lat
+                    route.append((lat * wave_count + wave, to * wave_count + (wave ^ u)))
+            if mirrored or u:
+                block = lax.ppermute(block, ("lat", "wave"), route)
+            sources.append(block)
+
     place, limits = pl.pallas_call(
         functools.partial(place_kernel, turns, lat_count, row_count, pairs, degrees),
         out_shape=[
             jax.ShapeDtypeStruct((wave_count * LANES, 2 * LANES), jnp.bfloat16),
             jax.ShapeDtypeStruct((slots, LANES), jnp.int32),
         ],
-        in_specs=[pl.BlockSpec(memory_space=pltpu.SMEM), anywhere],
+        in_specs=[pl.BlockSpec(memory_space=pltpu.SMEM), whole],
         out_specs=[whole] * 2,
         compiler_params=params,
         name="place",
-    )(wave_table, legendre)
-
-    passed = [ordered[0]] + [
-        lax.ppermute(ordered[t], "wave", [(w, w ^ t * low) for w in range(wave_count)])
-        for t in range(1, high)
-    ]
-    sources = []
-    for u in range(low):
-        for side in (0, 1):
-            block = jnp.stack([passed[t][u] for t in range(side * high // 2, (side + 1) * high // 2)])
-            route = []
-            for lat in range(lat_count):
-                for wave in range(wave_count):
-                    began = (wave >= wave_count // 2) != (side == 1)
-                    to = lat_count - 1 - lat if began else lat
-                    route.append((lat * wave_count + wave, to * wave_count + (wave ^ u)))
-            block, place = lax.optimization_barrier((block, place))
-            sources.append(lax.ppermute(block, ("lat", "wave"), route))
+    )(wave_table, token)
 
     rows = STEP * cols
     shape = (rows + rows // 4, 2 * LANES)

time: 56 us -> 59.4 us (1.061)
  local copies, waits for them, and re-layouts: 6.39 us -> 11.1 us
  starting transfers between devices: 21.8 us -> 19.8 us
  waiting for transfers between devices: 12.9 us -> 13.6 us
    unnamed x8 -> x18, local copies, waits for them, and re-layouts: 6.36 us -> 11.1 us
    ppermute x4 -> x3, starting transfers between devices: 5.55 us -> 3.27 us  [packed(): block = lax.ppermute(block, ('lat', 'wave'), route)]
    ppermute x5, waiting for transfers between devices: 8.41 us -> 7.12 us  [packed(): crossed.append(lax.ppermute(summed, 'lat', y_route))]
    ppermute x4 -> x3, waiting for transfers between devices: 1.76 us -> 2.84 us  [packed(): block = lax.ppermute(block, ('lat', 'wave'), route)]
    ppermute x5, starting transfers between devices: 6.99 us -> 8.05 us  [packed(): crossed.append(lax.ppermute(summed, 'lat', y_route))]
    ppermute x3, waiting for transfers between devices: 0.35 us -> 1.29 us  [packed(): lax.ppermute(ordered[t], 'wave', [(w, w ^ t * low) for w in range(wave_co...]
    ppermute x10, starting transfers between devices: 3.53 us -> 2.84 us  [settle(): return kept + lax.ppermute(sent, 'lat', core_route).astype(jnp.float32)]
  transfers between devices with their start and end apart: 22 -> 21, of which waited for: 10 -> 11; matrix products, arithmetic and copies ran while one was open for 1% -> 1% of each run, Pallas kernels for 19% -> 18%
where the time goes in v8:
time: 59.4 us; the launch traced here: 59.2 us
  starting transfers between devices  19.8 us (33%)
  Pallas kernels  13.8 us (23%)
  waiting for transfers between devices  13.6 us (23%)
  local copies, waits for them, and re-layouts  11.1 us (19%)
    unnamed x18, local copies, waits for them, and re-layouts  11.1 us
    ppermute x5, starting transfers between devices, packed(): crossed.append(lax.ppermute(summed, 'lat', y_route))  8.05 us
    ppermute x5, waiting for transfers between devices, packed(): crossed.append(lax.ppermute(summed, 'lat', y_route))  7.12 us
    pallas_call x5, Pallas kernels, packed(): pl.pallas_call(functools.partial(product_kernel, block, row_count, cols),...  7.09 us
    ppermute x3, starting transfers between devices, packed(): lax.ppermute(ordered[t], 'wave', [(w, w ^ t * low) for w in range(wave_co...  5.68 us
    pallas_call x5, Pallas kernels, packed(): pl.pallas_call(functools.partial(final_kernel, block * STEP, degrees, col...  5.06 us
    ppermute x3, starting transfers between devices, packed(): block = lax.ppermute(block, ('lat', 'wave'), route)  3.27 us
    ppermute x3, waiting for transfers between devices, packed(): block = lax.ppermute(block, ('lat', 'wave'), route)  2.84 us
  transfers between devices with their start and end apart: 21, of which 11 were waited for; matrix products, arithmetic and copies ran while one was open for 1% of the time, Pallas kernels for 18%

profile of v8, /device:TPU:0, one launch (start us, length us, event | category | flops | bytes accessed | tf_op | source)
XLA Modules:
  0.0 59.2 jit_solution(2646832314900280589)
XLA Ops:
  0.0 0.9 %copy-done.2 = bf16[8,12,1280]{2,0,1:T(8,128)(2,1)S(1)} copy-done((bf16[8,12,1280]{2,0,1:T(8,128)(2,1)S(1)}, bf16[8,12,1280]{2,0,1:T(8,128)(2,1)}, u32[]{:S(2)}) %copy-start.2) | copy-done | bytes 245784
  0.9 0.7 %copy-done.3 = s32[1280]{0:T(1024)S(1)} copy-done((s32[1280]{0:T(1024)S(1)}, s32[1280]{0:T(1024)}, u32[]{:S(2)}) %copy-start.3) | copy-done | bytes 5144
  1.6 0.8 %gather.1 = (bf16[2,32,512]{2,1,0:T(8,128)(2,1)S(1)}, bf16[2,32,512]{2,1,0:T(8,128)(2,1)S(1)}, bf16[2,32,512]{2,1,0:T(8,128)(2,1)S(1)}, bf16[2,32,512]{2,1,0:T(8,128)(2,1)S(1)}) custom-call(s32[10,128]{1,0:T(8,128)S(1)} %bitcast.8, bf16[96,1280]{1,0:T(8,128)(2,1)S(1)} %bitcast.7), custom_call_target="tpu_custom_call" | custom-call | tf_op jit(solution)/shard_map/gather/pallas_call | solution.py:241
  2.5 3.1 %collective-permute-start = (bf16[2,32,512]{2,1,0:T(8,128)(2,1)S(1)}, bf16[2,32,512]{2,1,0:T(8,128)(2,1)S(1)}, u32[]{:S(2)}, u32[]{:S(2)}) collective-permute-start(bf16[2,32,512]{2,1,0:T(8,128)(2,1)S(1)} %get-tuple-element.60), channel_id=1, source_target_pairs={{0,2},{1,3},{2,0},{3,1},{4,6},{5,7},{6,4},{7,5},{8,10},{9,11},{10,... | collective-permute-start | bytes 196616 | tf_op jit(solution)/shard_map/ppermute | solution.py:263
  5.6 2.6 %collective-permute-start.1 = (bf16[2,32,512]{2,1,0:T(8,128)(2,1)S(1)}, bf16[2,32,512]{2,1,0:T(8,128)(2,1)S(1)}, u32[]{:S(2)}, u32[]{:S(2)}) collective-permute-start(bf16[2,32,512]{2,1,0:T(8,128)(2,1)S(1)} %get-tuple-element.61), channel_id=1, source_target_pairs={{0,4},{1,5},{2,6},{3,7},{4,0},{5,1},{6,2},{7,3},{8,12},{9,13},{10,... | collective-permute-start | bytes 196616 | tf_op jit(solution)/shard_map/ppermute | solution.py:263
  8.1 0.0 collective-permute-start.2
  8.2 0.0 copy-start
  8.2 4.7 %copy-done = bf16[160,32,1280]{2,1,0:T(8,128)(2,1)S(1)} copy-done((bf16[160,32,1280]{2,1,0:T(8,128)(2,1)S(1)}, bf16[160,32,1280]{2,1,0:T(8,128)(2,1)}, u32[]{:S(2)}) %copy-start) | copy-done | bytes 13107224
  12.9 0.0 collective-permute-done
  12.9 0.0 collective-permute-done.1
  12.9 1.3 %collective-permute-done.2 = bf16[2,32,512]{2,1,0:T(8,128)(2,1)S(1)} collective-permute-done((bf16[2,32,512]{2,1,0:T(8,128)(2,1)S(1)}, bf16[2,32,512]{2,1,0:T(8,128)(2,1)S(1)}, u32[]{:S(2)}, u32[]{:S(2)}) %collective-permute-start.2) | collective-permute-done | bytes 65568 | tf_op jit(solution)/shard_map/ppermute | solution.py:263
  14.2 0.3 collective-permute-start.5
  14.6 2.4 %collective-permute-start.4 = (bf16[2,32,512]{2,1,0:T(8,128)(2,1)S(1)}, bf16[2,32,512]{2,1,0:T(8,128)(2,1)S(1)}, u32[]{:S(2)}, u32[]{:S(2)}) collective-permute-start(bf16[2,32,512]{2,1,0:T(8,128)(2,1)S(1)} %get-tuple-element.71), channel_id=1, source_target_pairs={{0,24},{1,25},{2,26},{3,27},{4,28},{5,29},{6,30},{7,31},{8,16},{9,... | collective-permute-start | bytes 196616 | tf_op jit(solution)/shard_map/ppermute | solution.py:282
  17.0 0.5 collective-permute-start.3
  17.5 0.9 %place.1 = (bf16[1024,256]{1,0:T(8,128)(2,1)S(1)}, s32[160,128]{1,0:T(8,128)S(1)}) custom-call(s32[1280]{0:T(1024)S(1)} %copy-done.4, bf16[16,128]{1,0:T(8,128)(2,1)S(1)} %touch.1.token_ref), custom_call_target="tpu_custom_call" | custom-call | tf_op jit(solution)/shard_map/place/pallas_call | solution.py:285
  18.4 1.2 %collective-permute-done.5.refs_3_ = bf16[2,32,512]{2,1,0:T(8,128)(2,1)S(1)} collective-permute-done((bf16[2,32,512]{2,1,0:T(8,128)(2,1)S(1)}, bf16[2,32,512]{2,1,0:T(8,128)(2,1)S(1)}, u32[]{:S(2)}, u32[]{:S(2)}) %collective-permute-start.5) | collective-permute-done | bytes 65568 | tf_op jit(solution)/shard_map/ppermute | solution.py:282
  19.6 0.9 %collective-permute-done.4.refs_2_ = bf16[2,32,512]{2,1,0:T(8,128)(2,1)S(1)} collective-permute-done((bf16[2,32,512]{2,1,0:T(8,128)(2,1)S(1)}, bf16[2,32,512]{2,1,0:T(8,128)(2,1)S(1)}, u32[]{:S(2)}, u32[]{:S(2)}) %collective-permute-start.4) | collective-permute-done | bytes 65568 | tf_op jit(solution)/shard_map/ppermute | solution.py:282
  20.5 0.7 %collective-permute-done.3.refs_1_ = bf16[2,32,512]{2,1,0:T(8,128)(2,1)S(1)} collective-permute-done((bf16[2,32,512]{2,1,0:T(8,128)(2,1)S(1)}, bf16[2,32,512]{2,1,0:T(8,128)(2,1)S(1)}, u32[]{:S(2)}, u32[]{:S(2)}) %collective-permute-start.3) | collective-permute-done | bytes 65568 | tf_op jit(solution)/shard_map/ppermute | solution.py:282
  21.3 4.7 %copy-done.1 = bf16[160,32,1280]{2,1,0:T(8,128)(2,1)S(1)} copy-done((bf16[160,32,1280]{2,1,0:T(8,128)(2,1)S(1)}, bf16[160,32,1280]{2,1,0:T(8,128)(2,1)}, u32[]{:S(2)}) %copy-start.1) | copy-done | bytes 13107224
  26.0 1.4 %product.5 = (bf16[480,256]{1,0:T(8,128)(2,1)S(1)}, f32[480,256]{1,0:T(8,128)S(1)}, bf16[480,256]{1,0:T(8,128)(2,1)S(1)}, f32[480,256]{1,0:T(8,128)S(1)}) custom-call(bf16[1024,256]{1,0:T(8,128)(2,1)S(1)} %get-tuple-element.68.place_ref, bf16[160,32,1280]{2,1,0:T(8,128)(2,1)S(1)} %copy-done.1, bf16[2,32,512]{2,1,0:T(8,128)(2,1)S(1)} %get-tuple-element.103.refs_0_, ...), custom_call_target="tpu_custom_call" | custom-call | bytes 1024 | tf_op jit(solution)/shard_map/product/pallas_call | solution.py:319
  27.4 0.1 collective-permute-start.6
  27.5 0.5 collective-permute-start.8
  28.0 1.0 %collective-permute-done.6 = bf16[480,256]{1,0:T(8,128)(2,1)S(1)} collective-permute-done((bf16[480,256]{1,0:T(8,128)(2,1)S(1)}, bf16[480,256]{1,0:T(8,128)(2,1)S(1)}, u32[]{:S(2)}, u32[]{:S(2)}) %collective-permute-start.6) | collective-permute-done | bytes 245792 | tf_op jit(solution)/shard_map/ppermute | solution.py:313
  29.0 0.1 add_convert_fusion.4
  29.0 1.6 %collective-permute-start.20 = (bf16[480,256]{1,0:T(8,128)(2,1)S(1)}, bf16[480,256]{1,0:T(8,128)(2,1)S(1)}, u32[]{:S(2)}, u32[]{:S(2)}) collective-permute-start(bf16[480,256]{1,0:T(8,128)(2,1)S(1)} %add_convert_fusion.4), channel_id=1, source_target_pairs={{0,16},{8,24},{16,0},{24,8},{1,17},{9,25},{17,1},{25,9},{2,18},{10... | collective-permute-start | bytes 737288 | tf_op jit(solution)/shard_map/ppermute | solution.py:331
  30.6 1.4 %product.6 = (bf16[480,256]{1,0:T(8,128)(2,1)S(1)}, f32[480,256]{1,0:T(8,128)S(1)}, bf16[480,256]{1,0:T(8,128)(2,1)S(1)}, f32[480,256]{1,0:T(8,128)S(1)}) custom-call(bf16[1024,256]{1,0:T(8,128)(2,1)S(1)} %get-tuple-element.68.place_ref, bf16[160,32,1280]{2,1,0:T(8,128)(2,1)S(1)} %copy-done.1, bf16[2,32,512]{2,1,0:T(8,128)(2,1)S(1)} %get-tuple-element.103.refs_0_, ...), custom_call_target="tpu_custom_call" | custom-call | bytes 1024 | tf_op jit(solution)/shard_map/product/pallas_call | solution.py:319
  32.1 0.1 collective-permute-start.10
  32.1 0.5 collective-permute-start.7
  32.6 0.0 collective-permute-done.8
  32.7 1.3 %collective-permute-done.7 = bf16[480,256]{1,0:T(8,128)(2,1)S(1)} collective-permute-done((bf16[480,256]{1,0:T(8,128)(2,1)S(1)}, bf16[480,256]{1,0:T(8,128)(2,1)S(1)}, u32[]{:S(2)}, u32[]{:S(2)}) %collective-permute-start.7) | collective-permute-done | bytes 245792 | tf_op jit(solution)/shard_map/ppermute | solution.py:313
  34.0 0.1 add_convert_fusion.3
  34.1 0.0 slice-start.2
  34.1 0.0 slice-start.3
  34.1 0.6 collective-permute-start.19
  34.6 1.4 %product.7 = (bf16[480,256]{1,0:T(8,128)(2,1)S(1)}, f32[480,256]{1,0:T(8,128)S(1)}, bf16[480,256]{1,0:T(8,128)(2,1)S(1)}, f32[480,256]{1,0:T(8,128)S(1)}) custom-call(bf16[1024,256]{1,0:T(8,128)(2,1)S(1)} %get-tuple-element.68.place_ref, bf16[160,32,1280]{2,1,0:T(8,128)(2,1)S(1)} %copy-done.1, bf16[2,32,512]{2,1,0:T(8,128)(2,1)S(1)} %get-tuple-element.103.refs_0_, ...), custom_call_target="tpu_custom_call" | custom-call | bytes 1024 | tf_op jit(solution)/shard_map/product/pallas_call | solution.py:319
  36.1 0.1 collective-permute-start.12
  36.1 0.5 collective-permute-start.9
  36.6 0.6 %collective-permute-done.20.far_ref = bf16[480,256]{1,0:T(8,128)(2,1)S(1)} collective-permute-done((bf16[480,256]{1,0:T(8,128)(2,1)S(1)}, bf16[480,256]{1,0:T(8,128)(2,1)S(1)}, u32[]{:S(2)}, u32[]{:S(2)}) %collective-permute-start.20) | collective-permute-done | bytes 245792 | tf_op jit(solution)/shard_map/ppermute | solution.py:331
  37.2 1.0 %final.5.refs_0_ = f32[12,160,320]{2,1,0:T(8,128)} custom-call(s32[160,128]{1,0:T(8,128)S(1)} %get-tuple-element.67.limits_ref, f32[480,256]{1,0:T(8,128)S(1)} %convert_add_fusion.4.near_ref, bf16[480,256]{1,0:T(8,128)(2,1)S(1)} %collective-permute-done.20.far_ref), custom_call_target="tpu_custom_call" | custom-call | bytes 1024 | tf_op jit(solution)/shard_map/final/pallas_call | solution.py:337
  38.3 0.0 collective-permute-done.10
  38.3 0.0 collective-permute-done.9
  38.3 0.1 add_convert_fusion.2
  38.4 2.2 %collective-permute-start.18 = (bf16[480,256]{1,0:T(8,128)(2,1)S(1)}, bf16[480,256]{1,0:T(8,128)(2,1)S(1)}, u32[]{:S(2)}, u32[]{:S(2)}) collective-permute-start(bf16[480,256]{1,0:T(8,128)(2,1)S(1)} %add_convert_fusion.2), channel_id=1, source_target_pairs={{0,16},{8,24},{16,0},{24,8},{1,17},{9,25},{17,1},{25,9},{2,18},{10... | collective-permute-start | bytes 737288 | tf_op jit(solution)/shard_map/ppermute | solution.py:331
  40.7 1.4 %product.8 = (bf16[480,256]{1,0:T(8,128)(2,1)S(1)}, f32[480,256]{1,0:T(8,128)S(1)}, bf16[480,256]{1,0:T(8,128)(2,1)S(1)}, f32[480,256]{1,0:T(8,128)S(1)}) custom-call(bf16[1024,256]{1,0:T(8,128)(2,1)S(1)} %get-tuple-element.68.place_ref, bf16[160,32,1280]{2,1,0:T(8,128)(2,1)S(1)} %bitcast.6, bf16[2,32,512]{2,1,0:T(8,128)(2,1)S(1)} %get-tuple-element.103.refs_0_, ...), custom_call_target="tpu_custom_call" | custom-call | bytes 1024 | tf_op jit(solution)/shard_map/product/pallas_call | solution.py:319
  42.1 0.1 collective-permute-start.16
  42.2 0.5 collective-permute-start.11
  42.7 0.3 collective-permute-done.19.far_ref
  42.9 1.0 %final.6.refs_0_ = f32[12,160,320]{2,1,0:T(8,128)} custom-call(s32[160,128]{1,0:T(8,128)S(1)} %get-tuple-element.67.limits_ref, f32[480,256]{1,0:T(8,128)S(1)} %convert_add_fusion.3.near_ref, bf16[480,256]{1,0:T(8,128)(2,1)S(1)} %collective-permute-done.19.far_ref, f32[12,160,320]{2,1,0:T(8,128)} %final.5.refs_0_), custom_call_target="tpu_custom_call", output_to_operand_aliasing={{}: (3, {})} | custom-call | bytes 1024 | tf_op jit(solution)/shard_map/final/pallas_call | solution.py:337
  44.0 0.0 collective-permute-done.12
  44.0 0.0 collective-permute-done.11
  44.0 0.1 add_convert_fusion.1
  44.1 1.8 %collective-permute-start.17 = (bf16[480,256]{1,0:T(8,128)(2,1)S(1)}, bf16[480,256]{1,0:T(8,128)(2,1)S(1)}, u32[]{:S(2)}, u32[]{:S(2)}) collective-permute-start(bf16[480,256]{1,0:T(8,128)(2,1)S(1)} %add_convert_fusion.1), channel_id=1, source_target_pairs={{0,16},{8,24},{16,0},{24,8},{1,17},{9,25},{17,1},{25,9},{2,18},{10... | collective-permute-start | bytes 737288 | tf_op jit(solution)/shard_map/ppermute | solution.py:331
  45.9 1.4 %product.9 = (bf16[480,256]{1,0:T(8,128)(2,1)S(1)}, f32[480,256]{1,0:T(8,128)S(1)}, bf16[480,256]{1,0:T(8,128)(2,1)S(1)}, f32[480,256]{1,0:T(8,128)S(1)}) custom-call(bf16[1024,256]{1,0:T(8,128)(2,1)S(1)} %get-tuple-element.68.place_ref, bf16[160,32,1280]{2,1,0:T(8,128)(2,1)S(1)} %bitcast.6, bf16[2,32,512]{2,1,0:T(8,128)(2,1)S(1)} %get-tuple-element.103.refs_0_, ...), custom_call_target="tpu_custom_call" | custom-call | bytes 1024 | tf_op jit(solution)/shard_map/product/pallas_call | solution.py:319
  47.3 0.1 collective-permute-start.14
  47.4 0.5 collective-permute-start.13
  47.9 0.3 collective-permute-done.18.far_ref
  48.2 1.0 %final.7.refs_0_ = f32[12,160,320]{2,1,0:T(8,128)} custom-call(s32[160,128]{1,0:T(8,128)S(1)} %get-tuple-element.67.limits_ref, f32[480,256]{1,0:T(8,128)S(1)} %convert_add_fusion.2.near_ref, bf16[480,256]{1,0:T(8,128)(2,1)S(1)} %collective-permute-done.18.far_ref, f32[12,160,320]{2,1,0:T(8,128)} %final.6.refs_0_), custom_call_target="tpu_custom_call", output_to_operand_aliasing={{}: (3, {})} | custom-call | bytes 1024 | tf_op jit(solution)/shard_map/final/pallas_call | solution.py:337
  49.3 0.0 collective-permute-done.14
  49.3 0.1 add_convert_fusion
  49.3 1.8 %collective-permute-start.15 = (bf16[480,256]{1,0:T(8,128)(2,1)S(1)}, bf16[480,256]{1,0:T(8,128)(2,1)S(1)}, u32[]{:S(2)}, u32[]{:S(2)}) collective-permute-start(bf16[480,256]{1,0:T(8,128)(2,1)S(1)} %add_convert_fusion), channel_id=1, source_target_pairs={{0,16},{8,24},{16,0},{24,8},{1,17},{9,25},{17,1},{25,9},{2,18},{10... | collective-permute-start | bytes 737288 | tf_op jit(solution)/shard_map/ppermute | solution.py:331
  51.2 2.3 %collective-permute-done.17.far_ref = bf16[480,256]{1,0:T(8,128)(2,1)S(1)} collective-permute-done((bf16[480,256]{1,0:T(8,128)(2,1)S(1)}, bf16[480,256]{1,0:T(8,128)(2,1)S(1)}, u32[]{:S(2)}, u32[]{:S(2)}) %collective-permute-start.17) | collective-permute-done | bytes 245792 | tf_op jit(solution)/shard_map/ppermute | solution.py:331
  53.5 1.0 %final.8.refs_0_ = f32[12,160,320]{2,1,0:T(8,128)} custom-call(s32[160,128]{1,0:T(8,128)S(1)} %get-tuple-element.67.limits_ref, f32[480,256]{1,0:T(8,128)S(1)} %convert_add_fusion.near_ref, bf16[480,256]{1,0:T(8,128)(2,1)S(1)} %collective-permute-done.17.far_ref, f32[12,160,320]{2,1,0:T(8,128)} %final.7.refs_0_), custom_call_target="tpu_custom_call", output_to_operand_aliasing={{}: (3, {})} | custom-call | bytes 1024 | tf_op jit(solution)/shard_map/final/pallas_call | solution.py:337
  54.5 3.6 %collective-permute-done.15.far_ref = bf16[480,256]{1,0:T(8,128)(2,1)S(1)} collective-permute-done((bf16[480,256]{1,0:T(8,128)(2,1)S(1)}, bf16[480,256]{1,0:T(8,128)(2,1)S(1)}, u32[]{:S(2)}, u32[]{:S(2)}) %collective-permute-start.15) | collective-permute-done | bytes 245792 | tf_op jit(solution)/shard_map/ppermute | solution.py:331
  58.2 1.0 %final.9 = f32[12,160,320]{2,1,0:T(8,128)} custom-call(s32[160,128]{1,0:T(8,128)S(1)} %get-tuple-element.67.limits_ref, f32[480,256]{1,0:T(8,128)S(1)} %convert_add_fusion.1.near_ref, bf16[480,256]{1,0:T(8,128)(2,1)S(1)} %collective-permute-done.15.far_ref, f32[12,160,320]{2,1,0:T(8,128)} %final.8.refs_0_), custom_call_target="tpu_custom_call", output_to_operand_aliasing={{}: (3, {})} | custom-call | bytes 1024 | tf_op jit(solution)/shard_map/final/pallas_call | solution.py:337
  (25 shorter events, 0.3 us)
Async XLA Ops:
  0.0 0.9 %copy-start.2 = (bf16[8,12,1280]{2,0,1:T(8,128)(2,1)S(1)}, bf16[8,12,1280]{2,0,1:T(8,128)(2,1)}, u32[]{:S(2)}) copy-start(bf16[8,12,1280]{2,0,1:T(8,128)(2,1)} %param.3) | copy-start | bytes 737284
  0.9 0.7 %copy-start.3 = (s32[1280]{0:T(1024)S(1)}, s32[1280]{0:T(1024)}, u32[]{:S(2)}) copy-start(s32[1280]{0:T(1024)} %table_ref.1) | copy-start | bytes 15364
  2.5 10.4 %collective-permute-start = (bf16[2,32,512]{2,1,0:T(8,128)(2,1)S(1)}, bf16[2,32,512]{2,1,0:T(8,128)(2,1)S(1)}, u32[]{:S(2)}, u32[]{:S(2)}) collective-permute-start(bf16[2,32,512]{2,1,0:T(8,128)(2,1)S(1)} %get-tuple-element.60), channel_id=1, source_target_pairs={{0,2},{1,3},{2,0},{3,1},{4,6},{5,7},{6,4},{7,5},{8,10},{9,11},{10,... | collective-permute-start | bytes 196616 | tf_op jit(solution)/shard_map/ppermute | solution.py:263
  5.6 7.4 %collective-permute-start.1 = (bf16[2,32,512]{2,1,0:T(8,128)(2,1)S(1)}, bf16[2,32,512]{2,1,0:T(8,128)(2,1)S(1)}, u32[]{:S(2)}, u32[]{:S(2)}) collective-permute-start(bf16[2,32,512]{2,1,0:T(8,128)(2,1)S(1)} %get-tuple-element.61), channel_id=1, source_target_pairs={{0,4},{1,5},{2,6},{3,7},{4,0},{5,1},{6,2},{7,3},{8,12},{9,13},{10,... | collective-permute-start | bytes 196616 | tf_op jit(solution)/shard_map/ppermute | solution.py:263
  8.1 6.1 %collective-permute-start.2 = (bf16[2,32,512]{2,1,0:T(8,128)(2,1)S(1)}, bf16[2,32,512]{2,1,0:T(8,128)(2,1)S(1)}, u32[]{:S(2)}, u32[]{:S(2)}) collective-permute-start(bf16[2,32,512]{2,1,0:T(8,128)(2,1)S(1)} %get-tuple-element.62), channel_id=1, source_target_pairs={{0,6},{1,7},{2,4},{3,5},{4,2},{5,3},{6,0},{7,1},{8,14},{9,15},{10,... | collective-permute-start | bytes 196616 | tf_op jit(solution)/shard_map/ppermute | solution.py:263
  8.2 4.7 %copy-start = (bf16[160,32,1280]{2,1,0:T(8,128)(2,1)S(1)}, bf16[160,32,1280]{2,1,0:T(8,128)(2,1)}, u32[]{:S(2)}) copy-start(bf16[160,32,1280]{2,1,0:T(8,128)(2,1)} %leg_ref.11) | copy-start | bytes 39321604
  12.9 4.6 %copy-start.4 = (s32[1280]{0:T(1024)S(1)}, s32[1280]{0:T(1024)}, u32[]{:S(2)}) copy-start(s32[1280]{0:T(1024)} %table_ref.1) | copy-start | bytes 15364
  14.2 5.4 %collective-permute-start.5 = (bf16[2,32,512]{2,1,0:T(8,128)(2,1)S(1)}, bf16[2,32,512]{2,1,0:T(8,128)(2,1)S(1)}, u32[]{:S(2)}, u32[]{:S(2)}) collective-permute-start(bf16[2,32,512]{2,1,0:T(8,128)(2,1)S(1)} %get-tuple-element.72), channel_id=1, source_target_pairs={{0,25},{1,24},{2,27},{3,26},{4,29},{5,28},{6,31},{7,30},{8,17},{9,... | collective-permute-start | bytes 196616 | tf_op jit(solution)/shard_map/ppermute | solution.py:282
  14.6 5.9 %collective-permute-start.4 = (bf16[2,32,512]{2,1,0:T(8,128)(2,1)S(1)}, bf16[2,32,512]{2,1,0:T(8,128)(2,1)S(1)}, u32[]{:S(2)}, u32[]{:S(2)}) collective-permute-start(bf16[2,32,512]{2,1,0:T(8,128)(2,1)S(1)} %get-tuple-element.71), channel_id=1, source_target_pairs={{0,24},{1,25},{2,26},{3,27},{4,28},{5,29},{6,30},{7,31},{8,16},{9,... | collective-permute-start | bytes 196616 | tf_op jit(solution)/shard_map/ppermute | solution.py:282
  17.0 4.3 %collective-permute-start.3 = (bf16[2,32,512]{2,1,0:T(8,128)(2,1)S(1)}, bf16[2,32,512]{2,1,0:T(8,128)(2,1)S(1)}, u32[]{:S(2)}, u32[]{:S(2)}) collective-permute-start(bf16[2,32,512]{2,1,0:T(8,128)(2,1)S(1)} %get-tuple-element.70), channel_id=1, source_target_pairs={{0,1},{1,0},{2,3},{3,2},{4,5},{5,4},{6,7},{7,6},{8,9},{9,8},{10,11... | collective-permute-start | bytes 196616 | tf_op jit(solution)/shard_map/ppermute | solution.py:282
  21.3 4.7 %copy-start.1 = (bf16[160,32,1280]{2,1,0:T(8,128)(2,1)S(1)}, bf16[160,32,1280]{2,1,0:T(8,128)(2,1)}, u32[]{:S(2)}) copy-start(bf16[160,32,1280]{2,1,0:T(8,128)(2,1)} %leg_ref.11) | copy-start | bytes 39321604
  27.4 1.6 %collective-permute-start.6 = (bf16[480,256]{1,0:T(8,128)(2,1)S(1)}, bf16[480,256]{1,0:T(8,128)(2,1)S(1)}, u32[]{:S(2)}, u32[]{:S(2)}) collective-permute-start(bf16[480,256]{1,0:T(8,128)(2,1)S(1)} %get-tuple-element.78), channel_id=1, source_target_pairs={{0,8},{8,0},{16,24},{24,16},{1,9},{9,1},{17,25},{25,17},{2,10},{10... | collective-permute-start | bytes 737288 | tf_op jit(solution)/shard_map/ppermute | solution.py:313
  27.5 5.2 %collective-permute-start.8 = (bf16[480,256]{1,0:T(8,128)(2,1)S(1)}, bf16[480,256]{1,0:T(8,128)(2,1)S(1)}, u32[]{:S(2)}, u32[]{:S(2)}) collective-permute-start(bf16[480,256]{1,0:T(8,128)(2,1)S(1)} %get-tuple-element.86), channel_id=1, source_target_pairs={{0,8},{8,0},{16,24},{24,16},{1,9},{9,1},{17,25},{25,17},{2,10},{10... | collective-permute-start | bytes 737288 | tf_op jit(solution)/shard_map/ppermute | solution.py:313
  29.0 8.2 %collective-permute-start.20 = (bf16[480,256]{1,0:T(8,128)(2,1)S(1)}, bf16[480,256]{1,0:T(8,128)(2,1)S(1)}, u32[]{:S(2)}, u32[]{:S(2)}) collective-permute-start(bf16[480,256]{1,0:T(8,128)(2,1)S(1)} %add_convert_fusion.4), channel_id=1, source_target_pairs={{0,16},{8,24},{16,0},{24,8},{1,17},{9,25},{17,1},{25,9},{2,18},{10... | collective-permute-start | bytes 737288 | tf_op jit(solution)/shard_map/ppermute | solution.py:331
  30.6 10.0 %slice-start = ((s8[13107200]{0:T(1024)(128)(4,1)}), s8[4194304]{0:T(1024)(128)(4,1)S(1)}, s32[]{:S(2)}) async-start(s8[13107200]{0:T(1024)(128)(4,1)} %bitcast.5), calls=%async_computation | async-start | bytes 8388608
  30.6 10.0 %slice-start.1 = ((s8[13107200]{0:T(1024)(128)(4,1)}), s8[4194304]{0:T(1024)(128)(4,1)S(1)}, s32[]{:S(2)}) async-start(s8[13107200]{0:T(1024)(128)(4,1)} %bitcast.5), calls=%async_computation.1 | async-start | bytes 8388608
  32.1 6.2 %collective-permute-start.10 = (bf16[480,256]{1,0:T(8,128)(2,1)S(1)}, bf16[480,256]{1,0:T(8,128)(2,1)S(1)}, u32[]{:S(2)}, u32[]{:S(2)}) collective-permute-start(bf16[480,256]{1,0:T(8,128)(2,1)S(1)} %get-tuple-element.94), channel_id=1, source_target_pairs={{0,8},{8,0},{16,24},{24,16},{1,9},{9,1},{17,25},{25,17},{2,10},{10... | collective-permute-start | bytes 737288 | tf_op jit(solution)/shard_map/ppermute | solution.py:313
  32.1 1.9 %collective-permute-start.7 = (bf16[480,256]{1,0:T(8,128)(2,1)S(1)}, bf16[480,256]{1,0:T(8,128)(2,1)S(1)}, u32[]{:S(2)}, u32[]{:S(2)}) collective-permute-start(bf16[480,256]{1,0:T(8,128)(2,1)S(1)} %get-tuple-element.84), channel_id=1, source_target_pairs={{0,8},{8,0},{16,24},{24,16},{1,9},{9,1},{17,25},{25,17},{2,10},{10... | collective-permute-start | bytes 737288 | tf_op jit(solution)/shard_map/ppermute | solution.py:313
  34.1 6.6 %slice-start.2 = ((s8[13107200]{0:T(1024)(128)(4,1)}), s8[4194304]{0:T(1024)(128)(4,1)S(1)}, s32[]{:S(2)}) async-start(s8[13107200]{0:T(1024)(128)(4,1)} %bitcast.5), calls=%async_computation.2 | async-start | bytes 8388608
  34.1 6.6 %slice-start.3 = ((s8[13107200]{0:T(1024)(128)(4,1)}), s8[524288]{0:T(1024)(128)(4,1)S(1)}, s32[]{:S(2)}) async-start(s8[13107200]{0:T(1024)(128)(4,1)} %bitcast.5), calls=%async_computation.3 | async-start | bytes 1048576
  34.1 8.9 %collective-permute-start.19 = (bf16[480,256]{1,0:T(8,128)(2,1)S(1)}, bf16[480,256]{1,0:T(8,128)(2,1)S(1)}, u32[]{:S(2)}, u32[]{:S(2)}) collective-permute-start(bf16[480,256]{1,0:T(8,128)(2,1)S(1)} %add_convert_fusion.3), channel_id=1, source_target_pairs={{0,16},{8,24},{16,0},{24,8},{1,17},{9,25},{17,1},{25,9},{2,18},{10... | collective-permute-start | bytes 737288 | tf_op jit(solution)/shard_map/ppermute | solution.py:331
  36.1 7.9 %collective-permute-start.12 = (bf16[480,256]{1,0:T(8,128)(2,1)S(1)}, bf16[480,256]{1,0:T(8,128)(2,1)S(1)}, u32[]{:S(2)}, u32[]{:S(2)}) collective-permute-start(bf16[480,256]{1,0:T(8,128)(2,1)S(1)} %get-tuple-element.102), channel_id=1, source_target_pairs={{0,8},{8,0},{16,24},{24,16},{1,9},{9,1},{17,25},{25,17},{2,10},{10... | collective-permute-start | bytes 737288 | tf_op jit(solution)/shard_map/ppermute | solution.py:313
  36.1 2.2 %collective-permute-start.9 = (bf16[480,256]{1,0:T(8,128)(2,1)S(1)}, bf16[480,256]{1,0:T(8,128)(2,1)S(1)}, u32[]{:S(2)}, u32[]{:S(2)}) collective-permute-start(bf16[480,256]{1,0:T(8,128)(2,1)S(1)} %get-tuple-element.92), channel_id=1, source_target_pairs={{0,8},{8,0},{16,24},{24,16},{1,9},{9,1},{17,25},{25,17},{2,10},{10... | collective-permute-start | bytes 737288 | tf_op jit(solution)/shard_map/ppermute | solution.py:313
  38.4 9.8 %collective-permute-start.18 = (bf16[480,256]{1,0:T(8,128)(2,1)S(1)}, bf16[480,256]{1,0:T(8,128)(2,1)S(1)}, u32[]{:S(2)}, u32[]{:S(2)}) collective-permute-start(bf16[480,256]{1,0:T(8,128)(2,1)S(1)} %add_convert_fusion.2), channel_id=1, source_target_pairs={{0,16},{8,24},{16,0},{24,8},{1,17},{9,25},{17,1},{25,9},{2,18},{10... | collective-permute-start | bytes 737288 | tf_op jit(solution)/shard_map/ppermute | solution.py:331
  42.1 7.1 %collective-permute-start.16 = (bf16[480,256]{1,0:T(8,128)(2,1)S(1)}, bf16[480,256]{1,0:T(8,128)(2,1)S(1)}, u32[]{:S(2)}, u32[]{:S(2)}) collective-permute-start(bf16[480,256]{1,0:T(8,128)(2,1)S(1)} %get-tuple-element.112), channel_id=1, source_target_pairs={{0,8},{8,0},{16,24},{24,16},{1,9},{9,1},{17,25},{25,17},{2,10},{10... | collective-permute-start | bytes 737288 | tf_op jit(solution)/shard_map/ppermute | solution.py:313
  42.2 1.9 %collective-permute-start.11 = (bf16[480,256]{1,0:T(8,128)(2,1)S(1)}, bf16[480,256]{1,0:T(8,128)(2,1)S(1)}, u32[]{:S(2)}, u32[]{:S(2)}) collective-permute-start(bf16[480,256]{1,0:T(8,128)(2,1)S(1)} %get-tuple-element.100), channel_id=1, source_target_pairs={{0,8},{8,0},{16,24},{24,16},{1,9},{9,1},{17,25},{25,17},{2,10},{10... | collective-permute-start | bytes 737288 | tf_op jit(solution)/shard_map/ppermute | solution.py:313
  44.1 9.4 %collective-permute-start.17 = (bf16[480,256]{1,0:T(8,128)(2,1)S(1)}, bf16[480,256]{1,0:T(8,128)(2,1)S(1)}, u32[]{:S(2)}, u32[]{:S(2)}) collective-permute-start(bf16[480,256]{1,0:T(8,128)(2,1)S(1)} %add_convert_fusion.1), channel_id=1, source_target_pairs={{0,16},{8,24},{16,0},{24,8},{1,17},{9,25},{17,1},{25,9},{2,18},{10... | collective-permute-start | bytes 737288 | tf_op jit(solution)/shard_map/ppermute | solution.py:331
  47.3 1.9 %collective-permute-start.14 = (bf16[480,256]{1,0:T(8,128)(2,1)S(1)}, bf16[480,256]{1,0:T(8,128)(2,1)S(1)}, u32[]{:S(2)}, u32[]{:S(2)}) collective-permute-start(bf16[480,256]{1,0:T(8,128)(2,1)S(1)} %get-tuple-element.110), channel_id=1, source_target_pairs={{0,8},{8,0},{16,24},{24,16},{1,9},{9,1},{17,25},{25,17},{2,10},{10... | collective-permute-start | bytes 737288 | tf_op jit(solution)/shard_map/ppermute | solution.py:313
  47.4 7.1 %collective-permute-start.13 = (bf16[480,256]{1,0:T(8,128)(2,1)S(1)}, bf16[480,256]{1,0:T(8,128)(2,1)S(1)}, u32[]{:S(2)}, u32[]{:S(2)}) collective-permute-start(bf16[480,256]{1,0:T(8,128)(2,1)S(1)} %get-tuple-element.108), channel_id=1, source_target_pairs={{0,8},{8,0},{16,24},{24,16},{1,9},{9,1},{17,25},{25,17},{2,10},{10... | collective-permute-start | bytes 737288 | tf_op jit(solution)/shard_map/ppermute | solution.py:313
  49.3 8.8 %collective-permute-start.15 = (bf16[480,256]{1,0:T(8,128)(2,1)S(1)}, bf16[480,256]{1,0:T(8,128)(2,1)S(1)}, u32[]{:S(2)}, u32[]{:S(2)}) collective-permute-start(bf16[480,256]{1,0:T(8,128)(2,1)S(1)} %add_convert_fusion), channel_id=1, source_target_pairs={{0,16},{8,24},{16,0},{24,8},{1,17},{9,25},{17,1},{25,9},{2,18},{10... | collective-permute-start | bytes 737288 | tf_op jit(solution)/shard_map/ppermute | solution.py:331

commit v9 on v8

--- a/solution.py
+++ b/solution.py
@@ -10,7 +10,7 @@
 LANES = 128
 STEP = 32
 TILE = 8
-VMEM = 20 * 1024 * 1024
+VMEM = 32 * 1024 * 1024
 
 
 def partner(block, axis, stride):
@@ -92,11 +92,7 @@
                 out[u, :, k * LANES : (k + 1) * LANES] = tile.astype(jnp.bfloat16)
 
 
-def touch_kernel(leg_ref, out):
-    out[...] = leg_ref[0, : out.shape[0], : out.shape[1]]
-
-
-def place_kernel(turns, lat_count, row_count, pairs, degrees, table_ref, token_ref, out, limits):
+def place_kernel(turns, lat_count, row_count, pairs, degrees, table_ref, out, limits):
     northern = lax.axis_index("lat") < lat_count // 2
     me = lax.axis_index("wave")
     row = lax.broadcasted_iota(jnp.int32, (LANES, 2 * LANES), 0) & (row_count - 1)
@@ -161,7 +157,6 @@
     sources = refs[:-6]
     far_sent, far_own, near_sent, near_own, far, near = refs[-6:]
     half = far.shape[1]
-    table = leg_ref.at[block * STEP : (block + 1) * STEP]
     lat = lax.axis_index("lat")
     y, core = lat // 2, lat % 2
     tile, off = shift_of(block, row_count * cols)
@@ -185,8 +180,8 @@
     north, south = both[:, :LANES], both[:, LANES:]
     even, odd = north + south, north - south
     far_coefs, near_coefs = jnp.where(y == 0, odd, even), jnp.where(y == 0, even, odd)
-    multiply(far_coefs, table, pl.multiple_of((1 - y) * half, LANES), half, far)
-    multiply(near_coefs, table, pl.multiple_of(y * half, LANES), half, near)
+    multiply(far_coefs, leg_ref, pl.multiple_of((1 - y) * half, LANES), half, far)
+    multiply(near_coefs, leg_ref, pl.multiple_of(y * half, LANES), half, near)
     pack(far, core, far_sent, far_own)
     pack(near, core, near_sent, near_own)
 
@@ -250,20 +245,15 @@
         wave_table.reshape(-1, LANES),
         jnp.transpose(fourier, (1, 0, 2)).reshape(used, waves),
     )
-    token = pl.pallas_call(
-        touch_kernel,
-        out_shape=jax.ShapeDtypeStruct((2 * TILE, LANES), legendre.dtype),
-        in_specs=[whole],
-        out_specs=whole,
-        compiler_params=params,
-        name="touch",
-    )(legendre)
     turns = [t * low + u for u in range(low) for t in range(high // 2)]
     passed = [ordered[0]] + [
         lax.ppermute(ordered[t], "wave", [(w, w ^ t * low) for w in range(wave_count)])
         for t in range(1, high)
     ]
     lower = lax.axis_index("wave") < wave_count // 2
+    count = slots // STEP
+    early = count - count // 2
+    tables = [legendre[block * STEP : (block + 1) * STEP] for block in range(early)]
     sources = []
     for mirrored in (False, True):
         for u in range(low):
@@ -272,7 +262,7 @@
                 for side in (0, 1)
             ]
             block = jnp.where(lower != mirrored, sides[0], sides[1])
-            block, token = lax.optimization_barrier((block, token))
+            block, tables = lax.optimization_barrier((block, tables))
             route = []
             for lat in range(lat_count):
                 for wave in range(wave_count):
@@ -288,11 +278,11 @@
             jax.ShapeDtypeStruct((wave_count * LANES, 2 * LANES), jnp.bfloat16),
             jax.ShapeDtypeStruct((slots, LANES), jnp.int32),
         ],
-        in_specs=[pl.BlockSpec(memory_space=pltpu.SMEM), whole],
+        in_specs=[pl.BlockSpec(memory_space=pltpu.SMEM)],
         out_specs=[whole] * 2,
         compiler_params=params,
         name="place",
-    )(wave_table, token)
+    )(wave_table)
 
     rows = STEP * cols
     shape = (rows + rows // 4, 2 * LANES)
@@ -307,15 +297,17 @@
         jax.ShapeDtypeStruct(shape, jnp.bfloat16),
         jax.ShapeDtypeStruct(shape, jnp.float32),
     ]
-    count = slots // STEP
-
     def settle(sent, kept):
         return kept + lax.ppermute(sent, "lat", core_route).astype(jnp.float32)
 
     crossed, settled = [], []
     ties = []
     for block in range(count):
-        sources, ties = lax.optimization_barrier((sources, ties))
+        if block == early - 1:
+            legendre, sources, ties = lax.optimization_barrier((legendre, sources, ties))
+            tables = tables + [legendre[k * STEP : (k + 1) * STEP] for k in range(early, count)]
+        else:
+            sources, ties = lax.optimization_barrier((sources, ties))
         far_sent, far_own, near_sent, near_own = pl.pallas_call(
             functools.partial(product_kernel, block, row_count, cols),
             out_shape=pair_of_sums * 2,
@@ -325,7 +317,7 @@
             compiler_params=params,
             cost_estimate=cost,
             name="product",
-        )(place, legendre, *sources)
+        )(place, tables[block], *sources)
         summed = settle(far_sent, far_own).astype(jnp.bfloat16)
         ties = [summed] + settled[-1:]
         crossed.append(lax.ppermute(summed, "lat", y_route))

time: 59.4 us -> 57.1 us (0.961)
  starting transfers between devices: 19.8 us -> 18.1 us
  waiting for transfers between devices: 13.6 us -> 12.6 us
    slice x0 -> x2, local copies, waits for them, and re-layouts: none -> 8.03 us  [the longest x1 5.17 us: packed(): legendre[block * STEP:(block + 1) * STEP]]
    unnamed x18 -> x10, local copies, waits for them, and re-layouts: 11.1 us -> 3.39 us
    ppermute x5, starting transfers between devices: 8.05 us -> 6.32 us  [packed(): crossed.append(lax.ppermute(summed, 'lat', y_route))]
  transfers between devices with their start and end apart: 21 -> 21, of which waited for: 11 -> 9; matrix products, arithmetic and copies ran while one was open for 1% -> 15% of each run, Pallas kernels for 18% -> 19%
where the time goes in v9:
time: 57.1 us; the launch traced here: 56.9 us
  starting transfers between devices  18.1 us (32%)
  Pallas kernels  13.8 us (24%)
  waiting for transfers between devices  12.6 us (22%)
  local copies, waits for them, and re-layouts  11.4 us (20%)
  other arithmetic  0.59 us (1%)
    pallas_call x5, Pallas kernels, packed(): pl.pallas_call(functools.partial(product_kernel, block, row_count, cols),...  7.09 us
    ppermute x5, waiting for transfers between devices, packed(): crossed.append(lax.ppermute(summed, 'lat', y_route))  6.99 us
    ppermute x5, starting transfers between devices, packed(): crossed.append(lax.ppermute(summed, 'lat', y_route))  6.32 us
    ppermute x3, starting transfers between devices, packed(): lax.ppermute(ordered[t], 'wave', [(w, w ^ t * low) for w in range(wave_co...  5.68 us
    slice x1, local copies, waits for them, and re-layouts, packed(): legendre[block * STEP:(block + 1) * STEP]  5.17 us
    pallas_call x5, Pallas kernels, packed(): pl.pallas_call(functools.partial(final_kernel, block * STEP, degrees, col...  5.07 us
    unnamed x10, local copies, waits for them, and re-layouts  3.39 us
    ppermute x3, starting transfers between devices, packed(): block = lax.ppermute(block, ('lat', 'wave'), route)  3.27 us
  transfers between devices with their start and end apart: 21, of which 9 were waited for; matrix products, arithmetic and copies ran while one was open for 15% of the time, Pallas kernels for 19%

profile of v9, /device:TPU:0, one launch (start us, length us, event | category | flops | bytes accessed | tf_op | source)
XLA Modules:
  0.0 56.9 jit_solution(17867204378216849141)
XLA Ops:
  0.0 0.9 %copy-done.2 = bf16[8,12,1280]{2,0,1:T(8,128)(2,1)S(1)} copy-done((bf16[8,12,1280]{2,0,1:T(8,128)(2,1)S(1)}, bf16[8,12,1280]{2,0,1:T(8,128)(2,1)}, u32[]{:S(2)}) %copy-start.2) | copy-done | bytes 245784
  0.9 0.7 %copy-done.3 = s32[1280]{0:T(1024)S(1)} copy-done((s32[1280]{0:T(1024)S(1)}, s32[1280]{0:T(1024)}, u32[]{:S(2)}) %copy-start.3) | copy-done | bytes 5144
  1.6 0.8 %gather.1 = (bf16[2,32,512]{2,1,0:T(8,128)(2,1)S(1)}, bf16[2,32,512]{2,1,0:T(8,128)(2,1)S(1)}, bf16[2,32,512]{2,1,0:T(8,128)(2,1)S(1)}, bf16[2,32,512]{2,1,0:T(8,128)(2,1)S(1)}) custom-call(s32[10,128]{1,0:T(8,128)S(1)} %bitcast.6, bf16[96,1280]{1,0:T(8,128)(2,1)S(1)} %bitcast.5), custom_call_target="tpu_custom_call" | custom-call | tf_op jit(solution)/shard_map/gather/pallas_call | solution.py:236
  2.5 3.1 %collective-permute-start = (bf16[2,32,512]{2,1,0:T(8,128)(2,1)S(1)}, bf16[2,32,512]{2,1,0:T(8,128)(2,1)S(1)}, u32[]{:S(2)}, u32[]{:S(2)}) collective-permute-start(bf16[2,32,512]{2,1,0:T(8,128)(2,1)S(1)} %get-tuple-element.71), channel_id=1, source_target_pairs={{0,2},{1,3},{2,0},{3,1},{4,6},{5,7},{6,4},{7,5},{8,10},{9,11},{10,... | collective-permute-start | bytes 196616 | tf_op jit(solution)/shard_map/ppermute | solution.py:250
  5.6 2.6 %collective-permute-start.1 = (bf16[2,32,512]{2,1,0:T(8,128)(2,1)S(1)}, bf16[2,32,512]{2,1,0:T(8,128)(2,1)S(1)}, u32[]{:S(2)}, u32[]{:S(2)}) collective-permute-start(bf16[2,32,512]{2,1,0:T(8,128)(2,1)S(1)} %get-tuple-element.72), channel_id=1, source_target_pairs={{0,4},{1,5},{2,6},{3,7},{4,0},{5,1},{6,2},{7,3},{8,12},{9,13},{10,... | collective-permute-start | bytes 196616 | tf_op jit(solution)/shard_map/ppermute | solution.py:250
  8.1 0.0 collective-permute-start.2
  8.1 5.2 %fusion.1 = (bf16[32,32,1280]{2,1,0:T(8,128)(2,1)S(1)}, bf16[32,32,1280]{2,1,0:T(8,128)(2,1)}, bf16[32,32,1280]{2,1,0:T(8,128)(2,1)}) fusion(bf16[160,32,1280]{2,1,0:T(8,128)(2,1)} %param.5), kind=kLoop, calls=%fused_computation.19 | loop fusion | bytes 15728640 | tf_op jit(solution)/shard_map/slice | solution.py:256
  13.3 0.0 collective-permute-done
  13.4 0.0 copy-start
  13.4 0.0 collective-permute-done.1
  13.4 0.8 %collective-permute-done.2 = bf16[2,32,512]{2,1,0:T(8,128)(2,1)S(1)} collective-permute-done((bf16[2,32,512]{2,1,0:T(8,128)(2,1)S(1)}, bf16[2,32,512]{2,1,0:T(8,128)(2,1)S(1)}, u32[]{:S(2)}, u32[]{:S(2)}) %collective-permute-start.2) | collective-permute-done | bytes 65568 | tf_op jit(solution)/shard_map/ppermute | solution.py:250
  14.3 0.6 %collective-permute-start.5 = (bf16[2,32,512]{2,1,0:T(8,128)(2,1)S(1)}, bf16[2,32,512]{2,1,0:T(8,128)(2,1)S(1)}, u32[]{:S(2)}, u32[]{:S(2)}) collective-permute-start(bf16[2,32,512]{2,1,0:T(8,128)(2,1)S(1)} %get-tuple-element.86), channel_id=1, source_target_pairs={{0,25},{1,24},{2,27},{3,26},{4,29},{5,28},{6,31},{7,30},{8,17},{9,... | collective-permute-start | bytes 196616 | tf_op jit(solution)/shard_map/ppermute | solution.py:272
  14.9 2.1 %collective-permute-start.4 = (bf16[2,32,512]{2,1,0:T(8,128)(2,1)S(1)}, bf16[2,32,512]{2,1,0:T(8,128)(2,1)S(1)}, u32[]{:S(2)}, u32[]{:S(2)}) collective-permute-start(bf16[2,32,512]{2,1,0:T(8,128)(2,1)S(1)} %get-tuple-element.82), channel_id=1, source_target_pairs={{0,24},{1,25},{2,26},{3,27},{4,28},{5,29},{6,30},{7,31},{8,16},{9,... | collective-permute-start | bytes 196616 | tf_op jit(solution)/shard_map/ppermute | solution.py:272
  17.0 0.5 collective-permute-start.3
  17.5 0.9 %place.1 = (bf16[1024,256]{1,0:T(8,128)(2,1)S(1)}, s32[160,128]{1,0:T(8,128)S(1)}) custom-call(s32[1280]{0:T(1024)S(1)} %copy-done.4), custom_call_target="tpu_custom_call" | custom-call | tf_op jit(solution)/shard_map/place/pallas_call | solution.py:275
  18.4 1.2 %collective-permute-done.5.refs_3_ = bf16[2,32,512]{2,1,0:T(8,128)(2,1)S(1)} collective-permute-done((bf16[2,32,512]{2,1,0:T(8,128)(2,1)S(1)}, bf16[2,32,512]{2,1,0:T(8,128)(2,1)S(1)}, u32[]{:S(2)}, u32[]{:S(2)}) %collective-permute-start.5) | collective-permute-done | bytes 65568 | tf_op jit(solution)/shard_map/ppermute | solution.py:272
  19.6 0.9 %collective-permute-done.4.refs_2_ = bf16[2,32,512]{2,1,0:T(8,128)(2,1)S(1)} collective-permute-done((bf16[2,32,512]{2,1,0:T(8,128)(2,1)S(1)}, bf16[2,32,512]{2,1,0:T(8,128)(2,1)S(1)}, u32[]{:S(2)}, u32[]{:S(2)}) %collective-permute-start.4) | collective-permute-done | bytes 65568 | tf_op jit(solution)/shard_map/ppermute | solution.py:272
  20.5 0.7 %collective-permute-done.3.refs_1_ = bf16[2,32,512]{2,1,0:T(8,128)(2,1)S(1)} collective-permute-done((bf16[2,32,512]{2,1,0:T(8,128)(2,1)S(1)}, bf16[2,32,512]{2,1,0:T(8,128)(2,1)S(1)}, u32[]{:S(2)}, u32[]{:S(2)}) %collective-permute-start.3) | collective-permute-done | bytes 65568 | tf_op jit(solution)/shard_map/ppermute | solution.py:272
  21.3 1.7 %copy-done.1 = bf16[32,32,1280]{2,1,0:T(8,128)(2,1)S(1)} copy-done((bf16[32,32,1280]{2,1,0:T(8,128)(2,1)S(1)}, bf16[32,32,1280]{2,1,0:T(8,128)(2,1)}, u32[]{:S(2)}) %copy-start.1) | copy-done | bytes 2621464
  23.0 1.4 %product.5 = (bf16[480,256]{1,0:T(8,128)(2,1)S(1)}, f32[480,256]{1,0:T(8,128)S(1)}, bf16[480,256]{1,0:T(8,128)(2,1)S(1)}, f32[480,256]{1,0:T(8,128)S(1)}) custom-call(bf16[1024,256]{1,0:T(8,128)(2,1)S(1)} %get-tuple-element.69.place_ref, bf16[32,32,1280]{2,1,0:T(8,128)(2,1)S(1)} %copy-done.1, bf16[2,32,512]{2,1,0:T(8,128)(2,1)S(1)} %get-tuple-element.121.refs_0_, ...), custom_call_target="tpu_custom_call" | custom-call | bytes 1024 | tf_op jit(solution)/shard_map/product/pallas_call | solution.py:311
  24.4 0.1 collective-permute-start.6
  24.5 0.5 collective-permute-start.8
  25.0 1.0 %collective-permute-done.6 = bf16[480,256]{1,0:T(8,128)(2,1)S(1)} collective-permute-done((bf16[480,256]{1,0:T(8,128)(2,1)S(1)}, bf16[480,256]{1,0:T(8,128)(2,1)S(1)}, u32[]{:S(2)}, u32[]{:S(2)}) %collective-permute-start.6) | collective-permute-done | bytes 245792 | tf_op jit(solution)/shard_map/ppermute | solution.py:301
  26.0 0.1 add_convert_fusion.4
  26.1 1.6 %collective-permute-start.20 = (bf16[480,256]{1,0:T(8,128)(2,1)S(1)}, bf16[480,256]{1,0:T(8,128)(2,1)S(1)}, u32[]{:S(2)}, u32[]{:S(2)}) collective-permute-start(bf16[480,256]{1,0:T(8,128)(2,1)S(1)} %add_convert_fusion.4), channel_id=1, source_target_pairs={{0,16},{8,24},{16,0},{24,8},{1,17},{9,25},{17,1},{25,9},{2,18},{10... | collective-permute-start | bytes 737288 | tf_op jit(solution)/shard_map/ppermute | solution.py:323
  27.7 1.4 %product.6 = (bf16[480,256]{1,0:T(8,128)(2,1)S(1)}, f32[480,256]{1,0:T(8,128)S(1)}, bf16[480,256]{1,0:T(8,128)(2,1)S(1)}, f32[480,256]{1,0:T(8,128)S(1)}) custom-call(bf16[1024,256]{1,0:T(8,128)(2,1)S(1)} %get-tuple-element.69.place_ref, bf16[32,32,1280]{2,1,0:T(8,128)(2,1)S(1)} %copy-done, bf16[2,32,512]{2,1,0:T(8,128)(2,1)S(1)} %get-tuple-element.121.refs_0_, ...), custom_call_target="tpu_custom_call" | custom-call | bytes 1024 | tf_op jit(solution)/shard_map/product/pallas_call | solution.py:311
  29.1 0.1 collective-permute-start.7
  29.2 0.5 collective-permute-start.10
  29.7 0.0 collective-permute-done.8
  29.7 0.9 %collective-permute-done.7 = bf16[480,256]{1,0:T(8,128)(2,1)S(1)} collective-permute-done((bf16[480,256]{1,0:T(8,128)(2,1)S(1)}, bf16[480,256]{1,0:T(8,128)(2,1)S(1)}, u32[]{:S(2)}, u32[]{:S(2)}) %collective-permute-start.7) | collective-permute-done | bytes 245792 | tf_op jit(solution)/shard_map/ppermute | solution.py:301
  30.7 0.1 add_convert_fusion.3
  30.7 0.6 collective-permute-start.19
  31.3 1.4 %product.7 = (bf16[480,256]{1,0:T(8,128)(2,1)S(1)}, f32[480,256]{1,0:T(8,128)S(1)}, bf16[480,256]{1,0:T(8,128)(2,1)S(1)}, f32[480,256]{1,0:T(8,128)S(1)}) custom-call(bf16[1024,256]{1,0:T(8,128)(2,1)S(1)} %get-tuple-element.69.place_ref, bf16[32,32,1280]{2,1,0:T(8,128)(2,1)S(1)} %get-tuple-element.108.leg_ref, ...), custom_call_target="tpu_custom_call" | custom-call | bytes 1024 | tf_op jit(solution)/shard_map/product/pallas_call | solution.py:311
  32.7 0.1 collective-permute-start.9
  32.8 0.5 collective-permute-start.12
  33.3 2.9 %fusion = (bf16[32,32,1280]{2,1,0:T(8,128)(2,1)S(1)}, bf16[32,32,1280]{2,1,0:T(8,128)(2,1)S(1)}) fusion(bf16[160,32,1280]{2,1,0:T(8,128)(2,1)} %param.5), kind=kLoop, calls=%fused_computation.18 | loop fusion | bytes 10485760 | tf_op jit(solution)/shard_map/slice | solution.py:308
  36.2 0.0 collective-permute-done.20.far_ref
  36.2 1.0 %final.5.refs_0_ = f32[12,160,320]{2,1,0:T(8,128)} custom-call(s32[160,128]{1,0:T(8,128)S(1)} %get-tuple-element.68.limits_ref, f32[480,256]{1,0:T(8,128)S(1)} %convert_add_fusion.4.near_ref, bf16[480,256]{1,0:T(8,128)(2,1)S(1)} %collective-permute-done.20.far_ref), custom_call_target="tpu_custom_call" | custom-call | bytes 1024 | tf_op jit(solution)/shard_map/final/pallas_call | solution.py:329
  37.2 0.0 collective-permute-done.10
  37.2 0.0 collective-permute-done.9
  37.3 0.1 add_convert_fusion.2
  37.3 1.6 %collective-permute-start.18 = (bf16[480,256]{1,0:T(8,128)(2,1)S(1)}, bf16[480,256]{1,0:T(8,128)(2,1)S(1)}, u32[]{:S(2)}, u32[]{:S(2)}) collective-permute-start(bf16[480,256]{1,0:T(8,128)(2,1)S(1)} %add_convert_fusion.2), channel_id=1, source_target_pairs={{0,16},{8,24},{16,0},{24,8},{1,17},{9,25},{17,1},{25,9},{2,18},{10... | collective-permute-start | bytes 737288 | tf_op jit(solution)/shard_map/ppermute | solution.py:323
  38.9 1.4 %product.8 = (bf16[480,256]{1,0:T(8,128)(2,1)S(1)}, f32[480,256]{1,0:T(8,128)S(1)}, bf16[480,256]{1,0:T(8,128)(2,1)S(1)}, f32[480,256]{1,0:T(8,128)S(1)}) custom-call(bf16[1024,256]{1,0:T(8,128)(2,1)S(1)} %get-tuple-element.69.place_ref, bf16[32,32,1280]{2,1,0:T(8,128)(2,1)S(1)} %get-tuple-element.131.leg_ref, ...), custom_call_target="tpu_custom_call" | custom-call | bytes 1024 | tf_op jit(solution)/shard_map/product/pallas_call | solution.py:311
  40.3 0.1 collective-permute-start.11
  40.4 0.5 collective-permute-start.16
  40.9 0.0 collective-permute-done.19.far_ref
  40.9 1.0 %final.6.refs_0_ = f32[12,160,320]{2,1,0:T(8,128)} custom-call(s32[160,128]{1,0:T(8,128)S(1)} %get-tuple-element.68.limits_ref, f32[480,256]{1,0:T(8,128)S(1)} %convert_add_fusion.3.near_ref, bf16[480,256]{1,0:T(8,128)(2,1)S(1)} %collective-permute-done.19.far_ref, f32[12,160,320]{2,1,0:T(8,128)} %final.5.refs_0_), custom_call_target="tpu_custom_call", output_to_operand_aliasing={{}: (3, {})} | custom-call | bytes 1024 | tf_op jit(solution)/shard_map/final/pallas_call | solution.py:329
  42.0 0.0 collective-permute-done.11
  42.0 0.1 add_convert_fusion.1
  42.1 0.6 collective-permute-start.17
  42.6 1.4 %product.9 = (bf16[480,256]{1,0:T(8,128)(2,1)S(1)}, f32[480,256]{1,0:T(8,128)S(1)}, bf16[480,256]{1,0:T(8,128)(2,1)S(1)}, f32[480,256]{1,0:T(8,128)S(1)}) custom-call(bf16[1024,256]{1,0:T(8,128)(2,1)S(1)} %get-tuple-element.69.place_ref, bf16[32,32,1280]{2,1,0:T(8,128)(2,1)S(1)} %get-tuple-element.132.leg_ref, ...), custom_call_target="tpu_custom_call" | custom-call | bytes 1024 | tf_op jit(solution)/shard_map/product/pallas_call | solution.py:311
  44.0 0.1 collective-permute-start.13
  44.1 0.5 collective-permute-start.14
  44.6 1.2 %collective-permute-done.18.far_ref = bf16[480,256]{1,0:T(8,128)(2,1)S(1)} collective-permute-done((bf16[480,256]{1,0:T(8,128)(2,1)S(1)}, bf16[480,256]{1,0:T(8,128)(2,1)S(1)}, u32[]{:S(2)}, u32[]{:S(2)}) %collective-permute-start.18) | collective-permute-done | bytes 245792 | tf_op jit(solution)/shard_map/ppermute | solution.py:323
  45.8 1.0 %final.7.refs_0_ = f32[12,160,320]{2,1,0:T(8,128)} custom-call(s32[160,128]{1,0:T(8,128)S(1)} %get-tuple-element.68.limits_ref, f32[480,256]{1,0:T(8,128)S(1)} %convert_add_fusion.2.near_ref, bf16[480,256]{1,0:T(8,128)(2,1)S(1)} %collective-permute-done.18.far_ref, f32[12,160,320]{2,1,0:T(8,128)} %final.6.refs_0_), custom_call_target="tpu_custom_call", output_to_operand_aliasing={{}: (3, {})} | custom-call | bytes 1024 | tf_op jit(solution)/shard_map/final/pallas_call | solution.py:329
  46.8 0.1 convert_add_fusion.near_ref
  46.9 0.1 add_convert_fusion
  46.9 2.0 %collective-permute-start.15 = (bf16[480,256]{1,0:T(8,128)(2,1)S(1)}, bf16[480,256]{1,0:T(8,128)(2,1)S(1)}, u32[]{:S(2)}, u32[]{:S(2)}) collective-permute-start(bf16[480,256]{1,0:T(8,128)(2,1)S(1)} %add_convert_fusion), channel_id=1, source_target_pairs={{0,16},{8,24},{16,0},{24,8},{1,17},{9,25},{17,1},{25,9},{2,18},{10... | collective-permute-start | bytes 737288 | tf_op jit(solution)/shard_map/ppermute | solution.py:323
  48.9 2.1 %collective-permute-done.17.far_ref = bf16[480,256]{1,0:T(8,128)(2,1)S(1)} collective-permute-done((bf16[480,256]{1,0:T(8,128)(2,1)S(1)}, bf16[480,256]{1,0:T(8,128)(2,1)S(1)}, u32[]{:S(2)}, u32[]{:S(2)}) %collective-permute-start.17) | collective-permute-done | bytes 245792 | tf_op jit(solution)/shard_map/ppermute | solution.py:323
  51.0 1.0 %final.8.refs_0_ = f32[12,160,320]{2,1,0:T(8,128)} custom-call(s32[160,128]{1,0:T(8,128)S(1)} %get-tuple-element.68.limits_ref, f32[480,256]{1,0:T(8,128)S(1)} %convert_add_fusion.near_ref, bf16[480,256]{1,0:T(8,128)(2,1)S(1)} %collective-permute-done.17.far_ref, f32[12,160,320]{2,1,0:T(8,128)} %final.7.refs_0_), custom_call_target="tpu_custom_call", output_to_operand_aliasing={{}: (3, {})} | custom-call | bytes 1024 | tf_op jit(solution)/shard_map/final/pallas_call | solution.py:329
  52.1 0.0 collective-permute-done.13
  52.1 0.1 convert_add_fusion.1.near_ref
  52.1 3.7 %collective-permute-done.15.far_ref = bf16[480,256]{1,0:T(8,128)(2,1)S(1)} collective-permute-done((bf16[480,256]{1,0:T(8,128)(2,1)S(1)}, bf16[480,256]{1,0:T(8,128)(2,1)S(1)}, u32[]{:S(2)}, u32[]{:S(2)}) %collective-permute-start.15) | collective-permute-done | bytes 245792 | tf_op jit(solution)/shard_map/ppermute | solution.py:323
  55.9 1.0 %final.9 = f32[12,160,320]{2,1,0:T(8,128)} custom-call(s32[160,128]{1,0:T(8,128)S(1)} %get-tuple-element.68.limits_ref, f32[480,256]{1,0:T(8,128)S(1)} %convert_add_fusion.1.near_ref, bf16[480,256]{1,0:T(8,128)(2,1)S(1)} %collective-permute-done.15.far_ref, f32[12,160,320]{2,1,0:T(8,128)} %final.8.refs_0_), custom_call_target="tpu_custom_call", output_to_operand_aliasing={{}: (3, {})} | custom-call | bytes 1024 | tf_op jit(solution)/shard_map/final/pallas_call | solution.py:329
  (17 shorter events, 0.2 us)
Async XLA Ops:
  0.0 0.9 %copy-start.2 = (bf16[8,12,1280]{2,0,1:T(8,128)(2,1)S(1)}, bf16[8,12,1280]{2,0,1:T(8,128)(2,1)}, u32[]{:S(2)}) copy-start(bf16[8,12,1280]{2,0,1:T(8,128)(2,1)} %param.3) | copy-start | bytes 737284
  0.9 0.7 %copy-start.3 = (s32[1280]{0:T(1024)S(1)}, s32[1280]{0:T(1024)}, u32[]{:S(2)}) copy-start(s32[1280]{0:T(1024)} %table_ref.1) | copy-start | bytes 15364
  2.5 10.9 %collective-permute-start = (bf16[2,32,512]{2,1,0:T(8,128)(2,1)S(1)}, bf16[2,32,512]{2,1,0:T(8,128)(2,1)S(1)}, u32[]{:S(2)}, u32[]{:S(2)}) collective-permute-start(bf16[2,32,512]{2,1,0:T(8,128)(2,1)S(1)} %get-tuple-element.71), channel_id=1, source_target_pairs={{0,2},{1,3},{2,0},{3,1},{4,6},{5,7},{6,4},{7,5},{8,10},{9,11},{10,... | collective-permute-start | bytes 196616 | tf_op jit(solution)/shard_map/ppermute | solution.py:250
  5.6 7.8 %collective-permute-start.1 = (bf16[2,32,512]{2,1,0:T(8,128)(2,1)S(1)}, bf16[2,32,512]{2,1,0:T(8,128)(2,1)S(1)}, u32[]{:S(2)}, u32[]{:S(2)}) collective-permute-start(bf16[2,32,512]{2,1,0:T(8,128)(2,1)S(1)} %get-tuple-element.72), channel_id=1, source_target_pairs={{0,4},{1,5},{2,6},{3,7},{4,0},{5,1},{6,2},{7,3},{8,12},{9,13},{10,... | collective-permute-start | bytes 196616 | tf_op jit(solution)/shard_map/ppermute | solution.py:250
  8.1 9.4 %copy-start.4 = (s32[1280]{0:T(1024)S(1)}, s32[1280]{0:T(1024)}, u32[]{:S(2)}) copy-start(s32[1280]{0:T(1024)} %table_ref.1) | copy-start | bytes 15364
  8.1 6.1 %collective-permute-start.2 = (bf16[2,32,512]{2,1,0:T(8,128)(2,1)S(1)}, bf16[2,32,512]{2,1,0:T(8,128)(2,1)S(1)}, u32[]{:S(2)}, u32[]{:S(2)}) collective-permute-start(bf16[2,32,512]{2,1,0:T(8,128)(2,1)S(1)} %get-tuple-element.73), channel_id=1, source_target_pairs={{0,6},{1,7},{2,4},{3,5},{4,2},{5,3},{6,0},{7,1},{8,14},{9,15},{10,... | collective-permute-start | bytes 196616 | tf_op jit(solution)/shard_map/ppermute | solution.py:250
  13.4 14.3 %copy-start = (bf16[32,32,1280]{2,1,0:T(8,128)(2,1)S(1)}, bf16[32,32,1280]{2,1,0:T(8,128)(2,1)}, u32[]{:S(2)}) copy-start(bf16[32,32,1280]{2,1,0:T(8,128)(2,1)} %get-tuple-element.98.leg_ref) | copy-start | bytes 7864324
  14.3 5.4 %collective-permute-start.5 = (bf16[2,32,512]{2,1,0:T(8,128)(2,1)S(1)}, bf16[2,32,512]{2,1,0:T(8,128)(2,1)S(1)}, u32[]{:S(2)}, u32[]{:S(2)}) collective-permute-start(bf16[2,32,512]{2,1,0:T(8,128)(2,1)S(1)} %get-tuple-element.86), channel_id=1, source_target_pairs={{0,25},{1,24},{2,27},{3,26},{4,29},{5,28},{6,31},{7,30},{8,17},{9,... | collective-permute-start | bytes 196616 | tf_op jit(solution)/shard_map/ppermute | solution.py:272
  14.9 5.7 %collective-permute-start.4 = (bf16[2,32,512]{2,1,0:T(8,128)(2,1)S(1)}, bf16[2,32,512]{2,1,0:T(8,128)(2,1)S(1)}, u32[]{:S(2)}, u32[]{:S(2)}) collective-permute-start(bf16[2,32,512]{2,1,0:T(8,128)(2,1)S(1)} %get-tuple-element.82), channel_id=1, source_target_pairs={{0,24},{1,25},{2,26},{3,27},{4,28},{5,29},{6,30},{7,31},{8,16},{9,... | collective-permute-start | bytes 196616 | tf_op jit(solution)/shard_map/ppermute | solution.py:272
  17.0 4.3 %collective-permute-start.3 = (bf16[2,32,512]{2,1,0:T(8,128)(2,1)S(1)}, bf16[2,32,512]{2,1,0:T(8,128)(2,1)S(1)}, u32[]{:S(2)}, u32[]{:S(2)}) collective-permute-start(bf16[2,32,512]{2,1,0:T(8,128)(2,1)S(1)} %get-tuple-element.78), channel_id=1, source_target_pairs={{0,1},{1,0},{2,3},{3,2},{4,5},{5,4},{6,7},{7,6},{8,9},{9,8},{10,11... | collective-permute-start | bytes 196616 | tf_op jit(solution)/shard_map/ppermute | solution.py:272
  21.3 1.7 %copy-start.1 = (bf16[32,32,1280]{2,1,0:T(8,128)(2,1)S(1)}, bf16[32,32,1280]{2,1,0:T(8,128)(2,1)}, u32[]{:S(2)}) copy-start(bf16[32,32,1280]{2,1,0:T(8,128)(2,1)} %get-tuple-element.91.leg_ref) | copy-start | bytes 7864324
  24.4 1.6 %collective-permute-start.6 = (bf16[480,256]{1,0:T(8,128)(2,1)S(1)}, bf16[480,256]{1,0:T(8,128)(2,1)S(1)}, u32[]{:S(2)}, u32[]{:S(2)}) collective-permute-start(bf16[480,256]{1,0:T(8,128)(2,1)S(1)} %get-tuple-element.93), channel_id=1, source_target_pairs={{0,8},{8,0},{16,24},{24,16},{1,9},{9,1},{17,25},{25,17},{2,10},{10... | collective-permute-start | bytes 737288 | tf_op jit(solution)/shard_map/ppermute | solution.py:301
  24.5 5.2 %collective-permute-start.8 = (bf16[480,256]{1,0:T(8,128)(2,1)S(1)}, bf16[480,256]{1,0:T(8,128)(2,1)S(1)}, u32[]{:S(2)}, u32[]{:S(2)}) collective-permute-start(bf16[480,256]{1,0:T(8,128)(2,1)S(1)} %get-tuple-element.102), channel_id=1, source_target_pairs={{0,8},{8,0},{16,24},{24,16},{1,9},{9,1},{17,25},{25,17},{2,10},{10... | collective-permute-start | bytes 737288 | tf_op jit(solution)/shard_map/ppermute | solution.py:301
  26.1 10.1 %collective-permute-start.20 = (bf16[480,256]{1,0:T(8,128)(2,1)S(1)}, bf16[480,256]{1,0:T(8,128)(2,1)S(1)}, u32[]{:S(2)}, u32[]{:S(2)}) collective-permute-start(bf16[480,256]{1,0:T(8,128)(2,1)S(1)} %add_convert_fusion.4), channel_id=1, source_target_pairs={{0,16},{8,24},{16,0},{24,8},{1,17},{9,25},{17,1},{25,9},{2,18},{10... | collective-permute-start | bytes 737288 | tf_op jit(solution)/shard_map/ppermute | solution.py:323
  29.1 1.6 %collective-permute-start.7 = (bf16[480,256]{1,0:T(8,128)(2,1)S(1)}, bf16[480,256]{1,0:T(8,128)(2,1)S(1)}, u32[]{:S(2)}, u32[]{:S(2)}) collective-permute-start(bf16[480,256]{1,0:T(8,128)(2,1)S(1)} %get-tuple-element.100), channel_id=1, source_target_pairs={{0,8},{8,0},{16,24},{24,16},{1,9},{9,1},{17,25},{25,17},{2,10},{10... | collective-permute-start | bytes 737288 | tf_op jit(solution)/shard_map/ppermute | solution.py:301
  29.2 8.0 %collective-permute-start.10 = (bf16[480,256]{1,0:T(8,128)(2,1)S(1)}, bf16[480,256]{1,0:T(8,128)(2,1)S(1)}, u32[]{:S(2)}, u32[]{:S(2)}) collective-permute-start(bf16[480,256]{1,0:T(8,128)(2,1)S(1)} %get-tuple-element.112), channel_id=1, source_target_pairs={{0,8},{8,0},{16,24},{24,16},{1,9},{9,1},{17,25},{25,17},{2,10},{10... | collective-permute-start | bytes 737288 | tf_op jit(solution)/shard_map/ppermute | solution.py:301
  30.7 10.2 %collective-permute-start.19 = (bf16[480,256]{1,0:T(8,128)(2,1)S(1)}, bf16[480,256]{1,0:T(8,128)(2,1)S(1)}, u32[]{:S(2)}, u32[]{:S(2)}) collective-permute-start(bf16[480,256]{1,0:T(8,128)(2,1)S(1)} %add_convert_fusion.3), channel_id=1, source_target_pairs={{0,16},{8,24},{16,0},{24,8},{1,17},{9,25},{17,1},{25,9},{2,18},{10... | collective-permute-start | bytes 737288 | tf_op jit(solution)/shard_map/ppermute | solution.py:323
  32.7 4.5 %collective-permute-start.9 = (bf16[480,256]{1,0:T(8,128)(2,1)S(1)}, bf16[480,256]{1,0:T(8,128)(2,1)S(1)}, u32[]{:S(2)}, u32[]{:S(2)}) collective-permute-start(bf16[480,256]{1,0:T(8,128)(2,1)S(1)} %get-tuple-element.110), channel_id=1, source_target_pairs={{0,8},{8,0},{16,24},{24,16},{1,9},{9,1},{17,25},{25,17},{2,10},{10... | collective-permute-start | bytes 737288 | tf_op jit(solution)/shard_map/ppermute | solution.py:301
  32.8 9.1 %collective-permute-start.12 = (bf16[480,256]{1,0:T(8,128)(2,1)S(1)}, bf16[480,256]{1,0:T(8,128)(2,1)S(1)}, u32[]{:S(2)}, u32[]{:S(2)}) collective-permute-start(bf16[480,256]{1,0:T(8,128)(2,1)S(1)} %get-tuple-element.120), channel_id=1, source_target_pairs={{0,8},{8,0},{16,24},{24,16},{1,9},{9,1},{17,25},{25,17},{2,10},{10... | collective-permute-start | bytes 737288 | tf_op jit(solution)/shard_map/ppermute | solution.py:301
  37.3 8.5 %collective-permute-start.18 = (bf16[480,256]{1,0:T(8,128)(2,1)S(1)}, bf16[480,256]{1,0:T(8,128)(2,1)S(1)}, u32[]{:S(2)}, u32[]{:S(2)}) collective-permute-start(bf16[480,256]{1,0:T(8,128)(2,1)S(1)} %add_convert_fusion.2), channel_id=1, source_target_pairs={{0,16},{8,24},{16,0},{24,8},{1,17},{9,25},{17,1},{25,9},{2,18},{10... | collective-permute-start | bytes 737288 | tf_op jit(solution)/shard_map/ppermute | solution.py:323
  40.3 1.7 %collective-permute-start.11 = (bf16[480,256]{1,0:T(8,128)(2,1)S(1)}, bf16[480,256]{1,0:T(8,128)(2,1)S(1)}, u32[]{:S(2)}, u32[]{:S(2)}) collective-permute-start(bf16[480,256]{1,0:T(8,128)(2,1)S(1)} %get-tuple-element.118), channel_id=1, source_target_pairs={{0,8},{8,0},{16,24},{24,16},{1,9},{9,1},{17,25},{25,17},{2,10},{10... | collective-permute-start | bytes 737288 | tf_op jit(solution)/shard_map/ppermute | solution.py:301
  40.4 6.4 %collective-permute-start.16 = (bf16[480,256]{1,0:T(8,128)(2,1)S(1)}, bf16[480,256]{1,0:T(8,128)(2,1)S(1)}, u32[]{:S(2)}, u32[]{:S(2)}) collective-permute-start(bf16[480,256]{1,0:T(8,128)(2,1)S(1)} %get-tuple-element.130), channel_id=1, source_target_pairs={{0,8},{8,0},{16,24},{24,16},{1,9},{9,1},{17,25},{25,17},{2,10},{10... | collective-permute-start | bytes 737288 | tf_op jit(solution)/shard_map/ppermute | solution.py:301
  42.1 9.0 %collective-permute-start.17 = (bf16[480,256]{1,0:T(8,128)(2,1)S(1)}, bf16[480,256]{1,0:T(8,128)(2,1)S(1)}, u32[]{:S(2)}, u32[]{:S(2)}) collective-permute-start(bf16[480,256]{1,0:T(8,128)(2,1)S(1)} %add_convert_fusion.1), channel_id=1, source_target_pairs={{0,16},{8,24},{16,0},{24,8},{1,17},{9,25},{17,1},{25,9},{2,18},{10... | collective-permute-start | bytes 737288 | tf_op jit(solution)/shard_map/ppermute | solution.py:323
  44.0 8.0 %collective-permute-start.13 = (bf16[480,256]{1,0:T(8,128)(2,1)S(1)}, bf16[480,256]{1,0:T(8,128)(2,1)S(1)}, u32[]{:S(2)}, u32[]{:S(2)}) collective-permute-start(bf16[480,256]{1,0:T(8,128)(2,1)S(1)} %get-tuple-element.126), channel_id=1, source_target_pairs={{0,8},{8,0},{16,24},{24,16},{1,9},{9,1},{17,25},{25,17},{2,10},{10... | collective-permute-start | bytes 737288 | tf_op jit(solution)/shard_map/ppermute | solution.py:301
  44.1 2.7 %collective-permute-start.14 = (bf16[480,256]{1,0:T(8,128)(2,1)S(1)}, bf16[480,256]{1,0:T(8,128)(2,1)S(1)}, u32[]{:S(2)}, u32[]{:S(2)}) collective-permute-start(bf16[480,256]{1,0:T(8,128)(2,1)S(1)} %get-tuple-element.128), channel_id=1, source_target_pairs={{0,8},{8,0},{16,24},{24,16},{1,9},{9,1},{17,25},{25,17},{2,10},{10... | collective-permute-start | bytes 737288 | tf_op jit(solution)/shard_map/ppermute | solution.py:301
  46.9 8.9 %collective-permute-start.15 = (bf16[480,256]{1,0:T(8,128)(2,1)S(1)}, bf16[480,256]{1,0:T(8,128)(2,1)S(1)}, u32[]{:S(2)}, u32[]{:S(2)}) collective-permute-start(bf16[480,256]{1,0:T(8,128)(2,1)S(1)} %add_convert_fusion), channel_id=1, source_target_pairs={{0,16},{8,24},{16,0},{24,8},{1,17},{9,25},{17,1},{25,9},{2,18},{10... | collective-permute-start | bytes 737288 | tf_op jit(solution)/shard_map/ppermute | solution.py:323

commit v10 on v9

--- a/solution.py
+++ b/solution.py
@@ -10,7 +10,7 @@
 LANES = 128
 STEP = 32
 TILE = 8
-VMEM = 32 * 1024 * 1024
+VMEM = 20 * 1024 * 1024
 
 
 def partner(block, axis, stride):

time: 57.1 us -> 57.1 us (level)
  no operation moved by 1% of the time
where the time goes in v10:
time: 57.1 us; the launch traced here: 56.9 us
  starting transfers between devices  18.1 us (32%)
  Pallas kernels  13.8 us (24%)
  waiting for transfers between devices  12.7 us (22%)
  local copies, waits for them, and re-layouts  11.4 us (20%)
    pallas_call x5, Pallas kernels, packed(): pl.pallas_call(functools.partial(product_kernel, block, row_count, cols),...  7.09 us
    ppermute x5, waiting for transfers between devices, packed(): crossed.append(lax.ppermute(summed, 'lat', y_route))  7.03 us
    ppermute x5, starting transfers between devices, packed(): crossed.append(lax.ppermute(summed, 'lat', y_route))  6.32 us
    ppermute x3, starting transfers between devices, packed(): lax.ppermute(ordered[t], 'wave', [(w, w ^ t * low) for w in range(wave_co...  5.68 us
    slice x1, local copies, waits for them, and re-layouts, packed(): legendre[block * STEP:(block + 1) * STEP]  5.17 us
    pallas_call x5, Pallas kernels, packed(): pl.pallas_call(functools.partial(final_kernel, block * STEP, degrees, col...  5.07 us
    unnamed x10, local copies, waits for them, and re-layouts  3.39 us
    ppermute x3, starting transfers between devices, packed(): block = lax.ppermute(block, ('lat', 'wave'), route)  3.27 us
  transfers between devices with their start and end apart: 21, of which 9 were waited for; matrix products, arithmetic and copies ran while one was open for 15% of the time, Pallas kernels for 19%

profile of v10, /device:TPU:0, one launch (start us, length us, event | category | flops | bytes accessed | tf_op | source)
XLA Modules:
  0.0 56.9 jit_solution(6277005086596028311)
XLA Ops:
  0.0 0.9 %copy-done.2 = bf16[8,12,1280]{2,0,1:T(8,128)(2,1)S(1)} copy-done((bf16[8,12,1280]{2,0,1:T(8,128)(2,1)S(1)}, bf16[8,12,1280]{2,0,1:T(8,128)(2,1)}, u32[]{:S(2)}) %copy-start.2) | copy-done | bytes 245784
  0.9 0.7 %copy-done.3 = s32[1280]{0:T(1024)S(1)} copy-done((s32[1280]{0:T(1024)S(1)}, s32[1280]{0:T(1024)}, u32[]{:S(2)}) %copy-start.3) | copy-done | bytes 5144
  1.6 0.8 %gather.1 = (bf16[2,32,512]{2,1,0:T(8,128)(2,1)S(1)}, bf16[2,32,512]{2,1,0:T(8,128)(2,1)S(1)}, bf16[2,32,512]{2,1,0:T(8,128)(2,1)S(1)}, bf16[2,32,512]{2,1,0:T(8,128)(2,1)S(1)}) custom-call(s32[10,128]{1,0:T(8,128)S(1)} %bitcast.6, bf16[96,1280]{1,0:T(8,128)(2,1)S(1)} %bitcast.5), custom_call_target="tpu_custom_call" | custom-call | tf_op jit(solution)/shard_map/gather/pallas_call | solution.py:236
  2.5 3.1 %collective-permute-start = (bf16[2,32,512]{2,1,0:T(8,128)(2,1)S(1)}, bf16[2,32,512]{2,1,0:T(8,128)(2,1)S(1)}, u32[]{:S(2)}, u32[]{:S(2)}) collective-permute-start(bf16[2,32,512]{2,1,0:T(8,128)(2,1)S(1)} %get-tuple-element.71), channel_id=1, source_target_pairs={{0,2},{1,3},{2,0},{3,1},{4,6},{5,7},{6,4},{7,5},{8,10},{9,11},{10,... | collective-permute-start | bytes 196616 | tf_op jit(solution)/shard_map/ppermute | solution.py:250
  5.6 2.6 %collective-permute-start.1 = (bf16[2,32,512]{2,1,0:T(8,128)(2,1)S(1)}, bf16[2,32,512]{2,1,0:T(8,128)(2,1)S(1)}, u32[]{:S(2)}, u32[]{:S(2)}) collective-permute-start(bf16[2,32,512]{2,1,0:T(8,128)(2,1)S(1)} %get-tuple-element.72), channel_id=1, source_target_pairs={{0,4},{1,5},{2,6},{3,7},{4,0},{5,1},{6,2},{7,3},{8,12},{9,13},{10,... | collective-permute-start | bytes 196616 | tf_op jit(solution)/shard_map/ppermute | solution.py:250
  8.1 0.0 collective-permute-start.2
  8.1 5.2 %fusion.1 = (bf16[32,32,1280]{2,1,0:T(8,128)(2,1)S(1)}, bf16[32,32,1280]{2,1,0:T(8,128)(2,1)}, bf16[32,32,1280]{2,1,0:T(8,128)(2,1)}) fusion(bf16[160,32,1280]{2,1,0:T(8,128)(2,1)} %param.5), kind=kLoop, calls=%fused_computation.19 | loop fusion | bytes 15728640 | tf_op jit(solution)/shard_map/slice | solution.py:256
  13.3 0.0 collective-permute-done
  13.4 0.0 copy-start
  13.4 0.0 collective-permute-done.1
  13.4 0.8 %collective-permute-done.2 = bf16[2,32,512]{2,1,0:T(8,128)(2,1)S(1)} collective-permute-done((bf16[2,32,512]{2,1,0:T(8,128)(2,1)S(1)}, bf16[2,32,512]{2,1,0:T(8,128)(2,1)S(1)}, u32[]{:S(2)}, u32[]{:S(2)}) %collective-permute-start.2) | collective-permute-done | bytes 65568 | tf_op jit(solution)/shard_map/ppermute | solution.py:250
  14.3 0.6 %collective-permute-start.5 = (bf16[2,32,512]{2,1,0:T(8,128)(2,1)S(1)}, bf16[2,32,512]{2,1,0:T(8,128)(2,1)S(1)}, u32[]{:S(2)}, u32[]{:S(2)}) collective-permute-start(bf16[2,32,512]{2,1,0:T(8,128)(2,1)S(1)} %get-tuple-element.86), channel_id=1, source_target_pairs={{0,25},{1,24},{2,27},{3,26},{4,29},{5,28},{6,31},{7,30},{8,17},{9,... | collective-permute-start | bytes 196616 | tf_op jit(solution)/shard_map/ppermute | solution.py:272
  14.9 2.1 %collective-permute-start.4 = (bf16[2,32,512]{2,1,0:T(8,128)(2,1)S(1)}, bf16[2,32,512]{2,1,0:T(8,128)(2,1)S(1)}, u32[]{:S(2)}, u32[]{:S(2)}) collective-permute-start(bf16[2,32,512]{2,1,0:T(8,128)(2,1)S(1)} %get-tuple-element.82), channel_id=1, source_target_pairs={{0,24},{1,25},{2,26},{3,27},{4,28},{5,29},{6,30},{7,31},{8,16},{9,... | collective-permute-start | bytes 196616 | tf_op jit(solution)/shard_map/ppermute | solution.py:272
  17.0 0.5 collective-permute-start.3
  17.5 0.9 %place.1 = (bf16[1024,256]{1,0:T(8,128)(2,1)S(1)}, s32[160,128]{1,0:T(8,128)S(1)}) custom-call(s32[1280]{0:T(1024)S(1)} %copy-done.4), custom_call_target="tpu_custom_call" | custom-call | tf_op jit(solution)/shard_map/place/pallas_call | solution.py:275
  18.4 1.2 %collective-permute-done.5.refs_3_ = bf16[2,32,512]{2,1,0:T(8,128)(2,1)S(1)} collective-permute-done((bf16[2,32,512]{2,1,0:T(8,128)(2,1)S(1)}, bf16[2,32,512]{2,1,0:T(8,128)(2,1)S(1)}, u32[]{:S(2)}, u32[]{:S(2)}) %collective-permute-start.5) | collective-permute-done | bytes 65568 | tf_op jit(solution)/shard_map/ppermute | solution.py:272
  19.6 0.9 %collective-permute-done.4.refs_2_ = bf16[2,32,512]{2,1,0:T(8,128)(2,1)S(1)} collective-permute-done((bf16[2,32,512]{2,1,0:T(8,128)(2,1)S(1)}, bf16[2,32,512]{2,1,0:T(8,128)(2,1)S(1)}, u32[]{:S(2)}, u32[]{:S(2)}) %collective-permute-start.4) | collective-permute-done | bytes 65568 | tf_op jit(solution)/shard_map/ppermute | solution.py:272
  20.5 0.7 %collective-permute-done.3.refs_1_ = bf16[2,32,512]{2,1,0:T(8,128)(2,1)S(1)} collective-permute-done((bf16[2,32,512]{2,1,0:T(8,128)(2,1)S(1)}, bf16[2,32,512]{2,1,0:T(8,128)(2,1)S(1)}, u32[]{:S(2)}, u32[]{:S(2)}) %collective-permute-start.3) | collective-permute-done | bytes 65568 | tf_op jit(solution)/shard_map/ppermute | solution.py:272
  21.3 1.7 %copy-done.1 = bf16[32,32,1280]{2,1,0:T(8,128)(2,1)S(1)} copy-done((bf16[32,32,1280]{2,1,0:T(8,128)(2,1)S(1)}, bf16[32,32,1280]{2,1,0:T(8,128)(2,1)}, u32[]{:S(2)}) %copy-start.1) | copy-done | bytes 2621464
  23.0 1.4 %product.5 = (bf16[480,256]{1,0:T(8,128)(2,1)S(1)}, f32[480,256]{1,0:T(8,128)S(1)}, bf16[480,256]{1,0:T(8,128)(2,1)S(1)}, f32[480,256]{1,0:T(8,128)S(1)}) custom-call(bf16[1024,256]{1,0:T(8,128)(2,1)S(1)} %get-tuple-element.69.place_ref, bf16[32,32,1280]{2,1,0:T(8,128)(2,1)S(1)} %copy-done.1, bf16[2,32,512]{2,1,0:T(8,128)(2,1)S(1)} %get-tuple-element.121.refs_0_, ...), custom_call_target="tpu_custom_call" | custom-call | bytes 1024 | tf_op jit(solution)/shard_map/product/pallas_call | solution.py:311
  24.4 0.1 collective-permute-start.6
  24.5 0.5 collective-permute-start.8
  25.0 1.0 %collective-permute-done.6 = bf16[480,256]{1,0:T(8,128)(2,1)S(1)} collective-permute-done((bf16[480,256]{1,0:T(8,128)(2,1)S(1)}, bf16[480,256]{1,0:T(8,128)(2,1)S(1)}, u32[]{:S(2)}, u32[]{:S(2)}) %collective-permute-start.6) | collective-permute-done | bytes 245792 | tf_op jit(solution)/shard_map/ppermute | solution.py:301
  26.0 0.1 add_convert_fusion.4
  26.1 1.6 %collective-permute-start.20 = (bf16[480,256]{1,0:T(8,128)(2,1)S(1)}, bf16[480,256]{1,0:T(8,128)(2,1)S(1)}, u32[]{:S(2)}, u32[]{:S(2)}) collective-permute-start(bf16[480,256]{1,0:T(8,128)(2,1)S(1)} %add_convert_fusion.4), channel_id=1, source_target_pairs={{0,16},{8,24},{16,0},{24,8},{1,17},{9,25},{17,1},{25,9},{2,18},{10... | collective-permute-start | bytes 737288 | tf_op jit(solution)/shard_map/ppermute | solution.py:323
  27.7 1.4 %product.6 = (bf16[480,256]{1,0:T(8,128)(2,1)S(1)}, f32[480,256]{1,0:T(8,128)S(1)}, bf16[480,256]{1,0:T(8,128)(2,1)S(1)}, f32[480,256]{1,0:T(8,128)S(1)}) custom-call(bf16[1024,256]{1,0:T(8,128)(2,1)S(1)} %get-tuple-element.69.place_ref, bf16[32,32,1280]{2,1,0:T(8,128)(2,1)S(1)} %copy-done, bf16[2,32,512]{2,1,0:T(8,128)(2,1)S(1)} %get-tuple-element.121.refs_0_, ...), custom_call_target="tpu_custom_call" | custom-call | bytes 1024 | tf_op jit(solution)/shard_map/product/pallas_call | solution.py:311
  29.1 0.1 collective-permute-start.7
  29.2 0.5 collective-permute-start.10
  29.7 0.0 collective-permute-done.8
  29.7 0.9 %collective-permute-done.7 = bf16[480,256]{1,0:T(8,128)(2,1)S(1)} collective-permute-done((bf16[480,256]{1,0:T(8,128)(2,1)S(1)}, bf16[480,256]{1,0:T(8,128)(2,1)S(1)}, u32[]{:S(2)}, u32[]{:S(2)}) %collective-permute-start.7) | collective-permute-done | bytes 245792 | tf_op jit(solution)/shard_map/ppermute | solution.py:301
  30.7 0.1 add_convert_fusion.3
  30.7 0.6 collective-permute-start.19
  31.3 1.4 %product.7 = (bf16[480,256]{1,0:T(8,128)(2,1)S(1)}, f32[480,256]{1,0:T(8,128)S(1)}, bf16[480,256]{1,0:T(8,128)(2,1)S(1)}, f32[480,256]{1,0:T(8,128)S(1)}) custom-call(bf16[1024,256]{1,0:T(8,128)(2,1)S(1)} %get-tuple-element.69.place_ref, bf16[32,32,1280]{2,1,0:T(8,128)(2,1)S(1)} %get-tuple-element.108.leg_ref, ...), custom_call_target="tpu_custom_call" | custom-call | bytes 1024 | tf_op jit(solution)/shard_map/product/pallas_call | solution.py:311
  32.7 0.1 collective-permute-start.9
  32.8 0.5 collective-permute-start.12
  33.3 2.9 %fusion = (bf16[32,32,1280]{2,1,0:T(8,128)(2,1)S(1)}, bf16[32,32,1280]{2,1,0:T(8,128)(2,1)S(1)}) fusion(bf16[160,32,1280]{2,1,0:T(8,128)(2,1)} %param.5), kind=kLoop, calls=%fused_computation.18 | loop fusion | bytes 10485760 | tf_op jit(solution)/shard_map/slice | solution.py:308
  36.2 0.0 collective-permute-done.20.far_ref
  36.2 1.0 %final.5.refs_0_ = f32[12,160,320]{2,1,0:T(8,128)} custom-call(s32[160,128]{1,0:T(8,128)S(1)} %get-tuple-element.68.limits_ref, f32[480,256]{1,0:T(8,128)S(1)} %convert_add_fusion.4.near_ref, bf16[480,256]{1,0:T(8,128)(2,1)S(1)} %collective-permute-done.20.far_ref), custom_call_target="tpu_custom_call" | custom-call | bytes 1024 | tf_op jit(solution)/shard_map/final/pallas_call | solution.py:329
  37.2 0.0 collective-permute-done.10
  37.2 0.0 collective-permute-done.9
  37.3 0.1 add_convert_fusion.2
  37.3 1.6 %collective-permute-start.18 = (bf16[480,256]{1,0:T(8,128)(2,1)S(1)}, bf16[480,256]{1,0:T(8,128)(2,1)S(1)}, u32[]{:S(2)}, u32[]{:S(2)}) collective-permute-start(bf16[480,256]{1,0:T(8,128)(2,1)S(1)} %add_convert_fusion.2), channel_id=1, source_target_pairs={{0,16},{8,24},{16,0},{24,8},{1,17},{9,25},{17,1},{25,9},{2,18},{10... | collective-permute-start | bytes 737288 | tf_op jit(solution)/shard_map/ppermute | solution.py:323
  38.9 1.4 %product.8 = (bf16[480,256]{1,0:T(8,128)(2,1)S(1)}, f32[480,256]{1,0:T(8,128)S(1)}, bf16[480,256]{1,0:T(8,128)(2,1)S(1)}, f32[480,256]{1,0:T(8,128)S(1)}) custom-call(bf16[1024,256]{1,0:T(8,128)(2,1)S(1)} %get-tuple-element.69.place_ref, bf16[32,32,1280]{2,1,0:T(8,128)(2,1)S(1)} %get-tuple-element.131.leg_ref, ...), custom_call_target="tpu_custom_call" | custom-call | bytes 1024 | tf_op jit(solution)/shard_map/product/pallas_call | solution.py:311
  40.3 0.1 collective-permute-start.11
  40.4 0.5 collective-permute-start.16
  40.9 0.0 collective-permute-done.19.far_ref
  40.9 1.0 %final.6.refs_0_ = f32[12,160,320]{2,1,0:T(8,128)} custom-call(s32[160,128]{1,0:T(8,128)S(1)} %get-tuple-element.68.limits_ref, f32[480,256]{1,0:T(8,128)S(1)} %convert_add_fusion.3.near_ref, bf16[480,256]{1,0:T(8,128)(2,1)S(1)} %collective-permute-done.19.far_ref, f32[12,160,320]{2,1,0:T(8,128)} %final.5.refs_0_), custom_call_target="tpu_custom_call", output_to_operand_aliasing={{}: (3, {})} | custom-call | bytes 1024 | tf_op jit(solution)/shard_map/final/pallas_call | solution.py:329
  41.9 0.0 collective-permute-done.12
  42.0 0.0 collective-permute-done.11
  42.0 0.1 add_convert_fusion.1
  42.1 0.6 collective-permute-start.17
  42.6 1.4 %product.9 = (bf16[480,256]{1,0:T(8,128)(2,1)S(1)}, f32[480,256]{1,0:T(8,128)S(1)}, bf16[480,256]{1,0:T(8,128)(2,1)S(1)}, f32[480,256]{1,0:T(8,128)S(1)}) custom-call(bf16[1024,256]{1,0:T(8,128)(2,1)S(1)} %get-tuple-element.69.place_ref, bf16[32,32,1280]{2,1,0:T(8,128)(2,1)S(1)} %get-tuple-element.132.leg_ref, ...), custom_call_target="tpu_custom_call" | custom-call | bytes 1024 | tf_op jit(solution)/shard_map/product/pallas_call | solution.py:311
  44.0 0.1 collective-permute-start.13
  44.1 0.5 collective-permute-start.14
  44.6 1.2 %collective-permute-done.18.far_ref = bf16[480,256]{1,0:T(8,128)(2,1)S(1)} collective-permute-done((bf16[480,256]{1,0:T(8,128)(2,1)S(1)}, bf16[480,256]{1,0:T(8,128)(2,1)S(1)}, u32[]{:S(2)}, u32[]{:S(2)}) %collective-permute-start.18) | collective-permute-done | bytes 245792 | tf_op jit(solution)/shard_map/ppermute | solution.py:323
  45.8 1.0 %final.7.refs_0_ = f32[12,160,320]{2,1,0:T(8,128)} custom-call(s32[160,128]{1,0:T(8,128)S(1)} %get-tuple-element.68.limits_ref, f32[480,256]{1,0:T(8,128)S(1)} %convert_add_fusion.2.near_ref, bf16[480,256]{1,0:T(8,128)(2,1)S(1)} %collective-permute-done.18.far_ref, f32[12,160,320]{2,1,0:T(8,128)} %final.6.refs_0_), custom_call_target="tpu_custom_call", output_to_operand_aliasing={{}: (3, {})} | custom-call | bytes 1024 | tf_op jit(solution)/shard_map/final/pallas_call | solution.py:329
  46.8 0.0 collective-permute-done.16
  46.9 0.0 collective-permute-done.14
  46.9 0.1 add_convert_fusion
  46.9 2.0 %collective-permute-start.15 = (bf16[480,256]{1,0:T(8,128)(2,1)S(1)}, bf16[480,256]{1,0:T(8,128)(2,1)S(1)}, u32[]{:S(2)}, u32[]{:S(2)}) collective-permute-start(bf16[480,256]{1,0:T(8,128)(2,1)S(1)} %add_convert_fusion), channel_id=1, source_target_pairs={{0,16},{8,24},{16,0},{24,8},{1,17},{9,25},{17,1},{25,9},{2,18},{10... | collective-permute-start | bytes 737288 | tf_op jit(solution)/shard_map/ppermute | solution.py:323
  48.9 2.1 %collective-permute-done.17.far_ref = bf16[480,256]{1,0:T(8,128)(2,1)S(1)} collective-permute-done((bf16[480,256]{1,0:T(8,128)(2,1)S(1)}, bf16[480,256]{1,0:T(8,128)(2,1)S(1)}, u32[]{:S(2)}, u32[]{:S(2)}) %collective-permute-start.17) | collective-permute-done | bytes 245792 | tf_op jit(solution)/shard_map/ppermute | solution.py:323
  51.0 1.0 %final.8.refs_0_ = f32[12,160,320]{2,1,0:T(8,128)} custom-call(s32[160,128]{1,0:T(8,128)S(1)} %get-tuple-element.68.limits_ref, f32[480,256]{1,0:T(8,128)S(1)} %convert_add_fusion.near_ref, bf16[480,256]{1,0:T(8,128)(2,1)S(1)} %collective-permute-done.17.far_ref, f32[12,160,320]{2,1,0:T(8,128)} %final.7.refs_0_), custom_call_target="tpu_custom_call", output_to_operand_aliasing={{}: (3, {})} | custom-call | bytes 1024 | tf_op jit(solution)/shard_map/final/pallas_call | solution.py:329
  52.1 3.7 %collective-permute-done.15.far_ref = bf16[480,256]{1,0:T(8,128)(2,1)S(1)} collective-permute-done((bf16[480,256]{1,0:T(8,128)(2,1)S(1)}, bf16[480,256]{1,0:T(8,128)(2,1)S(1)}, u32[]{:S(2)}, u32[]{:S(2)}) %collective-permute-start.15) | collective-permute-done | bytes 245792 | tf_op jit(solution)/shard_map/ppermute | solution.py:323
  55.9 1.0 %final.9 = f32[12,160,320]{2,1,0:T(8,128)} custom-call(s32[160,128]{1,0:T(8,128)S(1)} %get-tuple-element.68.limits_ref, f32[480,256]{1,0:T(8,128)S(1)} %convert_add_fusion.1.near_ref, bf16[480,256]{1,0:T(8,128)(2,1)S(1)} %collective-permute-done.15.far_ref, f32[12,160,320]{2,1,0:T(8,128)} %final.8.refs_0_), custom_call_target="tpu_custom_call", output_to_operand_aliasing={{}: (3, {})} | custom-call | bytes 1024 | tf_op jit(solution)/shard_map/final/pallas_call | solution.py:329
  (17 shorter events, 0.3 us)
Async XLA Ops:
  0.0 0.9 %copy-start.2 = (bf16[8,12,1280]{2,0,1:T(8,128)(2,1)S(1)}, bf16[8,12,1280]{2,0,1:T(8,128)(2,1)}, u32[]{:S(2)}) copy-start(bf16[8,12,1280]{2,0,1:T(8,128)(2,1)} %param.3) | copy-start | bytes 737284
  0.9 0.7 %copy-start.3 = (s32[1280]{0:T(1024)S(1)}, s32[1280]{0:T(1024)}, u32[]{:S(2)}) copy-start(s32[1280]{0:T(1024)} %table_ref.1) | copy-start | bytes 15364
  2.5 10.9 %collective-permute-start = (bf16[2,32,512]{2,1,0:T(8,128)(2,1)S(1)}, bf16[2,32,512]{2,1,0:T(8,128)(2,1)S(1)}, u32[]{:S(2)}, u32[]{:S(2)}) collective-permute-start(bf16[2,32,512]{2,1,0:T(8,128)(2,1)S(1)} %get-tuple-element.71), channel_id=1, source_target_pairs={{0,2},{1,3},{2,0},{3,1},{4,6},{5,7},{6,4},{7,5},{8,10},{9,11},{10,... | collective-permute-start | bytes 196616 | tf_op jit(solution)/shard_map/ppermute | solution.py:250
  5.6 7.8 %collective-permute-start.1 = (bf16[2,32,512]{2,1,0:T(8,128)(2,1)S(1)}, bf16[2,32,512]{2,1,0:T(8,128)(2,1)S(1)}, u32[]{:S(2)}, u32[]{:S(2)}) collective-permute-start(bf16[2,32,512]{2,1,0:T(8,128)(2,1)S(1)} %get-tuple-element.72), channel_id=1, source_target_pairs={{0,4},{1,5},{2,6},{3,7},{4,0},{5,1},{6,2},{7,3},{8,12},{9,13},{10,... | collective-permute-start | bytes 196616 | tf_op jit(solution)/shard_map/ppermute | solution.py:250
  8.1 9.4 %copy-start.4 = (s32[1280]{0:T(1024)S(1)}, s32[1280]{0:T(1024)}, u32[]{:S(2)}) copy-start(s32[1280]{0:T(1024)} %table_ref.1) | copy-start | bytes 15364
  8.1 6.1 %collective-permute-start.2 = (bf16[2,32,512]{2,1,0:T(8,128)(2,1)S(1)}, bf16[2,32,512]{2,1,0:T(8,128)(2,1)S(1)}, u32[]{:S(2)}, u32[]{:S(2)}) collective-permute-start(bf16[2,32,512]{2,1,0:T(8,128)(2,1)S(1)} %get-tuple-element.73), channel_id=1, source_target_pairs={{0,6},{1,7},{2,4},{3,5},{4,2},{5,3},{6,0},{7,1},{8,14},{9,15},{10,... | collective-permute-start | bytes 196616 | tf_op jit(solution)/shard_map/ppermute | solution.py:250
  13.4 14.3 %copy-start = (bf16[32,32,1280]{2,1,0:T(8,128)(2,1)S(1)}, bf16[32,32,1280]{2,1,0:T(8,128)(2,1)}, u32[]{:S(2)}) copy-start(bf16[32,32,1280]{2,1,0:T(8,128)(2,1)} %get-tuple-element.98.leg_ref) | copy-start | bytes 7864324
  14.3 5.4 %collective-permute-start.5 = (bf16[2,32,512]{2,1,0:T(8,128)(2,1)S(1)}, bf16[2,32,512]{2,1,0:T(8,128)(2,1)S(1)}, u32[]{:S(2)}, u32[]{:S(2)}) collective-permute-start(bf16[2,32,512]{2,1,0:T(8,128)(2,1)S(1)} %get-tuple-element.86), channel_id=1, source_target_pairs={{0,25},{1,24},{2,27},{3,26},{4,29},{5,28},{6,31},{7,30},{8,17},{9,... | collective-permute-start | bytes 196616 | tf_op jit(solution)/shard_map/ppermute | solution.py:272
  14.9 5.7 %collective-permute-start.4 = (bf16[2,32,512]{2,1,0:T(8,128)(2,1)S(1)}, bf16[2,32,512]{2,1,0:T(8,128)(2,1)S(1)}, u32[]{:S(2)}, u32[]{:S(2)}) collective-permute-start(bf16[2,32,512]{2,1,0:T(8,128)(2,1)S(1)} %get-tuple-element.82), channel_id=1, source_target_pairs={{0,24},{1,25},{2,26},{3,27},{4,28},{5,29},{6,30},{7,31},{8,16},{9,... | collective-permute-start | bytes 196616 | tf_op jit(solution)/shard_map/ppermute | solution.py:272
  17.0 4.3 %collective-permute-start.3 = (bf16[2,32,512]{2,1,0:T(8,128)(2,1)S(1)}, bf16[2,32,512]{2,1,0:T(8,128)(2,1)S(1)}, u32[]{:S(2)}, u32[]{:S(2)}) collective-permute-start(bf16[2,32,512]{2,1,0:T(8,128)(2,1)S(1)} %get-tuple-element.78), channel_id=1, source_target_pairs={{0,1},{1,0},{2,3},{3,2},{4,5},{5,4},{6,7},{7,6},{8,9},{9,8},{10,11... | collective-permute-start | bytes 196616 | tf_op jit(solution)/shard_map/ppermute | solution.py:272
  21.3 1.7 %copy-start.1 = (bf16[32,32,1280]{2,1,0:T(8,128)(2,1)S(1)}, bf16[32,32,1280]{2,1,0:T(8,128)(2,1)}, u32[]{:S(2)}) copy-start(bf16[32,32,1280]{2,1,0:T(8,128)(2,1)} %get-tuple-element.91.leg_ref) | copy-start | bytes 7864324
  24.4 1.6 %collective-permute-start.6 = (bf16[480,256]{1,0:T(8,128)(2,1)S(1)}, bf16[480,256]{1,0:T(8,128)(2,1)S(1)}, u32[]{:S(2)}, u32[]{:S(2)}) collective-permute-start(bf16[480,256]{1,0:T(8,128)(2,1)S(1)} %get-tuple-element.93), channel_id=1, source_target_pairs={{0,8},{8,0},{16,24},{24,16},{1,9},{9,1},{17,25},{25,17},{2,10},{10... | collective-permute-start | bytes 737288 | tf_op jit(solution)/shard_map/ppermute | solution.py:301
  24.5 5.2 %collective-permute-start.8 = (bf16[480,256]{1,0:T(8,128)(2,1)S(1)}, bf16[480,256]{1,0:T(8,128)(2,1)S(1)}, u32[]{:S(2)}, u32[]{:S(2)}) collective-permute-start(bf16[480,256]{1,0:T(8,128)(2,1)S(1)} %get-tuple-element.102), channel_id=1, source_target_pairs={{0,8},{8,0},{16,24},{24,16},{1,9},{9,1},{17,25},{25,17},{2,10},{10... | collective-permute-start | bytes 737288 | tf_op jit(solution)/shard_map/ppermute | solution.py:301
  26.1 10.1 %collective-permute-start.20 = (bf16[480,256]{1,0:T(8,128)(2,1)S(1)}, bf16[480,256]{1,0:T(8,128)(2,1)S(1)}, u32[]{:S(2)}, u32[]{:S(2)}) collective-permute-start(bf16[480,256]{1,0:T(8,128)(2,1)S(1)} %add_convert_fusion.4), channel_id=1, source_target_pairs={{0,16},{8,24},{16,0},{24,8},{1,17},{9,25},{17,1},{25,9},{2,18},{10... | collective-permute-start | bytes 737288 | tf_op jit(solution)/shard_map/ppermute | solution.py:323
  29.1 1.6 %collective-permute-start.7 = (bf16[480,256]{1,0:T(8,128)(2,1)S(1)}, bf16[480,256]{1,0:T(8,128)(2,1)S(1)}, u32[]{:S(2)}, u32[]{:S(2)}) collective-permute-start(bf16[480,256]{1,0:T(8,128)(2,1)S(1)} %get-tuple-element.100), channel_id=1, source_target_pairs={{0,8},{8,0},{16,24},{24,16},{1,9},{9,1},{17,25},{25,17},{2,10},{10... | collective-permute-start | bytes 737288 | tf_op jit(solution)/shard_map/ppermute | solution.py:301
  29.2 8.0 %collective-permute-start.10 = (bf16[480,256]{1,0:T(8,128)(2,1)S(1)}, bf16[480,256]{1,0:T(8,128)(2,1)S(1)}, u32[]{:S(2)}, u32[]{:S(2)}) collective-permute-start(bf16[480,256]{1,0:T(8,128)(2,1)S(1)} %get-tuple-element.112), channel_id=1, source_target_pairs={{0,8},{8,0},{16,24},{24,16},{1,9},{9,1},{17,25},{25,17},{2,10},{10... | collective-permute-start | bytes 737288 | tf_op jit(solution)/shard_map/ppermute | solution.py:301
  30.7 10.2 %collective-permute-start.19 = (bf16[480,256]{1,0:T(8,128)(2,1)S(1)}, bf16[480,256]{1,0:T(8,128)(2,1)S(1)}, u32[]{:S(2)}, u32[]{:S(2)}) collective-permute-start(bf16[480,256]{1,0:T(8,128)(2,1)S(1)} %add_convert_fusion.3), channel_id=1, source_target_pairs={{0,16},{8,24},{16,0},{24,8},{1,17},{9,25},{17,1},{25,9},{2,18},{10... | collective-permute-start | bytes 737288 | tf_op jit(solution)/shard_map/ppermute | solution.py:323
  32.7 4.5 %collective-permute-start.9 = (bf16[480,256]{1,0:T(8,128)(2,1)S(1)}, bf16[480,256]{1,0:T(8,128)(2,1)S(1)}, u32[]{:S(2)}, u32[]{:S(2)}) collective-permute-start(bf16[480,256]{1,0:T(8,128)(2,1)S(1)} %get-tuple-element.110), channel_id=1, source_target_pairs={{0,8},{8,0},{16,24},{24,16},{1,9},{9,1},{17,25},{25,17},{2,10},{10... | collective-permute-start | bytes 737288 | tf_op jit(solution)/shard_map/ppermute | solution.py:301
  32.8 9.1 %collective-permute-start.12 = (bf16[480,256]{1,0:T(8,128)(2,1)S(1)}, bf16[480,256]{1,0:T(8,128)(2,1)S(1)}, u32[]{:S(2)}, u32[]{:S(2)}) collective-permute-start(bf16[480,256]{1,0:T(8,128)(2,1)S(1)} %get-tuple-element.120), channel_id=1, source_target_pairs={{0,8},{8,0},{16,24},{24,16},{1,9},{9,1},{17,25},{25,17},{2,10},{10... | collective-permute-start | bytes 737288 | tf_op jit(solution)/shard_map/ppermute | solution.py:301
  37.3 8.5 %collective-permute-start.18 = (bf16[480,256]{1,0:T(8,128)(2,1)S(1)}, bf16[480,256]{1,0:T(8,128)(2,1)S(1)}, u32[]{:S(2)}, u32[]{:S(2)}) collective-permute-start(bf16[480,256]{1,0:T(8,128)(2,1)S(1)} %add_convert_fusion.2), channel_id=1, source_target_pairs={{0,16},{8,24},{16,0},{24,8},{1,17},{9,25},{17,1},{25,9},{2,18},{10... | collective-permute-start | bytes 737288 | tf_op jit(solution)/shard_map/ppermute | solution.py:323
  40.3 1.7 %collective-permute-start.11 = (bf16[480,256]{1,0:T(8,128)(2,1)S(1)}, bf16[480,256]{1,0:T(8,128)(2,1)S(1)}, u32[]{:S(2)}, u32[]{:S(2)}) collective-permute-start(bf16[480,256]{1,0:T(8,128)(2,1)S(1)} %get-tuple-element.118), channel_id=1, source_target_pairs={{0,8},{8,0},{16,24},{24,16},{1,9},{9,1},{17,25},{25,17},{2,10},{10... | collective-permute-start | bytes 737288 | tf_op jit(solution)/shard_map/ppermute | solution.py:301
  40.4 6.4 %collective-permute-start.16 = (bf16[480,256]{1,0:T(8,128)(2,1)S(1)}, bf16[480,256]{1,0:T(8,128)(2,1)S(1)}, u32[]{:S(2)}, u32[]{:S(2)}) collective-permute-start(bf16[480,256]{1,0:T(8,128)(2,1)S(1)} %get-tuple-element.130), channel_id=1, source_target_pairs={{0,8},{8,0},{16,24},{24,16},{1,9},{9,1},{17,25},{25,17},{2,10},{10... | collective-permute-start | bytes 737288 | tf_op jit(solution)/shard_map/ppermute | solution.py:301
  42.1 9.0 %collective-permute-start.17 = (bf16[480,256]{1,0:T(8,128)(2,1)S(1)}, bf16[480,256]{1,0:T(8,128)(2,1)S(1)}, u32[]{:S(2)}, u32[]{:S(2)}) collective-permute-start(bf16[480,256]{1,0:T(8,128)(2,1)S(1)} %add_convert_fusion.1), channel_id=1, source_target_pairs={{0,16},{8,24},{16,0},{24,8},{1,17},{9,25},{17,1},{25,9},{2,18},{10... | collective-permute-start | bytes 737288 | tf_op jit(solution)/shard_map/ppermute | solution.py:323
  44.0 8.0 %collective-permute-start.13 = (bf16[480,256]{1,0:T(8,128)(2,1)S(1)}, bf16[480,256]{1,0:T(8,128)(2,1)S(1)}, u32[]{:S(2)}, u32[]{:S(2)}) collective-permute-start(bf16[480,256]{1,0:T(8,128)(2,1)S(1)} %get-tuple-element.126), channel_id=1, source_target_pairs={{0,8},{8,0},{16,24},{24,16},{1,9},{9,1},{17,25},{25,17},{2,10},{10... | collective-permute-start | bytes 737288 | tf_op jit(solution)/shard_map/ppermute | solution.py:301
  44.1 2.7 %collective-permute-start.14 = (bf16[480,256]{1,0:T(8,128)(2,1)S(1)}, bf16[480,256]{1,0:T(8,128)(2,1)S(1)}, u32[]{:S(2)}, u32[]{:S(2)}) collective-permute-start(bf16[480,256]{1,0:T(8,128)(2,1)S(1)} %get-tuple-element.128), channel_id=1, source_target_pairs={{0,8},{8,0},{16,24},{24,16},{1,9},{9,1},{17,25},{25,17},{2,10},{10... | collective-permute-start | bytes 737288 | tf_op jit(solution)/shard_map/ppermute | solution.py:301
  46.9 8.9 %collective-permute-start.15 = (bf16[480,256]{1,0:T(8,128)(2,1)S(1)}, bf16[480,256]{1,0:T(8,128)(2,1)S(1)}, u32[]{:S(2)}, u32[]{:S(2)}) collective-permute-start(bf16[480,256]{1,0:T(8,128)(2,1)S(1)} %add_convert_fusion), channel_id=1, source_target_pairs={{0,16},{8,24},{16,0},{24,8},{1,17},{9,25},{17,1},{25,9},{2,18},{10... | collective-permute-start | bytes 737288 | tf_op jit(solution)/shard_map/ppermute | solution.py:323

commit v11 on v8

--- a/solution.py
+++ b/solution.py
@@ -92,11 +92,7 @@
                 out[u, :, k * LANES : (k + 1) * LANES] = tile.astype(jnp.bfloat16)
 
 
-def touch_kernel(leg_ref, out):
-    out[...] = leg_ref[0, : out.shape[0], : out.shape[1]]
-
-
-def place_kernel(turns, lat_count, row_count, pairs, degrees, table_ref, token_ref, out, limits):
+def place_kernel(turns, lat_count, row_count, pairs, degrees, table_ref, leg_ref, out, limits):
     northern = lax.axis_index("lat") < lat_count // 2
     me = lax.axis_index("wave")
     row = lax.broadcasted_iota(jnp.int32, (LANES, 2 * LANES), 0) & (row_count - 1)
@@ -250,15 +246,19 @@
         wave_table.reshape(-1, LANES),
         jnp.transpose(fourier, (1, 0, 2)).reshape(used, waves),
     )
-    token = pl.pallas_call(
-        touch_kernel,
-        out_shape=jax.ShapeDtypeStruct((2 * TILE, LANES), legendre.dtype),
-        in_specs=[whole],
-        out_specs=whole,
+    turns = [t * low + u for u in range(low) for t in range(high // 2)]
+    place, limits = pl.pallas_call(
+        functools.partial(place_kernel, turns, lat_count, row_count, pairs, degrees),
+        out_shape=[
+            jax.ShapeDtypeStruct((wave_count * LANES, 2 * LANES), jnp.bfloat16),
+            jax.ShapeDtypeStruct((slots, LANES), jnp.int32),
+        ],
+        in_specs=[pl.BlockSpec(memory_space=pltpu.SMEM), anywhere],
+        out_specs=[whole] * 2,
         compiler_params=params,
-        name="touch",
-    )(legendre)
-    turns = [t * low + u for u in range(low) for t in range(high // 2)]
+        name="place",
+    )(wave_table, legendre)
+
     passed = [ordered[0]] + [
         lax.ppermute(ordered[t], "wave", [(w, w ^ t * low) for w in range(wave_count)])
         for t in range(1, high)
@@ -272,7 +272,7 @@
                 for side in (0, 1)
             ]
             block = jnp.where(lower != mirrored, sides[0], sides[1])
-            block, token = lax.optimization_barrier((block, token))
+            block, place = lax.optimization_barrier((block, place))
             route = []
             for lat in range(lat_count):
                 for wave in range(wave_count):
@@ -281,18 +281,6 @@
             if mirrored or u:
                 block = lax.ppermute(block, ("lat", "wave"), route)
             sources.append(block)
-
-    place, limits = pl.pallas_call(
-        functools.partial(place_kernel, turns, lat_count, row_count, pairs, degrees),
-        out_shape=[
-            jax.ShapeDtypeStruct((wave_count * LANES, 2 * LANES), jnp.bfloat16),
-            jax.ShapeDtypeStruct((slots, LANES), jnp.int32),
-        ],
-        in_specs=[pl.BlockSpec(memory_space=pltpu.SMEM), whole],
-        out_specs=[whole] * 2,
-        compiler_params=params,
-        name="place",
-    )(wave_table, token)
 
     rows = STEP * cols
     shape = (rows + rows // 4, 2 * LANES)

time: 59.4 us -> 60 us (1.010)
  local copies, waits for them, and re-layouts: 11.1 us -> 11.8 us
    ppermute x3, waiting for transfers between devices: 1.29 us -> 0.01 us  [packed(): lax.ppermute(ordered[t], 'wave', [(w, w ^ t * low) for w in range(wave_co...]
    ppermute x3, waiting for transfers between devices: 2.84 us -> 3.94 us  [packed(): block = lax.ppermute(block, ('lat', 'wave'), route)]
    unnamed x18, local copies, waits for them, and re-layouts: 11.1 us -> 11.8 us
  transfers between devices with their start and end apart: 21 -> 21, of which waited for: 11 -> 10; matrix products, arithmetic and copies ran while one was open for 1% -> 1% of each run, Pallas kernels for 18% -> 18%
where the time goes in v11:
time: 60 us; the launch traced here: 59.7 us
  starting transfers between devices  19.8 us (33%)
  Pallas kernels  13.8 us (23%)
  waiting for transfers between devices  13.4 us (22%)
  local copies, waits for them, and re-layouts  11.8 us (20%)
    unnamed x18, local copies, waits for them, and re-layouts  11.8 us
    ppermute x5, starting transfers between devices, packed(): crossed.append(lax.ppermute(summed, 'lat', y_route))  8.05 us
    ppermute x5, waiting for transfers between devices, packed(): crossed.append(lax.ppermute(summed, 'lat', y_route))  7.12 us
    pallas_call x5, Pallas kernels, packed(): pl.pallas_call(functools.partial(product_kernel, block, row_count, cols),...  7.08 us
    ppermute x3, starting transfers between devices, packed(): lax.ppermute(ordered[t], 'wave', [(w, w ^ t * low) for w in range(wave_co...  5.68 us
    pallas_call x5, Pallas kernels, packed(): pl.pallas_call(functools.partial(final_kernel, block * STEP, degrees, col...  5.06 us
    ppermute x3, waiting for transfers between devices, packed(): block = lax.ppermute(block, ('lat', 'wave'), route)  3.94 us
    ppermute x3, starting transfers between devices, packed(): block = lax.ppermute(block, ('lat', 'wave'), route)  3.27 us
  transfers between devices with their start and end apart: 21, of which 10 were waited for; matrix products, arithmetic and copies ran while one was open for 1% of the time, Pallas kernels for 18%

profile of v11, /device:TPU:0, one launch (start us, length us, event | category | flops | bytes accessed | tf_op | source)
XLA Modules:
  0.0 59.7 jit_solution(17075163280256388526)
XLA Ops:
  0.0 0.9 %copy-done.2 = bf16[8,12,1280]{2,0,1:T(8,128)(2,1)S(1)} copy-done((bf16[8,12,1280]{2,0,1:T(8,128)(2,1)S(1)}, bf16[8,12,1280]{2,0,1:T(8,128)(2,1)}, u32[]{:S(2)}) %copy-start.2) | copy-done | bytes 245784
  0.9 0.7 %copy-done.3 = s32[1280]{0:T(1024)S(1)} copy-done((s32[1280]{0:T(1024)S(1)}, s32[1280]{0:T(1024)}, u32[]{:S(2)}) %copy-start.3) | copy-done | bytes 5144
  1.6 0.8 %gather.1 = (bf16[2,32,512]{2,1,0:T(8,128)(2,1)S(1)}, bf16[2,32,512]{2,1,0:T(8,128)(2,1)S(1)}, bf16[2,32,512]{2,1,0:T(8,128)(2,1)S(1)}, bf16[2,32,512]{2,1,0:T(8,128)(2,1)S(1)}) custom-call(s32[10,128]{1,0:T(8,128)S(1)} %bitcast.8, bf16[96,1280]{1,0:T(8,128)(2,1)S(1)} %bitcast.7), custom_call_target="tpu_custom_call" | custom-call | tf_op jit(solution)/shard_map/gather/pallas_call | solution.py:237
  2.5 3.1 %collective-permute-start = (bf16[2,32,512]{2,1,0:T(8,128)(2,1)S(1)}, bf16[2,32,512]{2,1,0:T(8,128)(2,1)S(1)}, u32[]{:S(2)}, u32[]{:S(2)}) collective-permute-start(bf16[2,32,512]{2,1,0:T(8,128)(2,1)S(1)} %get-tuple-element.61), channel_id=1, source_target_pairs={{0,2},{1,3},{2,0},{3,1},{4,6},{5,7},{6,4},{7,5},{8,10},{9,11},{10,... | collective-permute-start | bytes 196616 | tf_op jit(solution)/shard_map/ppermute | solution.py:263
  5.6 2.6 %collective-permute-start.1 = (bf16[2,32,512]{2,1,0:T(8,128)(2,1)S(1)}, bf16[2,32,512]{2,1,0:T(8,128)(2,1)S(1)}, u32[]{:S(2)}, u32[]{:S(2)}) collective-permute-start(bf16[2,32,512]{2,1,0:T(8,128)(2,1)S(1)} %get-tuple-element.62), channel_id=1, source_target_pairs={{0,4},{1,5},{2,6},{3,7},{4,0},{5,1},{6,2},{7,3},{8,12},{9,13},{10,... | collective-permute-start | bytes 196616 | tf_op jit(solution)/shard_map/ppermute | solution.py:263
  8.1 0.0 collective-permute-start.2
  8.2 0.0 copy-start
  8.2 4.7 %copy-done = bf16[160,32,1280]{2,1,0:T(8,128)(2,1)S(1)} copy-done((bf16[160,32,1280]{2,1,0:T(8,128)(2,1)S(1)}, bf16[160,32,1280]{2,1,0:T(8,128)(2,1)}, u32[]{:S(2)}) %copy-start) | copy-done | bytes 13107224
  12.9 0.7 %copy-done.4 = s32[1280]{0:T(1024)S(1)} copy-done((s32[1280]{0:T(1024)S(1)}, s32[1280]{0:T(1024)}, u32[]{:S(2)}) %copy-start.4) | copy-done | bytes 5144
  13.6 0.9 %place.1 = (bf16[1024,256]{1,0:T(8,128)(2,1)S(1)}, s32[160,128]{1,0:T(8,128)S(1)}) custom-call(s32[1280]{0:T(1024)S(1)} %copy-done.4, bf16[160,32,1280]{2,1,0:T(8,128)(2,1)S(1)} %copy-done), custom_call_target="tpu_custom_call" | custom-call | tf_op jit(solution)/shard_map/place/pallas_call | solution.py:250
  14.5 0.0 collective-permute-done
  14.5 0.0 collective-permute-done.1
  14.5 0.0 collective-permute-done.2
  14.6 1.4 %collective-permute-start.5 = (bf16[2,32,512]{2,1,0:T(8,128)(2,1)S(1)}, bf16[2,32,512]{2,1,0:T(8,128)(2,1)S(1)}, u32[]{:S(2)}, u32[]{:S(2)}) collective-permute-start(bf16[2,32,512]{2,1,0:T(8,128)(2,1)S(1)} %get-tuple-element.72), channel_id=1, source_target_pairs={{0,25},{1,24},{2,27},{3,26},{4,29},{5,28},{6,31},{7,30},{8,17},{9,... | collective-permute-start | bytes 196616 | tf_op jit(solution)/shard_map/ppermute | solution.py:282
  16.0 1.6 %collective-permute-start.4 = (bf16[2,32,512]{2,1,0:T(8,128)(2,1)S(1)}, bf16[2,32,512]{2,1,0:T(8,128)(2,1)S(1)}, u32[]{:S(2)}, u32[]{:S(2)}) collective-permute-start(bf16[2,32,512]{2,1,0:T(8,128)(2,1)S(1)} %get-tuple-element.71), channel_id=1, source_target_pairs={{0,24},{1,25},{2,26},{3,27},{4,28},{5,29},{6,30},{7,31},{8,16},{9,... | collective-permute-start | bytes 196616 | tf_op jit(solution)/shard_map/ppermute | solution.py:282
  17.5 0.3 collective-permute-start.3
  17.9 1.8 %collective-permute-done.5.refs_3_ = bf16[2,32,512]{2,1,0:T(8,128)(2,1)S(1)} collective-permute-done((bf16[2,32,512]{2,1,0:T(8,128)(2,1)S(1)}, bf16[2,32,512]{2,1,0:T(8,128)(2,1)S(1)}, u32[]{:S(2)}, u32[]{:S(2)}) %collective-permute-start.5) | collective-permute-done | bytes 65568 | tf_op jit(solution)/shard_map/ppermute | solution.py:282
  19.7 0.9 %collective-permute-done.4.refs_2_ = bf16[2,32,512]{2,1,0:T(8,128)(2,1)S(1)} collective-permute-done((bf16[2,32,512]{2,1,0:T(8,128)(2,1)S(1)}, bf16[2,32,512]{2,1,0:T(8,128)(2,1)S(1)}, u32[]{:S(2)}, u32[]{:S(2)}) %collective-permute-start.4) | collective-permute-done | bytes 65568 | tf_op jit(solution)/shard_map/ppermute | solution.py:282
  20.7 1.2 %collective-permute-done.3.refs_1_ = bf16[2,32,512]{2,1,0:T(8,128)(2,1)S(1)} collective-permute-done((bf16[2,32,512]{2,1,0:T(8,128)(2,1)S(1)}, bf16[2,32,512]{2,1,0:T(8,128)(2,1)S(1)}, u32[]{:S(2)}, u32[]{:S(2)}) %collective-permute-start.3) | collective-permute-done | bytes 65568 | tf_op jit(solution)/shard_map/ppermute | solution.py:282
  21.8 4.7 %copy-done.1 = bf16[160,32,1280]{2,1,0:T(8,128)(2,1)S(1)} copy-done((bf16[160,32,1280]{2,1,0:T(8,128)(2,1)S(1)}, bf16[160,32,1280]{2,1,0:T(8,128)(2,1)}, u32[]{:S(2)}) %copy-start.1) | copy-done | bytes 13107224
  26.5 1.4 %product.5 = (bf16[480,256]{1,0:T(8,128)(2,1)S(1)}, f32[480,256]{1,0:T(8,128)S(1)}, bf16[480,256]{1,0:T(8,128)(2,1)S(1)}, f32[480,256]{1,0:T(8,128)S(1)}) custom-call(bf16[1024,256]{1,0:T(8,128)(2,1)S(1)} %get-tuple-element.68.place_ref, bf16[160,32,1280]{2,1,0:T(8,128)(2,1)S(1)} %copy-done.1, bf16[2,32,512]{2,1,0:T(8,128)(2,1)S(1)} %get-tuple-element.103.refs_0_, ...), custom_call_target="tpu_custom_call" | custom-call | bytes 1024 | tf_op jit(solution)/shard_map/product/pallas_call | solution.py:307
  28.0 0.1 collective-permute-start.6
  28.0 0.5 collective-permute-start.8
  28.5 1.0 %collective-permute-done.6 = bf16[480,256]{1,0:T(8,128)(2,1)S(1)} collective-permute-done((bf16[480,256]{1,0:T(8,128)(2,1)S(1)}, bf16[480,256]{1,0:T(8,128)(2,1)S(1)}, u32[]{:S(2)}, u32[]{:S(2)}) %collective-permute-start.6) | collective-permute-done | bytes 245792 | tf_op jit(solution)/shard_map/ppermute | solution.py:301
  29.5 0.1 add_convert_fusion.4
  29.6 1.6 %collective-permute-start.20 = (bf16[480,256]{1,0:T(8,128)(2,1)S(1)}, bf16[480,256]{1,0:T(8,128)(2,1)S(1)}, u32[]{:S(2)}, u32[]{:S(2)}) collective-permute-start(bf16[480,256]{1,0:T(8,128)(2,1)S(1)} %add_convert_fusion.4), channel_id=1, source_target_pairs={{0,16},{8,24},{16,0},{24,8},{1,17},{9,25},{17,1},{25,9},{2,18},{10... | collective-permute-start | bytes 737288 | tf_op jit(solution)/shard_map/ppermute | solution.py:319
  31.2 1.4 %product.6 = (bf16[480,256]{1,0:T(8,128)(2,1)S(1)}, f32[480,256]{1,0:T(8,128)S(1)}, bf16[480,256]{1,0:T(8,128)(2,1)S(1)}, f32[480,256]{1,0:T(8,128)S(1)}) custom-call(bf16[1024,256]{1,0:T(8,128)(2,1)S(1)} %get-tuple-element.68.place_ref, bf16[160,32,1280]{2,1,0:T(8,128)(2,1)S(1)} %copy-done.1, bf16[2,32,512]{2,1,0:T(8,128)(2,1)S(1)} %get-tuple-element.103.refs_0_, ...), custom_call_target="tpu_custom_call" | custom-call | bytes 1024 | tf_op jit(solution)/shard_map/product/pallas_call | solution.py:307
  32.6 0.1 collective-permute-start.10
  32.7 0.5 collective-permute-start.7
  33.2 0.0 collective-permute-done.8
  33.2 1.3 %collective-permute-done.7 = bf16[480,256]{1,0:T(8,128)(2,1)S(1)} collective-permute-done((bf16[480,256]{1,0:T(8,128)(2,1)S(1)}, bf16[480,256]{1,0:T(8,128)(2,1)S(1)}, u32[]{:S(2)}, u32[]{:S(2)}) %collective-permute-start.7) | collective-permute-done | bytes 245792 | tf_op jit(solution)/shard_map/ppermute | solution.py:301
  34.5 0.1 add_convert_fusion.3
  34.6 0.0 slice-start.2
  34.6 0.0 slice-start.3
  34.6 0.6 collective-permute-start.19
  35.2 1.4 %product.7 = (bf16[480,256]{1,0:T(8,128)(2,1)S(1)}, f32[480,256]{1,0:T(8,128)S(1)}, bf16[480,256]{1,0:T(8,128)(2,1)S(1)}, f32[480,256]{1,0:T(8,128)S(1)}) custom-call(bf16[1024,256]{1,0:T(8,128)(2,1)S(1)} %get-tuple-element.68.place_ref, bf16[160,32,1280]{2,1,0:T(8,128)(2,1)S(1)} %copy-done.1, bf16[2,32,512]{2,1,0:T(8,128)(2,1)S(1)} %get-tuple-element.103.refs_0_, ...), custom_call_target="tpu_custom_call" | custom-call | bytes 1024 | tf_op jit(solution)/shard_map/product/pallas_call | solution.py:307
  36.6 0.1 collective-permute-start.12
  36.7 0.5 collective-permute-start.9
  37.2 0.6 %collective-permute-done.20.far_ref = bf16[480,256]{1,0:T(8,128)(2,1)S(1)} collective-permute-done((bf16[480,256]{1,0:T(8,128)(2,1)S(1)}, bf16[480,256]{1,0:T(8,128)(2,1)S(1)}, u32[]{:S(2)}, u32[]{:S(2)}) %collective-permute-start.20) | collective-permute-done | bytes 245792 | tf_op jit(solution)/shard_map/ppermute | solution.py:319
  37.8 1.0 %final.5.refs_0_ = f32[12,160,320]{2,1,0:T(8,128)} custom-call(s32[160,128]{1,0:T(8,128)S(1)} %get-tuple-element.59.limits_ref, f32[480,256]{1,0:T(8,128)S(1)} %convert_add_fusion.4.near_ref, bf16[480,256]{1,0:T(8,128)(2,1)S(1)} %collective-permute-done.20.far_ref), custom_call_target="tpu_custom_call" | custom-call | bytes 1024 | tf_op jit(solution)/shard_map/final/pallas_call | solution.py:325
  38.8 0.0 collective-permute-done.10
  38.9 0.0 collective-permute-done.9
  38.9 0.1 add_convert_fusion.2
  38.9 2.2 %collective-permute-start.18 = (bf16[480,256]{1,0:T(8,128)(2,1)S(1)}, bf16[480,256]{1,0:T(8,128)(2,1)S(1)}, u32[]{:S(2)}, u32[]{:S(2)}) collective-permute-start(bf16[480,256]{1,0:T(8,128)(2,1)S(1)} %add_convert_fusion.2), channel_id=1, source_target_pairs={{0,16},{8,24},{16,0},{24,8},{1,17},{9,25},{17,1},{25,9},{2,18},{10... | collective-permute-start | bytes 737288 | tf_op jit(solution)/shard_map/ppermute | solution.py:319
  41.2 1.4 %product.8 = (bf16[480,256]{1,0:T(8,128)(2,1)S(1)}, f32[480,256]{1,0:T(8,128)S(1)}, bf16[480,256]{1,0:T(8,128)(2,1)S(1)}, f32[480,256]{1,0:T(8,128)S(1)}) custom-call(bf16[1024,256]{1,0:T(8,128)(2,1)S(1)} %get-tuple-element.68.place_ref, bf16[160,32,1280]{2,1,0:T(8,128)(2,1)S(1)} %bitcast.6, bf16[2,32,512]{2,1,0:T(8,128)(2,1)S(1)} %get-tuple-element.103.refs_0_, ...), custom_call_target="tpu_custom_call" | custom-call | bytes 1024 | tf_op jit(solution)/shard_map/product/pallas_call | solution.py:307
  42.6 0.1 collective-permute-start.16
  42.7 0.5 collective-permute-start.11
  43.2 0.3 collective-permute-done.19.far_ref
  43.5 1.0 %final.6.refs_0_ = f32[12,160,320]{2,1,0:T(8,128)} custom-call(s32[160,128]{1,0:T(8,128)S(1)} %get-tuple-element.59.limits_ref, f32[480,256]{1,0:T(8,128)S(1)} %convert_add_fusion.3.near_ref, bf16[480,256]{1,0:T(8,128)(2,1)S(1)} %collective-permute-done.19.far_ref, f32[12,160,320]{2,1,0:T(8,128)} %final.5.refs_0_), custom_call_target="tpu_custom_call", output_to_operand_aliasing={{}: (3, {})} | custom-call | bytes 1024 | tf_op jit(solution)/shard_map/final/pallas_call | solution.py:325
  44.5 0.0 collective-permute-done.11
  44.6 0.1 add_convert_fusion.1
  44.6 1.8 %collective-permute-start.17 = (bf16[480,256]{1,0:T(8,128)(2,1)S(1)}, bf16[480,256]{1,0:T(8,128)(2,1)S(1)}, u32[]{:S(2)}, u32[]{:S(2)}) collective-permute-start(bf16[480,256]{1,0:T(8,128)(2,1)S(1)} %add_convert_fusion.1), channel_id=1, source_target_pairs={{0,16},{8,24},{16,0},{24,8},{1,17},{9,25},{17,1},{25,9},{2,18},{10... | collective-permute-start | bytes 737288 | tf_op jit(solution)/shard_map/ppermute | solution.py:319
  46.4 1.4 %product.9 = (bf16[480,256]{1,0:T(8,128)(2,1)S(1)}, f32[480,256]{1,0:T(8,128)S(1)}, bf16[480,256]{1,0:T(8,128)(2,1)S(1)}, f32[480,256]{1,0:T(8,128)S(1)}) custom-call(bf16[1024,256]{1,0:T(8,128)(2,1)S(1)} %get-tuple-element.68.place_ref, bf16[160,32,1280]{2,1,0:T(8,128)(2,1)S(1)} %bitcast.6, bf16[2,32,512]{2,1,0:T(8,128)(2,1)S(1)} %get-tuple-element.103.refs_0_, ...), custom_call_target="tpu_custom_call" | custom-call | bytes 1024 | tf_op jit(solution)/shard_map/product/pallas_call | solution.py:307
  47.9 0.1 collective-permute-start.14
  48.0 0.5 collective-permute-start.13
  48.4 0.3 collective-permute-done.18.far_ref
  48.7 1.0 %final.7.refs_0_ = f32[12,160,320]{2,1,0:T(8,128)} custom-call(s32[160,128]{1,0:T(8,128)S(1)} %get-tuple-element.59.limits_ref, f32[480,256]{1,0:T(8,128)S(1)} %convert_add_fusion.2.near_ref, bf16[480,256]{1,0:T(8,128)(2,1)S(1)} %collective-permute-done.18.far_ref, f32[12,160,320]{2,1,0:T(8,128)} %final.6.refs_0_), custom_call_target="tpu_custom_call", output_to_operand_aliasing={{}: (3, {})} | custom-call | bytes 1024 | tf_op jit(solution)/shard_map/final/pallas_call | solution.py:325
  49.8 0.0 collective-permute-done.14
  49.8 0.1 add_convert_fusion
  49.9 1.8 %collective-permute-start.15 = (bf16[480,256]{1,0:T(8,128)(2,1)S(1)}, bf16[480,256]{1,0:T(8,128)(2,1)S(1)}, u32[]{:S(2)}, u32[]{:S(2)}) collective-permute-start(bf16[480,256]{1,0:T(8,128)(2,1)S(1)} %add_convert_fusion), channel_id=1, source_target_pairs={{0,16},{8,24},{16,0},{24,8},{1,17},{9,25},{17,1},{25,9},{2,18},{10... | collective-permute-start | bytes 737288 | tf_op jit(solution)/shard_map/ppermute | solution.py:319
  51.7 2.3 %collective-permute-done.17.far_ref = bf16[480,256]{1,0:T(8,128)(2,1)S(1)} collective-permute-done((bf16[480,256]{1,0:T(8,128)(2,1)S(1)}, bf16[480,256]{1,0:T(8,128)(2,1)S(1)}, u32[]{:S(2)}, u32[]{:S(2)}) %collective-permute-start.17) | collective-permute-done | bytes 245792 | tf_op jit(solution)/shard_map/ppermute | solution.py:319
  54.0 1.0 %final.8.refs_0_ = f32[12,160,320]{2,1,0:T(8,128)} custom-call(s32[160,128]{1,0:T(8,128)S(1)} %get-tuple-element.59.limits_ref, f32[480,256]{1,0:T(8,128)S(1)} %convert_add_fusion.near_ref, bf16[480,256]{1,0:T(8,128)(2,1)S(1)} %collective-permute-done.17.far_ref, f32[12,160,320]{2,1,0:T(8,128)} %final.7.refs_0_), custom_call_target="tpu_custom_call", output_to_operand_aliasing={{}: (3, {})} | custom-call | bytes 1024 | tf_op jit(solution)/shard_map/final/pallas_call | solution.py:325
  55.1 3.6 %collective-permute-done.15.far_ref = bf16[480,256]{1,0:T(8,128)(2,1)S(1)} collective-permute-done((bf16[480,256]{1,0:T(8,128)(2,1)S(1)}, bf16[480,256]{1,0:T(8,128)(2,1)S(1)}, u32[]{:S(2)}, u32[]{:S(2)}) %collective-permute-start.15) | collective-permute-done | bytes 245792 | tf_op jit(solution)/shard_map/ppermute | solution.py:319
  58.7 1.0 %final.9 = f32[12,160,320]{2,1,0:T(8,128)} custom-call(s32[160,128]{1,0:T(8,128)S(1)} %get-tuple-element.59.limits_ref, f32[480,256]{1,0:T(8,128)S(1)} %convert_add_fusion.1.near_ref, bf16[480,256]{1,0:T(8,128)(2,1)S(1)} %collective-permute-done.15.far_ref, f32[12,160,320]{2,1,0:T(8,128)} %final.8.refs_0_), custom_call_target="tpu_custom_call", output_to_operand_aliasing={{}: (3, {})} | custom-call | bytes 1024 | tf_op jit(solution)/shard_map/final/pallas_call | solution.py:325
  (24 shorter events, 0.3 us)
Async XLA Ops:
  0.0 0.9 %copy-start.2 = (bf16[8,12,1280]{2,0,1:T(8,128)(2,1)S(1)}, bf16[8,12,1280]{2,0,1:T(8,128)(2,1)}, u32[]{:S(2)}) copy-start(bf16[8,12,1280]{2,0,1:T(8,128)(2,1)} %param.3) | copy-start | bytes 737284
  0.9 0.7 %copy-start.3 = (s32[1280]{0:T(1024)S(1)}, s32[1280]{0:T(1024)}, u32[]{:S(2)}) copy-start(s32[1280]{0:T(1024)} %table_ref.1) | copy-start | bytes 15364
  2.5 12.0 %collective-permute-start = (bf16[2,32,512]{2,1,0:T(8,128)(2,1)S(1)}, bf16[2,32,512]{2,1,0:T(8,128)(2,1)S(1)}, u32[]{:S(2)}, u32[]{:S(2)}) collective-permute-start(bf16[2,32,512]{2,1,0:T(8,128)(2,1)S(1)} %get-tuple-element.61), channel_id=1, source_target_pairs={{0,2},{1,3},{2,0},{3,1},{4,6},{5,7},{6,4},{7,5},{8,10},{9,11},{10,... | collective-permute-start | bytes 196616 | tf_op jit(solution)/shard_map/ppermute | solution.py:263
  5.6 9.0 %collective-permute-start.1 = (bf16[2,32,512]{2,1,0:T(8,128)(2,1)S(1)}, bf16[2,32,512]{2,1,0:T(8,128)(2,1)S(1)}, u32[]{:S(2)}, u32[]{:S(2)}) collective-permute-start(bf16[2,32,512]{2,1,0:T(8,128)(2,1)S(1)} %get-tuple-element.62), channel_id=1, source_target_pairs={{0,4},{1,5},{2,6},{3,7},{4,0},{5,1},{6,2},{7,3},{8,12},{9,13},{10,... | collective-permute-start | bytes 196616 | tf_op jit(solution)/shard_map/ppermute | solution.py:263
  8.1 6.4 %collective-permute-start.2 = (bf16[2,32,512]{2,1,0:T(8,128)(2,1)S(1)}, bf16[2,32,512]{2,1,0:T(8,128)(2,1)S(1)}, u32[]{:S(2)}, u32[]{:S(2)}) collective-permute-start(bf16[2,32,512]{2,1,0:T(8,128)(2,1)S(1)} %get-tuple-element.63), channel_id=1, source_target_pairs={{0,6},{1,7},{2,4},{3,5},{4,2},{5,3},{6,0},{7,1},{8,14},{9,15},{10,... | collective-permute-start | bytes 196616 | tf_op jit(solution)/shard_map/ppermute | solution.py:263
  8.2 4.7 %copy-start = (bf16[160,32,1280]{2,1,0:T(8,128)(2,1)S(1)}, bf16[160,32,1280]{2,1,0:T(8,128)(2,1)}, u32[]{:S(2)}) copy-start(bf16[160,32,1280]{2,1,0:T(8,128)(2,1)} %leg_ref.11) | copy-start | bytes 39321604
  12.9 0.7 %copy-start.4 = (s32[1280]{0:T(1024)S(1)}, s32[1280]{0:T(1024)}, u32[]{:S(2)}) copy-start(s32[1280]{0:T(1024)} %table_ref.1) | copy-start | bytes 15364
  14.6 5.1 %collective-permute-start.5 = (bf16[2,32,512]{2,1,0:T(8,128)(2,1)S(1)}, bf16[2,32,512]{2,1,0:T(8,128)(2,1)S(1)}, u32[]{:S(2)}, u32[]{:S(2)}) collective-permute-start(bf16[2,32,512]{2,1,0:T(8,128)(2,1)S(1)} %get-tuple-element.72), channel_id=1, source_target_pairs={{0,25},{1,24},{2,27},{3,26},{4,29},{5,28},{6,31},{7,30},{8,17},{9,... | collective-permute-start | bytes 196616 | tf_op jit(solution)/shard_map/ppermute | solution.py:282
  16.0 4.7 %collective-permute-start.4 = (bf16[2,32,512]{2,1,0:T(8,128)(2,1)S(1)}, bf16[2,32,512]{2,1,0:T(8,128)(2,1)S(1)}, u32[]{:S(2)}, u32[]{:S(2)}) collective-permute-start(bf16[2,32,512]{2,1,0:T(8,128)(2,1)S(1)} %get-tuple-element.71), channel_id=1, source_target_pairs={{0,24},{1,25},{2,26},{3,27},{4,28},{5,29},{6,30},{7,31},{8,16},{9,... | collective-permute-start | bytes 196616 | tf_op jit(solution)/shard_map/ppermute | solution.py:282
  17.5 4.3 %collective-permute-start.3 = (bf16[2,32,512]{2,1,0:T(8,128)(2,1)S(1)}, bf16[2,32,512]{2,1,0:T(8,128)(2,1)S(1)}, u32[]{:S(2)}, u32[]{:S(2)}) collective-permute-start(bf16[2,32,512]{2,1,0:T(8,128)(2,1)S(1)} %get-tuple-element.70), channel_id=1, source_target_pairs={{0,1},{1,0},{2,3},{3,2},{4,5},{5,4},{6,7},{7,6},{8,9},{9,8},{10,11... | collective-permute-start | bytes 196616 | tf_op jit(solution)/shard_map/ppermute | solution.py:282
  21.8 4.7 %copy-start.1 = (bf16[160,32,1280]{2,1,0:T(8,128)(2,1)S(1)}, bf16[160,32,1280]{2,1,0:T(8,128)(2,1)}, u32[]{:S(2)}) copy-start(bf16[160,32,1280]{2,1,0:T(8,128)(2,1)} %leg_ref.11) | copy-start | bytes 39321604
  28.0 1.6 %collective-permute-start.6 = (bf16[480,256]{1,0:T(8,128)(2,1)S(1)}, bf16[480,256]{1,0:T(8,128)(2,1)S(1)}, u32[]{:S(2)}, u32[]{:S(2)}) collective-permute-start(bf16[480,256]{1,0:T(8,128)(2,1)S(1)} %get-tuple-element.78), channel_id=1, source_target_pairs={{0,8},{8,0},{16,24},{24,16},{1,9},{9,1},{17,25},{25,17},{2,10},{10... | collective-permute-start | bytes 737288 | tf_op jit(solution)/shard_map/ppermute | solution.py:301
  28.0 5.1 %collective-permute-start.8 = (bf16[480,256]{1,0:T(8,128)(2,1)S(1)}, bf16[480,256]{1,0:T(8,128)(2,1)S(1)}, u32[]{:S(2)}, u32[]{:S(2)}) collective-permute-start(bf16[480,256]{1,0:T(8,128)(2,1)S(1)} %get-tuple-element.86), channel_id=1, source_target_pairs={{0,8},{8,0},{16,24},{24,16},{1,9},{9,1},{17,25},{25,17},{2,10},{10... | collective-permute-start | bytes 737288 | tf_op jit(solution)/shard_map/ppermute | solution.py:301
  29.6 8.2 %collective-permute-start.20 = (bf16[480,256]{1,0:T(8,128)(2,1)S(1)}, bf16[480,256]{1,0:T(8,128)(2,1)S(1)}, u32[]{:S(2)}, u32[]{:S(2)}) collective-permute-start(bf16[480,256]{1,0:T(8,128)(2,1)S(1)} %add_convert_fusion.4), channel_id=1, source_target_pairs={{0,16},{8,24},{16,0},{24,8},{1,17},{9,25},{17,1},{25,9},{2,18},{10... | collective-permute-start | bytes 737288 | tf_op jit(solution)/shard_map/ppermute | solution.py:319
  31.2 10.0 %slice-start = ((s8[13107200]{0:T(1024)(128)(4,1)}), s8[4194304]{0:T(1024)(128)(4,1)S(1)}, s32[]{:S(2)}) async-start(s8[13107200]{0:T(1024)(128)(4,1)} %bitcast.5), calls=%async_computation | async-start | bytes 8388608
  31.2 10.0 %slice-start.1 = ((s8[13107200]{0:T(1024)(128)(4,1)}), s8[4194304]{0:T(1024)(128)(4,1)S(1)}, s32[]{:S(2)}) async-start(s8[13107200]{0:T(1024)(128)(4,1)} %bitcast.5), calls=%async_computation.1 | async-start | bytes 8388608
  32.6 6.2 %collective-permute-start.10 = (bf16[480,256]{1,0:T(8,128)(2,1)S(1)}, bf16[480,256]{1,0:T(8,128)(2,1)S(1)}, u32[]{:S(2)}, u32[]{:S(2)}) collective-permute-start(bf16[480,256]{1,0:T(8,128)(2,1)S(1)} %get-tuple-element.94), channel_id=1, source_target_pairs={{0,8},{8,0},{16,24},{24,16},{1,9},{9,1},{17,25},{25,17},{2,10},{10... | collective-permute-start | bytes 737288 | tf_op jit(solution)/shard_map/ppermute | solution.py:301
  32.7 1.9 %collective-permute-start.7 = (bf16[480,256]{1,0:T(8,128)(2,1)S(1)}, bf16[480,256]{1,0:T(8,128)(2,1)S(1)}, u32[]{:S(2)}, u32[]{:S(2)}) collective-permute-start(bf16[480,256]{1,0:T(8,128)(2,1)S(1)} %get-tuple-element.84), channel_id=1, source_target_pairs={{0,8},{8,0},{16,24},{24,16},{1,9},{9,1},{17,25},{25,17},{2,10},{10... | collective-permute-start | bytes 737288 | tf_op jit(solution)/shard_map/ppermute | solution.py:301
  34.6 6.6 %slice-start.2 = ((s8[13107200]{0:T(1024)(128)(4,1)}), s8[4194304]{0:T(1024)(128)(4,1)S(1)}, s32[]{:S(2)}) async-start(s8[13107200]{0:T(1024)(128)(4,1)} %bitcast.5), calls=%async_computation.2 | async-start | bytes 8388608
  34.6 6.6 %slice-start.3 = ((s8[13107200]{0:T(1024)(128)(4,1)}), s8[524288]{0:T(1024)(128)(4,1)S(1)}, s32[]{:S(2)}) async-start(s8[13107200]{0:T(1024)(128)(4,1)} %bitcast.5), calls=%async_computation.3 | async-start | bytes 1048576
  34.6 8.9 %collective-permute-start.19 = (bf16[480,256]{1,0:T(8,128)(2,1)S(1)}, bf16[480,256]{1,0:T(8,128)(2,1)S(1)}, u32[]{:S(2)}, u32[]{:S(2)}) collective-permute-start(bf16[480,256]{1,0:T(8,128)(2,1)S(1)} %add_convert_fusion.3), channel_id=1, source_target_pairs={{0,16},{8,24},{16,0},{24,8},{1,17},{9,25},{17,1},{25,9},{2,18},{10... | collective-permute-start | bytes 737288 | tf_op jit(solution)/shard_map/ppermute | solution.py:319
  36.6 7.9 %collective-permute-start.12 = (bf16[480,256]{1,0:T(8,128)(2,1)S(1)}, bf16[480,256]{1,0:T(8,128)(2,1)S(1)}, u32[]{:S(2)}, u32[]{:S(2)}) collective-permute-start(bf16[480,256]{1,0:T(8,128)(2,1)S(1)} %get-tuple-element.102), channel_id=1, source_target_pairs={{0,8},{8,0},{16,24},{24,16},{1,9},{9,1},{17,25},{25,17},{2,10},{10... | collective-permute-start | bytes 737288 | tf_op jit(solution)/shard_map/ppermute | solution.py:301
  36.7 2.2 %collective-permute-start.9 = (bf16[480,256]{1,0:T(8,128)(2,1)S(1)}, bf16[480,256]{1,0:T(8,128)(2,1)S(1)}, u32[]{:S(2)}, u32[]{:S(2)}) collective-permute-start(bf16[480,256]{1,0:T(8,128)(2,1)S(1)} %get-tuple-element.92), channel_id=1, source_target_pairs={{0,8},{8,0},{16,24},{24,16},{1,9},{9,1},{17,25},{25,17},{2,10},{10... | collective-permute-start | bytes 737288 | tf_op jit(solution)/shard_map/ppermute | solution.py:301
  38.9 9.8 %collective-permute-start.18 = (bf16[480,256]{1,0:T(8,128)(2,1)S(1)}, bf16[480,256]{1,0:T(8,128)(2,1)S(1)}, u32[]{:S(2)}, u32[]{:S(2)}) collective-permute-start(bf16[480,256]{1,0:T(8,128)(2,1)S(1)} %add_convert_fusion.2), channel_id=1, source_target_pairs={{0,16},{8,24},{16,0},{24,8},{1,17},{9,25},{17,1},{25,9},{2,18},{10... | collective-permute-start | bytes 737288 | tf_op jit(solution)/shard_map/ppermute | solution.py:319
  42.6 7.1 %collective-permute-start.16 = (bf16[480,256]{1,0:T(8,128)(2,1)S(1)}, bf16[480,256]{1,0:T(8,128)(2,1)S(1)}, u32[]{:S(2)}, u32[]{:S(2)}) collective-permute-start(bf16[480,256]{1,0:T(8,128)(2,1)S(1)} %get-tuple-element.112), channel_id=1, source_target_pairs={{0,8},{8,0},{16,24},{24,16},{1,9},{9,1},{17,25},{25,17},{2,10},{10... | collective-permute-start | bytes 737288 | tf_op jit(solution)/shard_map/ppermute | solution.py:301
  42.7 1.9 %collective-permute-start.11 = (bf16[480,256]{1,0:T(8,128)(2,1)S(1)}, bf16[480,256]{1,0:T(8,128)(2,1)S(1)}, u32[]{:S(2)}, u32[]{:S(2)}) collective-permute-start(bf16[480,256]{1,0:T(8,128)(2,1)S(1)} %get-tuple-element.100), channel_id=1, source_target_pairs={{0,8},{8,0},{16,24},{24,16},{1,9},{9,1},{17,25},{25,17},{2,10},{10... | collective-permute-start | bytes 737288 | tf_op jit(solution)/shard_map/ppermute | solution.py:301
  44.6 9.4 %collective-permute-start.17 = (bf16[480,256]{1,0:T(8,128)(2,1)S(1)}, bf16[480,256]{1,0:T(8,128)(2,1)S(1)}, u32[]{:S(2)}, u32[]{:S(2)}) collective-permute-start(bf16[480,256]{1,0:T(8,128)(2,1)S(1)} %add_convert_fusion.1), channel_id=1, source_target_pairs={{0,16},{8,24},{16,0},{24,8},{1,17},{9,25},{17,1},{25,9},{2,18},{10... | collective-permute-start | bytes 737288 | tf_op jit(solution)/shard_map/ppermute | solution.py:319
  47.9 1.9 %collective-permute-start.14 = (bf16[480,256]{1,0:T(8,128)(2,1)S(1)}, bf16[480,256]{1,0:T(8,128)(2,1)S(1)}, u32[]{:S(2)}, u32[]{:S(2)}) collective-permute-start(bf16[480,256]{1,0:T(8,128)(2,1)S(1)} %get-tuple-element.110), channel_id=1, source_target_pairs={{0,8},{8,0},{16,24},{24,16},{1,9},{9,1},{17,25},{25,17},{2,10},{10... | collective-permute-start | bytes 737288 | tf_op jit(solution)/shard_map/ppermute | solution.py:301
  48.0 7.1 %collective-permute-start.13 = (bf16[480,256]{1,0:T(8,128)(2,1)S(1)}, bf16[480,256]{1,0:T(8,128)(2,1)S(1)}, u32[]{:S(2)}, u32[]{:S(2)}) collective-permute-start(bf16[480,256]{1,0:T(8,128)(2,1)S(1)} %get-tuple-element.108), channel_id=1, source_target_pairs={{0,8},{8,0},{16,24},{24,16},{1,9},{9,1},{17,25},{25,17},{2,10},{10... | collective-permute-start | bytes 737288 | tf_op jit(solution)/shard_map/ppermute | solution.py:301
  49.9 8.8 %collective-permute-start.15 = (bf16[480,256]{1,0:T(8,128)(2,1)S(1)}, bf16[480,256]{1,0:T(8,128)(2,1)S(1)}, u32[]{:S(2)}, u32[]{:S(2)}) collective-permute-start(bf16[480,256]{1,0:T(8,128)(2,1)S(1)} %add_convert_fusion), channel_id=1, source_target_pairs={{0,16},{8,24},{16,0},{24,8},{1,17},{9,25},{17,1},{25,9},{2,18},{10... | collective-permute-start | bytes 737288 | tf_op jit(solution)/shard_map/ppermute | solution.py:319

commit v12 on v11

--- a/solution.py
+++ b/solution.py
@@ -10,7 +10,7 @@
 LANES = 128
 STEP = 32
 TILE = 8
-VMEM = 20 * 1024 * 1024
+VMEM = 32 * 1024 * 1024
 
 
 def partner(block, axis, stride):
@@ -92,7 +92,7 @@
                 out[u, :, k * LANES : (k + 1) * LANES] = tile.astype(jnp.bfloat16)
 
 
-def place_kernel(turns, lat_count, row_count, pairs, degrees, table_ref, leg_ref, out, limits):
+def place_kernel(turns, lat_count, row_count, pairs, degrees, table_ref, out, limits):
     northern = lax.axis_index("lat") < lat_count // 2
     me = lax.axis_index("wave")
     row = lax.broadcasted_iota(jnp.int32, (LANES, 2 * LANES), 0) & (row_count - 1)
@@ -157,7 +157,6 @@
     sources = refs[:-6]
     far_sent, far_own, near_sent, near_own, far, near = refs[-6:]
     half = far.shape[1]
-    table = leg_ref.at[block * STEP : (block + 1) * STEP]
     lat = lax.axis_index("lat")
     y, core = lat // 2, lat % 2
     tile, off = shift_of(block, row_count * cols)
@@ -181,8 +180,8 @@
     north, south = both[:, :LANES], both[:, LANES:]
     even, odd = north + south, north - south
     far_coefs, near_coefs = jnp.where(y == 0, odd, even), jnp.where(y == 0, even, odd)
-    multiply(far_coefs, table, pl.multiple_of((1 - y) * half, LANES), half, far)
-    multiply(near_coefs, table, pl.multiple_of(y * half, LANES), half, near)
+    multiply(far_coefs, leg_ref, pl.multiple_of((1 - y) * half, LANES), half, far)
+    multiply(near_coefs, leg_ref, pl.multiple_of(y * half, LANES), half, near)
     pack(far, core, far_sent, far_own)
     pack(near, core, near_sent, near_own)
 
@@ -253,16 +252,19 @@
             jax.ShapeDtypeStruct((wave_count * LANES, 2 * LANES), jnp.bfloat16),
             jax.ShapeDtypeStruct((slots, LANES), jnp.int32),
         ],
-        in_specs=[pl.BlockSpec(memory_space=pltpu.SMEM), anywhere],
+        in_specs=[pl.BlockSpec(memory_space=pltpu.SMEM)],
         out_specs=[whole] * 2,
         compiler_params=params,
         name="place",
-    )(wave_table, legendre)
+    )(wave_table)
 
     passed = [ordered[0]] + [
         lax.ppermute(ordered[t], "wave", [(w, w ^ t * low) for w in range(wave_count)])
         for t in range(1, high)
     ]
+    count = slots // STEP
+    early = count - count // 2
+    tables = [legendre[block * STEP : (block + 1) * STEP] for block in range(early)]
     lower = lax.axis_index("wave") < wave_count // 2
     sources = []
     for mirrored in (False, True):
@@ -272,7 +274,9 @@
                 for side in (0, 1)
             ]
             block = jnp.where(lower != mirrored, sides[0], sides[1])
-            block, place = lax.optimization_barrier((block, place))
+            block, tables = lax.optimization_barrier((block, tables))
+            if not mirrored and u == 0:
+                later, block = lax.optimization_barrier((legendre, block))
             route = []
             for lat in range(lat_count):
                 for wave in range(wave_count):
@@ -281,6 +285,9 @@
             if mirrored or u:
                 block = lax.ppermute(block, ("lat", "wave"), route)
             sources.append(block)
+
+    tables += [later[block * STEP : (block + 1) * STEP] for block in range(early, count)]
+    sources, tables = lax.optimization_barrier((sources, tables))
 
     rows = STEP * cols
     shape = (rows + rows // 4, 2 * LANES)
@@ -295,8 +302,6 @@
         jax.ShapeDtypeStruct(shape, jnp.bfloat16),
         jax.ShapeDtypeStruct(shape, jnp.float32),
     ]
-    count = slots // STEP
-
     def settle(sent, kept):
         return kept + lax.ppermute(sent, "lat", core_route).astype(jnp.float32)
 
@@ -313,7 +318,7 @@
             compiler_params=params,
             cost_estimate=cost,
             name="product",
-        )(place, legendre, *sources)
+        )(place, tables[block], *sources)
         summed = settle(far_sent, far_own).astype(jnp.bfloat16)
         ties = [summed] + settled[-1:]
         crossed.append(lax.ppermute(summed, "lat", y_route))

time: 60 us -> 56.5 us (0.942)
  waiting for transfers between devices: 13.4 us -> 10.9 us
  local copies, waits for them, and re-layouts: 11.8 us -> 11.2 us
    unnamed x18 -> x8, local copies, waits for them, and re-layouts: 11.8 us -> 1.65 us
    slice x0 -> x2, local copies, waits for them, and re-layouts: none -> 7.97 us  [the longest x1 5.1 us: packed(): legendre[block * STEP:(block + 1) * STEP]]
    ppermute x3, waiting for transfers between devices: 3.94 us -> 1.04 us  [packed(): block = lax.ppermute(block, ('lat', 'wave'), route)]
    slice x4, local copies, waits for them, and re-layouts: 0.03 us -> 1.57 us  [packed(): passed[t][u]]
    ppermute x5, waiting for transfers between devices: 7.12 us -> 7.86 us  [packed(): crossed.append(lax.ppermute(summed, 'lat', y_route))]
  transfers between devices with their start and end apart: 21 -> 21, of which waited for: 10 -> 8; matrix products, arithmetic and copies ran while one was open for 1% -> 18% of each run, Pallas kernels for 18% -> 19%
where the time goes in v12:
time: 56.5 us; the launch traced here: 56.2 us
  starting transfers between devices  19.5 us (35%)
  Pallas kernels  13.8 us (24%)
  local copies, waits for them, and re-layouts  11.2 us (20%)
  waiting for transfers between devices  10.9 us (19%)
  other arithmetic  0.58 us (1%)
    ppermute x5, waiting for transfers between devices, packed(): crossed.append(lax.ppermute(summed, 'lat', y_route))  7.86 us
    ppermute x5, starting transfers between devices, packed(): crossed.append(lax.ppermute(summed, 'lat', y_route))  7.69 us
    pallas_call x5, Pallas kernels, packed(): pl.pallas_call(functools.partial(product_kernel, block, row_count, cols),...  7.09 us
    ppermute x3, starting transfers between devices, packed(): lax.ppermute(ordered[t], 'wave', [(w, w ^ t * low) for w in range(wave_co...  5.68 us
    slice x1, local copies, waits for them, and re-layouts, packed(): legendre[block * STEP:(block + 1) * STEP]  5.1 us
    pallas_call x5, Pallas kernels, packed(): pl.pallas_call(functools.partial(final_kernel, block * STEP, degrees, col...  5.06 us
    ppermute x3, starting transfers between devices, packed(): block = lax.ppermute(block, ('lat', 'wave'), route)  3.27 us
    slice x1, local copies, waits for them, and re-layouts, packed(): later[block * STEP:(block + 1) * STEP]  2.87 us
  transfers between devices with their start and end apart: 21, of which 8 were waited for; matrix products, arithmetic and copies ran while one was open for 18% of the time, Pallas kernels for 19%

profile of v12, /device:TPU:0, one launch (start us, length us, event | category | flops | bytes accessed | tf_op | source)
XLA Modules:
  0.0 56.2 jit_solution(3199489731951409133)
XLA Ops:
  0.0 0.9 %copy-done.2 = bf16[8,12,1280]{2,0,1:T(8,128)(2,1)S(1)} copy-done((bf16[8,12,1280]{2,0,1:T(8,128)(2,1)S(1)}, bf16[8,12,1280]{2,0,1:T(8,128)(2,1)}, u32[]{:S(2)}) %copy-start.2) | copy-done | bytes 245784
  0.9 0.7 %copy-done.3 = s32[1280]{0:T(1024)S(1)} copy-done((s32[1280]{0:T(1024)S(1)}, s32[1280]{0:T(1024)}, u32[]{:S(2)}) %copy-start.3) | copy-done | bytes 5144
  1.6 0.8 %gather.1 = (bf16[2,32,512]{2,1,0:T(8,128)(2,1)S(1)}, bf16[2,32,512]{2,1,0:T(8,128)(2,1)S(1)}, bf16[2,32,512]{2,1,0:T(8,128)(2,1)S(1)}, bf16[2,32,512]{2,1,0:T(8,128)(2,1)S(1)}) custom-call(s32[10,128]{1,0:T(8,128)S(1)} %bitcast.6, bf16[96,1280]{1,0:T(8,128)(2,1)S(1)} %bitcast.5), custom_call_target="tpu_custom_call" | custom-call | tf_op jit(solution)/shard_map/gather/pallas_call | solution.py:236
  2.5 3.1 %collective-permute-start = (bf16[2,32,512]{2,1,0:T(8,128)(2,1)S(1)}, bf16[2,32,512]{2,1,0:T(8,128)(2,1)}, u32[]{:S(2)}, u32[]{:S(2)}) collective-permute-start(bf16[2,32,512]{2,1,0:T(8,128)(2,1)S(1)} %get-tuple-element.81), channel_id=1, source_target_pairs={{0,2},{1,3},{2,0},{3,1},{4,6},{5,7},{6,4},{7,5},{8,10},{9,11},{10,... | collective-permute-start | bytes 196616 | tf_op jit(solution)/shard_map/ppermute | solution.py:262
  5.6 2.6 %collective-permute-start.1 = (bf16[2,32,512]{2,1,0:T(8,128)(2,1)S(1)}, bf16[2,32,512]{2,1,0:T(8,128)(2,1)}, u32[]{:S(2)}, u32[]{:S(2)}) collective-permute-start(bf16[2,32,512]{2,1,0:T(8,128)(2,1)S(1)} %get-tuple-element.82), channel_id=1, source_target_pairs={{0,4},{1,5},{2,6},{3,7},{4,0},{5,1},{6,2},{7,3},{8,12},{9,13},{10,... | collective-permute-start | bytes 196616 | tf_op jit(solution)/shard_map/ppermute | solution.py:262
  8.1 0.0 collective-permute-start.2
  8.1 5.1 %fusion.1 = (bf16[32,32,1280]{2,1,0:T(8,128)(2,1)S(1)}, bf16[32,32,1280]{2,1,0:T(8,128)(2,1)}, bf16[32,32,1280]{2,1,0:T(8,128)(2,1)}) fusion(bf16[160,32,1280]{2,1,0:T(8,128)(2,1)} %param.5), kind=kLoop, calls=%fused_computation.19 | loop fusion | bytes 15728640 | tf_op jit(solution)/shard_map/slice | solution.py:267
  13.3 0.9 %place.1 = (bf16[1024,256]{1,0:T(8,128)(2,1)S(1)}, s32[160,128]{1,0:T(8,128)S(1)}) custom-call(s32[1280]{0:T(1024)S(1)} %copy-done.3), custom_call_target="tpu_custom_call" | custom-call | tf_op jit(solution)/shard_map/place/pallas_call | solution.py:249
  14.2 0.0 collective-permute-done
  14.2 0.8 %fusion.3 = (bf16[1,32,512]{2,1,0:T(8,128)(2,1)S(1)}, bf16[1,32,512]{2,1,0:T(8,128)(2,1)S(1)}) fusion(bf16[2,32,512]{2,1,0:T(8,128)(2,1)} %collective-permute-done), kind=kLoop, calls=%fused_computation.21 | loop fusion | bytes 131072 | tf_op jit(solution)/shard_map/slice | solution.py:273
  15.0 0.0 collective-permute-done.1
  15.0 0.8 %fusion.4 = (bf16[1,32,512]{2,1,0:T(8,128)(2,1)S(1)}, bf16[1,32,512]{2,1,0:T(8,128)(2,1)S(1)}) fusion(bf16[2,32,512]{2,1,0:T(8,128)(2,1)} %collective-permute-done.1), kind=kLoop, calls=%fused_computation.22 | loop fusion | bytes 131072 | tf_op jit(solution)/shard_map/slice | solution.py:273
  15.7 0.0 collective-permute-done.2
  15.8 1.4 %collective-permute-start.5 = (bf16[2,32,512]{2,1,0:T(8,128)(2,1)S(1)}, bf16[2,32,512]{2,1,0:T(8,128)(2,1)S(1)}, u32[]{:S(2)}, u32[]{:S(2)}) collective-permute-start(bf16[2,32,512]{2,1,0:T(8,128)(2,1)S(1)} %get-tuple-element.97), channel_id=1, source_target_pairs={{0,25},{1,24},{2,27},{3,26},{4,29},{5,28},{6,31},{7,30},{8,17},{9,... | collective-permute-start | bytes 196616 | tf_op jit(solution)/shard_map/ppermute | solution.py:286
  17.2 1.6 %collective-permute-start.4 = (bf16[2,32,512]{2,1,0:T(8,128)(2,1)S(1)}, bf16[2,32,512]{2,1,0:T(8,128)(2,1)S(1)}, u32[]{:S(2)}, u32[]{:S(2)}) collective-permute-start(bf16[2,32,512]{2,1,0:T(8,128)(2,1)S(1)} %get-tuple-element.93), channel_id=1, source_target_pairs={{0,24},{1,25},{2,26},{3,27},{4,28},{5,29},{6,30},{7,31},{8,16},{9,... | collective-permute-start | bytes 196616 | tf_op jit(solution)/shard_map/ppermute | solution.py:286
  18.8 0.3 collective-permute-start.3
  19.1 2.9 %fusion = (bf16[32,32,1280]{2,1,0:T(8,128)(2,1)S(1)}, bf16[32,32,1280]{2,1,0:T(8,128)(2,1)S(1)}) fusion(bf16[160,32,1280]{2,1,0:T(8,128)(2,1)} %param.5), kind=kLoop, calls=%fused_computation.18 | loop fusion | bytes 10485760 | tf_op jit(solution)/shard_map/slice | solution.py:289
  21.9 0.0 copy-start
  22.0 0.0 collective-permute-done.5.refs_3_
  22.0 1.0 %collective-permute-done.3.refs_1_ = bf16[2,32,512]{2,1,0:T(8,128)(2,1)S(1)} collective-permute-done((bf16[2,32,512]{2,1,0:T(8,128)(2,1)S(1)}, bf16[2,32,512]{2,1,0:T(8,128)(2,1)S(1)}, u32[]{:S(2)}, u32[]{:S(2)}) %collective-permute-start.3) | collective-permute-done | bytes 65568 | tf_op jit(solution)/shard_map/ppermute | solution.py:286
  23.0 1.4 %product.5 = (bf16[480,256]{1,0:T(8,128)(2,1)S(1)}, f32[480,256]{1,0:T(8,128)S(1)}, bf16[480,256]{1,0:T(8,128)(2,1)S(1)}, f32[480,256]{1,0:T(8,128)S(1)}) custom-call(bf16[1024,256]{1,0:T(8,128)(2,1)S(1)} %get-tuple-element.79.place_ref, bf16[32,32,1280]{2,1,0:T(8,128)(2,1)S(1)} %copy-done.1, bf16[2,32,512]{2,1,0:T(8,128)(2,1)S(1)} %get-tuple-element.141.refs_0_, ...), custom_call_target="tpu_custom_call" | custom-call | bytes 1024 | tf_op jit(solution)/shard_map/product/pallas_call | solution.py:312
  24.4 0.1 collective-permute-start.6
  24.5 0.5 collective-permute-start.8
  25.0 1.0 %collective-permute-done.6 = bf16[480,256]{1,0:T(8,128)(2,1)S(1)} collective-permute-done((bf16[480,256]{1,0:T(8,128)(2,1)S(1)}, bf16[480,256]{1,0:T(8,128)(2,1)S(1)}, u32[]{:S(2)}, u32[]{:S(2)}) %collective-permute-start.6) | collective-permute-done | bytes 245792 | tf_op jit(solution)/shard_map/ppermute | solution.py:306
  26.0 0.1 add_convert_fusion.4
  26.1 1.6 %collective-permute-start.20 = (bf16[480,256]{1,0:T(8,128)(2,1)S(1)}, bf16[480,256]{1,0:T(8,128)(2,1)S(1)}, u32[]{:S(2)}, u32[]{:S(2)}) collective-permute-start(bf16[480,256]{1,0:T(8,128)(2,1)S(1)} %add_convert_fusion.4), channel_id=1, source_target_pairs={{0,16},{8,24},{16,0},{24,8},{1,17},{9,25},{17,1},{25,9},{2,18},{10... | collective-permute-start | bytes 737288 | tf_op jit(solution)/shard_map/ppermute | solution.py:324
  27.7 1.4 %product.6 = (bf16[480,256]{1,0:T(8,128)(2,1)S(1)}, f32[480,256]{1,0:T(8,128)S(1)}, bf16[480,256]{1,0:T(8,128)(2,1)S(1)}, f32[480,256]{1,0:T(8,128)S(1)}) custom-call(bf16[1024,256]{1,0:T(8,128)(2,1)S(1)} %get-tuple-element.79.place_ref, bf16[32,32,1280]{2,1,0:T(8,128)(2,1)S(1)} %copy-done, bf16[2,32,512]{2,1,0:T(8,128)(2,1)S(1)} %get-tuple-element.141.refs_0_, ...), custom_call_target="tpu_custom_call" | custom-call | bytes 1024 | tf_op jit(solution)/shard_map/product/pallas_call | solution.py:312
  29.1 0.1 collective-permute-start.7
  29.2 0.5 collective-permute-start.10
  29.7 0.0 collective-permute-done.8
  29.7 0.1 convert_add_fusion.4.near_ref
  29.7 0.9 %collective-permute-done.7 = bf16[480,256]{1,0:T(8,128)(2,1)S(1)} collective-permute-done((bf16[480,256]{1,0:T(8,128)(2,1)S(1)}, bf16[480,256]{1,0:T(8,128)(2,1)S(1)}, u32[]{:S(2)}, u32[]{:S(2)}) %collective-permute-start.7) | collective-permute-done | bytes 245792 | tf_op jit(solution)/shard_map/ppermute | solution.py:306
  30.7 0.1 add_convert_fusion.3
  30.7 0.6 %collective-permute-start.19 = (bf16[480,256]{1,0:T(8,128)(2,1)S(1)}, bf16[480,256]{1,0:T(8,128)(2,1)S(1)}, u32[]{:S(2)}, u32[]{:S(2)}) collective-permute-start(bf16[480,256]{1,0:T(8,128)(2,1)S(1)} %add_convert_fusion.3), channel_id=1, source_target_pairs={{0,16},{8,24},{16,0},{24,8},{1,17},{9,25},{17,1},{25,9},{2,18},{10... | collective-permute-start | bytes 737288 | tf_op jit(solution)/shard_map/ppermute | solution.py:324
  31.3 1.4 %product.7 = (bf16[480,256]{1,0:T(8,128)(2,1)S(1)}, f32[480,256]{1,0:T(8,128)S(1)}, bf16[480,256]{1,0:T(8,128)(2,1)S(1)}, f32[480,256]{1,0:T(8,128)S(1)}) custom-call(bf16[1024,256]{1,0:T(8,128)(2,1)S(1)} %get-tuple-element.79.place_ref, bf16[32,32,1280]{2,1,0:T(8,128)(2,1)S(1)} %get-tuple-element.127.leg_ref, ...), custom_call_target="tpu_custom_call" | custom-call | bytes 1024 | tf_op jit(solution)/shard_map/product/pallas_call | solution.py:312
  32.7 0.1 collective-permute-start.9
  32.8 0.5 collective-permute-start.12
  33.3 1.4 %collective-permute-done.20.far_ref = bf16[480,256]{1,0:T(8,128)(2,1)S(1)} collective-permute-done((bf16[480,256]{1,0:T(8,128)(2,1)S(1)}, bf16[480,256]{1,0:T(8,128)(2,1)S(1)}, u32[]{:S(2)}, u32[]{:S(2)}) %collective-permute-start.20) | collective-permute-done | bytes 245792 | tf_op jit(solution)/shard_map/ppermute | solution.py:324
  34.7 1.0 %final.5.refs_0_ = f32[12,160,320]{2,1,0:T(8,128)} custom-call(s32[160,128]{1,0:T(8,128)S(1)} %get-tuple-element.78.limits_ref, f32[480,256]{1,0:T(8,128)S(1)} %convert_add_fusion.4.near_ref, bf16[480,256]{1,0:T(8,128)(2,1)S(1)} %collective-permute-done.20.far_ref), custom_call_target="tpu_custom_call" | custom-call | bytes 1024 | tf_op jit(solution)/shard_map/final/pallas_call | solution.py:330
  35.7 0.0 collective-permute-done.10
  35.7 0.1 convert_add_fusion.3.near_ref
  35.8 0.0 collective-permute-done.9
  35.8 0.1 add_convert_fusion.2
  35.8 1.8 %collective-permute-start.18 = (bf16[480,256]{1,0:T(8,128)(2,1)S(1)}, bf16[480,256]{1,0:T(8,128)(2,1)S(1)}, u32[]{:S(2)}, u32[]{:S(2)}) collective-permute-start(bf16[480,256]{1,0:T(8,128)(2,1)S(1)} %add_convert_fusion.2), channel_id=1, source_target_pairs={{0,16},{8,24},{16,0},{24,8},{1,17},{9,25},{17,1},{25,9},{2,18},{10... | collective-permute-start | bytes 737288 | tf_op jit(solution)/shard_map/ppermute | solution.py:324
  37.7 1.4 %product.8 = (bf16[480,256]{1,0:T(8,128)(2,1)S(1)}, f32[480,256]{1,0:T(8,128)S(1)}, bf16[480,256]{1,0:T(8,128)(2,1)S(1)}, f32[480,256]{1,0:T(8,128)S(1)}) custom-call(bf16[1024,256]{1,0:T(8,128)(2,1)S(1)} %get-tuple-element.79.place_ref, bf16[32,32,1280]{2,1,0:T(8,128)(2,1)S(1)} %get-tuple-element.136.leg_ref, ...), custom_call_target="tpu_custom_call" | custom-call | bytes 1024 | tf_op jit(solution)/shard_map/product/pallas_call | solution.py:312
  39.1 0.1 collective-permute-start.11
  39.2 0.5 collective-permute-start.16
  39.7 0.3 collective-permute-done.19.far_ref
  40.0 1.0 %final.6.refs_0_ = f32[12,160,320]{2,1,0:T(8,128)} custom-call(s32[160,128]{1,0:T(8,128)S(1)} %get-tuple-element.78.limits_ref, f32[480,256]{1,0:T(8,128)S(1)} %convert_add_fusion.3.near_ref, bf16[480,256]{1,0:T(8,128)(2,1)S(1)} %collective-permute-done.19.far_ref, f32[12,160,320]{2,1,0:T(8,128)} %final.5.refs_0_), custom_call_target="tpu_custom_call", output_to_operand_aliasing={{}: (3, {})} | custom-call | bytes 1024 | tf_op jit(solution)/shard_map/final/pallas_call | solution.py:330
  41.0 0.0 collective-permute-done.11
  41.0 0.1 add_convert_fusion.1
  41.1 1.8 %collective-permute-start.17 = (bf16[480,256]{1,0:T(8,128)(2,1)S(1)}, bf16[480,256]{1,0:T(8,128)(2,1)S(1)}, u32[]{:S(2)}, u32[]{:S(2)}) collective-permute-start(bf16[480,256]{1,0:T(8,128)(2,1)S(1)} %add_convert_fusion.1), channel_id=1, source_target_pairs={{0,16},{8,24},{16,0},{24,8},{1,17},{9,25},{17,1},{25,9},{2,18},{10... | collective-permute-start | bytes 737288 | tf_op jit(solution)/shard_map/ppermute | solution.py:324
  42.9 1.4 %product.9 = (bf16[480,256]{1,0:T(8,128)(2,1)S(1)}, f32[480,256]{1,0:T(8,128)S(1)}, bf16[480,256]{1,0:T(8,128)(2,1)S(1)}, f32[480,256]{1,0:T(8,128)S(1)}) custom-call(bf16[1024,256]{1,0:T(8,128)(2,1)S(1)} %get-tuple-element.79.place_ref, bf16[32,32,1280]{2,1,0:T(8,128)(2,1)S(1)} %get-tuple-element.102.leg_ref, ...), custom_call_target="tpu_custom_call" | custom-call | bytes 1024 | tf_op jit(solution)/shard_map/product/pallas_call | solution.py:312
  44.4 0.1 collective-permute-start.13
  44.4 0.5 collective-permute-start.14
  44.9 0.3 collective-permute-done.18.far_ref
  45.2 1.0 %final.7.refs_0_ = f32[12,160,320]{2,1,0:T(8,128)} custom-call(s32[160,128]{1,0:T(8,128)S(1)} %get-tuple-element.78.limits_ref, f32[480,256]{1,0:T(8,128)S(1)} %convert_add_fusion.2.near_ref, bf16[480,256]{1,0:T(8,128)(2,1)S(1)} %collective-permute-done.18.far_ref, f32[12,160,320]{2,1,0:T(8,128)} %final.6.refs_0_), custom_call_target="tpu_custom_call", output_to_operand_aliasing={{}: (3, {})} | custom-call | bytes 1024 | tf_op jit(solution)/shard_map/final/pallas_call | solution.py:330
  46.2 0.0 collective-permute-done.16
  46.3 0.1 add_convert_fusion
  46.4 1.8 %collective-permute-start.15 = (bf16[480,256]{1,0:T(8,128)(2,1)S(1)}, bf16[480,256]{1,0:T(8,128)(2,1)S(1)}, u32[]{:S(2)}, u32[]{:S(2)}) collective-permute-start(bf16[480,256]{1,0:T(8,128)(2,1)S(1)} %add_convert_fusion), channel_id=1, source_target_pairs={{0,16},{8,24},{16,0},{24,8},{1,17},{9,25},{17,1},{25,9},{2,18},{10... | collective-permute-start | bytes 737288 | tf_op jit(solution)/shard_map/ppermute | solution.py:324
  48.2 2.3 %collective-permute-done.17.far_ref = bf16[480,256]{1,0:T(8,128)(2,1)S(1)} collective-permute-done((bf16[480,256]{1,0:T(8,128)(2,1)S(1)}, bf16[480,256]{1,0:T(8,128)(2,1)S(1)}, u32[]{:S(2)}, u32[]{:S(2)}) %collective-permute-start.17) | collective-permute-done | bytes 245792 | tf_op jit(solution)/shard_map/ppermute | solution.py:324
  50.5 1.0 %final.8.refs_0_ = f32[12,160,320]{2,1,0:T(8,128)} custom-call(s32[160,128]{1,0:T(8,128)S(1)} %get-tuple-element.78.limits_ref, f32[480,256]{1,0:T(8,128)S(1)} %convert_add_fusion.near_ref, bf16[480,256]{1,0:T(8,128)(2,1)S(1)} %collective-permute-done.17.far_ref, f32[12,160,320]{2,1,0:T(8,128)} %final.7.refs_0_), custom_call_target="tpu_custom_call", output_to_operand_aliasing={{}: (3, {})} | custom-call | bytes 1024 | tf_op jit(solution)/shard_map/final/pallas_call | solution.py:330
  51.6 3.6 %collective-permute-done.15.far_ref = bf16[480,256]{1,0:T(8,128)(2,1)S(1)} collective-permute-done((bf16[480,256]{1,0:T(8,128)(2,1)S(1)}, bf16[480,256]{1,0:T(8,128)(2,1)S(1)}, u32[]{:S(2)}, u32[]{:S(2)}) %collective-permute-start.15) | collective-permute-done | bytes 245792 | tf_op jit(solution)/shard_map/ppermute | solution.py:324
  55.2 1.0 %final.9 = f32[12,160,320]{2,1,0:T(8,128)} custom-call(s32[160,128]{1,0:T(8,128)S(1)} %get-tuple-element.78.limits_ref, f32[480,256]{1,0:T(8,128)S(1)} %convert_add_fusion.1.near_ref, bf16[480,256]{1,0:T(8,128)(2,1)S(1)} %collective-permute-done.15.far_ref, f32[12,160,320]{2,1,0:T(8,128)} %final.8.refs_0_), custom_call_target="tpu_custom_call", output_to_operand_aliasing={{}: (3, {})} | custom-call | bytes 1024 | tf_op jit(solution)/shard_map/final/pallas_call | solution.py:330
  (15 shorter events, 0.2 us)
Async XLA Ops:
  0.0 0.9 %copy-start.2 = (bf16[8,12,1280]{2,0,1:T(8,128)(2,1)S(1)}, bf16[8,12,1280]{2,0,1:T(8,128)(2,1)}, u32[]{:S(2)}) copy-start(bf16[8,12,1280]{2,0,1:T(8,128)(2,1)} %param.3) | copy-start | bytes 737284
  0.9 0.7 %copy-start.3 = (s32[1280]{0:T(1024)S(1)}, s32[1280]{0:T(1024)}, u32[]{:S(2)}) copy-start(s32[1280]{0:T(1024)} %table_ref.1) | copy-start | bytes 15364
  2.5 11.7 %collective-permute-start = (bf16[2,32,512]{2,1,0:T(8,128)(2,1)S(1)}, bf16[2,32,512]{2,1,0:T(8,128)(2,1)}, u32[]{:S(2)}, u32[]{:S(2)}) collective-permute-start(bf16[2,32,512]{2,1,0:T(8,128)(2,1)S(1)} %get-tuple-element.81), channel_id=1, source_target_pairs={{0,2},{1,3},{2,0},{3,1},{4,6},{5,7},{6,4},{7,5},{8,10},{9,11},{10,... | collective-permute-start | bytes 196616 | tf_op jit(solution)/shard_map/ppermute | solution.py:262
  5.6 9.4 %collective-permute-start.1 = (bf16[2,32,512]{2,1,0:T(8,128)(2,1)S(1)}, bf16[2,32,512]{2,1,0:T(8,128)(2,1)}, u32[]{:S(2)}, u32[]{:S(2)}) collective-permute-start(bf16[2,32,512]{2,1,0:T(8,128)(2,1)S(1)} %get-tuple-element.82), channel_id=1, source_target_pairs={{0,4},{1,5},{2,6},{3,7},{4,0},{5,1},{6,2},{7,3},{8,12},{9,13},{10,... | collective-permute-start | bytes 196616 | tf_op jit(solution)/shard_map/ppermute | solution.py:262
  8.1 7.6 %collective-permute-start.2 = (bf16[2,32,512]{2,1,0:T(8,128)(2,1)S(1)}, bf16[2,32,512]{2,1,0:T(8,128)(2,1)S(1)}, u32[]{:S(2)}, u32[]{:S(2)}) collective-permute-start(bf16[2,32,512]{2,1,0:T(8,128)(2,1)S(1)} %get-tuple-element.83), channel_id=1, source_target_pairs={{0,6},{1,7},{2,4},{3,5},{4,2},{5,3},{6,0},{7,1},{8,14},{9,15},{10,... | collective-permute-start | bytes 196616 | tf_op jit(solution)/shard_map/ppermute | solution.py:262
  15.8 7.2 %copy-start.1 = (bf16[32,32,1280]{2,1,0:T(8,128)(2,1)S(1)}, bf16[32,32,1280]{2,1,0:T(8,128)(2,1)}, u32[]{:S(2)}) copy-start(bf16[32,32,1280]{2,1,0:T(8,128)(2,1)} %get-tuple-element.111.leg_ref) | copy-start | bytes 7864324
  15.8 6.2 %collective-permute-start.5 = (bf16[2,32,512]{2,1,0:T(8,128)(2,1)S(1)}, bf16[2,32,512]{2,1,0:T(8,128)(2,1)S(1)}, u32[]{:S(2)}, u32[]{:S(2)}) collective-permute-start(bf16[2,32,512]{2,1,0:T(8,128)(2,1)S(1)} %get-tuple-element.97), channel_id=1, source_target_pairs={{0,25},{1,24},{2,27},{3,26},{4,29},{5,28},{6,31},{7,30},{8,17},{9,... | collective-permute-start | bytes 196616 | tf_op jit(solution)/shard_map/ppermute | solution.py:286
  17.2 4.8 %collective-permute-start.4 = (bf16[2,32,512]{2,1,0:T(8,128)(2,1)S(1)}, bf16[2,32,512]{2,1,0:T(8,128)(2,1)S(1)}, u32[]{:S(2)}, u32[]{:S(2)}) collective-permute-start(bf16[2,32,512]{2,1,0:T(8,128)(2,1)S(1)} %get-tuple-element.93), channel_id=1, source_target_pairs={{0,24},{1,25},{2,26},{3,27},{4,28},{5,29},{6,30},{7,31},{8,16},{9,... | collective-permute-start | bytes 196616 | tf_op jit(solution)/shard_map/ppermute | solution.py:286
  18.8 4.3 %collective-permute-start.3 = (bf16[2,32,512]{2,1,0:T(8,128)(2,1)S(1)}, bf16[2,32,512]{2,1,0:T(8,128)(2,1)S(1)}, u32[]{:S(2)}, u32[]{:S(2)}) collective-permute-start(bf16[2,32,512]{2,1,0:T(8,128)(2,1)S(1)} %get-tuple-element.89), channel_id=1, source_target_pairs={{0,1},{1,0},{2,3},{3,2},{4,5},{5,4},{6,7},{7,6},{8,9},{9,8},{10,11... | collective-permute-start | bytes 196616 | tf_op jit(solution)/shard_map/ppermute | solution.py:286
  21.9 5.7 %copy-start = (bf16[32,32,1280]{2,1,0:T(8,128)(2,1)S(1)}, bf16[32,32,1280]{2,1,0:T(8,128)(2,1)}, u32[]{:S(2)}) copy-start(bf16[32,32,1280]{2,1,0:T(8,128)(2,1)} %get-tuple-element.118.leg_ref) | copy-start | bytes 7864324
  24.4 1.6 %collective-permute-start.6 = (bf16[480,256]{1,0:T(8,128)(2,1)S(1)}, bf16[480,256]{1,0:T(8,128)(2,1)S(1)}, u32[]{:S(2)}, u32[]{:S(2)}) collective-permute-start(bf16[480,256]{1,0:T(8,128)(2,1)S(1)} %get-tuple-element.113), channel_id=1, source_target_pairs={{0,8},{8,0},{16,24},{24,16},{1,9},{9,1},{17,25},{25,17},{2,10},{10... | collective-permute-start | bytes 737288 | tf_op jit(solution)/shard_map/ppermute | solution.py:306
  24.5 5.1 %collective-permute-start.8 = (bf16[480,256]{1,0:T(8,128)(2,1)S(1)}, bf16[480,256]{1,0:T(8,128)(2,1)S(1)}, u32[]{:S(2)}, u32[]{:S(2)}) collective-permute-start(bf16[480,256]{1,0:T(8,128)(2,1)S(1)} %get-tuple-element.122), channel_id=1, source_target_pairs={{0,8},{8,0},{16,24},{24,16},{1,9},{9,1},{17,25},{25,17},{2,10},{10... | collective-permute-start | bytes 737288 | tf_op jit(solution)/shard_map/ppermute | solution.py:306
  26.1 8.6 %collective-permute-start.20 = (bf16[480,256]{1,0:T(8,128)(2,1)S(1)}, bf16[480,256]{1,0:T(8,128)(2,1)S(1)}, u32[]{:S(2)}, u32[]{:S(2)}) collective-permute-start(bf16[480,256]{1,0:T(8,128)(2,1)S(1)} %add_convert_fusion.4), channel_id=1, source_target_pairs={{0,16},{8,24},{16,0},{24,8},{1,17},{9,25},{17,1},{25,9},{2,18},{10... | collective-permute-start | bytes 737288 | tf_op jit(solution)/shard_map/ppermute | solution.py:324
  29.1 1.6 %collective-permute-start.7 = (bf16[480,256]{1,0:T(8,128)(2,1)S(1)}, bf16[480,256]{1,0:T(8,128)(2,1)S(1)}, u32[]{:S(2)}, u32[]{:S(2)}) collective-permute-start(bf16[480,256]{1,0:T(8,128)(2,1)S(1)} %get-tuple-element.120), channel_id=1, source_target_pairs={{0,8},{8,0},{16,24},{24,16},{1,9},{9,1},{17,25},{25,17},{2,10},{10... | collective-permute-start | bytes 737288 | tf_op jit(solution)/shard_map/ppermute | solution.py:306
  29.2 6.5 %collective-permute-start.10 = (bf16[480,256]{1,0:T(8,128)(2,1)S(1)}, bf16[480,256]{1,0:T(8,128)(2,1)S(1)}, u32[]{:S(2)}, u32[]{:S(2)}) collective-permute-start(bf16[480,256]{1,0:T(8,128)(2,1)S(1)} %get-tuple-element.131), channel_id=1, source_target_pairs={{0,8},{8,0},{16,24},{24,16},{1,9},{9,1},{17,25},{25,17},{2,10},{10... | collective-permute-start | bytes 737288 | tf_op jit(solution)/shard_map/ppermute | solution.py:306
  30.7 9.2 %collective-permute-start.19 = (bf16[480,256]{1,0:T(8,128)(2,1)S(1)}, bf16[480,256]{1,0:T(8,128)(2,1)S(1)}, u32[]{:S(2)}, u32[]{:S(2)}) collective-permute-start(bf16[480,256]{1,0:T(8,128)(2,1)S(1)} %add_convert_fusion.3), channel_id=1, source_target_pairs={{0,16},{8,24},{16,0},{24,8},{1,17},{9,25},{17,1},{25,9},{2,18},{10... | collective-permute-start | bytes 737288 | tf_op jit(solution)/shard_map/ppermute | solution.py:324
  32.7 3.0 %collective-permute-start.9 = (bf16[480,256]{1,0:T(8,128)(2,1)S(1)}, bf16[480,256]{1,0:T(8,128)(2,1)S(1)}, u32[]{:S(2)}, u32[]{:S(2)}) collective-permute-start(bf16[480,256]{1,0:T(8,128)(2,1)S(1)} %get-tuple-element.129), channel_id=1, source_target_pairs={{0,8},{8,0},{16,24},{24,16},{1,9},{9,1},{17,25},{25,17},{2,10},{10... | collective-permute-start | bytes 737288 | tf_op jit(solution)/shard_map/ppermute | solution.py:306
  32.8 8.1 %collective-permute-start.12 = (bf16[480,256]{1,0:T(8,128)(2,1)S(1)}, bf16[480,256]{1,0:T(8,128)(2,1)S(1)}, u32[]{:S(2)}, u32[]{:S(2)}) collective-permute-start(bf16[480,256]{1,0:T(8,128)(2,1)S(1)} %get-tuple-element.140), channel_id=1, source_target_pairs={{0,8},{8,0},{16,24},{24,16},{1,9},{9,1},{17,25},{25,17},{2,10},{10... | collective-permute-start | bytes 737288 | tf_op jit(solution)/shard_map/ppermute | solution.py:306
  35.8 9.4 %collective-permute-start.18 = (bf16[480,256]{1,0:T(8,128)(2,1)S(1)}, bf16[480,256]{1,0:T(8,128)(2,1)S(1)}, u32[]{:S(2)}, u32[]{:S(2)}) collective-permute-start(bf16[480,256]{1,0:T(8,128)(2,1)S(1)} %add_convert_fusion.2), channel_id=1, source_target_pairs={{0,16},{8,24},{16,0},{24,8},{1,17},{9,25},{17,1},{25,9},{2,18},{10... | collective-permute-start | bytes 737288 | tf_op jit(solution)/shard_map/ppermute | solution.py:324
  39.1 1.9 %collective-permute-start.11 = (bf16[480,256]{1,0:T(8,128)(2,1)S(1)}, bf16[480,256]{1,0:T(8,128)(2,1)S(1)}, u32[]{:S(2)}, u32[]{:S(2)}) collective-permute-start(bf16[480,256]{1,0:T(8,128)(2,1)S(1)} %get-tuple-element.138), channel_id=1, source_target_pairs={{0,8},{8,0},{16,24},{24,16},{1,9},{9,1},{17,25},{25,17},{2,10},{10... | collective-permute-start | bytes 737288 | tf_op jit(solution)/shard_map/ppermute | solution.py:306
  39.2 7.1 %collective-permute-start.16 = (bf16[480,256]{1,0:T(8,128)(2,1)S(1)}, bf16[480,256]{1,0:T(8,128)(2,1)S(1)}, u32[]{:S(2)}, u32[]{:S(2)}) collective-permute-start(bf16[480,256]{1,0:T(8,128)(2,1)S(1)} %get-tuple-element.150), channel_id=1, source_target_pairs={{0,8},{8,0},{16,24},{24,16},{1,9},{9,1},{17,25},{25,17},{2,10},{10... | collective-permute-start | bytes 737288 | tf_op jit(solution)/shard_map/ppermute | solution.py:306
  41.1 9.4 %collective-permute-start.17 = (bf16[480,256]{1,0:T(8,128)(2,1)S(1)}, bf16[480,256]{1,0:T(8,128)(2,1)S(1)}, u32[]{:S(2)}, u32[]{:S(2)}) collective-permute-start(bf16[480,256]{1,0:T(8,128)(2,1)S(1)} %add_convert_fusion.1), channel_id=1, source_target_pairs={{0,16},{8,24},{16,0},{24,8},{1,17},{9,25},{17,1},{25,9},{2,18},{10... | collective-permute-start | bytes 737288 | tf_op jit(solution)/shard_map/ppermute | solution.py:324
  44.4 7.1 %collective-permute-start.13 = (bf16[480,256]{1,0:T(8,128)(2,1)S(1)}, bf16[480,256]{1,0:T(8,128)(2,1)S(1)}, u32[]{:S(2)}, u32[]{:S(2)}) collective-permute-start(bf16[480,256]{1,0:T(8,128)(2,1)S(1)} %get-tuple-element.146), channel_id=1, source_target_pairs={{0,8},{8,0},{16,24},{24,16},{1,9},{9,1},{17,25},{25,17},{2,10},{10... | collective-permute-start | bytes 737288 | tf_op jit(solution)/shard_map/ppermute | solution.py:306
  44.4 1.9 %collective-permute-start.14 = (bf16[480,256]{1,0:T(8,128)(2,1)S(1)}, bf16[480,256]{1,0:T(8,128)(2,1)S(1)}, u32[]{:S(2)}, u32[]{:S(2)}) collective-permute-start(bf16[480,256]{1,0:T(8,128)(2,1)S(1)} %get-tuple-element.148), channel_id=1, source_target_pairs={{0,8},{8,0},{16,24},{24,16},{1,9},{9,1},{17,25},{25,17},{2,10},{10... | collective-permute-start | bytes 737288 | tf_op jit(solution)/shard_map/ppermute | solution.py:306
  46.4 8.8 %collective-permute-start.15 = (bf16[480,256]{1,0:T(8,128)(2,1)S(1)}, bf16[480,256]{1,0:T(8,128)(2,1)S(1)}, u32[]{:S(2)}, u32[]{:S(2)}) collective-permute-start(bf16[480,256]{1,0:T(8,128)(2,1)S(1)} %add_convert_fusion), channel_id=1, source_target_pairs={{0,16},{8,24},{16,0},{24,8},{1,17},{9,25},{17,1},{25,9},{2,18},{10... | collective-permute-start | bytes 737288 | tf_op jit(solution)/shard_map/ppermute | solution.py:324

commit v13 on v7

--- a/solution.py
+++ b/solution.py
@@ -282,12 +282,7 @@
                     to = lat_count - 1 - lat if began else lat
                     route.append((lat * wave_count + wave, to * wave_count + (wave ^ u)))
             block, tables = lax.optimization_barrier((block, tables))
-            if side == 0 and u == 0:
-                later, block = lax.optimization_barrier((legendre, block))
             sources.append(lax.ppermute(block, ("lat", "wave"), route))
-
-    tables += [later[block * STEP : (block + 1) * STEP] for block in range(early, count)]
-    sources, tables = lax.optimization_barrier((sources, tables))
 
     rows = STEP * cols
     shape = (rows + rows // 4, 2 * LANES)
@@ -308,7 +303,11 @@
     crossed, settled = [], []
     ties = []
     for block in range(count):
-        sources, ties = lax.optimization_barrier((sources, ties))
+        if block == early - 1:
+            legendre, sources, ties = lax.optimization_barrier((legendre, sources, ties))
+            tables = tables + [legendre[k * STEP : (k + 1) * STEP] for k in range(early, count)]
+        else:
+            sources, ties = lax.optimization_barrier((sources, ties))
         far_sent, far_own, near_sent, near_own = pl.pallas_call(
             functools.partial(product_kernel, block, row_count, cols),
             out_shape=pair_of_sums * 2,

time: 56.3 us -> 56.5 us (level)
  waiting for transfers between devices: 12.1 us -> 13 us
  starting transfers between devices: 21 us -> 20.3 us
    ppermute x5, starting transfers between devices: 6.95 us -> 5.4 us  [packed(): crossed.append(lax.ppermute(summed, 'lat', y_route))]
    ppermute x3, waiting for transfers between devices: 1.39 us -> 2.32 us  [packed(): lax.ppermute(ordered[t], 'wave', [(w, w ^ t * low) for w in range(wave_co...]
    ppermute x10, starting transfers between devices: 2.85 us -> 3.66 us  [settle(): return kept + lax.ppermute(sent, 'lat', core_route).astype(jnp.float32)]
    ppermute x5, waiting for transfers between devices: 8.73 us -> 7.96 us  [packed(): crossed.append(lax.ppermute(summed, 'lat', y_route))]
    ppermute x4, waiting for transfers between devices: 0.01 us -> 0.71 us  [packed(): sources.append(lax.ppermute(block, ('lat', 'wave'), route))]
where the time goes in v13:
time: 56.5 us; the launch traced here: 56.2 us
  starting transfers between devices  20.3 us (36%)
  Pallas kernels  13.9 us (25%)
  waiting for transfers between devices  13 us (23%)
  local copies, waits for them, and re-layouts  8.22 us (15%)
    ppermute x5, waiting for transfers between devices, packed(): crossed.append(lax.ppermute(summed, 'lat', y_route))  7.96 us
    pallas_call x5, Pallas kernels, packed(): pl.pallas_call(functools.partial(product_kernel, block, row_count, cols),...  7.09 us
    ppermute x3, starting transfers between devices, packed(): lax.ppermute(ordered[t], 'wave', [(w, w ^ t * low) for w in range(wave_co...  5.68 us
    ppermute x4, starting transfers between devices, packed(): sources.append(lax.ppermute(block, ('lat', 'wave'), route))  5.55 us
    ppermute x5, starting transfers between devices, packed(): crossed.append(lax.ppermute(summed, 'lat', y_route))  5.4 us
    pallas_call x5, Pallas kernels, packed(): pl.pallas_call(functools.partial(final_kernel, block * STEP, degrees, col...  5.07 us
    slice x1, local copies, waits for them, and re-layouts, packed(): legendre[block * STEP:(block + 1) * STEP]  3.69 us
    ppermute x10, starting transfers between devices, settle(): return kept + lax.ppermute(sent, 'lat', core_route).astype(jnp.float32)  3.66 us
  transfers between devices with their start and end apart: 22, of which 8 were waited for; matrix products, arithmetic and copies ran while one was open for 13% of the time, Pallas kernels for 19%

profile of v13, /device:TPU:0, one launch (start us, length us, event | category | flops | bytes accessed | tf_op | source)
XLA Modules:
  0.0 56.2 jit_solution(14683029666012420019)
XLA Ops:
  0.0 0.9 %copy-done = bf16[8,12,1280]{2,0,1:T(8,128)(2,1)S(1)} copy-done((bf16[8,12,1280]{2,0,1:T(8,128)(2,1)S(1)}, bf16[8,12,1280]{2,0,1:T(8,128)(2,1)}, u32[]{:S(2)}) %copy-start) | copy-done | bytes 245784
  0.9 0.7 %copy-done.1 = s32[1280]{0:T(1024)S(1)} copy-done((s32[1280]{0:T(1024)S(1)}, s32[1280]{0:T(1024)}, u32[]{:S(2)}) %copy-start.1) | copy-done | bytes 5144
  1.6 0.8 %gather.1 = (bf16[2,32,512]{2,1,0:T(8,128)(2,1)S(1)}, bf16[2,32,512]{2,1,0:T(8,128)(2,1)S(1)}, bf16[2,32,512]{2,1,0:T(8,128)(2,1)S(1)}, bf16[2,32,512]{2,1,0:T(8,128)(2,1)S(1)}) custom-call(s32[10,128]{1,0:T(8,128)S(1)} %bitcast.6, bf16[96,1280]{1,0:T(8,128)(2,1)S(1)} %bitcast.5), custom_call_target="tpu_custom_call" | custom-call | tf_op jit(solution)/shard_map/gather/pallas_call | solution.py:237
  2.5 3.1 %collective-permute-start = (bf16[2,32,512]{2,1,0:T(8,128)(2,1)S(1)}, bf16[2,32,512]{2,1,0:T(8,128)(2,1)S(1)}, u32[]{:S(2)}, u32[]{:S(2)}) collective-permute-start(bf16[2,32,512]{2,1,0:T(8,128)(2,1)S(1)} %get-tuple-element.71), channel_id=1, source_target_pairs={{0,2},{1,3},{2,0},{3,1},{4,6},{5,7},{6,4},{7,5},{8,10},{9,11},{10,... | collective-permute-start | bytes 196616 | tf_op jit(solution)/shard_map/ppermute | solution.py:268
  5.6 2.6 %collective-permute-start.2 = (bf16[2,32,512]{2,1,0:T(8,128)(2,1)S(1)}, bf16[2,32,512]{2,1,0:T(8,128)(2,1)S(1)}, u32[]{:S(2)}, u32[]{:S(2)}) collective-permute-start(bf16[2,32,512]{2,1,0:T(8,128)(2,1)S(1)} %get-tuple-element.73), channel_id=1, source_target_pairs={{0,4},{1,5},{2,6},{3,7},{4,0},{5,1},{6,2},{7,3},{8,12},{9,13},{10,... | collective-permute-start | bytes 196616 | tf_op jit(solution)/shard_map/ppermute | solution.py:268
  8.1 0.0 collective-permute-start.3
  8.1 3.7 %fusion.1 = (bf16[32,32,1280]{2,1,0:T(8,128)(2,1)S(1)}, bf16[32,32,1280]{2,1,0:T(8,128)(2,1)S(1)}, bf16[32,32,1280]{2,1,0:T(8,128)(2,1)S(1)}) fusion(bf16[160,32,1280]{2,1,0:T(8,128)(2,1)} %param.5), kind=kLoop, calls=%fused_computation.15 | loop fusion | bytes 15728640 | tf_op jit(solution)/shard_map/slice | solution.py:273
  11.9 0.0 collective-permute-done
  11.9 0.9 %collective-permute-done.2 = bf16[2,32,512]{2,1,0:T(8,128)(2,1)S(1)} collective-permute-done((bf16[2,32,512]{2,1,0:T(8,128)(2,1)S(1)}, bf16[2,32,512]{2,1,0:T(8,128)(2,1)S(1)}, u32[]{:S(2)}, u32[]{:S(2)}) %collective-permute-start.2) | collective-permute-done | bytes 65568 | tf_op jit(solution)/shard_map/ppermute | solution.py:268
  12.8 1.4 %collective-permute-done.3 = bf16[2,32,512]{2,1,0:T(8,128)(2,1)S(1)} collective-permute-done((bf16[2,32,512]{2,1,0:T(8,128)(2,1)S(1)}, bf16[2,32,512]{2,1,0:T(8,128)(2,1)S(1)}, u32[]{:S(2)}, u32[]{:S(2)}) %collective-permute-start.3) | collective-permute-done | bytes 65568 | tf_op jit(solution)/shard_map/ppermute | solution.py:268
  14.2 0.3 collective-permute-start.6
  14.6 1.3 %collective-permute-start.5 = (bf16[2,32,512]{2,1,0:T(8,128)(2,1)S(1)}, bf16[2,32,512]{2,1,0:T(8,128)(2,1)S(1)}, u32[]{:S(2)}, u32[]{:S(2)}) collective-permute-start(bf16[2,32,512]{2,1,0:T(8,128)(2,1)S(1)} %get-tuple-element.82), channel_id=1, source_target_pairs={{0,1},{1,0},{2,3},{3,2},{4,29},{5,28},{6,31},{7,30},{8,9},{9,8},{1... | collective-permute-start | bytes 196616 | tf_op jit(solution)/shard_map/ppermute | solution.py:285
  15.9 3.3 %collective-permute-start.4 = (bf16[2,32,512]{2,1,0:T(8,128)(2,1)S(1)}, bf16[2,32,512]{2,1,0:T(8,128)(2,1)S(1)}, u32[]{:S(2)}, u32[]{:S(2)}) collective-permute-start(bf16[2,32,512]{2,1,0:T(8,128)(2,1)S(1)} %get-tuple-element.78), channel_id=1, source_target_pairs={{0,24},{1,25},{2,26},{3,27},{4,4},{5,5},{6,6},{7,7},{8,16},{9,17},... | collective-permute-start | bytes 196616 | tf_op jit(solution)/shard_map/ppermute | solution.py:285
  19.1 0.7 %collective-permute-start.1 = (bf16[2,32,512]{2,1,0:T(8,128)(2,1)S(1)}, bf16[2,32,512]{2,1,0:T(8,128)(2,1)S(1)}, u32[]{:S(2)}, u32[]{:S(2)}) collective-permute-start(bf16[2,32,512]{2,1,0:T(8,128)(2,1)S(1)} %get-tuple-element.72), channel_id=1, source_target_pairs={{0,0},{1,1},{2,2},{3,3},{4,28},{5,29},{6,30},{7,31},{8,8},{9,9},{1... | collective-permute-start | bytes 196616 | tf_op jit(solution)/shard_map/ppermute | solution.py:285
  19.8 0.9 %place.1 = (bf16[1024,256]{1,0:T(8,128)(2,1)S(1)}, s32[160,128]{1,0:T(8,128)S(1)}) custom-call(s32[1280]{0:T(1024)S(1)} %copy-done.1), custom_call_target="tpu_custom_call" | custom-call | tf_op jit(solution)/shard_map/place/pallas_call | solution.py:255
  20.7 0.0 collective-permute-done.6.refs_3_
  20.7 0.0 collective-permute-done.5.refs_2_
  20.7 0.7 %collective-permute-done.4.refs_1_ = bf16[2,32,512]{2,1,0:T(8,128)(2,1)S(1)} collective-permute-done((bf16[2,32,512]{2,1,0:T(8,128)(2,1)S(1)}, bf16[2,32,512]{2,1,0:T(8,128)(2,1)S(1)}, u32[]{:S(2)}, u32[]{:S(2)}) %collective-permute-start.4) | collective-permute-done | bytes 65568 | tf_op jit(solution)/shard_map/ppermute | solution.py:285
  21.4 0.0 collective-permute-done.1.refs_0_
  21.4 1.4 %product.5 = (bf16[480,256]{1,0:T(8,128)(2,1)S(1)}, f32[480,256]{1,0:T(8,128)S(1)}, bf16[480,256]{1,0:T(8,128)(2,1)S(1)}, f32[480,256]{1,0:T(8,128)S(1)}) custom-call(bf16[1024,256]{1,0:T(8,128)(2,1)S(1)} %get-tuple-element.69.place_ref, bf16[32,32,1280]{2,1,0:T(8,128)(2,1)S(1)} %get-tuple-element.91.leg_ref, ...), custom_call_target="tpu_custom_call" | custom-call | bytes 1024 | tf_op jit(solution)/shard_map/product/pallas_call | solution.py:311
  22.9 1.3 %collective-permute-start.7 = (bf16[480,256]{1,0:T(8,128)(2,1)S(1)}, bf16[480,256]{1,0:T(8,128)(2,1)S(1)}, u32[]{:S(2)}, u32[]{:S(2)}) collective-permute-start(bf16[480,256]{1,0:T(8,128)(2,1)S(1)} %get-tuple-element.93), channel_id=1, source_target_pairs={{0,8},{8,0},{16,24},{24,16},{1,9},{9,1},{17,25},{25,17},{2,10},{10... | collective-permute-start | bytes 737288 | tf_op jit(solution)/shard_map/ppermute | solution.py:301
  24.2 0.1 collective-permute-start.9
  24.3 1.1 %collective-permute-done.7 = bf16[480,256]{1,0:T(8,128)(2,1)S(1)} collective-permute-done((bf16[480,256]{1,0:T(8,128)(2,1)S(1)}, bf16[480,256]{1,0:T(8,128)(2,1)S(1)}, u32[]{:S(2)}, u32[]{:S(2)}) %collective-permute-start.7) | collective-permute-done | bytes 245792 | tf_op jit(solution)/shard_map/ppermute | solution.py:301
  25.3 0.1 add_convert_fusion.4
  25.4 1.1 %collective-permute-start.21 = (bf16[480,256]{1,0:T(8,128)(2,1)S(1)}, bf16[480,256]{1,0:T(8,128)(2,1)S(1)}, u32[]{:S(2)}, u32[]{:S(2)}) collective-permute-start(bf16[480,256]{1,0:T(8,128)(2,1)S(1)} %add_convert_fusion.4), channel_id=1, source_target_pairs={{0,16},{8,24},{16,0},{24,8},{1,17},{9,25},{17,1},{25,9},{2,18},{10... | collective-permute-start | bytes 737288 | tf_op jit(solution)/shard_map/ppermute | solution.py:323
  26.5 1.4 %product.6 = (bf16[480,256]{1,0:T(8,128)(2,1)S(1)}, f32[480,256]{1,0:T(8,128)S(1)}, bf16[480,256]{1,0:T(8,128)(2,1)S(1)}, f32[480,256]{1,0:T(8,128)S(1)}) custom-call(bf16[1024,256]{1,0:T(8,128)(2,1)S(1)} %get-tuple-element.69.place_ref, bf16[32,32,1280]{2,1,0:T(8,128)(2,1)S(1)} %get-tuple-element.98.leg_ref, ...), custom_call_target="tpu_custom_call" | custom-call | bytes 1024 | tf_op jit(solution)/shard_map/product/pallas_call | solution.py:311
  27.9 0.1 collective-permute-start.8
  28.0 0.5 collective-permute-start.11
  28.5 0.0 collective-permute-done.9
  28.5 0.9 %collective-permute-done.8 = bf16[480,256]{1,0:T(8,128)(2,1)S(1)} collective-permute-done((bf16[480,256]{1,0:T(8,128)(2,1)S(1)}, bf16[480,256]{1,0:T(8,128)(2,1)S(1)}, u32[]{:S(2)}, u32[]{:S(2)}) %collective-permute-start.8) | collective-permute-done | bytes 245792 | tf_op jit(solution)/shard_map/ppermute | solution.py:301
  29.5 0.1 add_convert_fusion.3
  29.5 1.1 %collective-permute-start.20 = (bf16[480,256]{1,0:T(8,128)(2,1)S(1)}, bf16[480,256]{1,0:T(8,128)(2,1)S(1)}, u32[]{:S(2)}, u32[]{:S(2)}) collective-permute-start(bf16[480,256]{1,0:T(8,128)(2,1)S(1)} %add_convert_fusion.3), channel_id=1, source_target_pairs={{0,16},{8,24},{16,0},{24,8},{1,17},{9,25},{17,1},{25,9},{2,18},{10... | collective-permute-start | bytes 737288 | tf_op jit(solution)/shard_map/ppermute | solution.py:323
  30.6 1.4 %product.7 = (bf16[480,256]{1,0:T(8,128)(2,1)S(1)}, f32[480,256]{1,0:T(8,128)S(1)}, bf16[480,256]{1,0:T(8,128)(2,1)S(1)}, f32[480,256]{1,0:T(8,128)S(1)}) custom-call(bf16[1024,256]{1,0:T(8,128)(2,1)S(1)} %get-tuple-element.69.place_ref, bf16[32,32,1280]{2,1,0:T(8,128)(2,1)S(1)} %get-tuple-element.108.leg_ref, ...), custom_call_target="tpu_custom_call" | custom-call | bytes 1024 | tf_op jit(solution)/shard_map/product/pallas_call | solution.py:311
  32.0 0.1 collective-permute-start.10
  32.1 0.5 collective-permute-start.13
  32.6 2.9 %fusion = (bf16[32,32,1280]{2,1,0:T(8,128)(2,1)S(1)}, bf16[32,32,1280]{2,1,0:T(8,128)(2,1)S(1)}) fusion(bf16[160,32,1280]{2,1,0:T(8,128)(2,1)} %param.5), kind=kLoop, calls=%fused_computation.14 | loop fusion | bytes 10485760 | tf_op jit(solution)/shard_map/slice | solution.py:308
  35.5 0.0 collective-permute-done.21.far_ref
  35.5 1.0 %final.5.refs_0_ = f32[12,160,320]{2,1,0:T(8,128)} custom-call(s32[160,128]{1,0:T(8,128)S(1)} %get-tuple-element.68.limits_ref, f32[480,256]{1,0:T(8,128)S(1)} %convert_add_fusion.4.near_ref, bf16[480,256]{1,0:T(8,128)(2,1)S(1)} %collective-permute-done.21.far_ref), custom_call_target="tpu_custom_call" | custom-call | bytes 1024 | tf_op jit(solution)/shard_map/final/pallas_call | solution.py:329
  36.5 0.0 collective-permute-done.11
  36.6 0.0 collective-permute-done.10
  36.6 0.1 add_convert_fusion.2
  36.7 1.1 %collective-permute-start.19 = (bf16[480,256]{1,0:T(8,128)(2,1)S(1)}, bf16[480,256]{1,0:T(8,128)(2,1)S(1)}, u32[]{:S(2)}, u32[]{:S(2)}) collective-permute-start(bf16[480,256]{1,0:T(8,128)(2,1)S(1)} %add_convert_fusion.2), channel_id=1, source_target_pairs={{0,16},{8,24},{16,0},{24,8},{1,17},{9,25},{17,1},{25,9},{2,18},{10... | collective-permute-start | bytes 737288 | tf_op jit(solution)/shard_map/ppermute | solution.py:323
  37.7 1.4 %product.8 = (bf16[480,256]{1,0:T(8,128)(2,1)S(1)}, f32[480,256]{1,0:T(8,128)S(1)}, bf16[480,256]{1,0:T(8,128)(2,1)S(1)}, f32[480,256]{1,0:T(8,128)S(1)}) custom-call(bf16[1024,256]{1,0:T(8,128)(2,1)S(1)} %get-tuple-element.69.place_ref, bf16[32,32,1280]{2,1,0:T(8,128)(2,1)S(1)} %get-tuple-element.131.leg_ref, ...), custom_call_target="tpu_custom_call" | custom-call | bytes 1024 | tf_op jit(solution)/shard_map/product/pallas_call | solution.py:311
  39.1 0.1 collective-permute-start.12
  39.2 0.5 collective-permute-start.17
  39.7 0.0 collective-permute-done.20.far_ref
  39.7 1.0 %final.6.refs_0_ = f32[12,160,320]{2,1,0:T(8,128)} custom-call(s32[160,128]{1,0:T(8,128)S(1)} %get-tuple-element.68.limits_ref, f32[480,256]{1,0:T(8,128)S(1)} %convert_add_fusion.3.near_ref, bf16[480,256]{1,0:T(8,128)(2,1)S(1)} %collective-permute-done.20.far_ref, f32[12,160,320]{2,1,0:T(8,128)} %final.5.refs_0_), custom_call_target="tpu_custom_call", output_to_operand_aliasing={{}: (3, {})} | custom-call | bytes 1024 | tf_op jit(solution)/shard_map/final/pallas_call | solution.py:329
  40.7 0.0 collective-permute-done.13
  40.8 0.0 collective-permute-done.12
  40.8 0.1 add_convert_fusion.1
  40.9 1.1 %collective-permute-start.18 = (bf16[480,256]{1,0:T(8,128)(2,1)S(1)}, bf16[480,256]{1,0:T(8,128)(2,1)S(1)}, u32[]{:S(2)}, u32[]{:S(2)}) collective-permute-start(bf16[480,256]{1,0:T(8,128)(2,1)S(1)} %add_convert_fusion.1), channel_id=1, source_target_pairs={{0,16},{8,24},{16,0},{24,8},{1,17},{9,25},{17,1},{25,9},{2,18},{10... | collective-permute-start | bytes 737288 | tf_op jit(solution)/shard_map/ppermute | solution.py:323
  42.0 1.4 %product.9 = (bf16[480,256]{1,0:T(8,128)(2,1)S(1)}, f32[480,256]{1,0:T(8,128)S(1)}, bf16[480,256]{1,0:T(8,128)(2,1)S(1)}, f32[480,256]{1,0:T(8,128)S(1)}) custom-call(bf16[1024,256]{1,0:T(8,128)(2,1)S(1)} %get-tuple-element.69.place_ref, bf16[32,32,1280]{2,1,0:T(8,128)(2,1)S(1)} %get-tuple-element.132.leg_ref, ...), custom_call_target="tpu_custom_call" | custom-call | bytes 1024 | tf_op jit(solution)/shard_map/product/pallas_call | solution.py:311
  43.4 0.1 collective-permute-start.14
  43.5 0.5 collective-permute-start.15
  44.0 1.6 %collective-permute-done.19.far_ref = bf16[480,256]{1,0:T(8,128)(2,1)S(1)} collective-permute-done((bf16[480,256]{1,0:T(8,128)(2,1)S(1)}, bf16[480,256]{1,0:T(8,128)(2,1)S(1)}, u32[]{:S(2)}, u32[]{:S(2)}) %collective-permute-start.19) | collective-permute-done | bytes 245792 | tf_op jit(solution)/shard_map/ppermute | solution.py:323
  45.5 1.0 %final.7.refs_0_ = f32[12,160,320]{2,1,0:T(8,128)} custom-call(s32[160,128]{1,0:T(8,128)S(1)} %get-tuple-element.68.limits_ref, f32[480,256]{1,0:T(8,128)S(1)} %convert_add_fusion.2.near_ref, bf16[480,256]{1,0:T(8,128)(2,1)S(1)} %collective-permute-done.19.far_ref, f32[12,160,320]{2,1,0:T(8,128)} %final.6.refs_0_), custom_call_target="tpu_custom_call", output_to_operand_aliasing={{}: (3, {})} | custom-call | bytes 1024 | tf_op jit(solution)/shard_map/final/pallas_call | solution.py:329
  46.5 0.0 collective-permute-done.17
  46.6 0.0 collective-permute-done.15
  46.6 0.1 add_convert_fusion
  46.7 1.1 %collective-permute-start.16 = (bf16[480,256]{1,0:T(8,128)(2,1)S(1)}, bf16[480,256]{1,0:T(8,128)(2,1)S(1)}, u32[]{:S(2)}, u32[]{:S(2)}) collective-permute-start(bf16[480,256]{1,0:T(8,128)(2,1)S(1)} %add_convert_fusion), channel_id=1, source_target_pairs={{0,16},{8,24},{16,0},{24,8},{1,17},{9,25},{17,1},{25,9},{2,18},{10... | collective-permute-start | bytes 737288 | tf_op jit(solution)/shard_map/ppermute | solution.py:323
  47.7 3.1 %collective-permute-done.18.far_ref = bf16[480,256]{1,0:T(8,128)(2,1)S(1)} collective-permute-done((bf16[480,256]{1,0:T(8,128)(2,1)S(1)}, bf16[480,256]{1,0:T(8,128)(2,1)S(1)}, u32[]{:S(2)}, u32[]{:S(2)}) %collective-permute-start.18) | collective-permute-done | bytes 245792 | tf_op jit(solution)/shard_map/ppermute | solution.py:323
  50.8 1.0 %final.8.refs_0_ = f32[12,160,320]{2,1,0:T(8,128)} custom-call(s32[160,128]{1,0:T(8,128)S(1)} %get-tuple-element.68.limits_ref, f32[480,256]{1,0:T(8,128)S(1)} %convert_add_fusion.near_ref, bf16[480,256]{1,0:T(8,128)(2,1)S(1)} %collective-permute-done.18.far_ref, f32[12,160,320]{2,1,0:T(8,128)} %final.7.refs_0_), custom_call_target="tpu_custom_call", output_to_operand_aliasing={{}: (3, {})} | custom-call | bytes 1024 | tf_op jit(solution)/shard_map/final/pallas_call | solution.py:329
  51.9 3.3 %collective-permute-done.16.far_ref = bf16[480,256]{1,0:T(8,128)(2,1)S(1)} collective-permute-done((bf16[480,256]{1,0:T(8,128)(2,1)S(1)}, bf16[480,256]{1,0:T(8,128)(2,1)S(1)}, u32[]{:S(2)}, u32[]{:S(2)}) %collective-permute-start.16) | collective-permute-done | bytes 245792 | tf_op jit(solution)/shard_map/ppermute | solution.py:323
  55.2 1.0 %final.9 = f32[12,160,320]{2,1,0:T(8,128)} custom-call(s32[160,128]{1,0:T(8,128)S(1)} %get-tuple-element.68.limits_ref, f32[480,256]{1,0:T(8,128)S(1)} %convert_add_fusion.1.near_ref, bf16[480,256]{1,0:T(8,128)(2,1)S(1)} %collective-permute-done.16.far_ref, f32[12,160,320]{2,1,0:T(8,128)} %final.8.refs_0_), custom_call_target="tpu_custom_call", output_to_operand_aliasing={{}: (3, {})} | custom-call | bytes 1024 | tf_op jit(solution)/shard_map/final/pallas_call | solution.py:329
  (14 shorter events, 0.3 us)
Async XLA Ops:
  0.0 0.9 %copy-start = (bf16[8,12,1280]{2,0,1:T(8,128)(2,1)S(1)}, bf16[8,12,1280]{2,0,1:T(8,128)(2,1)}, u32[]{:S(2)}) copy-start(bf16[8,12,1280]{2,0,1:T(8,128)(2,1)} %param.3) | copy-start | bytes 737284
  0.9 0.7 %copy-start.1 = (s32[1280]{0:T(1024)S(1)}, s32[1280]{0:T(1024)}, u32[]{:S(2)}) copy-start(s32[1280]{0:T(1024)} %table_ref.1) | copy-start | bytes 15364
  2.5 9.4 %collective-permute-start = (bf16[2,32,512]{2,1,0:T(8,128)(2,1)S(1)}, bf16[2,32,512]{2,1,0:T(8,128)(2,1)S(1)}, u32[]{:S(2)}, u32[]{:S(2)}) collective-permute-start(bf16[2,32,512]{2,1,0:T(8,128)(2,1)S(1)} %get-tuple-element.71), channel_id=1, source_target_pairs={{0,2},{1,3},{2,0},{3,1},{4,6},{5,7},{6,4},{7,5},{8,10},{9,11},{10,... | collective-permute-start | bytes 196616 | tf_op jit(solution)/shard_map/ppermute | solution.py:268
  5.6 7.3 %collective-permute-start.2 = (bf16[2,32,512]{2,1,0:T(8,128)(2,1)S(1)}, bf16[2,32,512]{2,1,0:T(8,128)(2,1)S(1)}, u32[]{:S(2)}, u32[]{:S(2)}) collective-permute-start(bf16[2,32,512]{2,1,0:T(8,128)(2,1)S(1)} %get-tuple-element.73), channel_id=1, source_target_pairs={{0,4},{1,5},{2,6},{3,7},{4,0},{5,1},{6,2},{7,3},{8,12},{9,13},{10,... | collective-permute-start | bytes 196616 | tf_op jit(solution)/shard_map/ppermute | solution.py:268
  8.1 6.1 %collective-permute-start.3 = (bf16[2,32,512]{2,1,0:T(8,128)(2,1)S(1)}, bf16[2,32,512]{2,1,0:T(8,128)(2,1)S(1)}, u32[]{:S(2)}, u32[]{:S(2)}) collective-permute-start(bf16[2,32,512]{2,1,0:T(8,128)(2,1)S(1)} %get-tuple-element.74), channel_id=1, source_target_pairs={{0,6},{1,7},{2,4},{3,5},{4,2},{5,3},{6,0},{7,1},{8,14},{9,15},{10,... | collective-permute-start | bytes 196616 | tf_op jit(solution)/shard_map/ppermute | solution.py:268
  14.2 6.5 %collective-permute-start.6 = (bf16[2,32,512]{2,1,0:T(8,128)(2,1)S(1)}, bf16[2,32,512]{2,1,0:T(8,128)(2,1)S(1)}, u32[]{:S(2)}, u32[]{:S(2)}) collective-permute-start(bf16[2,32,512]{2,1,0:T(8,128)(2,1)S(1)} %get-tuple-element.86), channel_id=1, source_target_pairs={{0,25},{1,24},{2,27},{3,26},{4,5},{5,4},{6,7},{7,6},{8,17},{9,16},... | collective-permute-start | bytes 196616 | tf_op jit(solution)/shard_map/ppermute | solution.py:285
  14.6 6.2 %collective-permute-start.5 = (bf16[2,32,512]{2,1,0:T(8,128)(2,1)S(1)}, bf16[2,32,512]{2,1,0:T(8,128)(2,1)S(1)}, u32[]{:S(2)}, u32[]{:S(2)}) collective-permute-start(bf16[2,32,512]{2,1,0:T(8,128)(2,1)S(1)} %get-tuple-element.82), channel_id=1, source_target_pairs={{0,1},{1,0},{2,3},{3,2},{4,29},{5,28},{6,31},{7,30},{8,9},{9,8},{1... | collective-permute-start | bytes 196616 | tf_op jit(solution)/shard_map/ppermute | solution.py:285
  15.9 5.6 %collective-permute-start.4 = (bf16[2,32,512]{2,1,0:T(8,128)(2,1)S(1)}, bf16[2,32,512]{2,1,0:T(8,128)(2,1)S(1)}, u32[]{:S(2)}, u32[]{:S(2)}) collective-permute-start(bf16[2,32,512]{2,1,0:T(8,128)(2,1)S(1)} %get-tuple-element.78), channel_id=1, source_target_pairs={{0,24},{1,25},{2,26},{3,27},{4,4},{5,5},{6,6},{7,7},{8,16},{9,17},... | collective-permute-start | bytes 196616 | tf_op jit(solution)/shard_map/ppermute | solution.py:285
  19.1 2.3 %collective-permute-start.1 = (bf16[2,32,512]{2,1,0:T(8,128)(2,1)S(1)}, bf16[2,32,512]{2,1,0:T(8,128)(2,1)S(1)}, u32[]{:S(2)}, u32[]{:S(2)}) collective-permute-start(bf16[2,32,512]{2,1,0:T(8,128)(2,1)S(1)} %get-tuple-element.72), channel_id=1, source_target_pairs={{0,0},{1,1},{2,2},{3,3},{4,28},{5,29},{6,30},{7,31},{8,8},{9,9},{1... | collective-permute-start | bytes 196616 | tf_op jit(solution)/shard_map/ppermute | solution.py:285
  22.9 2.4 %collective-permute-start.7 = (bf16[480,256]{1,0:T(8,128)(2,1)S(1)}, bf16[480,256]{1,0:T(8,128)(2,1)S(1)}, u32[]{:S(2)}, u32[]{:S(2)}) collective-permute-start(bf16[480,256]{1,0:T(8,128)(2,1)S(1)} %get-tuple-element.93), channel_id=1, source_target_pairs={{0,8},{8,0},{16,24},{24,16},{1,9},{9,1},{17,25},{25,17},{2,10},{10... | collective-permute-start | bytes 737288 | tf_op jit(solution)/shard_map/ppermute | solution.py:301
  24.2 4.3 %collective-permute-start.9 = (bf16[480,256]{1,0:T(8,128)(2,1)S(1)}, bf16[480,256]{1,0:T(8,128)(2,1)S(1)}, u32[]{:S(2)}, u32[]{:S(2)}) collective-permute-start(bf16[480,256]{1,0:T(8,128)(2,1)S(1)} %get-tuple-element.102), channel_id=1, source_target_pairs={{0,8},{8,0},{16,24},{24,16},{1,9},{9,1},{17,25},{25,17},{2,10},{10... | collective-permute-start | bytes 737288 | tf_op jit(solution)/shard_map/ppermute | solution.py:301
  25.4 10.1 %collective-permute-start.21 = (bf16[480,256]{1,0:T(8,128)(2,1)S(1)}, bf16[480,256]{1,0:T(8,128)(2,1)S(1)}, u32[]{:S(2)}, u32[]{:S(2)}) collective-permute-start(bf16[480,256]{1,0:T(8,128)(2,1)S(1)} %add_convert_fusion.4), channel_id=1, source_target_pairs={{0,16},{8,24},{16,0},{24,8},{1,17},{9,25},{17,1},{25,9},{2,18},{10... | collective-permute-start | bytes 737288 | tf_op jit(solution)/shard_map/ppermute | solution.py:323
  27.9 1.6 %collective-permute-start.8 = (bf16[480,256]{1,0:T(8,128)(2,1)S(1)}, bf16[480,256]{1,0:T(8,128)(2,1)S(1)}, u32[]{:S(2)}, u32[]{:S(2)}) collective-permute-start(bf16[480,256]{1,0:T(8,128)(2,1)S(1)} %get-tuple-element.100), channel_id=1, source_target_pairs={{0,8},{8,0},{16,24},{24,16},{1,9},{9,1},{17,25},{25,17},{2,10},{10... | collective-permute-start | bytes 737288 | tf_op jit(solution)/shard_map/ppermute | solution.py:301
  28.0 8.6 %collective-permute-start.11 = (bf16[480,256]{1,0:T(8,128)(2,1)S(1)}, bf16[480,256]{1,0:T(8,128)(2,1)S(1)}, u32[]{:S(2)}, u32[]{:S(2)}) collective-permute-start(bf16[480,256]{1,0:T(8,128)(2,1)S(1)} %get-tuple-element.112), channel_id=1, source_target_pairs={{0,8},{8,0},{16,24},{24,16},{1,9},{9,1},{17,25},{25,17},{2,10},{10... | collective-permute-start | bytes 737288 | tf_op jit(solution)/shard_map/ppermute | solution.py:301
  29.5 10.2 %collective-permute-start.20 = (bf16[480,256]{1,0:T(8,128)(2,1)S(1)}, bf16[480,256]{1,0:T(8,128)(2,1)S(1)}, u32[]{:S(2)}, u32[]{:S(2)}) collective-permute-start(bf16[480,256]{1,0:T(8,128)(2,1)S(1)} %add_convert_fusion.3), channel_id=1, source_target_pairs={{0,16},{8,24},{16,0},{24,8},{1,17},{9,25},{17,1},{25,9},{2,18},{10... | collective-permute-start | bytes 737288 | tf_op jit(solution)/shard_map/ppermute | solution.py:323
  32.0 4.5 %collective-permute-start.10 = (bf16[480,256]{1,0:T(8,128)(2,1)S(1)}, bf16[480,256]{1,0:T(8,128)(2,1)S(1)}, u32[]{:S(2)}, u32[]{:S(2)}) collective-permute-start(bf16[480,256]{1,0:T(8,128)(2,1)S(1)} %get-tuple-element.110), channel_id=1, source_target_pairs={{0,8},{8,0},{16,24},{24,16},{1,9},{9,1},{17,25},{25,17},{2,10},{10... | collective-permute-start | bytes 737288 | tf_op jit(solution)/shard_map/ppermute | solution.py:301
  32.1 8.6 %collective-permute-start.13 = (bf16[480,256]{1,0:T(8,128)(2,1)S(1)}, bf16[480,256]{1,0:T(8,128)(2,1)S(1)}, u32[]{:S(2)}, u32[]{:S(2)}) collective-permute-start(bf16[480,256]{1,0:T(8,128)(2,1)S(1)} %get-tuple-element.120), channel_id=1, source_target_pairs={{0,8},{8,0},{16,24},{24,16},{1,9},{9,1},{17,25},{25,17},{2,10},{10... | collective-permute-start | bytes 737288 | tf_op jit(solution)/shard_map/ppermute | solution.py:301
  36.7 8.9 %collective-permute-start.19 = (bf16[480,256]{1,0:T(8,128)(2,1)S(1)}, bf16[480,256]{1,0:T(8,128)(2,1)S(1)}, u32[]{:S(2)}, u32[]{:S(2)}) collective-permute-start(bf16[480,256]{1,0:T(8,128)(2,1)S(1)} %add_convert_fusion.2), channel_id=1, source_target_pairs={{0,16},{8,24},{16,0},{24,8},{1,17},{9,25},{17,1},{25,9},{2,18},{10... | collective-permute-start | bytes 737288 | tf_op jit(solution)/shard_map/ppermute | solution.py:323
  39.1 1.7 %collective-permute-start.12 = (bf16[480,256]{1,0:T(8,128)(2,1)S(1)}, bf16[480,256]{1,0:T(8,128)(2,1)S(1)}, u32[]{:S(2)}, u32[]{:S(2)}) collective-permute-start(bf16[480,256]{1,0:T(8,128)(2,1)S(1)} %get-tuple-element.118), channel_id=1, source_target_pairs={{0,8},{8,0},{16,24},{24,16},{1,9},{9,1},{17,25},{25,17},{2,10},{10... | collective-permute-start | bytes 737288 | tf_op jit(solution)/shard_map/ppermute | solution.py:301
  39.2 7.3 %collective-permute-start.17 = (bf16[480,256]{1,0:T(8,128)(2,1)S(1)}, bf16[480,256]{1,0:T(8,128)(2,1)S(1)}, u32[]{:S(2)}, u32[]{:S(2)}) collective-permute-start(bf16[480,256]{1,0:T(8,128)(2,1)S(1)} %get-tuple-element.130), channel_id=1, source_target_pairs={{0,8},{8,0},{16,24},{24,16},{1,9},{9,1},{17,25},{25,17},{2,10},{10... | collective-permute-start | bytes 737288 | tf_op jit(solution)/shard_map/ppermute | solution.py:301
  40.9 9.9 %collective-permute-start.18 = (bf16[480,256]{1,0:T(8,128)(2,1)S(1)}, bf16[480,256]{1,0:T(8,128)(2,1)S(1)}, u32[]{:S(2)}, u32[]{:S(2)}) collective-permute-start(bf16[480,256]{1,0:T(8,128)(2,1)S(1)} %add_convert_fusion.1), channel_id=1, source_target_pairs={{0,16},{8,24},{16,0},{24,8},{1,17},{9,25},{17,1},{25,9},{2,18},{10... | collective-permute-start | bytes 737288 | tf_op jit(solution)/shard_map/ppermute | solution.py:323
  43.4 8.4 %collective-permute-start.14 = (bf16[480,256]{1,0:T(8,128)(2,1)S(1)}, bf16[480,256]{1,0:T(8,128)(2,1)S(1)}, u32[]{:S(2)}, u32[]{:S(2)}) collective-permute-start(bf16[480,256]{1,0:T(8,128)(2,1)S(1)} %get-tuple-element.126), channel_id=1, source_target_pairs={{0,8},{8,0},{16,24},{24,16},{1,9},{9,1},{17,25},{25,17},{2,10},{10... | collective-permute-start | bytes 737288 | tf_op jit(solution)/shard_map/ppermute | solution.py:301
  43.5 3.1 %collective-permute-start.15 = (bf16[480,256]{1,0:T(8,128)(2,1)S(1)}, bf16[480,256]{1,0:T(8,128)(2,1)S(1)}, u32[]{:S(2)}, u32[]{:S(2)}) collective-permute-start(bf16[480,256]{1,0:T(8,128)(2,1)S(1)} %get-tuple-element.128), channel_id=1, source_target_pairs={{0,8},{8,0},{16,24},{24,16},{1,9},{9,1},{17,25},{25,17},{2,10},{10... | collective-permute-start | bytes 737288 | tf_op jit(solution)/shard_map/ppermute | solution.py:301
  46.7 8.5 %collective-permute-start.16 = (bf16[480,256]{1,0:T(8,128)(2,1)S(1)}, bf16[480,256]{1,0:T(8,128)(2,1)S(1)}, u32[]{:S(2)}, u32[]{:S(2)}) collective-permute-start(bf16[480,256]{1,0:T(8,128)(2,1)S(1)} %add_convert_fusion), channel_id=1, source_target_pairs={{0,16},{8,24},{16,0},{24,8},{1,17},{9,25},{17,1},{25,9},{2,18},{10... | collective-permute-start | bytes 737288 | tf_op jit(solution)/shard_map/ppermute | solution.py:323

commit v14 on v10

--- a/solution.py
+++ b/solution.py
@@ -153,10 +153,11 @@
             )
 
 
-def product_kernel(block, row_count, cols, place_ref, leg_ref, *refs):
+def product_kernel(block, held_at, row_count, cols, place_ref, leg_ref, *refs):
     sources = refs[:-6]
     far_sent, far_own, near_sent, near_own, far, near = refs[-6:]
     half = far.shape[1]
+    table = leg_ref.at[held_at * STEP : (held_at + 1) * STEP]
     lat = lax.axis_index("lat")
     y, core = lat // 2, lat % 2
     tile, off = shift_of(block, row_count * cols)
@@ -180,8 +181,8 @@
     north, south = both[:, :LANES], both[:, LANES:]
     even, odd = north + south, north - south
     far_coefs, near_coefs = jnp.where(y == 0, odd, even), jnp.where(y == 0, even, odd)
-    multiply(far_coefs, leg_ref, pl.multiple_of((1 - y) * half, LANES), half, far)
-    multiply(near_coefs, leg_ref, pl.multiple_of(y * half, LANES), half, near)
+    multiply(far_coefs, table, pl.multiple_of((1 - y) * half, LANES), half, far)
+    multiply(near_coefs, table, pl.multiple_of(y * half, LANES), half, near)
     pack(far, core, far_sent, far_own)
     pack(near, core, near_sent, near_own)
 
@@ -253,7 +254,7 @@
     lower = lax.axis_index("wave") < wave_count // 2
     count = slots // STEP
     early = count - count // 2
-    tables = [legendre[block * STEP : (block + 1) * STEP] for block in range(early)]
+    first = legendre[: early * STEP]
     sources = []
     for mirrored in (False, True):
         for u in range(low):
@@ -262,7 +263,7 @@
                 for side in (0, 1)
             ]
             block = jnp.where(lower != mirrored, sides[0], sides[1])
-            block, tables = lax.optimization_barrier((block, tables))
+            block, first = lax.optimization_barrier((block, first))
             route = []
             for lat in range(lat_count):
                 for wave in range(wave_count):
@@ -305,11 +306,11 @@
     for block in range(count):
         if block == early - 1:
             legendre, sources, ties = lax.optimization_barrier((legendre, sources, ties))
-            tables = tables + [legendre[k * STEP : (k + 1) * STEP] for k in range(early, count)]
+            rest = legendre[early * STEP :]
         else:
             sources, ties = lax.optimization_barrier((sources, ties))
         far_sent, far_own, near_sent, near_own = pl.pallas_call(
-            functools.partial(product_kernel, block, row_count, cols),
+            functools.partial(product_kernel, block, block - early * (block >= early), row_count, cols),
             out_shape=pair_of_sums * 2,
             in_specs=[whole] * (2 + len(sources)),
             out_specs=[whole] * 4,
@@ -317,7 +318,7 @@
             compiler_params=params,
             cost_estimate=cost,
             name="product",
-        )(place, tables[block], *sources)
+        )(place, first if block < early else rest, *sources)
         summed = settle(far_sent, far_own).astype(jnp.bfloat16)
         ties = [summed] + settled[-1:]
         crossed.append(lax.ppermute(summed, "lat", y_route))

time: 57.1 us -> 59.6 us (1.044)
  local copies, waits for them, and re-layouts: 11.4 us -> 14.5 us
  waiting for transfers between devices: 12.7 us -> 12 us
    slice x2, local copies, waits for them, and re-layouts: 8.03 us -> 9.64 us  [the longest x1 6.82 us: packed(): first = legendre[:early * STEP]]
    unnamed x10 -> x8, local copies, waits for them, and re-layouts: 3.39 us -> 4.88 us
    ppermute x3, waiting for transfers between devices: 0.83 us -> 0.01 us  [packed(): lax.ppermute(ordered[t], 'wave', [(w, w ^ t * low) for w in range(wave_co...]
  transfers between devices with their start and end apart: 21 -> 21, of which waited for: 9 -> 8; matrix products, arithmetic and copies ran while one was open for 15% -> 17% of each run, Pallas kernels for 19% -> 18%
where the time goes in v14:
time: 59.6 us; the launch traced here: 59.3 us
  starting transfers between devices  18.1 us (30%)
  local copies, waits for them, and re-layouts  14.5 us (24%)
  Pallas kernels  13.8 us (23%)
  waiting for transfers between devices  12 us (20%)
    pallas_call x5, Pallas kernels, packed(): pl.pallas_call(functools.partial(product_kernel, block, block - early * (...  7.09 us
    ppermute x5, waiting for transfers between devices, packed(): crossed.append(lax.ppermute(summed, 'lat', y_route))  7.03 us
    slice x1, local copies, waits for them, and re-layouts, packed(): first = legendre[:early * STEP]  6.82 us
    ppermute x5, starting transfers between devices, packed(): crossed.append(lax.ppermute(summed, 'lat', y_route))  6.31 us
    ppermute x3, starting transfers between devices, packed(): lax.ppermute(ordered[t], 'wave', [(w, w ^ t * low) for w in range(wave_co...  5.68 us
    pallas_call x5, Pallas kernels, packed(): pl.pallas_call(functools.partial(final_kernel, block * STEP, degrees, col...  5.06 us
    unnamed x8, local copies, waits for them, and re-layouts  4.88 us
    ppermute x3, starting transfers between devices, packed(): block = lax.ppermute(block, ('lat', 'wave'), route)  3.27 us
  transfers between devices with their start and end apart: 21, of which 8 were waited for; matrix products, arithmetic and copies ran while one was open for 17% of the time, Pallas kernels for 18%

profile of v14, /device:TPU:0, one launch (start us, length us, event | category | flops | bytes accessed | tf_op | source)
XLA Modules:
  0.0 59.3 jit_solution(1187860820103980637)
XLA Ops:
  0.0 0.9 %copy-done.1 = bf16[8,12,1280]{2,0,1:T(8,128)(2,1)S(1)} copy-done((bf16[8,12,1280]{2,0,1:T(8,128)(2,1)S(1)}, bf16[8,12,1280]{2,0,1:T(8,128)(2,1)}, u32[]{:S(2)}) %copy-start.1) | copy-done | bytes 245784
  0.9 0.7 %copy-done.2 = s32[1280]{0:T(1024)S(1)} copy-done((s32[1280]{0:T(1024)S(1)}, s32[1280]{0:T(1024)}, u32[]{:S(2)}) %copy-start.2) | copy-done | bytes 5144
  1.6 0.8 %gather.1 = (bf16[2,32,512]{2,1,0:T(8,128)(2,1)S(1)}, bf16[2,32,512]{2,1,0:T(8,128)(2,1)S(1)}, bf16[2,32,512]{2,1,0:T(8,128)(2,1)S(1)}, bf16[2,32,512]{2,1,0:T(8,128)(2,1)S(1)}) custom-call(s32[10,128]{1,0:T(8,128)S(1)} %bitcast.6, bf16[96,1280]{1,0:T(8,128)(2,1)S(1)} %bitcast.5), custom_call_target="tpu_custom_call" | custom-call | tf_op jit(solution)/shard_map/gather/pallas_call | solution.py:237
  2.5 3.1 %collective-permute-start = (bf16[2,32,512]{2,1,0:T(8,128)(2,1)S(1)}, bf16[2,32,512]{2,1,0:T(8,128)(2,1)S(1)}, u32[]{:S(2)}, u32[]{:S(2)}) collective-permute-start(bf16[2,32,512]{2,1,0:T(8,128)(2,1)S(1)} %get-tuple-element.63), channel_id=1, source_target_pairs={{0,2},{1,3},{2,0},{3,1},{4,6},{5,7},{6,4},{7,5},{8,10},{9,11},{10,... | collective-permute-start | bytes 196616 | tf_op jit(solution)/shard_map/ppermute | solution.py:251
  5.6 2.6 %collective-permute-start.1 = (bf16[2,32,512]{2,1,0:T(8,128)(2,1)S(1)}, bf16[2,32,512]{2,1,0:T(8,128)(2,1)S(1)}, u32[]{:S(2)}, u32[]{:S(2)}) collective-permute-start(bf16[2,32,512]{2,1,0:T(8,128)(2,1)S(1)} %get-tuple-element.64), channel_id=1, source_target_pairs={{0,4},{1,5},{2,6},{3,7},{4,0},{5,1},{6,2},{7,3},{8,12},{9,13},{10,... | collective-permute-start | bytes 196616 | tf_op jit(solution)/shard_map/ppermute | solution.py:251
  8.1 0.0 collective-permute-start.2
  8.2 0.0 copy-start.3
  8.2 6.8 %slice.42.leg_ref = bf16[96,32,1280]{2,1,0:T(8,128)(2,1)} slice(bf16[160,32,1280]{2,1,0:T(8,128)(2,1)} %param.5), slice={[0:96], [0:32], [0:1280]} | slice | bytes 15728640 | tf_op jit(solution)/shard_map/slice | solution.py:257
  15.0 0.0 collective-permute-done
  15.0 0.0 collective-permute-done.1
  15.0 0.0 collective-permute-done.2
  15.1 1.4 %collective-permute-start.5 = (bf16[2,32,512]{2,1,0:T(8,128)(2,1)S(1)}, bf16[2,32,512]{2,1,0:T(8,128)(2,1)S(1)}, u32[]{:S(2)}, u32[]{:S(2)}) collective-permute-start(bf16[2,32,512]{2,1,0:T(8,128)(2,1)S(1)} %get-tuple-element.72), channel_id=1, source_target_pairs={{0,25},{1,24},{2,27},{3,26},{4,29},{5,28},{6,31},{7,30},{8,17},{9,... | collective-permute-start | bytes 196616 | tf_op jit(solution)/shard_map/ppermute | solution.py:273
  16.5 1.6 %collective-permute-start.4 = (bf16[2,32,512]{2,1,0:T(8,128)(2,1)S(1)}, bf16[2,32,512]{2,1,0:T(8,128)(2,1)S(1)}, u32[]{:S(2)}, u32[]{:S(2)}) collective-permute-start(bf16[2,32,512]{2,1,0:T(8,128)(2,1)S(1)} %get-tuple-element.70), channel_id=1, source_target_pairs={{0,24},{1,25},{2,26},{3,27},{4,28},{5,29},{6,30},{7,31},{8,16},{9,... | collective-permute-start | bytes 196616 | tf_op jit(solution)/shard_map/ppermute | solution.py:273
  18.0 0.3 collective-permute-start.3
  18.4 0.9 %place.1 = (bf16[1024,256]{1,0:T(8,128)(2,1)S(1)}, s32[160,128]{1,0:T(8,128)S(1)}) custom-call(s32[1280]{0:T(1024)S(1)} %copy-done.3), custom_call_target="tpu_custom_call" | custom-call | tf_op jit(solution)/shard_map/place/pallas_call | solution.py:276
  19.3 1.0 %collective-permute-done.5.refs_3_ = bf16[2,32,512]{2,1,0:T(8,128)(2,1)S(1)} collective-permute-done((bf16[2,32,512]{2,1,0:T(8,128)(2,1)S(1)}, bf16[2,32,512]{2,1,0:T(8,128)(2,1)S(1)}, u32[]{:S(2)}, u32[]{:S(2)}) %collective-permute-start.5) | collective-permute-done | bytes 65568 | tf_op jit(solution)/shard_map/ppermute | solution.py:273
  20.2 0.9 %collective-permute-done.4.refs_2_ = bf16[2,32,512]{2,1,0:T(8,128)(2,1)S(1)} collective-permute-done((bf16[2,32,512]{2,1,0:T(8,128)(2,1)S(1)}, bf16[2,32,512]{2,1,0:T(8,128)(2,1)S(1)}, u32[]{:S(2)}, u32[]{:S(2)}) %collective-permute-start.4) | collective-permute-done | bytes 65568 | tf_op jit(solution)/shard_map/ppermute | solution.py:273
  21.2 1.2 %collective-permute-done.3.refs_1_ = bf16[2,32,512]{2,1,0:T(8,128)(2,1)S(1)} collective-permute-done((bf16[2,32,512]{2,1,0:T(8,128)(2,1)S(1)}, bf16[2,32,512]{2,1,0:T(8,128)(2,1)S(1)}, u32[]{:S(2)}, u32[]{:S(2)}) %collective-permute-start.3) | collective-permute-done | bytes 65568 | tf_op jit(solution)/shard_map/ppermute | solution.py:273
  22.3 3.2 %copy-done = bf16[96,32,1280]{2,1,0:T(8,128)(2,1)S(1)} copy-done((bf16[96,32,1280]{2,1,0:T(8,128)(2,1)S(1)}, bf16[96,32,1280]{2,1,0:T(8,128)(2,1)}, u32[]{:S(2)}) %copy-start) | copy-done | bytes 7864344
  25.5 1.4 %product.5 = (bf16[480,256]{1,0:T(8,128)(2,1)S(1)}, f32[480,256]{1,0:T(8,128)S(1)}, bf16[480,256]{1,0:T(8,128)(2,1)S(1)}, f32[480,256]{1,0:T(8,128)S(1)}) custom-call(bf16[1024,256]{1,0:T(8,128)(2,1)S(1)} %get-tuple-element.61.place_ref, bf16[96,32,1280]{2,1,0:T(8,128)(2,1)S(1)} %copy-done, bf16[2,32,512]{2,1,0:T(8,128)(2,1)S(1)} %get-tuple-element.105.refs_0_, ...), custom_call_target="tpu_custom_call" | custom-call | bytes 1024 | tf_op jit(solution)/shard_map/product/pallas_call | solution.py:312
  27.0 0.1 collective-permute-start.6
  27.0 0.5 collective-permute-start.8
  27.5 1.0 %collective-permute-done.6 = bf16[480,256]{1,0:T(8,128)(2,1)S(1)} collective-permute-done((bf16[480,256]{1,0:T(8,128)(2,1)S(1)}, bf16[480,256]{1,0:T(8,128)(2,1)S(1)}, u32[]{:S(2)}, u32[]{:S(2)}) %collective-permute-start.6) | collective-permute-done | bytes 245792 | tf_op jit(solution)/shard_map/ppermute | solution.py:302
  28.5 0.1 add_convert_fusion.4
  28.6 1.6 %collective-permute-start.20 = (bf16[480,256]{1,0:T(8,128)(2,1)S(1)}, bf16[480,256]{1,0:T(8,128)(2,1)S(1)}, u32[]{:S(2)}, u32[]{:S(2)}) collective-permute-start(bf16[480,256]{1,0:T(8,128)(2,1)S(1)} %add_convert_fusion.4), channel_id=1, source_target_pairs={{0,16},{8,24},{16,0},{24,8},{1,17},{9,25},{17,1},{25,9},{2,18},{10... | collective-permute-start | bytes 737288 | tf_op jit(solution)/shard_map/ppermute | solution.py:324
  30.2 1.4 %product.6 = (bf16[480,256]{1,0:T(8,128)(2,1)S(1)}, f32[480,256]{1,0:T(8,128)S(1)}, bf16[480,256]{1,0:T(8,128)(2,1)S(1)}, f32[480,256]{1,0:T(8,128)S(1)}) custom-call(bf16[1024,256]{1,0:T(8,128)(2,1)S(1)} %get-tuple-element.61.place_ref, bf16[96,32,1280]{2,1,0:T(8,128)(2,1)S(1)} %copy-done, bf16[2,32,512]{2,1,0:T(8,128)(2,1)S(1)} %get-tuple-element.105.refs_0_, ...), custom_call_target="tpu_custom_call" | custom-call | bytes 1024 | tf_op jit(solution)/shard_map/product/pallas_call | solution.py:312
  31.6 0.1 collective-permute-start.7
  31.7 0.5 collective-permute-start.10
  32.2 0.0 collective-permute-done.8
  32.2 0.9 %collective-permute-done.7 = bf16[480,256]{1,0:T(8,128)(2,1)S(1)} collective-permute-done((bf16[480,256]{1,0:T(8,128)(2,1)S(1)}, bf16[480,256]{1,0:T(8,128)(2,1)S(1)}, u32[]{:S(2)}, u32[]{:S(2)}) %collective-permute-start.7) | collective-permute-done | bytes 245792 | tf_op jit(solution)/shard_map/ppermute | solution.py:302
  33.2 0.1 add_convert_fusion.3
  33.2 0.6 collective-permute-start.19
  33.8 1.4 %product.7 = (bf16[480,256]{1,0:T(8,128)(2,1)S(1)}, f32[480,256]{1,0:T(8,128)S(1)}, bf16[480,256]{1,0:T(8,128)(2,1)S(1)}, f32[480,256]{1,0:T(8,128)S(1)}) custom-call(bf16[1024,256]{1,0:T(8,128)(2,1)S(1)} %get-tuple-element.61.place_ref, bf16[96,32,1280]{2,1,0:T(8,128)(2,1)S(1)} %copy-done, bf16[2,32,512]{2,1,0:T(8,128)(2,1)S(1)} %get-tuple-element.105.refs_0_, ...), custom_call_target="tpu_custom_call" | custom-call | bytes 1024 | tf_op jit(solution)/shard_map/product/pallas_call | solution.py:312
  35.2 0.1 collective-permute-start.9
  35.3 0.5 collective-permute-start.12
  35.8 2.8 %slice.47.leg_ref = bf16[64,32,1280]{2,1,0:T(8,128)(2,1)S(1)} slice(bf16[160,32,1280]{2,1,0:T(8,128)(2,1)} %param.5), slice={[96:160], [0:32], [0:1280]} | slice | bytes 10485760 | tf_op jit(solution)/shard_map/slice | solution.py:309
  38.6 0.0 collective-permute-done.20.far_ref
  38.7 1.0 %final.5.refs_0_ = f32[12,160,320]{2,1,0:T(8,128)} custom-call(s32[160,128]{1,0:T(8,128)S(1)} %get-tuple-element.60.limits_ref, f32[480,256]{1,0:T(8,128)S(1)} %convert_add_fusion.4.near_ref, bf16[480,256]{1,0:T(8,128)(2,1)S(1)} %collective-permute-done.20.far_ref), custom_call_target="tpu_custom_call" | custom-call | bytes 1024 | tf_op jit(solution)/shard_map/final/pallas_call | solution.py:330
  39.7 0.0 collective-permute-done.10
  39.7 0.0 collective-permute-done.9
  39.7 0.1 add_convert_fusion.2
  39.8 1.6 %collective-permute-start.18 = (bf16[480,256]{1,0:T(8,128)(2,1)S(1)}, bf16[480,256]{1,0:T(8,128)(2,1)S(1)}, u32[]{:S(2)}, u32[]{:S(2)}) collective-permute-start(bf16[480,256]{1,0:T(8,128)(2,1)S(1)} %add_convert_fusion.2), channel_id=1, source_target_pairs={{0,16},{8,24},{16,0},{24,8},{1,17},{9,25},{17,1},{25,9},{2,18},{10... | collective-permute-start | bytes 737288 | tf_op jit(solution)/shard_map/ppermute | solution.py:324
  41.4 1.4 %product.8 = (bf16[480,256]{1,0:T(8,128)(2,1)S(1)}, f32[480,256]{1,0:T(8,128)S(1)}, bf16[480,256]{1,0:T(8,128)(2,1)S(1)}, f32[480,256]{1,0:T(8,128)S(1)}) custom-call(bf16[1024,256]{1,0:T(8,128)(2,1)S(1)} %get-tuple-element.61.place_ref, bf16[64,32,1280]{2,1,0:T(8,128)(2,1)S(1)} %slice.47.leg_ref, bf16[2,32,512]{2,1,0:T(8,128)(2,1)S(1)} %get-tuple-element.105.refs_0_, ...), custom_call_target="tpu_custom_call" | custom-call | bytes 1024 | tf_op jit(solution)/shard_map/product/pallas_call | solution.py:312
  42.8 0.1 collective-permute-start.11
  42.9 0.5 collective-permute-start.16
  43.4 0.0 collective-permute-done.19.far_ref
  43.4 1.0 %final.6.refs_0_ = f32[12,160,320]{2,1,0:T(8,128)} custom-call(s32[160,128]{1,0:T(8,128)S(1)} %get-tuple-element.60.limits_ref, f32[480,256]{1,0:T(8,128)S(1)} %convert_add_fusion.3.near_ref, bf16[480,256]{1,0:T(8,128)(2,1)S(1)} %collective-permute-done.19.far_ref, f32[12,160,320]{2,1,0:T(8,128)} %final.5.refs_0_), custom_call_target="tpu_custom_call", output_to_operand_aliasing={{}: (3, {})} | custom-call | bytes 1024 | tf_op jit(solution)/shard_map/final/pallas_call | solution.py:330
  44.4 0.0 collective-permute-done.12
  44.5 0.0 collective-permute-done.11
  44.5 0.1 add_convert_fusion.1
  44.5 0.6 collective-permute-start.17
  45.1 1.4 %product.9 = (bf16[480,256]{1,0:T(8,128)(2,1)S(1)}, f32[480,256]{1,0:T(8,128)S(1)}, bf16[480,256]{1,0:T(8,128)(2,1)S(1)}, f32[480,256]{1,0:T(8,128)S(1)}) custom-call(bf16[1024,256]{1,0:T(8,128)(2,1)S(1)} %get-tuple-element.61.place_ref, bf16[64,32,1280]{2,1,0:T(8,128)(2,1)S(1)} %slice.47.leg_ref, bf16[2,32,512]{2,1,0:T(8,128)(2,1)S(1)} %get-tuple-element.105.refs_0_, ...), custom_call_target="tpu_custom_call" | custom-call | bytes 1024 | tf_op jit(solution)/shard_map/product/pallas_call | solution.py:312
  46.5 0.1 collective-permute-start.13
  46.6 0.5 collective-permute-start.14
  47.1 1.2 %collective-permute-done.18.far_ref = bf16[480,256]{1,0:T(8,128)(2,1)S(1)} collective-permute-done((bf16[480,256]{1,0:T(8,128)(2,1)S(1)}, bf16[480,256]{1,0:T(8,128)(2,1)S(1)}, u32[]{:S(2)}, u32[]{:S(2)}) %collective-permute-start.18) | collective-permute-done | bytes 245792 | tf_op jit(solution)/shard_map/ppermute | solution.py:324
  48.3 1.0 %final.7.refs_0_ = f32[12,160,320]{2,1,0:T(8,128)} custom-call(s32[160,128]{1,0:T(8,128)S(1)} %get-tuple-element.60.limits_ref, f32[480,256]{1,0:T(8,128)S(1)} %convert_add_fusion.2.near_ref, bf16[480,256]{1,0:T(8,128)(2,1)S(1)} %collective-permute-done.18.far_ref, f32[12,160,320]{2,1,0:T(8,128)} %final.6.refs_0_), custom_call_target="tpu_custom_call", output_to_operand_aliasing={{}: (3, {})} | custom-call | bytes 1024 | tf_op jit(solution)/shard_map/final/pallas_call | solution.py:330
  49.3 0.0 collective-permute-done.16
  49.3 0.1 add_convert_fusion
  49.4 2.0 %collective-permute-start.15 = (bf16[480,256]{1,0:T(8,128)(2,1)S(1)}, bf16[480,256]{1,0:T(8,128)(2,1)S(1)}, u32[]{:S(2)}, u32[]{:S(2)}) collective-permute-start(bf16[480,256]{1,0:T(8,128)(2,1)S(1)} %add_convert_fusion), channel_id=1, source_target_pairs={{0,16},{8,24},{16,0},{24,8},{1,17},{9,25},{17,1},{25,9},{2,18},{10... | collective-permute-start | bytes 737288 | tf_op jit(solution)/shard_map/ppermute | solution.py:324
  51.4 2.1 %collective-permute-done.17.far_ref = bf16[480,256]{1,0:T(8,128)(2,1)S(1)} collective-permute-done((bf16[480,256]{1,0:T(8,128)(2,1)S(1)}, bf16[480,256]{1,0:T(8,128)(2,1)S(1)}, u32[]{:S(2)}, u32[]{:S(2)}) %collective-permute-start.17) | collective-permute-done | bytes 245792 | tf_op jit(solution)/shard_map/ppermute | solution.py:324
  53.5 1.0 %final.8.refs_0_ = f32[12,160,320]{2,1,0:T(8,128)} custom-call(s32[160,128]{1,0:T(8,128)S(1)} %get-tuple-element.60.limits_ref, f32[480,256]{1,0:T(8,128)S(1)} %convert_add_fusion.near_ref, bf16[480,256]{1,0:T(8,128)(2,1)S(1)} %collective-permute-done.17.far_ref, f32[12,160,320]{2,1,0:T(8,128)} %final.7.refs_0_), custom_call_target="tpu_custom_call", output_to_operand_aliasing={{}: (3, {})} | custom-call | bytes 1024 | tf_op jit(solution)/shard_map/final/pallas_call | solution.py:330
  54.5 0.0 collective-permute-done.13
  54.6 3.7 %collective-permute-done.15.far_ref = bf16[480,256]{1,0:T(8,128)(2,1)S(1)} collective-permute-done((bf16[480,256]{1,0:T(8,128)(2,1)S(1)}, bf16[480,256]{1,0:T(8,128)(2,1)S(1)}, u32[]{:S(2)}, u32[]{:S(2)}) %collective-permute-start.15) | collective-permute-done | bytes 245792 | tf_op jit(solution)/shard_map/ppermute | solution.py:324
  58.3 1.0 %final.9 = f32[12,160,320]{2,1,0:T(8,128)} custom-call(s32[160,128]{1,0:T(8,128)S(1)} %get-tuple-element.60.limits_ref, f32[480,256]{1,0:T(8,128)S(1)} %convert_add_fusion.1.near_ref, bf16[480,256]{1,0:T(8,128)(2,1)S(1)} %collective-permute-done.15.far_ref, f32[12,160,320]{2,1,0:T(8,128)} %final.8.refs_0_), custom_call_target="tpu_custom_call", output_to_operand_aliasing={{}: (3, {})} | custom-call | bytes 1024 | tf_op jit(solution)/shard_map/final/pallas_call | solution.py:330
  (15 shorter events, 0.3 us)
Async XLA Ops:
  0.0 0.9 %copy-start.1 = (bf16[8,12,1280]{2,0,1:T(8,128)(2,1)S(1)}, bf16[8,12,1280]{2,0,1:T(8,128)(2,1)}, u32[]{:S(2)}) copy-start(bf16[8,12,1280]{2,0,1:T(8,128)(2,1)} %param.3) | copy-start | bytes 737284
  0.9 0.7 %copy-start.2 = (s32[1280]{0:T(1024)S(1)}, s32[1280]{0:T(1024)}, u32[]{:S(2)}) copy-start(s32[1280]{0:T(1024)} %table_ref.1) | copy-start | bytes 15364
  2.5 12.5 %collective-permute-start = (bf16[2,32,512]{2,1,0:T(8,128)(2,1)S(1)}, bf16[2,32,512]{2,1,0:T(8,128)(2,1)S(1)}, u32[]{:S(2)}, u32[]{:S(2)}) collective-permute-start(bf16[2,32,512]{2,1,0:T(8,128)(2,1)S(1)} %get-tuple-element.63), channel_id=1, source_target_pairs={{0,2},{1,3},{2,0},{3,1},{4,6},{5,7},{6,4},{7,5},{8,10},{9,11},{10,... | collective-permute-start | bytes 196616 | tf_op jit(solution)/shard_map/ppermute | solution.py:251
  5.6 9.5 %collective-permute-start.1 = (bf16[2,32,512]{2,1,0:T(8,128)(2,1)S(1)}, bf16[2,32,512]{2,1,0:T(8,128)(2,1)S(1)}, u32[]{:S(2)}, u32[]{:S(2)}) collective-permute-start(bf16[2,32,512]{2,1,0:T(8,128)(2,1)S(1)} %get-tuple-element.64), channel_id=1, source_target_pairs={{0,4},{1,5},{2,6},{3,7},{4,0},{5,1},{6,2},{7,3},{8,12},{9,13},{10,... | collective-permute-start | bytes 196616 | tf_op jit(solution)/shard_map/ppermute | solution.py:251
  8.1 6.9 %collective-permute-start.2 = (bf16[2,32,512]{2,1,0:T(8,128)(2,1)S(1)}, bf16[2,32,512]{2,1,0:T(8,128)(2,1)S(1)}, u32[]{:S(2)}, u32[]{:S(2)}) collective-permute-start(bf16[2,32,512]{2,1,0:T(8,128)(2,1)S(1)} %get-tuple-element.65), channel_id=1, source_target_pairs={{0,6},{1,7},{2,4},{3,5},{4,2},{5,3},{6,0},{7,1},{8,14},{9,15},{10,... | collective-permute-start | bytes 196616 | tf_op jit(solution)/shard_map/ppermute | solution.py:251
  8.2 10.2 %copy-start.3 = (s32[1280]{0:T(1024)S(1)}, s32[1280]{0:T(1024)}, u32[]{:S(2)}) copy-start(s32[1280]{0:T(1024)} %table_ref.1) | copy-start | bytes 15364
  15.1 5.1 %collective-permute-start.5 = (bf16[2,32,512]{2,1,0:T(8,128)(2,1)S(1)}, bf16[2,32,512]{2,1,0:T(8,128)(2,1)S(1)}, u32[]{:S(2)}, u32[]{:S(2)}) collective-permute-start(bf16[2,32,512]{2,1,0:T(8,128)(2,1)S(1)} %get-tuple-element.72), channel_id=1, source_target_pairs={{0,25},{1,24},{2,27},{3,26},{4,29},{5,28},{6,31},{7,30},{8,17},{9,... | collective-permute-start | bytes 196616 | tf_op jit(solution)/shard_map/ppermute | solution.py:273
  16.5 4.7 %collective-permute-start.4 = (bf16[2,32,512]{2,1,0:T(8,128)(2,1)S(1)}, bf16[2,32,512]{2,1,0:T(8,128)(2,1)S(1)}, u32[]{:S(2)}, u32[]{:S(2)}) collective-permute-start(bf16[2,32,512]{2,1,0:T(8,128)(2,1)S(1)} %get-tuple-element.70), channel_id=1, source_target_pairs={{0,24},{1,25},{2,26},{3,27},{4,28},{5,29},{6,30},{7,31},{8,16},{9,... | collective-permute-start | bytes 196616 | tf_op jit(solution)/shard_map/ppermute | solution.py:273
  18.0 4.3 %collective-permute-start.3 = (bf16[2,32,512]{2,1,0:T(8,128)(2,1)S(1)}, bf16[2,32,512]{2,1,0:T(8,128)(2,1)S(1)}, u32[]{:S(2)}, u32[]{:S(2)}) collective-permute-start(bf16[2,32,512]{2,1,0:T(8,128)(2,1)S(1)} %get-tuple-element.68), channel_id=1, source_target_pairs={{0,1},{1,0},{2,3},{3,2},{4,5},{5,4},{6,7},{7,6},{8,9},{9,8},{10,11... | collective-permute-start | bytes 196616 | tf_op jit(solution)/shard_map/ppermute | solution.py:273
  22.3 3.2 %copy-start = (bf16[96,32,1280]{2,1,0:T(8,128)(2,1)S(1)}, bf16[96,32,1280]{2,1,0:T(8,128)(2,1)}, u32[]{:S(2)}) copy-start(bf16[96,32,1280]{2,1,0:T(8,128)(2,1)} %slice.42.leg_ref) | copy-start | bytes 23592964
  27.0 1.6 %collective-permute-start.6 = (bf16[480,256]{1,0:T(8,128)(2,1)S(1)}, bf16[480,256]{1,0:T(8,128)(2,1)S(1)}, u32[]{:S(2)}, u32[]{:S(2)}) collective-permute-start(bf16[480,256]{1,0:T(8,128)(2,1)S(1)} %get-tuple-element.79), channel_id=1, source_target_pairs={{0,8},{8,0},{16,24},{24,16},{1,9},{9,1},{17,25},{25,17},{2,10},{10... | collective-permute-start | bytes 737288 | tf_op jit(solution)/shard_map/ppermute | solution.py:302
  27.0 5.1 %collective-permute-start.8 = (bf16[480,256]{1,0:T(8,128)(2,1)S(1)}, bf16[480,256]{1,0:T(8,128)(2,1)S(1)}, u32[]{:S(2)}, u32[]{:S(2)}) collective-permute-start(bf16[480,256]{1,0:T(8,128)(2,1)S(1)} %get-tuple-element.87), channel_id=1, source_target_pairs={{0,8},{8,0},{16,24},{24,16},{1,9},{9,1},{17,25},{25,17},{2,10},{10... | collective-permute-start | bytes 737288 | tf_op jit(solution)/shard_map/ppermute | solution.py:302
  28.6 10.1 %collective-permute-start.20 = (bf16[480,256]{1,0:T(8,128)(2,1)S(1)}, bf16[480,256]{1,0:T(8,128)(2,1)S(1)}, u32[]{:S(2)}, u32[]{:S(2)}) collective-permute-start(bf16[480,256]{1,0:T(8,128)(2,1)S(1)} %add_convert_fusion.4), channel_id=1, source_target_pairs={{0,16},{8,24},{16,0},{24,8},{1,17},{9,25},{17,1},{25,9},{2,18},{10... | collective-permute-start | bytes 737288 | tf_op jit(solution)/shard_map/ppermute | solution.py:324
  31.6 1.6 %collective-permute-start.7 = (bf16[480,256]{1,0:T(8,128)(2,1)S(1)}, bf16[480,256]{1,0:T(8,128)(2,1)S(1)}, u32[]{:S(2)}, u32[]{:S(2)}) collective-permute-start(bf16[480,256]{1,0:T(8,128)(2,1)S(1)} %get-tuple-element.85), channel_id=1, source_target_pairs={{0,8},{8,0},{16,24},{24,16},{1,9},{9,1},{17,25},{25,17},{2,10},{10... | collective-permute-start | bytes 737288 | tf_op jit(solution)/shard_map/ppermute | solution.py:302
  31.7 8.0 %collective-permute-start.10 = (bf16[480,256]{1,0:T(8,128)(2,1)S(1)}, bf16[480,256]{1,0:T(8,128)(2,1)S(1)}, u32[]{:S(2)}, u32[]{:S(2)}) collective-permute-start(bf16[480,256]{1,0:T(8,128)(2,1)S(1)} %get-tuple-element.96), channel_id=1, source_target_pairs={{0,8},{8,0},{16,24},{24,16},{1,9},{9,1},{17,25},{25,17},{2,10},{10... | collective-permute-start | bytes 737288 | tf_op jit(solution)/shard_map/ppermute | solution.py:302
  33.2 10.1 %collective-permute-start.19 = (bf16[480,256]{1,0:T(8,128)(2,1)S(1)}, bf16[480,256]{1,0:T(8,128)(2,1)S(1)}, u32[]{:S(2)}, u32[]{:S(2)}) collective-permute-start(bf16[480,256]{1,0:T(8,128)(2,1)S(1)} %add_convert_fusion.3), channel_id=1, source_target_pairs={{0,16},{8,24},{16,0},{24,8},{1,17},{9,25},{17,1},{25,9},{2,18},{10... | collective-permute-start | bytes 737288 | tf_op jit(solution)/shard_map/ppermute | solution.py:324
  35.2 4.5 %collective-permute-start.9 = (bf16[480,256]{1,0:T(8,128)(2,1)S(1)}, bf16[480,256]{1,0:T(8,128)(2,1)S(1)}, u32[]{:S(2)}, u32[]{:S(2)}) collective-permute-start(bf16[480,256]{1,0:T(8,128)(2,1)S(1)} %get-tuple-element.94), channel_id=1, source_target_pairs={{0,8},{8,0},{16,24},{24,16},{1,9},{9,1},{17,25},{25,17},{2,10},{10... | collective-permute-start | bytes 737288 | tf_op jit(solution)/shard_map/ppermute | solution.py:302
  35.3 9.1 %collective-permute-start.12 = (bf16[480,256]{1,0:T(8,128)(2,1)S(1)}, bf16[480,256]{1,0:T(8,128)(2,1)S(1)}, u32[]{:S(2)}, u32[]{:S(2)}) collective-permute-start(bf16[480,256]{1,0:T(8,128)(2,1)S(1)} %get-tuple-element.104), channel_id=1, source_target_pairs={{0,8},{8,0},{16,24},{24,16},{1,9},{9,1},{17,25},{25,17},{2,10},{10... | collective-permute-start | bytes 737288 | tf_op jit(solution)/shard_map/ppermute | solution.py:302
  39.8 8.5 %collective-permute-start.18 = (bf16[480,256]{1,0:T(8,128)(2,1)S(1)}, bf16[480,256]{1,0:T(8,128)(2,1)S(1)}, u32[]{:S(2)}, u32[]{:S(2)}) collective-permute-start(bf16[480,256]{1,0:T(8,128)(2,1)S(1)} %add_convert_fusion.2), channel_id=1, source_target_pairs={{0,16},{8,24},{16,0},{24,8},{1,17},{9,25},{17,1},{25,9},{2,18},{10... | collective-permute-start | bytes 737288 | tf_op jit(solution)/shard_map/ppermute | solution.py:324
  42.8 1.7 %collective-permute-start.11 = (bf16[480,256]{1,0:T(8,128)(2,1)S(1)}, bf16[480,256]{1,0:T(8,128)(2,1)S(1)}, u32[]{:S(2)}, u32[]{:S(2)}) collective-permute-start(bf16[480,256]{1,0:T(8,128)(2,1)S(1)} %get-tuple-element.102), channel_id=1, source_target_pairs={{0,8},{8,0},{16,24},{24,16},{1,9},{9,1},{17,25},{25,17},{2,10},{10... | collective-permute-start | bytes 737288 | tf_op jit(solution)/shard_map/ppermute | solution.py:302
  42.9 6.4 %collective-permute-start.16 = (bf16[480,256]{1,0:T(8,128)(2,1)S(1)}, bf16[480,256]{1,0:T(8,128)(2,1)S(1)}, u32[]{:S(2)}, u32[]{:S(2)}) collective-permute-start(bf16[480,256]{1,0:T(8,128)(2,1)S(1)} %get-tuple-element.114), channel_id=1, source_target_pairs={{0,8},{8,0},{16,24},{24,16},{1,9},{9,1},{17,25},{25,17},{2,10},{10... | collective-permute-start | bytes 737288 | tf_op jit(solution)/shard_map/ppermute | solution.py:302
  44.5 9.0 %collective-permute-start.17 = (bf16[480,256]{1,0:T(8,128)(2,1)S(1)}, bf16[480,256]{1,0:T(8,128)(2,1)S(1)}, u32[]{:S(2)}, u32[]{:S(2)}) collective-permute-start(bf16[480,256]{1,0:T(8,128)(2,1)S(1)} %add_convert_fusion.1), channel_id=1, source_target_pairs={{0,16},{8,24},{16,0},{24,8},{1,17},{9,25},{17,1},{25,9},{2,18},{10... | collective-permute-start | bytes 737288 | tf_op jit(solution)/shard_map/ppermute | solution.py:324
  46.5 8.0 %collective-permute-start.13 = (bf16[480,256]{1,0:T(8,128)(2,1)S(1)}, bf16[480,256]{1,0:T(8,128)(2,1)S(1)}, u32[]{:S(2)}, u32[]{:S(2)}) collective-permute-start(bf16[480,256]{1,0:T(8,128)(2,1)S(1)} %get-tuple-element.110), channel_id=1, source_target_pairs={{0,8},{8,0},{16,24},{24,16},{1,9},{9,1},{17,25},{25,17},{2,10},{10... | collective-permute-start | bytes 737288 | tf_op jit(solution)/shard_map/ppermute | solution.py:302
  46.6 2.7 %collective-permute-start.14 = (bf16[480,256]{1,0:T(8,128)(2,1)S(1)}, bf16[480,256]{1,0:T(8,128)(2,1)S(1)}, u32[]{:S(2)}, u32[]{:S(2)}) collective-permute-start(bf16[480,256]{1,0:T(8,128)(2,1)S(1)} %get-tuple-element.112), channel_id=1, source_target_pairs={{0,8},{8,0},{16,24},{24,16},{1,9},{9,1},{17,25},{25,17},{2,10},{10... | collective-permute-start | bytes 737288 | tf_op jit(solution)/shard_map/ppermute | solution.py:302
  49.4 8.9 %collective-permute-start.15 = (bf16[480,256]{1,0:T(8,128)(2,1)S(1)}, bf16[480,256]{1,0:T(8,128)(2,1)S(1)}, u32[]{:S(2)}, u32[]{:S(2)}) collective-permute-start(bf16[480,256]{1,0:T(8,128)(2,1)S(1)} %add_convert_fusion), channel_id=1, source_target_pairs={{0,16},{8,24},{16,0},{24,8},{1,17},{9,25},{17,1},{25,9},{2,18},{10... | collective-permute-start | bytes 737288 | tf_op jit(solution)/shard_map/ppermute | solution.py:324

commit v15 on v12

--- a/solution.py
+++ b/solution.py
@@ -10,7 +10,7 @@
 LANES = 128
 STEP = 32
 TILE = 8
-VMEM = 32 * 1024 * 1024
+VMEM = 16 * 1024 * 1024
 
 
 def partner(block, axis, stride):

time: 56.5 us -> 56.5 us (level)
    unnamed x8 -> x10, local copies, waits for them, and re-layouts: 1.65 us -> 1.65 us
where the time goes in v15:
time: 56.5 us; the launch traced here: 56.2 us
  starting transfers between devices  19.5 us (35%)
  Pallas kernels  13.8 us (24%)
  local copies, waits for them, and re-layouts  11.2 us (20%)
  waiting for transfers between devices  10.9 us (19%)
    ppermute x5, waiting for transfers between devices, packed(): crossed.append(lax.ppermute(summed, 'lat', y_route))  7.88 us
    ppermute x5, starting transfers between devices, packed(): crossed.append(lax.ppermute(summed, 'lat', y_route))  7.68 us
    pallas_call x5, Pallas kernels, packed(): pl.pallas_call(functools.partial(product_kernel, block, row_count, cols),...  7.09 us
    ppermute x3, starting transfers between devices, packed(): lax.ppermute(ordered[t], 'wave', [(w, w ^ t * low) for w in range(wave_co...  5.68 us
    slice x1, local copies, waits for them, and re-layouts, packed(): legendre[block * STEP:(block + 1) * STEP]  5.11 us
    pallas_call x5, Pallas kernels, packed(): pl.pallas_call(functools.partial(final_kernel, block * STEP, degrees, col...  5.06 us
    ppermute x3, starting transfers between devices, packed(): block = lax.ppermute(block, ('lat', 'wave'), route)  3.27 us
    slice x1, local copies, waits for them, and re-layouts, packed(): later[block * STEP:(block + 1) * STEP]  2.87 us
  transfers between devices with their start and end apart: 21, of which 8 were waited for; matrix products, arithmetic and copies ran while one was open for 18% of the time, Pallas kernels for 19%

profile of v15, /device:TPU:0, one launch (start us, length us, event | category | flops | bytes accessed | tf_op | source)
XLA Modules:
  0.0 56.2 jit_solution(8742630193708385923)
XLA Ops:
  0.0 0.9 %copy-done.2 = bf16[8,12,1280]{2,0,1:T(8,128)(2,1)S(1)} copy-done((bf16[8,12,1280]{2,0,1:T(8,128)(2,1)S(1)}, bf16[8,12,1280]{2,0,1:T(8,128)(2,1)}, u32[]{:S(2)}) %copy-start.2) | copy-done | bytes 245784
  0.9 0.7 %copy-done.3 = s32[1280]{0:T(1024)S(1)} copy-done((s32[1280]{0:T(1024)S(1)}, s32[1280]{0:T(1024)}, u32[]{:S(2)}) %copy-start.3) | copy-done | bytes 5144
  1.6 0.8 %gather.1 = (bf16[2,32,512]{2,1,0:T(8,128)(2,1)S(1)}, bf16[2,32,512]{2,1,0:T(8,128)(2,1)S(1)}, bf16[2,32,512]{2,1,0:T(8,128)(2,1)S(1)}, bf16[2,32,512]{2,1,0:T(8,128)(2,1)S(1)}) custom-call(s32[10,128]{1,0:T(8,128)S(1)} %bitcast.6, bf16[96,1280]{1,0:T(8,128)(2,1)S(1)} %bitcast.5), custom_call_target="tpu_custom_call" | custom-call | tf_op jit(solution)/shard_map/gather/pallas_call | solution.py:236
  2.5 3.1 %collective-permute-start = (bf16[2,32,512]{2,1,0:T(8,128)(2,1)S(1)}, bf16[2,32,512]{2,1,0:T(8,128)(2,1)}, u32[]{:S(2)}, u32[]{:S(2)}) collective-permute-start(bf16[2,32,512]{2,1,0:T(8,128)(2,1)S(1)} %get-tuple-element.81), channel_id=1, source_target_pairs={{0,2},{1,3},{2,0},{3,1},{4,6},{5,7},{6,4},{7,5},{8,10},{9,11},{10,... | collective-permute-start | bytes 196616 | tf_op jit(solution)/shard_map/ppermute | solution.py:262
  5.6 2.6 %collective-permute-start.1 = (bf16[2,32,512]{2,1,0:T(8,128)(2,1)S(1)}, bf16[2,32,512]{2,1,0:T(8,128)(2,1)}, u32[]{:S(2)}, u32[]{:S(2)}) collective-permute-start(bf16[2,32,512]{2,1,0:T(8,128)(2,1)S(1)} %get-tuple-element.82), channel_id=1, source_target_pairs={{0,4},{1,5},{2,6},{3,7},{4,0},{5,1},{6,2},{7,3},{8,12},{9,13},{10,... | collective-permute-start | bytes 196616 | tf_op jit(solution)/shard_map/ppermute | solution.py:262
  8.1 0.0 collective-permute-start.2
  8.1 5.1 %fusion.1 = (bf16[32,32,1280]{2,1,0:T(8,128)(2,1)S(1)}, bf16[32,32,1280]{2,1,0:T(8,128)(2,1)}, bf16[32,32,1280]{2,1,0:T(8,128)(2,1)}) fusion(bf16[160,32,1280]{2,1,0:T(8,128)(2,1)} %param.5), kind=kLoop, calls=%fused_computation.19 | loop fusion | bytes 15728640 | tf_op jit(solution)/shard_map/slice | solution.py:267
  13.3 0.9 %place.1 = (bf16[1024,256]{1,0:T(8,128)(2,1)S(1)}, s32[160,128]{1,0:T(8,128)S(1)}) custom-call(s32[1280]{0:T(1024)S(1)} %copy-done.4), custom_call_target="tpu_custom_call" | custom-call | tf_op jit(solution)/shard_map/place/pallas_call | solution.py:249
  14.2 0.0 collective-permute-done
  14.2 0.8 %fusion.3 = (bf16[1,32,512]{2,1,0:T(8,128)(2,1)S(1)}, bf16[1,32,512]{2,1,0:T(8,128)(2,1)S(1)}) fusion(bf16[2,32,512]{2,1,0:T(8,128)(2,1)} %collective-permute-done), kind=kLoop, calls=%fused_computation.21 | loop fusion | bytes 131072 | tf_op jit(solution)/shard_map/slice | solution.py:273
  15.0 0.0 collective-permute-done.1
  15.0 0.8 %fusion.4 = (bf16[1,32,512]{2,1,0:T(8,128)(2,1)S(1)}, bf16[1,32,512]{2,1,0:T(8,128)(2,1)S(1)}) fusion(bf16[2,32,512]{2,1,0:T(8,128)(2,1)} %collective-permute-done.1), kind=kLoop, calls=%fused_computation.22 | loop fusion | bytes 131072 | tf_op jit(solution)/shard_map/slice | solution.py:273
  15.7 0.0 collective-permute-done.2
  15.8 1.4 %collective-permute-start.5 = (bf16[2,32,512]{2,1,0:T(8,128)(2,1)S(1)}, bf16[2,32,512]{2,1,0:T(8,128)(2,1)S(1)}, u32[]{:S(2)}, u32[]{:S(2)}) collective-permute-start(bf16[2,32,512]{2,1,0:T(8,128)(2,1)S(1)} %get-tuple-element.97), channel_id=1, source_target_pairs={{0,25},{1,24},{2,27},{3,26},{4,29},{5,28},{6,31},{7,30},{8,17},{9,... | collective-permute-start | bytes 196616 | tf_op jit(solution)/shard_map/ppermute | solution.py:286
  17.2 1.6 %collective-permute-start.4 = (bf16[2,32,512]{2,1,0:T(8,128)(2,1)S(1)}, bf16[2,32,512]{2,1,0:T(8,128)(2,1)S(1)}, u32[]{:S(2)}, u32[]{:S(2)}) collective-permute-start(bf16[2,32,512]{2,1,0:T(8,128)(2,1)S(1)} %get-tuple-element.93), channel_id=1, source_target_pairs={{0,24},{1,25},{2,26},{3,27},{4,28},{5,29},{6,30},{7,31},{8,16},{9,... | collective-permute-start | bytes 196616 | tf_op jit(solution)/shard_map/ppermute | solution.py:286
  18.8 0.3 collective-permute-start.3
  19.1 2.9 %fusion = (bf16[32,32,1280]{2,1,0:T(8,128)(2,1)S(1)}, bf16[32,32,1280]{2,1,0:T(8,128)(2,1)S(1)}) fusion(bf16[160,32,1280]{2,1,0:T(8,128)(2,1)} %param.5), kind=kLoop, calls=%fused_computation.18 | loop fusion | bytes 10485760 | tf_op jit(solution)/shard_map/slice | solution.py:289
  22.0 0.0 copy-start
  22.0 0.0 collective-permute-done.5.refs_3_
  22.0 0.0 collective-permute-done.4.refs_2_
  22.0 1.0 %collective-permute-done.3.refs_1_ = bf16[2,32,512]{2,1,0:T(8,128)(2,1)S(1)} collective-permute-done((bf16[2,32,512]{2,1,0:T(8,128)(2,1)S(1)}, bf16[2,32,512]{2,1,0:T(8,128)(2,1)S(1)}, u32[]{:S(2)}, u32[]{:S(2)}) %collective-permute-start.3) | collective-permute-done | bytes 65568 | tf_op jit(solution)/shard_map/ppermute | solution.py:286
  23.0 1.4 %product.5 = (bf16[480,256]{1,0:T(8,128)(2,1)S(1)}, f32[480,256]{1,0:T(8,128)S(1)}, bf16[480,256]{1,0:T(8,128)(2,1)S(1)}, f32[480,256]{1,0:T(8,128)S(1)}) custom-call(bf16[1024,256]{1,0:T(8,128)(2,1)S(1)} %get-tuple-element.79.place_ref, bf16[32,32,1280]{2,1,0:T(8,128)(2,1)S(1)} %copy-done.1, bf16[2,32,512]{2,1,0:T(8,128)(2,1)S(1)} %get-tuple-element.141.refs_0_, ...), custom_call_target="tpu_custom_call" | custom-call | bytes 1024 | tf_op jit(solution)/shard_map/product/pallas_call | solution.py:312
  24.5 0.1 collective-permute-start.6
  24.5 0.5 collective-permute-start.8
  25.0 1.0 %collective-permute-done.6 = bf16[480,256]{1,0:T(8,128)(2,1)S(1)} collective-permute-done((bf16[480,256]{1,0:T(8,128)(2,1)S(1)}, bf16[480,256]{1,0:T(8,128)(2,1)S(1)}, u32[]{:S(2)}, u32[]{:S(2)}) %collective-permute-start.6) | collective-permute-done | bytes 245792 | tf_op jit(solution)/shard_map/ppermute | solution.py:306
  26.0 0.1 add_convert_fusion.4
  26.1 1.6 %collective-permute-start.20 = (bf16[480,256]{1,0:T(8,128)(2,1)S(1)}, bf16[480,256]{1,0:T(8,128)(2,1)S(1)}, u32[]{:S(2)}, u32[]{:S(2)}) collective-permute-start(bf16[480,256]{1,0:T(8,128)(2,1)S(1)} %add_convert_fusion.4), channel_id=1, source_target_pairs={{0,16},{8,24},{16,0},{24,8},{1,17},{9,25},{17,1},{25,9},{2,18},{10... | collective-permute-start | bytes 737288 | tf_op jit(solution)/shard_map/ppermute | solution.py:324
  27.7 1.4 %product.6 = (bf16[480,256]{1,0:T(8,128)(2,1)S(1)}, f32[480,256]{1,0:T(8,128)S(1)}, bf16[480,256]{1,0:T(8,128)(2,1)S(1)}, f32[480,256]{1,0:T(8,128)S(1)}) custom-call(bf16[1024,256]{1,0:T(8,128)(2,1)S(1)} %get-tuple-element.79.place_ref, bf16[32,32,1280]{2,1,0:T(8,128)(2,1)S(1)} %copy-done, bf16[2,32,512]{2,1,0:T(8,128)(2,1)S(1)} %get-tuple-element.141.refs_0_, ...), custom_call_target="tpu_custom_call" | custom-call | bytes 1024 | tf_op jit(solution)/shard_map/product/pallas_call | solution.py:312
  29.1 0.1 collective-permute-start.7
  29.2 0.5 collective-permute-start.10
  29.7 0.0 collective-permute-done.8
  29.7 0.9 %collective-permute-done.7 = bf16[480,256]{1,0:T(8,128)(2,1)S(1)} collective-permute-done((bf16[480,256]{1,0:T(8,128)(2,1)S(1)}, bf16[480,256]{1,0:T(8,128)(2,1)S(1)}, u32[]{:S(2)}, u32[]{:S(2)}) %collective-permute-start.7) | collective-permute-done | bytes 245792 | tf_op jit(solution)/shard_map/ppermute | solution.py:306
  30.7 0.1 add_convert_fusion.3
  30.7 0.6 %collective-permute-start.19 = (bf16[480,256]{1,0:T(8,128)(2,1)S(1)}, bf16[480,256]{1,0:T(8,128)(2,1)S(1)}, u32[]{:S(2)}, u32[]{:S(2)}) collective-permute-start(bf16[480,256]{1,0:T(8,128)(2,1)S(1)} %add_convert_fusion.3), channel_id=1, source_target_pairs={{0,16},{8,24},{16,0},{24,8},{1,17},{9,25},{17,1},{25,9},{2,18},{10... | collective-permute-start | bytes 737288 | tf_op jit(solution)/shard_map/ppermute | solution.py:324
  31.3 1.4 %product.7 = (bf16[480,256]{1,0:T(8,128)(2,1)S(1)}, f32[480,256]{1,0:T(8,128)S(1)}, bf16[480,256]{1,0:T(8,128)(2,1)S(1)}, f32[480,256]{1,0:T(8,128)S(1)}) custom-call(bf16[1024,256]{1,0:T(8,128)(2,1)S(1)} %get-tuple-element.79.place_ref, bf16[32,32,1280]{2,1,0:T(8,128)(2,1)S(1)} %get-tuple-element.127.leg_ref, ...), custom_call_target="tpu_custom_call" | custom-call | bytes 1024 | tf_op jit(solution)/shard_map/product/pallas_call | solution.py:312
  32.7 0.1 collective-permute-start.9
  32.8 0.5 collective-permute-start.12
  33.3 1.4 %collective-permute-done.20.far_ref = bf16[480,256]{1,0:T(8,128)(2,1)S(1)} collective-permute-done((bf16[480,256]{1,0:T(8,128)(2,1)S(1)}, bf16[480,256]{1,0:T(8,128)(2,1)S(1)}, u32[]{:S(2)}, u32[]{:S(2)}) %collective-permute-start.20) | collective-permute-done | bytes 245792 | tf_op jit(solution)/shard_map/ppermute | solution.py:324
  34.7 1.0 %final.5.refs_0_ = f32[12,160,320]{2,1,0:T(8,128)} custom-call(s32[160,128]{1,0:T(8,128)S(1)} %get-tuple-element.78.limits_ref, f32[480,256]{1,0:T(8,128)S(1)} %convert_add_fusion.4.near_ref, bf16[480,256]{1,0:T(8,128)(2,1)S(1)} %collective-permute-done.20.far_ref), custom_call_target="tpu_custom_call" | custom-call | bytes 1024 | tf_op jit(solution)/shard_map/final/pallas_call | solution.py:330
  35.7 0.0 collective-permute-done.10
  35.8 0.0 collective-permute-done.9
  35.8 0.1 add_convert_fusion.2
  35.8 1.8 %collective-permute-start.18 = (bf16[480,256]{1,0:T(8,128)(2,1)S(1)}, bf16[480,256]{1,0:T(8,128)(2,1)S(1)}, u32[]{:S(2)}, u32[]{:S(2)}) collective-permute-start(bf16[480,256]{1,0:T(8,128)(2,1)S(1)} %add_convert_fusion.2), channel_id=1, source_target_pairs={{0,16},{8,24},{16,0},{24,8},{1,17},{9,25},{17,1},{25,9},{2,18},{10... | collective-permute-start | bytes 737288 | tf_op jit(solution)/shard_map/ppermute | solution.py:324
  37.7 1.4 %product.8 = (bf16[480,256]{1,0:T(8,128)(2,1)S(1)}, f32[480,256]{1,0:T(8,128)S(1)}, bf16[480,256]{1,0:T(8,128)(2,1)S(1)}, f32[480,256]{1,0:T(8,128)S(1)}) custom-call(bf16[1024,256]{1,0:T(8,128)(2,1)S(1)} %get-tuple-element.79.place_ref, bf16[32,32,1280]{2,1,0:T(8,128)(2,1)S(1)} %get-tuple-element.136.leg_ref, ...), custom_call_target="tpu_custom_call" | custom-call | bytes 1024 | tf_op jit(solution)/shard_map/product/pallas_call | solution.py:312
  39.1 0.1 collective-permute-start.11
  39.2 0.5 collective-permute-start.16
  39.7 0.3 collective-permute-done.19.far_ref
  40.0 1.0 %final.6.refs_0_ = f32[12,160,320]{2,1,0:T(8,128)} custom-call(s32[160,128]{1,0:T(8,128)S(1)} %get-tuple-element.78.limits_ref, f32[480,256]{1,0:T(8,128)S(1)} %convert_add_fusion.3.near_ref, bf16[480,256]{1,0:T(8,128)(2,1)S(1)} %collective-permute-done.19.far_ref, f32[12,160,320]{2,1,0:T(8,128)} %final.5.refs_0_), custom_call_target="tpu_custom_call", output_to_operand_aliasing={{}: (3, {})} | custom-call | bytes 1024 | tf_op jit(solution)/shard_map/final/pallas_call | solution.py:330
  41.0 0.0 collective-permute-done.11
  41.0 0.1 add_convert_fusion.1
  41.1 1.8 %collective-permute-start.17 = (bf16[480,256]{1,0:T(8,128)(2,1)S(1)}, bf16[480,256]{1,0:T(8,128)(2,1)S(1)}, u32[]{:S(2)}, u32[]{:S(2)}) collective-permute-start(bf16[480,256]{1,0:T(8,128)(2,1)S(1)} %add_convert_fusion.1), channel_id=1, source_target_pairs={{0,16},{8,24},{16,0},{24,8},{1,17},{9,25},{17,1},{25,9},{2,18},{10... | collective-permute-start | bytes 737288 | tf_op jit(solution)/shard_map/ppermute | solution.py:324
  42.9 1.4 %product.9 = (bf16[480,256]{1,0:T(8,128)(2,1)S(1)}, f32[480,256]{1,0:T(8,128)S(1)}, bf16[480,256]{1,0:T(8,128)(2,1)S(1)}, f32[480,256]{1,0:T(8,128)S(1)}) custom-call(bf16[1024,256]{1,0:T(8,128)(2,1)S(1)} %get-tuple-element.79.place_ref, bf16[32,32,1280]{2,1,0:T(8,128)(2,1)S(1)} %get-tuple-element.102.leg_ref, ...), custom_call_target="tpu_custom_call" | custom-call | bytes 1024 | tf_op jit(solution)/shard_map/product/pallas_call | solution.py:312
  44.4 0.1 collective-permute-start.13
  44.4 0.5 collective-permute-start.14
  44.9 0.3 collective-permute-done.18.far_ref
  45.2 1.0 %final.7.refs_0_ = f32[12,160,320]{2,1,0:T(8,128)} custom-call(s32[160,128]{1,0:T(8,128)S(1)} %get-tuple-element.78.limits_ref, f32[480,256]{1,0:T(8,128)S(1)} %convert_add_fusion.2.near_ref, bf16[480,256]{1,0:T(8,128)(2,1)S(1)} %collective-permute-done.18.far_ref, f32[12,160,320]{2,1,0:T(8,128)} %final.6.refs_0_), custom_call_target="tpu_custom_call", output_to_operand_aliasing={{}: (3, {})} | custom-call | bytes 1024 | tf_op jit(solution)/shard_map/final/pallas_call | solution.py:330
  46.2 0.0 collective-permute-done.16
  46.3 0.0 collective-permute-done.14
  46.3 0.1 add_convert_fusion
  46.4 1.8 %collective-permute-start.15 = (bf16[480,256]{1,0:T(8,128)(2,1)S(1)}, bf16[480,256]{1,0:T(8,128)(2,1)S(1)}, u32[]{:S(2)}, u32[]{:S(2)}) collective-permute-start(bf16[480,256]{1,0:T(8,128)(2,1)S(1)} %add_convert_fusion), channel_id=1, source_target_pairs={{0,16},{8,24},{16,0},{24,8},{1,17},{9,25},{17,1},{25,9},{2,18},{10... | collective-permute-start | bytes 737288 | tf_op jit(solution)/shard_map/ppermute | solution.py:324
  48.2 2.3 %collective-permute-done.17.far_ref = bf16[480,256]{1,0:T(8,128)(2,1)S(1)} collective-permute-done((bf16[480,256]{1,0:T(8,128)(2,1)S(1)}, bf16[480,256]{1,0:T(8,128)(2,1)S(1)}, u32[]{:S(2)}, u32[]{:S(2)}) %collective-permute-start.17) | collective-permute-done | bytes 245792 | tf_op jit(solution)/shard_map/ppermute | solution.py:324
  50.5 1.0 %final.8.refs_0_ = f32[12,160,320]{2,1,0:T(8,128)} custom-call(s32[160,128]{1,0:T(8,128)S(1)} %get-tuple-element.78.limits_ref, f32[480,256]{1,0:T(8,128)S(1)} %convert_add_fusion.near_ref, bf16[480,256]{1,0:T(8,128)(2,1)S(1)} %collective-permute-done.17.far_ref, f32[12,160,320]{2,1,0:T(8,128)} %final.7.refs_0_), custom_call_target="tpu_custom_call", output_to_operand_aliasing={{}: (3, {})} | custom-call | bytes 1024 | tf_op jit(solution)/shard_map/final/pallas_call | solution.py:330
  51.6 3.6 %collective-permute-done.15.far_ref = bf16[480,256]{1,0:T(8,128)(2,1)S(1)} collective-permute-done((bf16[480,256]{1,0:T(8,128)(2,1)S(1)}, bf16[480,256]{1,0:T(8,128)(2,1)S(1)}, u32[]{:S(2)}, u32[]{:S(2)}) %collective-permute-start.15) | collective-permute-done | bytes 245792 | tf_op jit(solution)/shard_map/ppermute | solution.py:324
  55.2 1.0 %final.9 = f32[12,160,320]{2,1,0:T(8,128)} custom-call(s32[160,128]{1,0:T(8,128)S(1)} %get-tuple-element.78.limits_ref, f32[480,256]{1,0:T(8,128)S(1)} %convert_add_fusion.1.near_ref, bf16[480,256]{1,0:T(8,128)(2,1)S(1)} %collective-permute-done.15.far_ref, f32[12,160,320]{2,1,0:T(8,128)} %final.8.refs_0_), custom_call_target="tpu_custom_call", output_to_operand_aliasing={{}: (3, {})} | custom-call | bytes 1024 | tf_op jit(solution)/shard_map/final/pallas_call | solution.py:330
  (17 shorter events, 0.3 us)
Async XLA Ops:
  0.0 0.9 %copy-start.2 = (bf16[8,12,1280]{2,0,1:T(8,128)(2,1)S(1)}, bf16[8,12,1280]{2,0,1:T(8,128)(2,1)}, u32[]{:S(2)}) copy-start(bf16[8,12,1280]{2,0,1:T(8,128)(2,1)} %param.3) | copy-start | bytes 737284
  0.9 0.7 %copy-start.3 = (s32[1280]{0:T(1024)S(1)}, s32[1280]{0:T(1024)}, u32[]{:S(2)}) copy-start(s32[1280]{0:T(1024)} %table_ref.1) | copy-start | bytes 15364
  2.5 11.7 %collective-permute-start = (bf16[2,32,512]{2,1,0:T(8,128)(2,1)S(1)}, bf16[2,32,512]{2,1,0:T(8,128)(2,1)}, u32[]{:S(2)}, u32[]{:S(2)}) collective-permute-start(bf16[2,32,512]{2,1,0:T(8,128)(2,1)S(1)} %get-tuple-element.81), channel_id=1, source_target_pairs={{0,2},{1,3},{2,0},{3,1},{4,6},{5,7},{6,4},{7,5},{8,10},{9,11},{10,... | collective-permute-start | bytes 196616 | tf_op jit(solution)/shard_map/ppermute | solution.py:262
  5.6 9.4 %collective-permute-start.1 = (bf16[2,32,512]{2,1,0:T(8,128)(2,1)S(1)}, bf16[2,32,512]{2,1,0:T(8,128)(2,1)}, u32[]{:S(2)}, u32[]{:S(2)}) collective-permute-start(bf16[2,32,512]{2,1,0:T(8,128)(2,1)S(1)} %get-tuple-element.82), channel_id=1, source_target_pairs={{0,4},{1,5},{2,6},{3,7},{4,0},{5,1},{6,2},{7,3},{8,12},{9,13},{10,... | collective-permute-start | bytes 196616 | tf_op jit(solution)/shard_map/ppermute | solution.py:262
  8.1 5.1 %copy-start.4 = (s32[1280]{0:T(1024)S(1)}, s32[1280]{0:T(1024)}, u32[]{:S(2)}) copy-start(s32[1280]{0:T(1024)} %table_ref.1) | copy-start | bytes 15364
  8.1 7.6 %collective-permute-start.2 = (bf16[2,32,512]{2,1,0:T(8,128)(2,1)S(1)}, bf16[2,32,512]{2,1,0:T(8,128)(2,1)S(1)}, u32[]{:S(2)}, u32[]{:S(2)}) collective-permute-start(bf16[2,32,512]{2,1,0:T(8,128)(2,1)S(1)} %get-tuple-element.83), channel_id=1, source_target_pairs={{0,6},{1,7},{2,4},{3,5},{4,2},{5,3},{6,0},{7,1},{8,14},{9,15},{10,... | collective-permute-start | bytes 196616 | tf_op jit(solution)/shard_map/ppermute | solution.py:262
  15.8 7.2 %copy-start.1 = (bf16[32,32,1280]{2,1,0:T(8,128)(2,1)S(1)}, bf16[32,32,1280]{2,1,0:T(8,128)(2,1)}, u32[]{:S(2)}) copy-start(bf16[32,32,1280]{2,1,0:T(8,128)(2,1)} %get-tuple-element.111.leg_ref) | copy-start | bytes 7864324
  15.8 6.2 %collective-permute-start.5 = (bf16[2,32,512]{2,1,0:T(8,128)(2,1)S(1)}, bf16[2,32,512]{2,1,0:T(8,128)(2,1)S(1)}, u32[]{:S(2)}, u32[]{:S(2)}) collective-permute-start(bf16[2,32,512]{2,1,0:T(8,128)(2,1)S(1)} %get-tuple-element.97), channel_id=1, source_target_pairs={{0,25},{1,24},{2,27},{3,26},{4,29},{5,28},{6,31},{7,30},{8,17},{9,... | collective-permute-start | bytes 196616 | tf_op jit(solution)/shard_map/ppermute | solution.py:286
  17.2 4.8 %collective-permute-start.4 = (bf16[2,32,512]{2,1,0:T(8,128)(2,1)S(1)}, bf16[2,32,512]{2,1,0:T(8,128)(2,1)S(1)}, u32[]{:S(2)}, u32[]{:S(2)}) collective-permute-start(bf16[2,32,512]{2,1,0:T(8,128)(2,1)S(1)} %get-tuple-element.93), channel_id=1, source_target_pairs={{0,24},{1,25},{2,26},{3,27},{4,28},{5,29},{6,30},{7,31},{8,16},{9,... | collective-permute-start | bytes 196616 | tf_op jit(solution)/shard_map/ppermute | solution.py:286
  18.8 4.3 %collective-permute-start.3 = (bf16[2,32,512]{2,1,0:T(8,128)(2,1)S(1)}, bf16[2,32,512]{2,1,0:T(8,128)(2,1)S(1)}, u32[]{:S(2)}, u32[]{:S(2)}) collective-permute-start(bf16[2,32,512]{2,1,0:T(8,128)(2,1)S(1)} %get-tuple-element.89), channel_id=1, source_target_pairs={{0,1},{1,0},{2,3},{3,2},{4,5},{5,4},{6,7},{7,6},{8,9},{9,8},{10,11... | collective-permute-start | bytes 196616 | tf_op jit(solution)/shard_map/ppermute | solution.py:286
  22.0 5.7 %copy-start = (bf16[32,32,1280]{2,1,0:T(8,128)(2,1)S(1)}, bf16[32,32,1280]{2,1,0:T(8,128)(2,1)}, u32[]{:S(2)}) copy-start(bf16[32,32,1280]{2,1,0:T(8,128)(2,1)} %get-tuple-element.118.leg_ref) | copy-start | bytes 7864324
  24.5 1.6 %collective-permute-start.6 = (bf16[480,256]{1,0:T(8,128)(2,1)S(1)}, bf16[480,256]{1,0:T(8,128)(2,1)S(1)}, u32[]{:S(2)}, u32[]{:S(2)}) collective-permute-start(bf16[480,256]{1,0:T(8,128)(2,1)S(1)} %get-tuple-element.113), channel_id=1, source_target_pairs={{0,8},{8,0},{16,24},{24,16},{1,9},{9,1},{17,25},{25,17},{2,10},{10... | collective-permute-start | bytes 737288 | tf_op jit(solution)/shard_map/ppermute | solution.py:306
  24.5 5.2 %collective-permute-start.8 = (bf16[480,256]{1,0:T(8,128)(2,1)S(1)}, bf16[480,256]{1,0:T(8,128)(2,1)S(1)}, u32[]{:S(2)}, u32[]{:S(2)}) collective-permute-start(bf16[480,256]{1,0:T(8,128)(2,1)S(1)} %get-tuple-element.122), channel_id=1, source_target_pairs={{0,8},{8,0},{16,24},{24,16},{1,9},{9,1},{17,25},{25,17},{2,10},{10... | collective-permute-start | bytes 737288 | tf_op jit(solution)/shard_map/ppermute | solution.py:306
  26.1 8.6 %collective-permute-start.20 = (bf16[480,256]{1,0:T(8,128)(2,1)S(1)}, bf16[480,256]{1,0:T(8,128)(2,1)S(1)}, u32[]{:S(2)}, u32[]{:S(2)}) collective-permute-start(bf16[480,256]{1,0:T(8,128)(2,1)S(1)} %add_convert_fusion.4), channel_id=1, source_target_pairs={{0,16},{8,24},{16,0},{24,8},{1,17},{9,25},{17,1},{25,9},{2,18},{10... | collective-permute-start | bytes 737288 | tf_op jit(solution)/shard_map/ppermute | solution.py:324
  29.1 1.6 %collective-permute-start.7 = (bf16[480,256]{1,0:T(8,128)(2,1)S(1)}, bf16[480,256]{1,0:T(8,128)(2,1)S(1)}, u32[]{:S(2)}, u32[]{:S(2)}) collective-permute-start(bf16[480,256]{1,0:T(8,128)(2,1)S(1)} %get-tuple-element.120), channel_id=1, source_target_pairs={{0,8},{8,0},{16,24},{24,16},{1,9},{9,1},{17,25},{25,17},{2,10},{10... | collective-permute-start | bytes 737288 | tf_op jit(solution)/shard_map/ppermute | solution.py:306
  29.2 6.5 %collective-permute-start.10 = (bf16[480,256]{1,0:T(8,128)(2,1)S(1)}, bf16[480,256]{1,0:T(8,128)(2,1)S(1)}, u32[]{:S(2)}, u32[]{:S(2)}) collective-permute-start(bf16[480,256]{1,0:T(8,128)(2,1)S(1)} %get-tuple-element.131), channel_id=1, source_target_pairs={{0,8},{8,0},{16,24},{24,16},{1,9},{9,1},{17,25},{25,17},{2,10},{10... | collective-permute-start | bytes 737288 | tf_op jit(solution)/shard_map/ppermute | solution.py:306
  30.7 9.2 %collective-permute-start.19 = (bf16[480,256]{1,0:T(8,128)(2,1)S(1)}, bf16[480,256]{1,0:T(8,128)(2,1)S(1)}, u32[]{:S(2)}, u32[]{:S(2)}) collective-permute-start(bf16[480,256]{1,0:T(8,128)(2,1)S(1)} %add_convert_fusion.3), channel_id=1, source_target_pairs={{0,16},{8,24},{16,0},{24,8},{1,17},{9,25},{17,1},{25,9},{2,18},{10... | collective-permute-start | bytes 737288 | tf_op jit(solution)/shard_map/ppermute | solution.py:324
  32.7 3.0 %collective-permute-start.9 = (bf16[480,256]{1,0:T(8,128)(2,1)S(1)}, bf16[480,256]{1,0:T(8,128)(2,1)S(1)}, u32[]{:S(2)}, u32[]{:S(2)}) collective-permute-start(bf16[480,256]{1,0:T(8,128)(2,1)S(1)} %get-tuple-element.129), channel_id=1, source_target_pairs={{0,8},{8,0},{16,24},{24,16},{1,9},{9,1},{17,25},{25,17},{2,10},{10... | collective-permute-start | bytes 737288 | tf_op jit(solution)/shard_map/ppermute | solution.py:306
  32.8 8.2 %collective-permute-start.12 = (bf16[480,256]{1,0:T(8,128)(2,1)S(1)}, bf16[480,256]{1,0:T(8,128)(2,1)S(1)}, u32[]{:S(2)}, u32[]{:S(2)}) collective-permute-start(bf16[480,256]{1,0:T(8,128)(2,1)S(1)} %get-tuple-element.140), channel_id=1, source_target_pairs={{0,8},{8,0},{16,24},{24,16},{1,9},{9,1},{17,25},{25,17},{2,10},{10... | collective-permute-start | bytes 737288 | tf_op jit(solution)/shard_map/ppermute | solution.py:306
  35.8 9.4 %collective-permute-start.18 = (bf16[480,256]{1,0:T(8,128)(2,1)S(1)}, bf16[480,256]{1,0:T(8,128)(2,1)S(1)}, u32[]{:S(2)}, u32[]{:S(2)}) collective-permute-start(bf16[480,256]{1,0:T(8,128)(2,1)S(1)} %add_convert_fusion.2), channel_id=1, source_target_pairs={{0,16},{8,24},{16,0},{24,8},{1,17},{9,25},{17,1},{25,9},{2,18},{10... | collective-permute-start | bytes 737288 | tf_op jit(solution)/shard_map/ppermute | solution.py:324
  39.1 1.9 %collective-permute-start.11 = (bf16[480,256]{1,0:T(8,128)(2,1)S(1)}, bf16[480,256]{1,0:T(8,128)(2,1)S(1)}, u32[]{:S(2)}, u32[]{:S(2)}) collective-permute-start(bf16[480,256]{1,0:T(8,128)(2,1)S(1)} %get-tuple-element.138), channel_id=1, source_target_pairs={{0,8},{8,0},{16,24},{24,16},{1,9},{9,1},{17,25},{25,17},{2,10},{10... | collective-permute-start | bytes 737288 | tf_op jit(solution)/shard_map/ppermute | solution.py:306
  39.2 7.1 %collective-permute-start.16 = (bf16[480,256]{1,0:T(8,128)(2,1)S(1)}, bf16[480,256]{1,0:T(8,128)(2,1)S(1)}, u32[]{:S(2)}, u32[]{:S(2)}) collective-permute-start(bf16[480,256]{1,0:T(8,128)(2,1)S(1)} %get-tuple-element.150), channel_id=1, source_target_pairs={{0,8},{8,0},{16,24},{24,16},{1,9},{9,1},{17,25},{25,17},{2,10},{10... | collective-permute-start | bytes 737288 | tf_op jit(solution)/shard_map/ppermute | solution.py:306
  41.1 9.4 %collective-permute-start.17 = (bf16[480,256]{1,0:T(8,128)(2,1)S(1)}, bf16[480,256]{1,0:T(8,128)(2,1)S(1)}, u32[]{:S(2)}, u32[]{:S(2)}) collective-permute-start(bf16[480,256]{1,0:T(8,128)(2,1)S(1)} %add_convert_fusion.1), channel_id=1, source_target_pairs={{0,16},{8,24},{16,0},{24,8},{1,17},{9,25},{17,1},{25,9},{2,18},{10... | collective-permute-start | bytes 737288 | tf_op jit(solution)/shard_map/ppermute | solution.py:324
  44.4 7.1 %collective-permute-start.13 = (bf16[480,256]{1,0:T(8,128)(2,1)S(1)}, bf16[480,256]{1,0:T(8,128)(2,1)S(1)}, u32[]{:S(2)}, u32[]{:S(2)}) collective-permute-start(bf16[480,256]{1,0:T(8,128)(2,1)S(1)} %get-tuple-element.146), channel_id=1, source_target_pairs={{0,8},{8,0},{16,24},{24,16},{1,9},{9,1},{17,25},{25,17},{2,10},{10... | collective-permute-start | bytes 737288 | tf_op jit(solution)/shard_map/ppermute | solution.py:306
  44.4 1.9 %collective-permute-start.14 = (bf16[480,256]{1,0:T(8,128)(2,1)S(1)}, bf16[480,256]{1,0:T(8,128)(2,1)S(1)}, u32[]{:S(2)}, u32[]{:S(2)}) collective-permute-start(bf16[480,256]{1,0:T(8,128)(2,1)S(1)} %get-tuple-element.148), channel_id=1, source_target_pairs={{0,8},{8,0},{16,24},{24,16},{1,9},{9,1},{17,25},{25,17},{2,10},{10... | collective-permute-start | bytes 737288 | tf_op jit(solution)/shard_map/ppermute | solution.py:306
  46.4 8.8 %collective-permute-start.15 = (bf16[480,256]{1,0:T(8,128)(2,1)S(1)}, bf16[480,256]{1,0:T(8,128)(2,1)S(1)}, u32[]{:S(2)}, u32[]{:S(2)}) collective-permute-start(bf16[480,256]{1,0:T(8,128)(2,1)S(1)} %add_convert_fusion), channel_id=1, source_target_pairs={{0,16},{8,24},{16,0},{24,8},{1,17},{9,25},{17,1},{25,9},{2,18},{10... | collective-permute-start | bytes 737288 | tf_op jit(solution)/shard_map/ppermute | solution.py:324
